TPU v7x, 32 devices: a whole 2x2x4 slice. The times are simulated.
32 devices in a mesh: row: 4 (over z), col: 8 (over y, x, core).
Axes of the slice: x: 2, y: 2, z: 4, core: 2. Of those that a mesh axis runs over, the one named last changes fastest.
Arguments:
- tokens: bfloat16 [8192, 2048], P('row', 'col'), may hold values from -6 to 6
- cotangent: bfloat16 [8192, 2048], P('row', 'col'), may hold values from -6 to 6
- dealing: int32 [8192], replicated, may hold values from 0 to 8191, each once
- doc_lengths: int32 [4, 4], P('row'), may hold values from 1 to 1024, 2048 in all within a row
- routes: int32 [8192, 6], P('row'), may hold values from 0 to 15, all different within a row; in each aligned block of 2048 rows (0 to 2047, 2048 to 4095, ...) at most 1024 rows name the same one
- gate_weights: float32 [8192, 6], P('row'), may hold values from 0.3 to 1
- attn_gain: bfloat16 [2048], P('row'), may hold values from 0.5 to 1.5
- w_query: bfloat16 [2048, 3072], P('row', 'col'), may hold values from -0.1875 to 0.1875
- w_latent: bfloat16 [2048, 576], P('row'), may hold values from -0.125 to 0.125
- latent_gain: bfloat16 [512], P('row'), may hold values from 0.5 to 1.5
- w_expand: bfloat16 [512, 4096], P('row', 'col'), may hold values from -0.25 to 0.25
- w_output: bfloat16 [2048, 2048], P('col', 'row'), may hold values from -1 to 1
- ffn_gain: bfloat16 [2048], P('row'), may hold values from 0.5 to 1.5
- shared_gate: bfloat16 [2048, 2816], P('row', 'col'), may hold values from -0.125 to 0.125
- shared_up: bfloat16 [2048, 2816], P('row', 'col'), may hold values from -0.125 to 0.125
- shared_down: bfloat16 [2816, 2048], P('col', 'row'), may hold values from -0.109375 to 0.109375
- expert_gate: bfloat16 [16, 2048, 1408], P('col', 'row'), may hold values from -0.125 to 0.125
- expert_up: bfloat16 [16, 2048, 1408], P('col', 'row'), may hold values from -0.125 to 0.125
- expert_down: bfloat16 [16, 1408, 2048], P('col', None, 'row'), may hold values from -0.15625 to 0.15625
Outputs:
- result: bfloat16 [8192, 2048], P('row', 'col')
- tokens_grad: bfloat16 [8192, 2048], P('row', 'col')
- attn_gain_grad: float32 [2048], P('row')
- w_query_grad: float32 [2048, 3072], P('row', 'col')
- w_latent_grad: float32 [2048, 576], P('row')
- latent_gain_grad: float32 [512], P('row')
- w_expand_grad: float32 [512, 4096], P('row', 'col')
- w_output_grad: float32 [2048, 2048], P('col', 'row')
- ffn_gain_grad: float32 [2048], P('row')
- shared_gate_grad: float32 [2048, 2816], P('row', 'col')
- shared_up_grad: float32 [2048, 2816], P('row', 'col')
- shared_down_grad: float32 [2816, 2048], P('col', 'row')
- expert_gate_grad: float32 [16, 2048, 1408], P('col', 'row')
- expert_up_grad: float32 [16, 2048, 1408], P('col', 'row')
- expert_down_grad: float32 [16, 1408, 2048], P('col', None, 'row')
Inputs may be any that keep to these rules, and one draw needn't show every extreme that they name: `dealing`: each number appears once. `doc_lengths`: each row holds 4 lengths that sum to 2048; its largest is exactly 1024. `routes`: a token's 6 experts differ; within the 2048 rows of one group no expert is named by more than 1024 rows, and some expert reaches 1024 in some groups.
All inputs are finite; a program needn't handle non-finite values.
Results may differ from a plain program's by a relative error of at most 0.023.
Values may be sent and summed in bfloat16 or wider, within the bound.
No kernel may reach another device: no remote copies, remote signals or barrier semaphores. Data moves between devices by JAX's collectives and lax.ppermute only.
A program may use at most 448 MiB of HBM per device.

v0:
```python
import jax
import jax.numpy as jnp
from jax import lax
from jax.sharding import PartitionSpec as P

D = 2048
NOPE = 128
ROPE = 64
VDIM = 128
LAT = 512
TOPK = 6


EPSILON = 1e-06


def rotate(value, position, orient):
    half_width = value.shape[-1] // 2
    frequency = 10000.0 ** (-jnp.arange(half_width, dtype=jnp.float32) / half_width)
    angles = position.astype(jnp.float32)[:, None] * frequency[None, :]
    shape_out = (value.shape[0],) + (1,) * (value.ndim - 2) + (half_width,)
    cosine = jnp.cos(angles).reshape(shape_out)
    sine_part = jnp.sin(angles).reshape(shape_out)
    first_half = value[..., :half_width]
    second = value[..., half_width:]
    return jnp.concatenate(
        [
            first_half * cosine - orient * second * sine_part,
            second * cosine + orient * first_half * sine_part,
        ],
        axis=-1,
    )


def documents(lengths_row, row_count):
    doc_ends = jnp.cumsum(lengths_row)
    starts = doc_ends - lengths_row
    row_number = jnp.arange(row_count, dtype=jnp.int32)
    document = jnp.sum((row_number[:, None] >= doc_ends[None, :]).astype(jnp.int32), axis=1)
    onehot = document[:, None] == jnp.arange(lengths_row.shape[0], dtype=jnp.int32)[None, :]
    position = row_number - jnp.sum(jnp.where(onehot, starts[None, :], 0), axis=1)
    return (document, position)


def expert_slots(flat_routes, expert, capacity):
    sentinel = flat_routes.shape[0]
    return jnp.nonzero(flat_routes == expert, size=capacity, fill_value=sentinel)[0].astype(
        jnp.int32
    )


def silu_parts(value):
    sigmoid_value = jax.nn.sigmoid(value)
    activation = value * sigmoid_value
    activ_slope = sigmoid_value * (1.0 + value * (1.0 - sigmoid_value))
    return (activation, activ_slope)


def norm_back(grad_normed, unit_rows, row_scale, gain_vector):
    scaled = grad_normed * gain_vector
    row_inner = jnp.mean(scaled * unit_rows, axis=-1, keepdims=True)
    return (row_scale * (scaled - unit_rows * row_inner), jnp.sum(grad_normed * unit_rows, axis=0))


def column_sum(partial_terms):
    return lax.psum_scatter(partial_terms, "col", scatter_dimension=1, tiled=True)


def column_total(partial_terms):
    return lax.psum(partial_terms, "col")


def body(
    tokens,
    cotangent,
    dealing,
    doc_lengths,
    routes,
    gate_weights,
    attn_gain,
    w_query,
    w_latent,
    latent_gain,
    w_expand,
    w_output,
    ffn_gain,
    shared_gate,
    shared_up,
    shared_down,
    expert_gate,
    expert_up,
    expert_down,
):
    group_rows = routes.shape[0]
    width_slice = tokens.shape[1]
    row_index = lax.axis_index("row")
    col_index = lax.axis_index("col")
    given_x, given_dy = (
        lax.all_gather(tokens, "row", axis=0, tiled=True),
        lax.all_gather(cotangent, "row", axis=0, tiled=True),
    )
    my_order = lax.dynamic_slice_in_dim(dealing, row_index * group_rows, group_rows)
    dealt_x = jnp.take(given_x, my_order, axis=0)
    dealt_dy = jnp.take(given_dy, my_order, axis=0)
    full_x, full_dy = (
        lax.all_gather(dealt_x, "col", axis=1, tiled=True),
        lax.all_gather(dealt_dy, "col", axis=1, tiled=True),
    )
    gain_one, query_w, latent_w, latent_g, expand_w, output_w = (
        lax.all_gather(attn_gain, "row", axis=0, tiled=True),
        lax.all_gather(w_query, "row", axis=0, tiled=True),
        lax.all_gather(w_latent, "row", axis=0, tiled=True),
        lax.all_gather(latent_gain, "row", axis=0, tiled=True),
        lax.all_gather(w_expand, "row", axis=0, tiled=True),
        lax.all_gather(w_output, "row", axis=1, tiled=True),
    )
    gain_two, shared_g_w, shared_u_w, shared_d_w, expert_g_w, expert_u_w, expert_d_w = (
        lax.all_gather(ffn_gain, "row", axis=0, tiled=True),
        lax.all_gather(shared_gate, "row", axis=0, tiled=True),
        lax.all_gather(shared_up, "row", axis=0, tiled=True),
        lax.all_gather(shared_down, "row", axis=1, tiled=True),
        lax.all_gather(expert_gate, "row", axis=1, tiled=True),
        lax.all_gather(expert_up, "row", axis=1, tiled=True),
        lax.all_gather(expert_down, "row", axis=2, tiled=True),
    )
    gain_one_f = gain_one.astype(jnp.float32)
    gain_two_f = gain_two.astype(jnp.float32)
    latent_g_f = latent_g.astype(jnp.float32)
    document, position = documents(doc_lengths[0], group_rows)
    head_count = query_w.shape[1] // (NOPE + ROPE)
    softmax_scale = (NOPE + ROPE) ** (-0.5)
    block_rows = min(512, group_rows)
    row_number = jnp.arange(group_rows, dtype=jnp.int32)
    residual = full_x.astype(jnp.float32)
    scale_one = lax.rsqrt(jnp.mean(residual * residual, axis=-1, keepdims=True) + EPSILON)
    unit_one = residual * scale_one
    normed_one = (unit_one * gain_one_f).astype(jnp.bfloat16)
    query_raw = jnp.dot(normed_one, query_w, preferred_element_type=jnp.float32)
    query_raw = query_raw.reshape(group_rows, head_count, NOPE + ROPE)
    query_heads = jnp.concatenate(
        [query_raw[..., :NOPE], rotate(query_raw[..., NOPE:], position, 1.0)], axis=-1
    ).astype(jnp.bfloat16)
    latent = jnp.dot(normed_one, latent_w, preferred_element_type=jnp.float32)
    latent_front = latent[:, :LAT]
    scale_lat = lax.rsqrt(jnp.mean(latent_front * latent_front, axis=-1, keepdims=True) + EPSILON)
    unit_lat = latent_front * scale_lat
    compressed = (unit_lat * latent_g_f).astype(jnp.bfloat16)
    rope_key = rotate(latent[:, LAT:], position, 1.0).astype(jnp.bfloat16)
    expanded = jnp.dot(compressed, expand_w, preferred_element_type=jnp.float32).astype(
        jnp.bfloat16
    )
    expanded = expanded.reshape(group_rows, head_count, NOPE + VDIM)
    key_heads = jnp.concatenate(
        [
            expanded[..., :NOPE],
            jnp.broadcast_to(rope_key[:, None, :], (group_rows, head_count, ROPE)),
        ],
        axis=-1,
    )
    value_heads = expanded[..., NOPE:]

    def block_scores(first_row, last_row):
        raw_scores = (
            jnp.einsum(
                "qhd,khd->hqk",
                query_heads[first_row:last_row],
                key_heads[:last_row],
                preferred_element_type=jnp.float32,
            )
            * softmax_scale
        )
        allowed = (document[first_row:last_row, None] == document[None, :last_row]) & (
            row_number[first_row:last_row, None] >= row_number[None, :last_row]
        )
        return jnp.where(allowed[None], raw_scores, -1e30)

    mixed_blocks = []
    lse_blocks = []
    for first_row in range(0, group_rows, block_rows):
        last_row = first_row + block_rows
        scores = block_scores(first_row, last_row)
        row_top = jnp.max(scores, axis=-1, keepdims=True)
        exp_scores = jnp.exp(scores - row_top)
        row_total = jnp.sum(exp_scores, axis=-1, keepdims=True)
        probs_low = (exp_scores / row_total).astype(jnp.bfloat16)
        lse_blocks.append(row_top[..., 0] + jnp.log(row_total[..., 0]))
        mixed_blocks.append(
            jnp.einsum(
                "hqk,khd->qhd",
                probs_low,
                value_heads[:last_row],
                preferred_element_type=jnp.float32,
            )
        )
    mixed = (
        jnp.concatenate(mixed_blocks, axis=0)
        .reshape(group_rows, head_count * VDIM)
        .astype(jnp.bfloat16)
    )
    attn_slice = column_sum(jnp.dot(mixed, output_w, preferred_element_type=jnp.float32))
    hidden_slice = dealt_x.astype(jnp.float32) + attn_slice
    hidden_one = lax.all_gather(hidden_slice, "col", axis=1, tiled=True)
    scale_two = lax.rsqrt(jnp.mean(hidden_one * hidden_one, axis=-1, keepdims=True) + EPSILON)
    unit_two = hidden_one * scale_two
    normed_two = (unit_two * gain_two_f).astype(jnp.bfloat16)
    shared_gate_out = jnp.dot(normed_two, shared_g_w, preferred_element_type=jnp.float32)
    shared_up_out = jnp.dot(normed_two, shared_u_w, preferred_element_type=jnp.float32)
    shared_act, shared_slope = silu_parts(shared_gate_out)
    shared_hidden = (shared_act * shared_up_out).astype(jnp.bfloat16)
    moe_terms = jnp.dot(shared_hidden, shared_d_w, preferred_element_type=jnp.float32)
    local_count = expert_g_w.shape[0]
    capacity = 4 * group_rows * TOPK // (3 * local_count * lax.axis_size("col"))
    flat_routes = routes.reshape(-1)
    sentinel = flat_routes.shape[0]
    picked = jnp.stack(
        [
            expert_slots(flat_routes, col_index * local_count + number, capacity)
            for number in range(local_count)
        ]
    )
    is_used = picked < sentinel
    token_of = (picked // TOPK).astype(jnp.int32)
    safe_token = jnp.minimum(token_of, group_rows - 1)
    weight = jnp.where(is_used, gate_weights.reshape(-1)[jnp.minimum(picked, sentinel - 1)], 0.0)
    expert_rows = normed_two[safe_token]
    expert_gate_out = jnp.einsum(
        "ecd,edf->ecf", expert_rows, expert_g_w, preferred_element_type=jnp.float32
    )
    expert_up_out = jnp.einsum(
        "ecd,edf->ecf", expert_rows, expert_u_w, preferred_element_type=jnp.float32
    )
    expert_act, expert_slope = silu_parts(expert_gate_out)
    expert_hidden = (expert_act * expert_up_out).astype(jnp.bfloat16)
    expert_result = jnp.einsum(
        "ecf,efd->ecd", expert_hidden, expert_d_w, preferred_element_type=jnp.float32
    )
    moe_terms = moe_terms.at[token_of.reshape(-1)].add(
        (weight[..., None] * expert_result).reshape(-1, D), mode="drop"
    )
    moe_slice = column_sum(moe_terms)
    result_slice = (hidden_slice + moe_slice).astype(jnp.bfloat16)
    shared_g_w, shared_u_w, shared_d_w, expert_g_w, expert_u_w, expert_d_w = (
        lax.all_gather(shared_gate, "row", axis=0, tiled=True),
        lax.all_gather(shared_up, "row", axis=0, tiled=True),
        lax.all_gather(shared_down, "row", axis=1, tiled=True),
        lax.all_gather(expert_gate, "row", axis=1, tiled=True),
        lax.all_gather(expert_up, "row", axis=1, tiled=True),
        lax.all_gather(expert_down, "row", axis=2, tiled=True),
    )
    grad_out_f = full_dy.astype(jnp.float32)
    shared_grad_hidden = jnp.dot(full_dy, shared_d_w.T, preferred_element_type=jnp.float32)
    grad_shared_down = jnp.dot(shared_hidden.T, full_dy, preferred_element_type=jnp.float32)
    shared_grad_gate = (shared_grad_hidden * shared_up_out * shared_slope).astype(jnp.bfloat16)
    shared_grad_up = (shared_grad_hidden * shared_act).astype(jnp.bfloat16)
    grad_shared_gate = jnp.dot(normed_two.T, shared_grad_gate, preferred_element_type=jnp.float32)
    grad_shared_up = jnp.dot(normed_two.T, shared_grad_up, preferred_element_type=jnp.float32)
    grad_normed_two = jnp.dot(
        shared_grad_gate, shared_g_w.T, preferred_element_type=jnp.float32
    ) + jnp.dot(shared_grad_up, shared_u_w.T, preferred_element_type=jnp.float32)
    expert_grad_result = (weight[..., None] * grad_out_f[safe_token]).astype(jnp.bfloat16)
    expert_grad_hidden = jnp.einsum(
        "ecd,efd->ecf", expert_grad_result, expert_d_w, preferred_element_type=jnp.float32
    )
    grad_expert_down = jnp.einsum(
        "ecf,ecd->efd", expert_hidden, expert_grad_result, preferred_element_type=jnp.float32
    )
    expert_grad_gate = (expert_grad_hidden * expert_up_out * expert_slope).astype(jnp.bfloat16)
    expert_grad_up = (expert_grad_hidden * expert_act).astype(jnp.bfloat16)
    grad_expert_gate = jnp.einsum(
        "ecd,ecf->edf", expert_rows, expert_grad_gate, preferred_element_type=jnp.float32
    )
    grad_expert_up = jnp.einsum(
        "ecd,ecf->edf", expert_rows, expert_grad_up, preferred_element_type=jnp.float32
    )
    grad_rows = jnp.einsum(
        "ecf,edf->ecd", expert_grad_gate, expert_g_w, preferred_element_type=jnp.float32
    )
    grad_rows = grad_rows + jnp.einsum(
        "ecf,edf->ecd", expert_grad_up, expert_u_w, preferred_element_type=jnp.float32
    )
    grad_normed_two = grad_normed_two.at[token_of.reshape(-1)].add(
        grad_rows.reshape(-1, D), mode="drop"
    )
    grad_normed_two = column_total(grad_normed_two)
    grad_hidden_part, grad_gain_two = norm_back(grad_normed_two, unit_two, scale_two, gain_two_f)
    grad_hidden_one = grad_out_f + grad_hidden_part
    grad_attn = grad_hidden_one.astype(jnp.bfloat16)
    grad_output_w = jnp.dot(mixed.T, grad_attn, preferred_element_type=jnp.float32)
    grad_mixed = jnp.dot(grad_attn, output_w.T, preferred_element_type=jnp.float32).astype(
        jnp.bfloat16
    )
    grad_mixed = grad_mixed.reshape(group_rows, head_count, VDIM)
    grad_query_blocks = []
    grad_keys = jnp.zeros((group_rows, head_count, NOPE + ROPE), jnp.float32)
    grad_values = jnp.zeros((group_rows, head_count, VDIM), jnp.float32)
    for block_number, first_row in enumerate(range(0, group_rows, block_rows)):
        last_row = first_row + block_rows
        scores = block_scores(first_row, last_row)
        probs_f = jnp.exp(scores - lse_blocks[block_number][..., None])
        probs_low = probs_f.astype(jnp.bfloat16)
        grad_block = grad_mixed[first_row:last_row]
        grad_probs = jnp.einsum(
            "qhd,khd->hqk", grad_block, value_heads[:last_row], preferred_element_type=jnp.float32
        )
        row_inner = jnp.sum(probs_f * grad_probs, axis=-1, keepdims=True)
        grad_scores = (probs_f * (grad_probs - row_inner)).astype(jnp.bfloat16)
        grad_values = grad_values.at[:last_row].add(
            jnp.einsum("hqk,qhd->khd", probs_low, grad_block, preferred_element_type=jnp.float32)
        )
        grad_query_blocks.append(
            softmax_scale
            * jnp.einsum(
                "hqk,khd->qhd",
                grad_scores,
                key_heads[:last_row],
                preferred_element_type=jnp.float32,
            )
        )
        grad_keys = grad_keys.at[:last_row].add(
            softmax_scale
            * jnp.einsum(
                "hqk,qhd->khd",
                grad_scores,
                query_heads[first_row:last_row],
                preferred_element_type=jnp.float32,
            )
        )
    grad_query = jnp.concatenate(grad_query_blocks, axis=0)
    grad_query_raw = (
        jnp.concatenate(
            [grad_query[..., :NOPE], rotate(grad_query[..., NOPE:], position, -1.0)], axis=-1
        )
        .astype(jnp.bfloat16)
        .reshape(group_rows, head_count * (NOPE + ROPE))
    )
    grad_query_w = jnp.dot(normed_one.T, grad_query_raw, preferred_element_type=jnp.float32)
    grad_normed_one = jnp.dot(grad_query_raw, query_w.T, preferred_element_type=jnp.float32)
    grad_expanded = jnp.concatenate([grad_keys[..., :NOPE], grad_values], axis=-1).astype(
        jnp.bfloat16
    )
    grad_expanded = grad_expanded.reshape(group_rows, head_count * (NOPE + VDIM))
    grad_expand_w = jnp.dot(compressed.T, grad_expanded, preferred_element_type=jnp.float32)
    grad_compressed = jnp.dot(grad_expanded, expand_w.T, preferred_element_type=jnp.float32)
    grad_rope_key = rotate(jnp.sum(grad_keys[..., NOPE:], axis=1), position, -1.0)
    grad_latent_sum = lax.psum(
        jnp.concatenate([grad_compressed, grad_rope_key], axis=1).astype(jnp.bfloat16), "col"
    ).astype(jnp.float32)
    grad_front, grad_latent_gain = norm_back(
        grad_latent_sum[:, :LAT], unit_lat, scale_lat, latent_g_f
    )
    grad_latent = jnp.concatenate([grad_front, grad_latent_sum[:, LAT:]], axis=1).astype(
        jnp.bfloat16
    )
    grad_latent_w = jnp.dot(normed_one.T, grad_latent, preferred_element_type=jnp.float32)
    latent_term = jnp.dot(grad_latent, latent_w.T, preferred_element_type=jnp.float32)
    grad_normed_one = column_total(grad_normed_one) + latent_term
    grad_input_part, grad_gain_one = norm_back(grad_normed_one, unit_one, scale_one, gain_one_f)
    grad_input = grad_hidden_one + grad_input_part
    grad_slice = lax.dynamic_slice_in_dim(
        grad_input, col_index * width_slice, width_slice, grad_input.ndim - 1
    ).astype(jnp.bfloat16)
    moe_grads = (
        lax.psum_scatter(
            grad_gain_two.astype(jnp.bfloat16), "row", scatter_dimension=0, tiled=True
        ).astype(jnp.float32),
        lax.psum_scatter(
            grad_shared_gate.astype(jnp.bfloat16), "row", scatter_dimension=0, tiled=True
        ).astype(jnp.float32),
        lax.psum_scatter(
            grad_shared_up.astype(jnp.bfloat16), "row", scatter_dimension=0, tiled=True
        ).astype(jnp.float32),
        lax.psum_scatter(
            grad_shared_down.astype(jnp.bfloat16), "row", scatter_dimension=1, tiled=True
        ).astype(jnp.float32),
        lax.psum_scatter(
            grad_expert_gate.astype(jnp.bfloat16), "row", scatter_dimension=1, tiled=True
        ).astype(jnp.float32),
        lax.psum_scatter(
            grad_expert_up.astype(jnp.bfloat16), "row", scatter_dimension=1, tiled=True
        ).astype(jnp.float32),
        lax.psum_scatter(
            grad_expert_down.astype(jnp.bfloat16), "row", scatter_dimension=2, tiled=True
        ).astype(jnp.float32),
    )
    attn_grads = (
        lax.psum_scatter(
            grad_gain_one.astype(jnp.bfloat16), "row", scatter_dimension=0, tiled=True
        ).astype(jnp.float32),
        lax.psum_scatter(
            grad_query_w.astype(jnp.bfloat16), "row", scatter_dimension=0, tiled=True
        ).astype(jnp.float32),
        lax.psum_scatter(
            grad_latent_w.astype(jnp.bfloat16), "row", scatter_dimension=0, tiled=True
        ).astype(jnp.float32),
        lax.psum_scatter(
            grad_latent_gain.astype(jnp.bfloat16), "row", scatter_dimension=0, tiled=True
        ).astype(jnp.float32),
        lax.psum_scatter(
            grad_expand_w.astype(jnp.bfloat16), "row", scatter_dimension=0, tiled=True
        ).astype(jnp.float32),
        lax.psum_scatter(
            grad_output_w.astype(jnp.bfloat16), "row", scatter_dimension=1, tiled=True
        ).astype(jnp.float32),
    )
    back_result, back_grad = (
        lax.all_gather(result_slice, "row", axis=0, tiled=True),
        lax.all_gather(grad_slice, "row", axis=0, tiled=True),
    )
    inverse = (
        jnp.zeros(dealing.shape, jnp.int32)
        .at[dealing]
        .set(jnp.arange(dealing.shape[0], dtype=jnp.int32))
    )
    my_inverse = lax.dynamic_slice_in_dim(inverse, row_index * group_rows, group_rows)
    return (
        jnp.take(back_result, my_inverse, axis=0),
        jnp.take(back_grad, my_inverse, axis=0),
        attn_grads[0],
        attn_grads[1],
        attn_grads[2],
        attn_grads[3],
        attn_grads[4],
        attn_grads[5],
        moe_grads[0],
        moe_grads[1],
        moe_grads[2],
        moe_grads[3],
        moe_grads[4],
        moe_grads[5],
        moe_grads[6],
    )


def solution(mesh):
    return jax.shard_map(
        body,
        mesh=mesh,
        in_specs=(
            P("row", "col"),
            P("row", "col"),
            P(),
            P("row", None),
            P("row", None),
            P("row", None),
            P("row"),
            P("row", "col"),
            P("row", None),
            P("row"),
            P("row", "col"),
            P("col", "row"),
            P("row"),
            P("row", "col"),
            P("row", "col"),
            P("col", "row"),
            P("col", "row", None),
            P("col", "row", None),
            P("col", None, "row"),
        ),
        out_specs=(
            P("row", "col"),
            P("row", "col"),
            P("row"),
            P("row", "col"),
            P("row", None),
            P("row"),
            P("row", "col"),
            P("col", "row"),
            P("row"),
            P("row", "col"),
            P("row", "col"),
            P("col", "row"),
            P("col", "row", None),
            P("col", "row", None),
            P("col", None, "row"),
        ),
        check_vma=False,
    )
```

profile of v0, /device:TPU:0, one launch (start us, length us, event | category | flops | bytes accessed | tf_op | source)
XLA Modules:
  0.0 3172.7 jit_solution(644645715776213110)
XLA Ops:
  10.1 83.0 %all-gather.20.cloned.1.call-done = bf16[8192,256]{1,0:T(8,128)(2,1)} async-done(((bf16[2048,256]{1,0:T(8,128)(2,1)}), bf16[8192,256]{1,0:T(8,128)(2,1)}) %all-gather.20.cloned.1.call-update) | async-done | bytes 4194320 | tf_op jit(solution)/shard_map/all_gather | solution.py:99
  102.4 71.5 %all-gather.46.cloned.1.call-done = bf16[8192,256]{1,0:T(8,128)(2,1)} async-done(((bf16[2048,256]{1,0:T(8,128)(2,1)}), bf16[8192,256]{1,0:T(8,128)(2,1)}) %all-gather.46.cloned.1.call-update) | async-done | bytes 4194320 | tf_op jit(solution)/shard_map/all_gather | solution.py:100
  187.2 11.9 all-gather
  206.7 15.8 all_gather.71
  226.0 13.6 all-gather.22.cloned.1.call-done
  244.7 33.4 %all-gather.26.cloned.1.call-done = bf16[2048,384]{1,0:T(8,128)(2,1)} async-done(((bf16[512,384]{1,0:T(8,128)(2,1)}), bf16[2048,384]{1,0:T(8,128)(2,1)}) %all-gather.26.cloned.1.call-update) | async-done | bytes 1572880 | tf_op jit(solution)/shard_map/all_gather | solution.py:111
  286.6 42.3 %all-gather.24.cloned.1.call-done = bf16[2048,576]{0,1:T(8,128)(2,1)} async-done(((bf16[512,576]{0,1:T(8,128)(2,1)}), bf16[2048,576]{0,1:T(8,128)(2,1)}) %all-gather.24.cloned.1.call-update) | async-done | bytes 2359312 | tf_op jit(solution)/shard_map/all_gather | solution.py:112
  372.4 114.2 %reduce-scatter.13.cloned.1.call-done = f32[2048,256]{1,0:T(8,128)} async-done(((f32[2048,2048]{1,0:T(8,128)}), f32[2048,256]{1,0:T(8,128)}) %reduce-scatter.13.cloned.1.call-update) | async-done | bytes 2097168 | tf_op jit(solution)/shard_map/reduce_scatter | solution.py:66
  496.2 85.2 %scatter_custom_fusion = s32[1024]{0:T(1024)S(1)} fusion(s32[12288]{0:T(1024)S(1)} %bitcast.216, s32[12288]{0:T(1024)S(1)} %broadcast.1028, s32[]{:T(128)} %constant.312.clone.1), kind=kCustom, calls=%fused_computation.286 | custom fusion | flops 12288 | bytes 4100 | tf_op jit(solution)/shard_map/scatter-add | solution.py:47
  583.8 85.2 %scatter_custom_fusion.1 = s32[1024]{0:T(1024)S(1)} fusion(s32[12288]{0:T(1024)S(1)} %bitcast.217, s32[12288]{0:T(1024)S(1)} %broadcast.1028, s32[]{:T(128)} %constant.312.clone.1), kind=kCustom, calls=%fused_computation.284 | custom fusion | flops 12288 | bytes 4100 | tf_op jit(solution)/shard_map/scatter-add | solution.py:47
  671.1 16.7 all-gather.2
  688.9 12.0 gather_fusion
  712.9 22.4 gather_fusion.2
  752.4 20.8 gather_fusion.1
  773.2 69.6 %all-gather.38.cloned.1.call-done = bf16[2,2048,1408]{2,1,0:T(8,128)(2,1)} async-done(((bf16[2,512,1408]{2,1,0:T(8,128)(2,1)}), bf16[2,2048,1408]{2,1,0:T(8,128)(2,1)}) %all-gather.38.cloned.1.call-update) | async-done | bytes 11534352 | tf_op jit(solution)/shard_map/all_gather | solution.py:122
  842.8 19.8 fusion.162
  862.6 181.1 %all-gather.40.cloned.1.call-done = bf16[2,2048,1408]{2,1,0:T(8,128)(2,1)} async-done(((bf16[2,512,1408]{2,1,0:T(8,128)(2,1)}), bf16[2,2048,1408]{2,1,0:T(8,128)(2,1)}) %all-gather.40.cloned.1.call-update) | async-done | bytes 11534352 | tf_op jit(solution)/shard_map/all_gather | solution.py:123
  1043.7 20.0 fusion.163
  1063.7 14.6 all-gather.32.cloned.1.call-done
  1086.8 26.9 all-gather.34.cloned.1.call-done
  1122.3 192.8 %all-gather.42.cloned.1.call-done = bf16[2,1408,2048]{2,1,0:T(8,128)(2,1)} async-done(((bf16[2,1408,512]{2,1,0:T(8,128)(2,1)}), bf16[2,1408,2048]{2,1,0:T(8,128)(2,1)}) %all-gather.42.cloned.1.call-update) | async-done | bytes 11534352 | tf_op jit(solution)/shard_map/all_gather | solution.py:124
  1315.1 29.8 multiply_convert_fusion.3
  1344.9 21.1 fusion.165
  1385.2 23.3 convolution_add_fusion.2
  1420.1 38.7 %scatter_fusion.1 = f32[2048,2048]{1,0:T(8,128)} fusion(f32[2048,2048]{1,0:T(8,128)} %convolution_add_fusion, s32[2048]{0:T(1024)S(1)} %bitcast.209, f32[2048,2048]{1,0:T(8,128)} %bitcast.170), kind=kCustom, calls=%fused_computation.11 | custom fusion | flops 4194304 | bytes 50339840 | tf_op jit(solution)/shard_map/scatter-add | solution.py:281
  1459.6 215.4 %all-reduce.10.cloned.1.call-done = f32[2048,2048]{1,0:T(8,128)} async-done(((f32[2048,2048]{1,0:T(8,128)}), f32[2048,2048]{1,0:T(8,128)}) %all-reduce.10.cloned.1.call-update) | async-done | bytes 16777232 | tf_op jit(solution)/shard_map/psum | solution.py:70
  1675.1 12.7 multiply_reduce_fusion
  1687.8 14.4 multiply_add_fusion
  1771.5 21.2 broadcast_multiply_fusion
  1792.8 39.2 %scatter_fusion = f32[2048,2048]{1,0:T(8,128)} fusion(f32[2048,2048]{1,0:T(8,128)} %fusion.161, s32[2048]{0:T(1024)S(1)} %bitcast.210, f32[2048,2048]{1,0:T(8,128)} %bitcast.171), kind=kCustom, calls=%fused_computation.9 | custom fusion | flops 4194304 | bytes 50339840 | tf_op jit(solution)/shard_map/scatter-add | solution.py:237
  1901.7 19.8 convolution_convert_fusion
  1921.8 19.9 convolution_convert_fusion.2
  1942.0 20.1 convolution_convert_fusion.1
  1962.2 71.8 %all-reduce.12.cloned.1.call-done = f32[2048,2048]{1,0:T(8,128)} async-done(((f32[2048,2048]{1,0:T(8,128)}), f32[2048,2048]{1,0:T(8,128)}) %all-reduce.12.cloned.1.call-update) | async-done | bytes 16777232 | tf_op jit(solution)/shard_map/psum | solution.py:70
  2034.0 21.1 multiply_reduce_fusion.1
  2059.5 94.5 %reduce-scatter.15.cloned.1.call-done = f32[2048,256]{1,0:T(8,128)} async-done(((f32[2048,2048]{1,0:T(8,128)}), f32[2048,256]{1,0:T(8,128)}) %reduce-scatter.15.cloned.1.call-update) | async-done | bytes 2097168 | tf_op jit(solution)/shard_map/reduce_scatter | solution.py:66
  2158.7 30.5 scatter_custom_fusion.3
  2191.4 32.7 %reduce-scatter.27.cloned.1.call-done = bf16[512,352]{0,1:T(8,128)(2,1)} async-done(((bf16[2048,352]{0,1:T(8,128)(2,1)}), bf16[512,352]{0,1:T(8,128)(2,1)}) %reduce-scatter.27.cloned.1.call-update) | async-done | bytes 360464 | tf_op jit(solution)/shard_map/reduce_scatter | solution.py:369
  2226.0 32.7 %reduce-scatter.29.cloned.1.call-done = bf16[352,512]{1,0:T(8,128)(2,1)} async-done(((bf16[352,2048]{1,0:T(8,128)(2,1)}), bf16[352,512]{1,0:T(8,128)(2,1)}) %reduce-scatter.29.cloned.1.call-update) | async-done | bytes 360464 | tf_op jit(solution)/shard_map/reduce_scatter | solution.py:372
  2260.6 21.6 reduce-scatter.21.cloned.1.call-done
  2283.8 26.6 reduce-scatter.23.cloned.1.call-done
  2312.2 34.5 %reduce-scatter.17.cloned.1.call-done = bf16[512,384]{1,0:T(8,128)(2,1)} async-done(((bf16[2048,384]{1,0:T(8,128)(2,1)}), bf16[512,384]{1,0:T(8,128)(2,1)}) %reduce-scatter.17.cloned.1.call-update) | async-done | bytes 393232 | tf_op jit(solution)/shard_map/reduce_scatter | solution.py:389
  2348.6 47.3 %reduce-scatter.19.cloned.1.call-done = bf16[512,576]{0,1:T(8,128)(2,1)} async-done(((bf16[2048,576]{0,1:T(8,128)(2,1)}), bf16[512,576]{0,1:T(8,128)(2,1)}) %reduce-scatter.19.cloned.1.call-update) | async-done | bytes 589840 | tf_op jit(solution)/shard_map/reduce_scatter | solution.py:392
  2410.8 182.0 %reduce-scatter.35.cloned.1.call-done = bf16[2,1408,512]{2,1,0:T(8,128)(2,1)} async-done(((bf16[2,1408,2048]{2,1,0:T(8,128)(2,1)}), bf16[2,1408,512]{2,1,0:T(8,128)(2,1)}) %reduce-scatter.35.cloned.1.call-update) | async-done | bytes 2883600 | tf_op jit(solution)/shard_map/reduce_scatter | solution.py:381
  2598.0 193.1 %reduce-scatter.31.cloned.1.call-done = bf16[2,512,1408]{2,1,0:T(8,128)(2,1)} async-done(((bf16[2,2048,1408]{2,1,0:T(8,128)(2,1)}), bf16[2,512,1408]{2,1,0:T(8,128)(2,1)}) %reduce-scatter.31.cloned.1.call-update) | async-done | bytes 2883600 | tf_op jit(solution)/shard_map/reduce_scatter | solution.py:375
  2795.7 193.6 %reduce-scatter.33.cloned.1.call-done = bf16[2,512,1408]{2,1,0:T(8,128)(2,1)} async-done(((bf16[2,2048,1408]{2,1,0:T(8,128)(2,1)}), bf16[2,512,1408]{2,1,0:T(8,128)(2,1)}) %reduce-scatter.33.cloned.1.call-update) | async-done | bytes 2883600 | tf_op jit(solution)/shard_map/reduce_scatter | solution.py:378
  2994.1 79.1 %all-gather.50.cloned.1.call-done = bf16[8192,256]{1,0:T(8,128)(2,1)} async-done(((bf16[2048,256]{1,0:T(8,128)(2,1)}), bf16[8192,256]{1,0:T(8,128)(2,1)}) %all-gather.50.cloned.1.call-update) | async-done | bytes 4194320 | tf_op jit(solution)/shard_map/all_gather | solution.py:407
  3082.6 72.1 %all-gather.44.cloned.1.call-done = bf16[8192,256]{1,0:T(8,128)(2,1)} async-done(((bf16[2048,256]{1,0:T(8,128)(2,1)}), bf16[8192,256]{1,0:T(8,128)(2,1)}) %all-gather.44.cloned.1.call-update) | async-done | bytes 4194320 | tf_op jit(solution)/shard_map/all_gather | solution.py:406
  (454 shorter events, 393.5 us)
Async XLA Ops:
  7.2 85.9 %all-gather.20.cloned.1.call-start = ((), (), s32[]{:S(2)}) async-start(), calls=%async_computation.12 | async-start | bytes 5242880 | tf_op jit(solution)/shard_map/all_gather | solution.py:99
  7.9 166.1 %all-gather.46.cloned.1.call-start = ((), (), s32[]{:S(2)}) async-start(), calls=%async_computation.27 | async-start | bytes 5242880 | tf_op jit(solution)/shard_map/all_gather | solution.py:100
  8.7 230.9 %all-gather.22.cloned.1.call-start = ((), (), s32[]{:S(2)}) async-start(), calls=%async_computation.13 | async-start | bytes 9437184 | tf_op jit(solution)/shard_map/all_gather | solution.py:106
  185.0 93.2 %all-gather.26.cloned.1.call-start = ((), (), s32[]{:S(2)}) async-start(), calls=%async_computation.15 | async-start | bytes 1966080 | tf_op jit(solution)/shard_map/all_gather | solution.py:111
  185.5 143.4 %all-gather.24.cloned.1.call-start = ((), (), s32[]{:S(2)}) async-start(), calls=%async_computation.14 | async-start | bytes 2949120 | tf_op jit(solution)/shard_map/all_gather | solution.py:112
  186.1 175.7 %all-gather.28.cloned.1.call-start = ((), (), s32[]{:S(2)}) async-start(), calls=%async_computation.16 | async-start | bytes 1310720 | tf_op jit(solution)/shard_map/all_gather | solution.py:115
  186.7 299.9 %reduce-scatter.13.cloned.1.call-start = ((), (), s32[]{:S(2)}) async-start(), calls=%async_computation.17 | async-start | bytes 18874368 | tf_op jit(solution)/shard_map/reduce_scatter | solution.py:66
  186.8 153.6 %copy-start.88 = (f32[32]{0:T(128)}, f32[32]{0:T(128)S(1)}, u32[]{:S(2)}) copy-start(f32[32]{0:T(128)S(1)} %multiply_power_fusion) | copy-start | bytes 388
  199.1 129.9 %copy-start.58 = (f32[4,1,512]{2,1,0:T(1,128)}, f32[4,1,512]{2,1,0:T(1,128)S(1)}, u32[]{:S(2)}) copy-start(f32[4,1,512]{2,1,0:T(1,128)S(1)} %convert_element_type.308) | copy-start | bytes 24580
  199.2 141.2 %copy-start.62 = (f32[2048]{0:T(1024)}, f32[2048]{0:T(1024)S(1)}, u32[]{:S(2)}) copy-start(f32[2048]{0:T(1024)S(1)} %subtract_convert_fusion.2) | copy-start | bytes 24580
  206.7 131.0 %copy-start.69 = (f32[4,1,128]{2,1,0:T(1,128)}, f32[4,1,128]{2,1,0:T(1,128)S(1)}, u32[]{:S(2)}) copy-start(f32[4,1,128]{2,1,0:T(1,128)S(1)} %convert_element_type.309) | copy-start | bytes 6148
  244.7 84.2 %copy-start.50 = (f32[2048]{0:T(1024)}, f32[2048]{0:T(1024)S(1)}, u32[]{:S(2)}) copy-start(f32[2048]{0:T(1024)S(1)} %add_rsqrt_fusion.2) | copy-start | bytes 24580
  371.6 115.0 %copy-start.15 = (bf16[2048,256]{1,0:T(8,128)(2,1)S(1)}, bf16[2048,256]{1,0:T(8,128)(2,1)}, u32[]{:S(2)}) copy-start(bf16[2048,256]{1,0:T(8,128)(2,1)} %get-tuple-element.178) | copy-start | bytes 3145732
  371.6 330.0 %all-gather.48.cloned.1.call-start = ((), (), s32[]{:S(2)}) async-start(), calls=%async_computation.28 | async-start | bytes 9437184 | tf_op jit(solution)/shard_map/all_gather | solution.py:107
  372.4 362.9 %all-gather.30.cloned.1.call-start = ((), (), s32[]{:S(2)}) async-start(), calls=%async_computation.18 | async-start | bytes 18874368 | tf_op jit(solution)/shard_map/all_gather | solution.py:202
  489.7 353.1 %all-gather.38.cloned.1.call-start = ((), (), s32[]{:S(2)}) async-start(), calls=%async_computation.22 | async-start | bytes 14417920 | tf_op jit(solution)/shard_map/all_gather | solution.py:122
  490.3 553.3 %all-gather.40.cloned.1.call-start = ((), (), s32[]{:S(2)}) async-start(), calls=%async_computation.23 | async-start | bytes 14417920 | tf_op jit(solution)/shard_map/all_gather | solution.py:123
  491.1 587.2 %all-gather.32.cloned.1.call-start = ((), (), s32[]{:S(2)}) async-start(), calls=%async_computation.19 | async-start | bytes 1802240 | tf_op jit(solution)/shard_map/all_gather | solution.py:119
  491.6 622.0 %all-gather.34.cloned.1.call-start = ((), (), s32[]{:S(2)}) async-start(), calls=%async_computation.20 | async-start | bytes 1802240 | tf_op jit(solution)/shard_map/all_gather | solution.py:120
  492.4 178.6 %copy-start.91 = (bf16[512]{0:T(512)(128)(2,1)S(1)}, bf16[512]{0:T(512)(128)(2,1)}, u32[]{:S(2)}) copy-start(bf16[512]{0:T(512)(128)(2,1)} %param.53) | copy-start | bytes 3076
  492.4 195.5 %copy-start.66 = (f32[2048,6]{0,1:T(8,128)S(1)}, f32[2048,6]{0,1:T(8,128)}, u32[]{:S(2)}) copy-start(f32[2048,6]{0,1:T(8,128)} %param.46) | copy-start | bytes 147460
  492.4 822.7 %all-gather.42.cloned.1.call-start = ((), (), s32[]{:S(2)}) async-start(), calls=%async_computation.24 | async-start | bytes 14417920 | tf_op jit(solution)/shard_map/all_gather | solution.py:124
  493.0 873.0 %all-gather.36.cloned.1.call-start = ((), (), s32[]{:S(2)}) async-start(), calls=%async_computation.21 | async-start | bytes 1802240 | tf_op jit(solution)/shard_map/all_gather | solution.py:121
  493.6 1181.5 %all-reduce.10.cloned.1.call-start = ((), (), s32[]{:S(2)}) async-start(), calls=%async_computation.29 | async-start | bytes 33554432 | tf_op jit(solution)/shard_map/psum | solution.py:70
  687.7 54.6 %copy-start.52 = (f32[4,1,512]{2,1,0:T(1,128)}, f32[4,1,512]{2,1,0:T(1,128)S(1)}, u32[]{:S(2)}) copy-start(f32[4,1,512]{2,1,0:T(1,128)S(1)} %convert_element_type.310) | copy-start | bytes 24580
  700.9 614.2 %copy-start.86 = (f32[2,1024]{1,0:T(2,128)}, f32[2,1024]{1,0:T(2,128)S(1)}, u32[]{:S(2)}) copy-start(f32[2,1024]{1,0:T(2,128)S(1)} %compare_select_fusion.8) | copy-start | bytes 24580
  1376.7 31.7 %copy-start.29 = (bf16[2048,352]{0,1:T(8,128)(2,1)}, bf16[2048,352]{0,1:T(8,128)(2,1)S(1)}, u32[]{:S(2)}) copy-start(bf16[2048,352]{0,1:T(8,128)(2,1)S(1)} %get-tuple-element.149) | copy-start | bytes 4325380
  1458.9 216.2 %copy-start.53 = (f32[4,1,512]{2,1,0:T(1,128)S(1)}, f32[4,1,512]{2,1,0:T(1,128)}, u32[]{:S(2)}) copy-start(f32[4,1,512]{2,1,0:T(1,128)} %copy-done.52) | copy-start | bytes 24580
  1458.9 216.2 %copy-start.55 = (f32[2048]{0:T(1024)S(1)}, f32[2048]{0:T(1024)}, u32[]{:S(2)}) copy-start(f32[2048]{0:T(1024)} %copy-done.54) | copy-start | bytes 24580
  1458.9 423.6 %all-reduce.14.cloned.1.call-start = ((), (), s32[]{:S(2)}) async-start(), calls=%async_computation.31 | async-start | bytes 4718592 | tf_op jit(solution)/shard_map/psum | solution.py:345
  1750.0 284.0 %all-reduce.12.cloned.1.call-start = ((), (), s32[]{:S(2)}) async-start(), calls=%async_computation.30 | async-start | bytes 33554432 | tf_op jit(solution)/shard_map/psum | solution.py:70
  1761.4 392.6 %reduce-scatter.15.cloned.1.call-start = ((), (), s32[]{:S(2)}) async-start(), calls=%async_computation.25 | async-start | bytes 18874368 | tf_op jit(solution)/shard_map/reduce_scatter | solution.py:66
  1832.1 357.4 %reduce-scatter.25.cloned.1.call-start = ((), (), s32[]{:S(2)}) async-start(), calls=%async_computation.37 | async-start | bytes 1802240 | tf_op jit(solution)/shard_map/reduce_scatter | solution.py:366
  1840.5 383.6 %reduce-scatter.27.cloned.1.call-start = ((), (), s32[]{:S(2)}) async-start(), calls=%async_computation.38 | async-start | bytes 1802240 | tf_op jit(solution)/shard_map/reduce_scatter | solution.py:369
  1848.6 410.1 %reduce-scatter.29.cloned.1.call-start = ((), (), s32[]{:S(2)}) async-start(), calls=%async_computation.39 | async-start | bytes 1802240 | tf_op jit(solution)/shard_map/reduce_scatter | solution.py:372
  1856.5 425.7 %reduce-scatter.21.cloned.1.call-start = ((), (), s32[]{:S(2)}) async-start(), calls=%async_computation.35 | async-start | bytes 655360 | tf_op jit(solution)/shard_map/reduce_scatter | solution.py:398
  1861.9 448.5 %reduce-scatter.23.cloned.1.call-start = ((), (), s32[]{:S(2)}) async-start(), calls=%async_computation.36 | async-start | bytes 1310720 | tf_op jit(solution)/shard_map/reduce_scatter | solution.py:401
  1871.9 474.8 %reduce-scatter.17.cloned.1.call-start = ((), (), s32[]{:S(2)}) async-start(), calls=%async_computation.33 | async-start | bytes 1966080 | tf_op jit(solution)/shard_map/reduce_scatter | solution.py:389
  1882.0 513.9 %reduce-scatter.19.cloned.1.call-start = ((), (), s32[]{:S(2)}) async-start(), calls=%async_computation.34 | async-start | bytes 2949120 | tf_op jit(solution)/shard_map/reduce_scatter | solution.py:392
  1901.5 691.3 %reduce-scatter.35.cloned.1.call-start = ((), (), s32[]{:S(2)}) async-start(), calls=%async_computation.42 | async-start | bytes 14417920 | tf_op jit(solution)/shard_map/reduce_scatter | solution.py:381
  1921.6 869.4 %reduce-scatter.31.cloned.1.call-start = ((), (), s32[]{:S(2)}) async-start(), calls=%async_computation.40 | async-start | bytes 14417920 | tf_op jit(solution)/shard_map/reduce_scatter | solution.py:375
  1941.7 1047.6 %reduce-scatter.33.cloned.1.call-start = ((), (), s32[]{:S(2)}) async-start(), calls=%async_computation.41 | async-start | bytes 14417920 | tf_op jit(solution)/shard_map/reduce_scatter | solution.py:378
  1962.1 1111.1 %all-gather.50.cloned.1.call-start = ((), (), s32[]{:S(2)}) async-start(), calls=%async_computation.32 | async-start | bytes 5242880 | tf_op jit(solution)/shard_map/all_gather | solution.py:407
  2055.1 98.9 %copy-start.8 = (f32[2048,256]{1,0:T(8,128)S(1)}, f32[2048,256]{1,0:T(8,128)}, u32[]{:S(2)}) copy-start(f32[2048,256]{1,0:T(8,128)} %convert_add_fusion) | copy-start | bytes 6291460
  2059.4 97.3 %copy-start.94 = (u32[32]{0:T(128)S(1)}, u32[32]{0:T(128)}, u32[]{:S(2)}) copy-start(u32[32]{0:T(128)} %constant.345) | copy-start | bytes 388
  2059.4 99.2 %copy-start.64 = (s32[8192]{0:T(1024)S(1)}, s32[8192]{0:T(1024)}, u32[]{:S(2)}) copy-start(s32[8192]{0:T(1024)} %param.43) | copy-start | bytes 98308
  2059.4 1095.2 %all-gather.44.cloned.1.call-start = ((), (), s32[]{:S(2)}) async-start(), calls=%async_computation.26 | async-start | bytes 5242880 | tf_op jit(solution)/shard_map/all_gather | solution.py:406
  2156.7 241.4 %copy-start.81 = (bf16[2048]{0:T(1024)(128)(2,1)S(1)}, bf16[2048]{0:T(1024)(128)(2,1)}, u32[]{:S(2)}) copy-start(bf16[2048]{0:T(1024)(128)(2,1)} %get-tuple-element.128) | copy-start | bytes 12292
  (82 other events, 406.4 us)
Sparse Core Ops, SparseCore 0:
  9.6 83.4 all-gather.19
  94.6 79.2 all-gather.45
  185.1 54.4 all-gather.21
  241.0 37.0 all-gather.25
  279.6 49.2 all-gather.23
  330.3 26.7 all-gather.27
  371.7 114.8 reduce-scatter.12
  489.0 55.9 all-gather.47
  546.9 93.2 all-gather.29
  641.6 201.1 all-gather.37
  844.4 199.2 all-gather.39
  1045.1 33.1 all-gather.31
  1079.8 33.8 all-gather.33
  1115.1 199.9 all-gather.41
  1316.5 33.1 all-gather.35
  1459.0 215.9 all-reduce.9
  1750.1 62.9 all-reduce.13
  1816.7 217.2 all-reduce.11
  2038.0 115.9 reduce-scatter.14
  2156.2 33.2 reduce-scatter.24
  2191.9 32.1 reduce-scatter.26
  2226.5 32.1 reduce-scatter.28
  2261.6 20.5 reduce-scatter.20
  2285.0 25.3 reduce-scatter.22
  2312.7 33.9 reduce-scatter.16
  2348.8 46.9 reduce-scatter.18
  2398.1 194.6 reduce-scatter.34
  2595.1 195.8 reduce-scatter.30
  2793.4 195.9 reduce-scatter.32
  2991.3 81.8 all-gather.49
  3075.4 79.2 all-gather.43
where the time goes:
time: 3180 us; the launch traced here: 3170 us
  waiting for transfers between devices  2150 us (68%)
  matrix products  405 us (13%)
  other arithmetic  388 us (12%)
  local copies, waits for them, and re-layouts  149 us (5%)
  blocking collectives  62.7 us (2%)
    psum x2, waiting for transfers between devices, column_total(): return lax.psum(partial_terms, 'col')  287 us
    reduce_scatter x2, waiting for transfers between devices, column_sum(): lax.psum_scatter(partial_terms, 'col', scatter_dimension=1, tiled=True)  209 us
    reduce_scatter x1, waiting for transfers between devices, body(): lax.psum_scatter(grad_expert_up.astype(jnp.bfloat16), 'row', scatter_dime...  194 us
    reduce_scatter x1, waiting for transfers between devices, body(): lax.psum_scatter(grad_expert_gate.astype(jnp.bfloat16), 'row', scatter_di...  193 us
    all_gather x1, waiting for transfers between devices, body(): lax.all_gather(expert_down, 'row', axis=2, tiled=True)  193 us
    reduce_scatter x1, waiting for transfers between devices, body(): lax.psum_scatter(grad_expert_down.astype(jnp.bfloat16), 'row', scatter_di...  182 us
    all_gather x1, waiting for transfers between devices, body(): lax.all_gather(expert_up, 'row', axis=1, tiled=True)  181 us
    scatter-add x2, other arithmetic, expert_slots(): jnp.nonzero(flat_routes == expert, size=capacity, fill_value=sentinel)[0]  170 us
  transfers between devices with their start and end apart: 31, of which 26 were waited for; matrix products, arithmetic and copies ran while one was open for 23% of the time, Pallas kernels for 0%

commit v1 on v0

v1 whole, which is shorter than its diff:
```python
import jax
import jax.numpy as jnp
from jax import lax
from jax.sharding import PartitionSpec as P

NOPE = 128
ROPE = 64
VDIM = 128
LAT = 512
TOPK = 6

EPSILON = 1e-06
F32 = jnp.float32
BF16 = jnp.bfloat16


def rotate(value, position, orient):
    half_width = value.shape[-1] // 2
    frequency = 10000.0 ** (-jnp.arange(half_width, dtype=F32) / half_width)
    angles = position.astype(F32)[:, None] * frequency[None, :]
    shape_out = (value.shape[0],) + (1,) * (value.ndim - 2) + (half_width,)
    cosine = jnp.cos(angles).reshape(shape_out)
    sine_part = jnp.sin(angles).reshape(shape_out)
    first_half = value[..., :half_width]
    second = value[..., half_width:]
    return jnp.concatenate(
        [
            first_half * cosine - orient * second * sine_part,
            second * cosine + orient * first_half * sine_part,
        ],
        axis=-1,
    )


def documents(lengths_row, row_count):
    doc_ends = jnp.cumsum(lengths_row)
    starts = doc_ends - lengths_row
    row_number = jnp.arange(row_count, dtype=jnp.int32)
    document = jnp.sum((row_number[:, None] >= doc_ends[None, :]).astype(jnp.int32), axis=1)
    onehot = document[:, None] == jnp.arange(lengths_row.shape[0], dtype=jnp.int32)[None, :]
    position = row_number - jnp.sum(jnp.where(onehot, starts[None, :], 0), axis=1)
    return (document, position)


def silu_parts(value):
    sigmoid_value = jax.nn.sigmoid(value)
    activation = value * sigmoid_value
    activ_slope = sigmoid_value * (1.0 + value * (1.0 - sigmoid_value))
    return (activation, activ_slope)


def norm_back(grad_normed, unit_rows, row_scale, gain_vector):
    scaled = grad_normed * gain_vector
    row_inner = jnp.mean(scaled * unit_rows, axis=-1, keepdims=True)
    return (row_scale * (scaled - unit_rows * row_inner), jnp.sum(grad_normed * unit_rows, axis=0))


def dot(left, right):
    return jnp.dot(left, right, preferred_element_type=F32)


def dot_nt(left, right):
    return lax.dot_general(left, right, (((1,), (1,)), ((), ())), preferred_element_type=F32)


def dot_tn(left, right):
    return lax.dot_general(left, right, (((0,), (0,)), ((), ())), preferred_element_type=F32)


def line_scatter(value, axis):
    count = lax.axis_size("row")
    index = lax.axis_index("row")
    width = value.shape[axis] // count

    def block(j):
        return lax.dynamic_slice_in_dim(value, jnp.clip(j, 0, count - 1) * width, width, axis)

    right, left = None, None
    for step in range(1, count):
        right_out, left_out = block(index + count - step), block(index - count + step)
        if right is not None:
            right_out = (right_out.astype(F32) + right.astype(F32)).astype(BF16)
            left_out = (left_out.astype(F32) + left.astype(F32)).astype(BF16)
        right = lax.ppermute(right_out, "row", [(j, j + 1) for j in range(0, step)])
        left = lax.ppermute(left_out, "row", [(j, j - 1) for j in range(count - step, count)])
    return block(index).astype(F32) + right.astype(F32) + left.astype(F32)


def swap(value, bit):
    return lax.ppermute(value, "col", [(j, j ^ bit) for j in range(lax.axis_size("col"))])


def chip_bits():
    return [1 << b for b in range(1, (lax.axis_size("col") - 1).bit_length())]


def cube_gather(block, axis):
    count = lax.axis_size("col")
    index = lax.axis_index("col")
    bits = chip_bits()
    half = block.shape[0] // 2
    kept, swapped = [], []
    for part, order in ((block[:half], bits), (block[half:], bits[::-1])):
        held, keys = part[None], [0]
        for bit in order:
            held = jnp.concatenate([held, swap(held, bit)], axis=0)
            keys = keys + [key ^ bit for key in keys]
        order_of = [keys.index(key) for key in range(0, count, 2)]
        kept.append((held, order_of))
    swapped = [swap(held, 1) for held, order_of in kept]
    out = []
    for j in range(count):
        rel = jnp.bitwise_xor(index, j)
        halves = []
        for (held, order_of), other in zip(kept, swapped):
            place = jnp.array(order_of, jnp.int32)[rel // 2]
            mine = lax.dynamic_index_in_dim(held, place, 0, False)
            theirs = lax.dynamic_index_in_dim(other, place, 0, False)
            halves.append(jnp.where(rel % 2 == 0, mine, theirs))
        out.append(jnp.concatenate(halves, axis=0))
    return jnp.concatenate(out, axis=axis)


def cube_scatter(value):
    count = lax.axis_size("col")
    index = lax.axis_index("col")
    bits = chip_bits()
    rows = value.shape[0] // count
    half = rows // 2
    evens = list(range(0, count, 2))

    def blocks(me):
        return jnp.stack(
            [
                lax.dynamic_slice_in_dim(value, jnp.bitwise_xor(me, key) * rows, rows, 0)
                for key in evens
            ]
        )

    got = swap(blocks(jnp.bitwise_xor(index, 1)), 1)
    total = (blocks(index).astype(F32) + got.astype(F32)).astype(BF16)
    parts = []
    for part, order in ((total[:, :half], bits), (total[:, half:], bits[::-1])):
        held = {key: part[n] for n, key in enumerate(evens)}
        for bit in order:
            leaving = [key for key in held if key & bit]
            arrived = swap(jnp.stack([held[key] for key in leaving]), bit)
            held = {
                key: (held[key].astype(F32) + arrived[leaving.index(key ^ bit)].astype(F32))
                for key in held
                if not key & bit
            }
            if len(held) > 1:
                held = {key: item.astype(BF16) for key, item in held.items()}
        parts.append(held[0])
    return jnp.concatenate(parts, axis=0)


def row_gather(shard, axis):
    return lax.all_gather(shard, "row", axis=axis, tiled=True)


def after(values, earlier):
    out = lax.optimization_barrier(tuple(values) + tuple(earlier))
    return out[: len(values)]


def col_gather(value, axis=0):
    return lax.all_gather(value, "col", axis=axis, tiled=True)


def col_scatter(value):
    return lax.psum_scatter(value, "col", scatter_dimension=0, tiled=True).astype(F32)


def body(
    tokens,
    cotangent,
    dealing,
    doc_lengths,
    routes,
    gate_weights,
    attn_gain,
    w_query,
    w_latent,
    latent_gain,
    w_expand,
    w_output,
    ffn_gain,
    shared_gate,
    shared_up,
    shared_down,
    expert_gate,
    expert_up,
    expert_down,
):
    group_rows = routes.shape[0]
    row_count = lax.axis_size("row")
    col_count = lax.axis_size("col")
    row_index = lax.axis_index("row")
    col_index = lax.axis_index("col")
    part_rows = group_rows // col_count
    local_count = expert_gate.shape[0]
    capacity = 4 * group_rows * TOPK // (3 * local_count * col_count)

    def my_part(value):
        return lax.dynamic_slice_in_dim(value, col_index * part_rows, part_rows, 0)

    my_order = lax.dynamic_slice_in_dim(dealing, row_index * group_rows, group_rows)
    token_ids = jnp.arange(group_rows, dtype=jnp.int32)
    given_ids = row_index * group_rows + token_ids
    my_inverse = jnp.sum(
        jnp.where(
            dealing[None, :] == given_ids[:, None],
            jnp.arange(dealing.shape[0], dtype=jnp.int32)[None, :],
            0,
        ),
        axis=1,
    )
    picks, weights = [], []
    slot_ids = jnp.arange(capacity, dtype=jnp.int32)
    for number in range(local_count):
        named = routes == (col_index * local_count + number)
        named_any = jnp.any(named, axis=1)
        running = jnp.cumsum(named_any.astype(jnp.int32))
        place = jnp.where(named_any, running - 1, -1)
        pick = place[None, :] == slot_ids[:, None]
        token_weight = jnp.sum(jnp.where(named, gate_weights, 0.0), axis=1)
        picks.append(pick.astype(BF16))
        weights.append(jnp.sum(jnp.where(pick, token_weight[None, :], 0.0), axis=1))
    document, position = documents(doc_lengths[0], group_rows)

    rows_in, dim = w_query.shape[0], w_query.shape[0] * row_count
    wide = attn_gain.shape[0]
    lat_width = latent_gain.shape[0]
    given_x = row_gather(tokens, 0)
    dealt_x = jnp.take(given_x, my_order, axis=0)
    gains = row_gather(jnp.concatenate([attn_gain, ffn_gain, latent_gain])[None], 0)
    gain_one = gains[:, :wide].reshape(-1).astype(F32)
    gain_two = gains[:, wide : 2 * wide].reshape(-1).astype(F32)
    latent_g = gains[:, 2 * wide :].reshape(-1).astype(F32)
    lat_rows = rows_in // col_count
    w_latent_s = lax.dynamic_slice_in_dim(w_latent, col_index * lat_rows, lat_rows, 0)
    latent_w = cube_gather(row_gather(w_latent_s, 0), 0)
    latent_w = latent_w.reshape(col_count, row_count, lat_rows, -1).transpose(1, 0, 2, 3)
    latent_w = latent_w.reshape(dim, -1)
    full_x = cube_gather(dealt_x, 1)

    (w_query_s, w_output_s, w_expand_s) = after((w_query, w_output, w_expand), (given_x,))
    query_w = row_gather(w_query_s, 0)
    expand_w = row_gather(w_expand_s, 0)
    output_w = row_gather(w_output_s, 1)
    (cotangent_s,) = after((cotangent,), (given_x,))
    given_dy = row_gather(cotangent_s, 0)
    dealt_dy = jnp.take(given_dy, my_order, axis=0)
    full_dy = cube_gather(dealt_dy, 1)

    expert_w = []
    earlier = [output_w, given_dy]
    for number in range(local_count):
        gu_s = jnp.concatenate([expert_gate[number], expert_up[number]], axis=1)
        (gu_s,) = after((gu_s,), (earlier[-2],))
        gate_up_w = row_gather(gu_s, 0)
        earlier.append(gate_up_w)
        (d_s,) = after((expert_down[number],), (earlier[-2],))
        down_w = row_gather(d_s, 1)
        earlier.append(down_w)
        expert_w.append((gate_up_w, down_w))
        if number == 0:
            sgu_s = jnp.concatenate([shared_gate, shared_up], axis=1)
            (sgu_s,) = after((sgu_s,), (earlier[-2],))
            shared_gu_w = row_gather(sgu_s, 0)
            earlier.append(shared_gu_w)
            (sd_s,) = after((shared_down,), (earlier[-2],))
            shared_d_w = row_gather(sd_s, 1)
            earlier.append(shared_d_w)

    head_count = query_w.shape[1] // (NOPE + ROPE)
    softmax_scale = (NOPE + ROPE) ** (-0.5)
    block_rows = min(512, group_rows)
    row_number = token_ids
    residual = full_x.astype(F32)
    scale_one = lax.rsqrt(jnp.mean(residual * residual, axis=-1, keepdims=True) + EPSILON)
    normed_one = (residual * scale_one * gain_one).astype(BF16)
    query_raw = dot(normed_one, query_w)
    query_raw = query_raw.reshape(group_rows, head_count, NOPE + ROPE)
    query_heads = jnp.concatenate(
        [query_raw[..., :NOPE], rotate(query_raw[..., NOPE:], position, 1.0)], axis=-1
    ).astype(BF16)
    latent = dot(normed_one, latent_w)
    latent_front = latent[:, :LAT]
    scale_lat = lax.rsqrt(jnp.mean(latent_front * latent_front, axis=-1, keepdims=True) + EPSILON)
    unit_lat = latent_front * scale_lat
    compressed = (unit_lat * latent_g).astype(BF16)
    rope_key = rotate(latent[:, LAT:], position, 1.0).astype(BF16)
    expanded = dot(compressed, expand_w).astype(BF16)
    expanded = expanded.reshape(group_rows, head_count, NOPE + VDIM)
    key_heads = jnp.concatenate(
        [
            expanded[..., :NOPE],
            jnp.broadcast_to(rope_key[:, None, :], (group_rows, head_count, ROPE)),
        ],
        axis=-1,
    )
    value_heads = expanded[..., NOPE:]

    def block_scores(first_row, last_row):
        raw_scores = (
            jnp.einsum(
                "qhd,khd->hqk",
                query_heads[first_row:last_row],
                key_heads[:last_row],
                preferred_element_type=F32,
            )
            * softmax_scale
        )
        allowed = (document[first_row:last_row, None] == document[None, :last_row]) & (
            row_number[first_row:last_row, None] >= row_number[None, :last_row]
        )
        return jnp.where(allowed[None], raw_scores, -1e30)

    mixed_blocks = []
    lse_blocks = []
    for first_row in range(0, group_rows, block_rows):
        last_row = first_row + block_rows
        scores = block_scores(first_row, last_row)
        row_top = jnp.max(scores, axis=-1, keepdims=True)
        exp_scores = jnp.exp(scores - row_top)
        row_total = jnp.sum(exp_scores, axis=-1, keepdims=True)
        probs_low = (exp_scores / row_total).astype(BF16)
        lse_blocks.append(row_top[..., 0] + jnp.log(row_total[..., 0]))
        mixed_blocks.append(
            jnp.einsum(
                "hqk,khd->qhd",
                probs_low,
                value_heads[:last_row],
                preferred_element_type=F32,
            )
        )
    mixed = (
        jnp.concatenate(mixed_blocks, axis=0).reshape(group_rows, head_count * VDIM).astype(BF16)
    )
    attn_part = cube_scatter(dot(mixed, output_w).astype(BF16))
    x_part = my_part(full_x).astype(F32)
    hidden_part = x_part + attn_part
    scale_two = lax.rsqrt(jnp.mean(hidden_part * hidden_part, axis=-1, keepdims=True) + EPSILON)
    unit_two = hidden_part * scale_two
    normed_two = cube_gather((unit_two * gain_two).astype(BF16), 0)

    def branch(rows, grad_result, gate_up_w, down_w):
        width = gate_up_w.shape[1] // 2
        gate_up = dot(rows, gate_up_w)
        gate_out, up_out = gate_up[:, :width], gate_up[:, width:]
        act, slope = silu_parts(gate_out)
        hidden = (act * up_out).astype(BF16)
        grad_hidden = dot_nt(grad_result, down_w)
        grad_gate_up = jnp.concatenate(
            [(grad_hidden * up_out * slope).astype(BF16), (grad_hidden * act).astype(BF16)], axis=1
        )
        result_rows = dot(hidden, down_w)
        grad_rows = dot_nt(grad_gate_up, gate_up_w)
        grad_down = line_scatter(dot_tn(hidden, grad_result).astype(BF16), 1)
        grad_gu = line_scatter(dot_tn(rows, grad_gate_up).astype(BF16), 0)
        return result_rows, grad_rows, grad_gu[:, :width], grad_gu[:, width:], grad_down

    moe_terms, grad_two, grad_shared_gate, grad_shared_up, grad_shared_down = branch(
        normed_two, full_dy, shared_gu_w, shared_d_w
    )
    grad_gates, grad_ups, grad_downs = [], [], []
    for number in range(local_count):
        gate_up_w, down_w = expert_w[number]
        pick, weight = picks[number], weights[number]
        rows = dot(pick, normed_two).astype(BF16)
        grad_result = (weight[:, None] * dot(pick, full_dy)).astype(BF16)
        result_rows, grad_rows, grad_gate, grad_up, grad_down = branch(
            rows, grad_result, gate_up_w, down_w
        )
        grad_gates.append(grad_gate)
        grad_ups.append(grad_up)
        grad_downs.append(grad_down)
        moe_terms = moe_terms + dot_tn(pick, (weight[:, None] * result_rows).astype(BF16))
        grad_two = grad_two + dot_tn(pick, grad_rows.astype(BF16))

    grad_two_part = col_scatter(grad_two.astype(BF16))
    dy_part = my_part(full_dy).astype(F32)
    hidden_back, gain_two_grad = norm_back(grad_two_part, unit_two, scale_two, gain_two)
    grad_hidden_part = dy_part + hidden_back
    grad_attn = col_gather(grad_hidden_part.astype(BF16))

    moe_part = col_scatter(moe_terms.astype(BF16))
    result_part = (hidden_part + moe_part).astype(BF16)
    result_slice = lax.all_to_all(result_part, "col", split_axis=1, concat_axis=0, tiled=True)
    back_result = lax.all_gather(result_slice, "row", axis=0, tiled=True)
    result = jnp.take(back_result, my_inverse, axis=0)

    grad_output_w = line_scatter(dot_tn(mixed, grad_attn).astype(BF16), 1)
    grad_mixed = dot_nt(grad_attn, output_w).astype(BF16)
    grad_mixed = grad_mixed.reshape(group_rows, head_count, VDIM)
    grad_query_blocks = []
    grad_keys = jnp.zeros((group_rows, head_count, NOPE + ROPE), F32)
    grad_values = jnp.zeros((group_rows, head_count, VDIM), F32)
    for block_number, first_row in enumerate(range(0, group_rows, block_rows)):
        last_row = first_row + block_rows
        scores = block_scores(first_row, last_row)
        probs_f = jnp.exp(scores - lse_blocks[block_number][..., None])
        probs_low = probs_f.astype(BF16)
        grad_block = grad_mixed[first_row:last_row]
        grad_probs = jnp.einsum(
            "qhd,khd->hqk", grad_block, value_heads[:last_row], preferred_element_type=F32
        )
        row_inner = jnp.sum(probs_f * grad_probs, axis=-1, keepdims=True)
        grad_scores = (probs_f * (grad_probs - row_inner)).astype(BF16)
        grad_values = grad_values.at[:last_row].add(
            jnp.einsum("hqk,qhd->khd", probs_low, grad_block, preferred_element_type=F32)
        )
        grad_query_blocks.append(
            softmax_scale
            * jnp.einsum(
                "hqk,khd->qhd", grad_scores, key_heads[:last_row], preferred_element_type=F32
            )
        )
        grad_keys = grad_keys.at[:last_row].add(
            softmax_scale
            * jnp.einsum(
                "hqk,qhd->khd",
                grad_scores,
                query_heads[first_row:last_row],
                preferred_element_type=F32,
            )
        )
    grad_query = jnp.concatenate(grad_query_blocks, axis=0)
    grad_query_raw = (
        jnp.concatenate(
            [grad_query[..., :NOPE], rotate(grad_query[..., NOPE:], position, -1.0)], axis=-1
        )
        .astype(BF16)
        .reshape(group_rows, head_count * (NOPE + ROPE))
    )
    grad_one = col_scatter(dot_nt(grad_query_raw, query_w).astype(BF16))
    grad_expanded = jnp.concatenate([grad_keys[..., :NOPE], grad_values], axis=-1).astype(BF16)
    grad_expanded = grad_expanded.reshape(group_rows, head_count * (NOPE + VDIM))
    grad_compressed = dot_nt(grad_expanded, expand_w)
    grad_rope_key = rotate(jnp.sum(grad_keys[..., NOPE:], axis=1), position, -1.0)
    grad_latent_part = col_scatter(
        jnp.concatenate([grad_compressed, grad_rope_key], axis=1).astype(BF16)
    )
    grad_front, latent_gain_grad = norm_back(
        grad_latent_part[:, :LAT], my_part(unit_lat), my_part(scale_lat), latent_g
    )
    grad_latent_part = jnp.concatenate([grad_front, grad_latent_part[:, LAT:]], axis=1).astype(BF16)
    latent_term = dot_nt(grad_latent_part, latent_w)
    grad_one = grad_one + latent_term
    scale_one_part = my_part(scale_one)
    input_back, gain_one_grad = norm_back(
        grad_one, x_part * scale_one_part, scale_one_part, gain_one
    )
    grad_input = (grad_hidden_part + input_back).astype(BF16)
    grad_slice = lax.all_to_all(grad_input, "col", split_axis=1, concat_axis=0, tiled=True)
    back_grad = lax.all_gather(grad_slice, "row", axis=0, tiled=True)
    tokens_grad = jnp.take(back_grad, my_inverse, axis=0)

    grad_query_w = line_scatter(dot_tn(normed_one, grad_query_raw).astype(BF16), 0)
    grad_expand_w = line_scatter(dot_tn(compressed, grad_expanded).astype(BF16), 0)
    grad_latent = col_gather(grad_latent_part)
    my_columns = lax.dynamic_index_in_dim(
        normed_one.reshape(group_rows, row_count, col_count, lat_rows), col_index, 2, False
    ).reshape(group_rows, row_count * lat_rows)
    grad_latent_w = col_gather(line_scatter(dot_tn(my_columns, grad_latent).astype(BF16), 0))
    gain_grads = lax.psum(
        jnp.concatenate([gain_one_grad, gain_two_grad, latent_gain_grad]), ("row", "col")
    )
    width_two = gain_one_grad.shape[0]
    width_lat = latent_gain_grad.shape[0]

    def my_rows(value):
        width = value.shape[0] // row_count
        return lax.dynamic_slice_in_dim(value, row_index * width, width, 0)

    return (
        result,
        tokens_grad,
        my_rows(gain_grads[:width_two]),
        grad_query_w,
        grad_latent_w,
        my_rows(gain_grads[2 * width_two : 2 * width_two + width_lat]),
        grad_expand_w,
        grad_output_w,
        my_rows(gain_grads[width_two : 2 * width_two]),
        grad_shared_gate,
        grad_shared_up,
        grad_shared_down,
        jnp.stack(grad_gates),
        jnp.stack(grad_ups),
        jnp.stack(grad_downs),
    )


def solution(mesh):
    return jax.shard_map(
        body,
        mesh=mesh,
        in_specs=(
            P("row", "col"),
            P("row", "col"),
            P(),
            P("row", None),
            P("row", None),
            P("row", None),
            P("row"),
            P("row", "col"),
            P("row", None),
            P("row"),
            P("row", "col"),
            P("col", "row"),
            P("row"),
            P("row", "col"),
            P("row", "col"),
            P("col", "row"),
            P("col", "row", None),
            P("col", "row", None),
            P("col", None, "row"),
        ),
        out_specs=(
            P("row", "col"),
            P("row", "col"),
            P("row"),
            P("row", "col"),
            P("row", None),
            P("row"),
            P("row", "col"),
            P("col", "row"),
            P("row"),
            P("row", "col"),
            P("row", "col"),
            P("col", "row"),
            P("col", "row", None),
            P("col", "row", None),
            P("col", None, "row"),
        ),
        check_vma=False,
    )
```

time: 3180 us -> 2340 us (0.74)
  waiting for transfers between devices: 2150 us -> 1000 us
  starting transfers between devices: 2.77 us -> 354 us
  other arithmetic: 388 us -> 246 us
  blocking collectives: 62.7 us -> 101 us
    reduce_scatter x12 -> x4, waiting for transfers between devices: 973 us -> 69.7 us  [col_scatter(): lax.psum_scatter(value, 'col', scatter_dimension=0, tiled=True).astype(F32)]
    ppermute x0 -> x89, waiting for transfers between devices: none -> 521 us  [the longest x30 262 us: line_scatter(): right = lax.ppermute(right_out, 'row', [(j, j + 1) for j in range(0, step)])]
    all_gather x16 -> x15, waiting for transfers between devices: 880 us -> 402 us  [the longest x10 376 us: row_gather(): return lax.all_gather(shard, 'row', axis=axis, tiled=True)]
    ppermute x0 -> x89, starting transfers between devices: none -> 344 us  [the longest x30 283 us: line_scatter(): right = lax.ppermute(right_out, 'row', [(j, j + 1) for j in range(0, step)])]
    psum x3 -> x0, waiting for transfers between devices: 287 us -> none  [the longest x2 287 us: column_total(): return lax.psum(partial_terms, 'col')]
    scatter-add x4 -> x0, other arithmetic: 248 us -> none  [the longest x2 170 us: expert_slots(): jnp.nonzero(flat_routes == expert, size=capacity, fill_value=sentinel)[0]]
    gather x6 -> x2, local copies, waits for them, and re-layouts: 73.9 us -> 18.8 us  [the longest x1 9.43 us: body(): tokens_grad = jnp.take(back_grad, my_inverse, axis=0)]
    psum x0 -> x1, blocking collectives: none -> 47 us  [body(): lax.psum(jnp.concatenate([gain_one_grad, gain_two_grad, latent_gain_grad]...]
  transfers between devices with their start and end apart: 31 -> 110, of which waited for: 26 -> 38; matrix products, arithmetic and copies ran while one was open for 23% -> 29% of each run, Pallas kernels for 0% -> 0%
where the time goes in v1:
time: 2340 us; the launch traced here: 2330 us
  waiting for transfers between devices  1000 us (43%)
  matrix products  425 us (18%)
  starting transfers between devices  354 us (15%)
  other arithmetic  246 us (11%)
  local copies, waits for them, and re-layouts  163 us (7%)
  blocking collectives  101 us (4%)
  between operations  33.9 us (1%)
    all_gather x10, waiting for transfers between devices, row_gather(): return lax.all_gather(shard, 'row', axis=axis, tiled=True)  376 us
    ppermute x30, starting transfers between devices, line_scatter(): right = lax.ppermute(right_out, 'row', [(j, j + 1) for j in range(0, step)])  283 us
    ppermute x30, waiting for transfers between devices, line_scatter(): right = lax.ppermute(right_out, 'row', [(j, j + 1) for j in range(0, step)])  262 us
    dot_general x14, matrix products, dot(): return jnp.dot(left, right, preferred_element_type=F32)  138 us
    ppermute x30, waiting for transfers between devices, line_scatter(): lax.ppermute(left_out, 'row', [(j, j - 1) for j in range(count - step, co...  136 us
    dot_general x14, matrix products, dot_tn(): lax.dot_general(left, right, (((0,), (0,)), ((), ())), preferred_element_...  135 us
    ppermute x29, waiting for transfers between devices, swap(): lax.ppermute(value, 'col', [(j, j ^ bit) for j in range(lax.axis_size('co...  123 us
    dot_general x10, matrix products, dot_nt(): lax.dot_general(left, right, (((1,), (1,)), ((), ())), preferred_element_...  111 us
  transfers between devices with their start and end apart: 110, of which 38 were waited for; matrix products, arithmetic and copies ran while one was open for 29% of the time, Pallas kernels for 0%

profile of v1, /device:TPU:0, one launch (start us, length us, event | category | flops | bytes accessed | tf_op | source)
XLA Modules:
  0.0 2325.7 jit_solution(13178654254175267361)
XLA Ops:
  8.0 85.1 %all-gather.18.cloned.1.call-done = bf16[8192,256]{1,0:T(8,128)(2,1)} async-done(((bf16[2048,256]{1,0:T(8,128)(2,1)}), bf16[8192,256]{1,0:T(8,128)(2,1)}) %all-gather.18.cloned.1.call-update) | async-done | bytes 4194320 | tf_op jit(solution)/shard_map/all_gather | solution.py:160
  101.0 20.2 all-gather.22.cloned.1.call-done
  123.1 15.3 all_gather.56
  141.7 13.3 all-gather.1
  204.2 11.2 gather_fusion.2
  246.7 17.6 collective-permute-done.4
  289.0 25.7 %all_gather.57 = bf16[512,512]{1,0:T(8,128)(2,1)S(1)} all-gather(bf16[128,512]{1,0:T(8,128)(2,1)S(1)} %copy-done.86), channel_id=1, replica_groups=mesh['row'=4,'col'=8] {'row'}, dimensions={0}, use_global_device_ids=true | all-gather | bytes 655360 | tf_op jit(solution)/shard_map/all_gather | solution.py:160
  355.0 96.9 %all-gather.24.cloned.1.call-done = bf16[2048,2816]{1,0:T(8,128)(2,1)} async-done(((bf16[512,2816]{1,0:T(8,128)(2,1)}), bf16[2048,2816]{1,0:T(8,128)(2,1)}) %all-gather.24.cloned.1.call-update) | async-done | bytes 11534352 | tf_op jit(solution)/shard_map/all_gather | solution.py:160
  471.2 87.1 %all-gather.30.cloned.1.call-done = bf16[1408,2048]{1,0:T(8,128)(2,1)} async-done(((bf16[1408,512]{1,0:T(8,128)(2,1)}), bf16[1408,2048]{1,0:T(8,128)(2,1)}) %all-gather.30.cloned.1.call-update) | async-done | bytes 5767184 | tf_op jit(solution)/shard_map/all_gather | solution.py:160
  571.5 46.4 %all-gather.26.cloned.1.call-done = bf16[2048,704]{0,1:T(8,128)(2,1)} async-done(((bf16[512,704]{0,1:T(8,128)(2,1)}), bf16[2048,704]{0,1:T(8,128)(2,1)}) %all-gather.26.cloned.1.call-update) | async-done | bytes 2883600 | tf_op jit(solution)/shard_map/all_gather | solution.py:160
  647.1 17.3 collective-permute-done.27
  672.2 12.3 collective-permute-done.13
  741.9 20.3 collective-permute-done.18
  817.7 16.2 fusion.191
  833.9 15.3 multiply_convert_fusion.10
  849.1 18.3 fusion.34
  867.4 14.2 fusion.4
  904.5 18.7 fusion.192
  923.2 37.9 %all-gather.36.cloned.1.call-done = bf16[1408,2048]{1,0:T(8,128)(2,1)} async-done(((bf16[1408,512]{1,0:T(8,128)(2,1)}), bf16[1408,2048]{1,0:T(8,128)(2,1)}) %all-gather.36.cloned.1.call-update) | async-done | bytes 5767184 | tf_op jit(solution)/shard_map/all_gather | solution.py:160
  961.1 16.6 multiply_convert_fusion.8
  977.7 18.3 fusion.33
  996.0 14.4 fusion
  1010.4 17.5 add_convert_fusion
  1027.9 69.7 %reduce-scatter.7.cloned.1.call-done = bf16[256,2048]{1,0:T(8,128)(2,1)} async-done(((bf16[2048,2048]{1,0:T(8,128)(2,1)}), bf16[256,2048]{1,0:T(8,128)(2,1)}) %reduce-scatter.7.cloned.1.call-update) | async-done | bytes 1048592 | tf_op jit(solution)/shard_map/reduce_scatter | solution.py:173
  1118.5 13.1 copy.237
  1131.8 26.0 %all-gather.40.cloned.1.call-done = bf16[2048,2048]{1,0:T(8,128)(2,1)} async-done(((bf16[256,2048]{1,0:T(8,128)(2,1)}), bf16[2048,2048]{1,0:T(8,128)(2,1)}) %all-gather.40.cloned.1.call-update) | async-done | bytes 8388624 | tf_op jit(solution)/shard_map/all_gather | solution.py:169
  1222.5 16.2 convolution_convert_fusion.1
  1288.5 14.6 fusion.6
  1303.1 41.8 %collective-permute-done.78 = bf16[1408,512]{1,0:T(8,128)(2,1)} collective-permute-done((bf16[1408,512]{1,0:T(8,128)(2,1)}, bf16[1408,512]{1,0:T(8,128)(2,1)}, u32[]{:S(2)}, u32[]{:S(2)}) %collective-permute-start.78) | collective-permute-done | bytes 1441824 | tf_op jit(solution)/shard_map/ppermute | solution.py:84
  1385.5 13.1 collective-permute-done.60
  1410.9 12.1 fusion.2
  1423.0 19.4 add_convert_fusion.1
  1442.6 18.3 convolution_convert_fusion
  1491.2 55.1 %collective-permute-done.61 = bf16[352,512]{1,0:T(8,128)(2,1)S(1)} collective-permute-done((bf16[352,512]{1,0:T(8,128)(2,1)S(1)}, bf16[352,512]{1,0:T(8,128)(2,1)S(1)}, u32[]{:S(2)}, u32[]{:S(2)}) %collective-permute-start.61) | collective-permute-done | bytes 360480 | tf_op jit(solution)/shard_map/ppermute | solution.py:84
  1599.5 35.5 %collective-permute-start.35 = (bf16[64,576]{0,1:T(8,128)(2,1)S(1)}, bf16[64,576]{0,1:T(8,128)(2,1)S(1)}, u32[]{:S(2)}, u32[]{:S(2)}) collective-permute-start(bf16[64,576]{0,1:T(8,128)(2,1)S(1)} %get-tuple-element.348), channel_id=1, source_target_pairs={{0,8},{1,9},{2,10},{3,11},{4,12},{5,13},{6,14},{7,15}} | collective-permute-start | bytes 221192 | tf_op jit(solution)/shard_map/ppermute | solution.py:84
  1639.9 37.7 %collective-permute-done.35 = bf16[64,576]{0,1:T(8,128)(2,1)S(1)} collective-permute-done((bf16[64,576]{0,1:T(8,128)(2,1)S(1)}, bf16[64,576]{0,1:T(8,128)(2,1)S(1)}, u32[]{:S(2)}, u32[]{:S(2)}) %collective-permute-start.35) | collective-permute-done | bytes 73760 | tf_op jit(solution)/shard_map/ppermute | solution.py:84
  1704.3 32.0 %collective-permute-start.37 = (bf16[64,576]{0,1:T(8,128)(2,1)S(1)}, bf16[64,576]{0,1:T(8,128)(2,1)S(1)}, u32[]{:S(2)}, u32[]{:S(2)}) collective-permute-start(bf16[64,576]{0,1:T(8,128)(2,1)S(1)} %get-tuple-element.346), channel_id=1, source_target_pairs={{0,8},{8,16},{16,24},{1,9},{9,17},{17,25},{2,10},{10,18},{18,26},{... | collective-permute-start | bytes 221192 | tf_op jit(solution)/shard_map/ppermute | solution.py:84
  1740.5 35.9 %collective-permute-start.55 = (bf16[512,704]{0,1:T(8,128)(2,1)}, bf16[512,704]{0,1:T(8,128)(2,1)}, u32[]{:S(2)}, u32[]{:S(2)}) collective-permute-start(bf16[512,704]{0,1:T(8,128)(2,1)} %get-tuple-element.286), channel_id=1, source_target_pairs={{0,8},{8,16},{16,24},{1,9},{9,17},{17,25},{2,10},{10,18},{18,26},{... | collective-permute-start | bytes 2162696 | tf_op jit(solution)/shard_map/ppermute | solution.py:84
  1784.0 51.6 %collective-permute-start.67 = (bf16[512,2816]{1,0:T(8,128)(2,1)}, bf16[512,2816]{1,0:T(8,128)(2,1)}, u32[]{:S(2)}, u32[]{:S(2)}) collective-permute-start(bf16[512,2816]{1,0:T(8,128)(2,1)} %get-tuple-element.213), channel_id=1, source_target_pairs={{0,8},{8,16},{16,24},{1,9},{9,17},{17,25},{2,10},{10,18},{18,26},{... | collective-permute-start | bytes 8650760 | tf_op jit(solution)/shard_map/ppermute | solution.py:84
  1878.8 36.0 %collective-permute-done.67 = bf16[512,2816]{1,0:T(8,128)(2,1)} collective-permute-done((bf16[512,2816]{1,0:T(8,128)(2,1)}, bf16[512,2816]{1,0:T(8,128)(2,1)}, u32[]{:S(2)}, u32[]{:S(2)}) %collective-permute-start.67) | collective-permute-done | bytes 2883616 | tf_op jit(solution)/shard_map/ppermute | solution.py:84
  1916.0 27.9 %collective-permute-done.70 = bf16[512,2816]{1,0:T(8,128)(2,1)} collective-permute-done((bf16[512,2816]{1,0:T(8,128)(2,1)}, bf16[512,2816]{1,0:T(8,128)(2,1)}, u32[]{:S(2)}, u32[]{:S(2)}) %collective-permute-start.70) | collective-permute-done | bytes 2883616 | tf_op jit(solution)/shard_map/ppermute | solution.py:85
  1951.3 25.2 %collective-permute-done.85 = bf16[1408,512]{1,0:T(8,128)(2,1)} collective-permute-done((bf16[1408,512]{1,0:T(8,128)(2,1)}, bf16[1408,512]{1,0:T(8,128)(2,1)}, u32[]{:S(2)}, u32[]{:S(2)}) %collective-permute-start.85) | collective-permute-done | bytes 1441824 | tf_op jit(solution)/shard_map/ppermute | solution.py:84
  1976.5 108.3 %collective-permute-done.88 = bf16[1408,512]{1,0:T(8,128)(2,1)S(1)} collective-permute-done((bf16[1408,512]{1,0:T(8,128)(2,1)S(1)}, bf16[1408,512]{1,0:T(8,128)(2,1)S(1)}, u32[]{:S(2)}, u32[]{:S(2)}) %collective-permute-start.88) | collective-permute-done | bytes 1441824 | tf_op jit(solution)/shard_map/ppermute | solution.py:85
  2127.0 12.4 collective-permute-start.47
  2162.5 11.6 collective-permute-done.29
  2191.8 15.9 collective-permute-done.30
  2217.0 14.7 collective-permute-start.31
  2249.7 47.0 %psum.7 = f32[4608]{0:T(1024)S(1)} all-reduce(f32[4608]{0:T(1024)S(1)} %pad_maximum_fusion.47), channel_id=1, replica_groups=mesh['row'=4,'col'=8] {'row','col'}, use_global_device_ids=true, to_apply=%region_40.42 | all-reduce | flops 4608 | bytes 36864 | tf_op jit(solution)/shard_map/psum | solution.py:469
  (922 shorter events, 844.9 us)
Async XLA Ops:
  7.2 85.9 %all-gather.18.cloned.1.call-start = ((), (), s32[]{:S(2)}) async-start(), calls=%async_computation.6 | async-start | bytes 5242880 | tf_op jit(solution)/shard_map/all_gather | solution.py:160
  7.9 113.2 %all-gather.22.cloned.1.call-start = ((), (), s32[]{:S(2)}) async-start(), calls=%async_computation.8 | async-start | bytes 1310720 | tf_op jit(solution)/shard_map/all_gather | solution.py:160
  93.1 111.1 %all-gather.28.cloned.1.call-start = ((), (), s32[]{:S(2)}) async-start(), calls=%async_computation.11 | async-start | bytes 5242880 | tf_op jit(solution)/shard_map/all_gather | solution.py:160
  93.9 232.4 %all-gather.20.cloned.1.call-start = ((), (), s32[]{:S(2)}) async-start(), calls=%async_computation.7 | async-start | bytes 1966080 | tf_op jit(solution)/shard_map/all_gather | solution.py:160
  94.4 357.5 %all-gather.24.cloned.1.call-start = ((), (), s32[]{:S(2)}) async-start(), calls=%async_computation.9 | async-start | bytes 14417920 | tf_op jit(solution)/shard_map/all_gather | solution.py:160
  121.2 437.2 %all-gather.30.cloned.1.call-start = ((), (), s32[]{:S(2)}) async-start(), calls=%async_computation.12 | async-start | bytes 7208960 | tf_op jit(solution)/shard_map/all_gather | solution.py:160
  266.1 53.0 %collective-permute-start.2 = (bf16[4,1024,256]{2,1,0:T(8,128)(2,1)S(1)}, bf16[4,1024,256]{2,1,0:T(8,128)(2,1)}, u32[]{:S(2)}, u32[]{:S(2)}) collective-permute-start(bf16[4,1024,256]{2,1,0:T(8,128)(2,1)S(1)} %pad_maximum_fusion.16), channel_id=1, source_target_pairs={{0,1},{1,0},{2,3},{3,2},{4,5},{5,4},{6,7},{7,6},{8,9},{9,8},{10,11... | collective-permute-start | bytes 6291464 | tf_op jit(solution)/shard_map/ppermute | solution.py:90
  314.7 303.2 %all-gather.26.cloned.1.call-start = ((), (), s32[]{:S(2)}) async-start(), calls=%async_computation.10 | async-start | bytes 3604480 | tf_op jit(solution)/shard_map/all_gather | solution.py:160
  452.0 333.9 %all-gather.32.cloned.1.call-start = ((), (), s32[]{:S(2)}) async-start(), calls=%async_computation.13 | async-start | bytes 1802240 | tf_op jit(solution)/shard_map/all_gather | solution.py:160
  558.4 346.1 %all-gather.34.cloned.1.call-start = ((), (), s32[]{:S(2)}) async-start(), calls=%async_computation.14 | async-start | bytes 14417920 | tf_op jit(solution)/shard_map/all_gather | solution.py:160
  568.7 70.7 %collective-permute-start.12 = (bf16[4,256,2048]{2,1,0:T(8,128)(2,1)}, bf16[4,256,2048]{2,1,0:T(8,128)(2,1)}, u32[]{:S(2)}, u32[]{:S(2)}) collective-permute-start(bf16[4,256,2048]{2,1,0:T(8,128)(2,1)} %pad_maximum_fusion.5), channel_id=1, source_target_pairs={{0,1},{1,0},{2,3},{3,2},{4,5},{5,4},{6,7},{7,6},{8,9},{9,8},{10,11... | collective-permute-start | bytes 12582920 | tf_op jit(solution)/shard_map/ppermute | solution.py:90
  618.0 343.1 %all-gather.36.cloned.1.call-start = ((), (), s32[]{:S(2)}) async-start(), calls=%async_computation.15 | async-start | bytes 7208960 | tf_op jit(solution)/shard_map/all_gather | solution.py:160
  785.9 311.7 %reduce-scatter.7.cloned.1.call-start = ((), (), s32[]{:S(2)}) async-start(), calls=%async_computation.18 | async-start | bytes 9437184 | tf_op jit(solution)/shard_map/reduce_scatter | solution.py:173
  1027.9 129.9 %all-gather.40.cloned.1.call-start = ((), (), s32[]{:S(2)}) async-start(), calls=%async_computation.19 | async-start | bytes 9437184 | tf_op jit(solution)/shard_map/all_gather | solution.py:169
  1103.2 146.6 %reduce-scatter.11.cloned.1.call-start = ((), (), s32[]{:S(2)}) async-start(), calls=%async_computation.21 | async-start | bytes 2654208 | tf_op jit(solution)/shard_map/reduce_scatter | solution.py:173
  1204.9 391.4 %all-gather.44.cloned.1.call-start = ((), (), s32[]{:S(2)}) async-start(), calls=%async_computation.23 | async-start | bytes 2654208 | tf_op jit(solution)/shard_map/all_gather | solution.py:169
  1221.8 81.3 %collective-permute-start.80 = (bf16[1408,512]{1,0:T(8,128)(2,1)}, bf16[1408,512]{1,0:T(8,128)(2,1)S(1)}, u32[]{:S(2)}, u32[]{:S(2)}) collective-permute-start(bf16[1408,512]{1,0:T(8,128)(2,1)} %get-tuple-element.236), channel_id=1, source_target_pairs={{24,16},{25,17},{26,18},{27,19},{28,20},{29,21},{30,22},{31,23}} | collective-permute-start | bytes 4325384 | tf_op jit(solution)/shard_map/ppermute | solution.py:85
  1244.7 129.8 %collective-permute-start.65 = (bf16[512,2816]{1,0:T(8,128)(2,1)}, bf16[512,2816]{1,0:T(8,128)(2,1)}, u32[]{:S(2)}, u32[]{:S(2)}) collective-permute-start(bf16[512,2816]{1,0:T(8,128)(2,1)} %get-tuple-element.215), channel_id=1, source_target_pairs={{0,8},{1,9},{2,10},{3,11},{4,12},{5,13},{6,14},{7,15}} | collective-permute-start | bytes 8650760 | tf_op jit(solution)/shard_map/ppermute | solution.py:84
  1247.6 310.9 %collective-permute-start.68 = (bf16[512,2816]{1,0:T(8,128)(2,1)}, bf16[512,2816]{1,0:T(8,128)(2,1)}, u32[]{:S(2)}, u32[]{:S(2)}) collective-permute-start(bf16[512,2816]{1,0:T(8,128)(2,1)} %get-tuple-element.216), channel_id=1, source_target_pairs={{24,16},{25,17},{26,18},{27,19},{28,20},{29,21},{30,22},{31,23}} | collective-permute-start | bytes 8650760 | tf_op jit(solution)/shard_map/ppermute | solution.py:85
  1254.7 524.1 %reduce-scatter.9.cloned.1.call-start = ((), (), s32[]{:S(2)}) async-start(), calls=%async_computation.20 | async-start | bytes 9437184 | tf_op jit(solution)/shard_map/reduce_scatter | solution.py:173
  1269.2 75.7 %collective-permute-start.78 = (bf16[1408,512]{1,0:T(8,128)(2,1)}, bf16[1408,512]{1,0:T(8,128)(2,1)}, u32[]{:S(2)}, u32[]{:S(2)}) collective-permute-start(bf16[1408,512]{1,0:T(8,128)(2,1)} %add_convert_fusion.18), channel_id=1, source_target_pairs={{0,8},{8,16},{1,9},{9,17},{2,10},{10,18},{3,11},{11,19},{4,12},{12... | collective-permute-start | bytes 4325384 | tf_op jit(solution)/shard_map/ppermute | solution.py:84
  1287.8 549.4 %reduce-scatter.5.cloned.1.call-start = ((), (), s32[]{:S(2)}) async-start(), calls=%async_computation.16 | async-start | bytes 9437184 | tf_op jit(solution)/shard_map/reduce_scatter | solution.py:173
  1349.8 140.0 %collective-permute-start.81 = (bf16[1408,512]{1,0:T(8,128)(2,1)}, bf16[1408,512]{1,0:T(8,128)(2,1)}, u32[]{:S(2)}, u32[]{:S(2)}) collective-permute-start(bf16[1408,512]{1,0:T(8,128)(2,1)} %get-tuple-element.234), channel_id=1, source_target_pairs={{16,8},{24,16},{17,9},{25,17},{18,10},{26,18},{19,11},{27,19},{20,... | collective-permute-start | bytes 4325384 | tf_op jit(solution)/shard_map/ppermute | solution.py:85
  1381.1 177.5 %collective-permute-start.66 = (bf16[512,2816]{1,0:T(8,128)(2,1)}, bf16[512,2816]{1,0:T(8,128)(2,1)}, u32[]{:S(2)}, u32[]{:S(2)}) collective-permute-start(bf16[512,2816]{1,0:T(8,128)(2,1)} %add_convert_fusion.10), channel_id=1, source_target_pairs={{0,8},{8,16},{1,9},{9,17},{2,10},{10,18},{3,11},{11,19},{4,12},{12... | collective-permute-start | bytes 8650760 | tf_op jit(solution)/shard_map/ppermute | solution.py:84
  1398.6 62.4 %collective-permute-start.56 = (bf16[512,704]{0,1:T(8,128)(2,1)}, bf16[512,704]{0,1:T(8,128)(2,1)}, u32[]{:S(2)}, u32[]{:S(2)}) collective-permute-start(bf16[512,704]{0,1:T(8,128)(2,1)} %get-tuple-element.289), channel_id=1, source_target_pairs={{24,16},{25,17},{26,18},{27,19},{28,20},{29,21},{30,22},{31,23}} | collective-permute-start | bytes 2162696 | tf_op jit(solution)/shard_map/ppermute | solution.py:85
  1401.1 70.5 %collective-permute-start.63 = (bf16[352,512]{1,0:T(8,128)(2,1)}, bf16[352,512]{1,0:T(8,128)(2,1)}, u32[]{:S(2)}, u32[]{:S(2)}) collective-permute-start(bf16[352,512]{1,0:T(8,128)(2,1)} %get-tuple-element.303), channel_id=1, source_target_pairs={{16,8},{24,16},{17,9},{25,17},{18,10},{26,18},{19,11},{27,19},{20,... | collective-permute-start | bytes 1081352 | tf_op jit(solution)/shard_map/ppermute | solution.py:85
  1442.4 804.6 %all-gather.46.cloned.1.call-start = ((), (), s32[]{:S(2)}) async-start(), calls=%async_computation.24 | async-start | bytes 1474560 | tf_op jit(solution)/shard_map/all_gather | solution.py:169
  1471.5 98.5 %collective-permute-start.71 = (bf16[512,2816]{1,0:T(8,128)(2,1)}, bf16[512,2816]{1,0:T(8,128)(2,1)}, u32[]{:S(2)}, u32[]{:S(2)}) collective-permute-start(bf16[512,2816]{1,0:T(8,128)(2,1)} %get-tuple-element.219), channel_id=1, source_target_pairs={{0,8},{1,9},{2,10},{3,11},{4,12},{5,13},{6,14},{7,15}} | collective-permute-start | bytes 8650760 | tf_op jit(solution)/shard_map/ppermute | solution.py:84
  1481.6 64.6 %collective-permute-start.61 = (bf16[352,512]{1,0:T(8,128)(2,1)S(1)}, bf16[352,512]{1,0:T(8,128)(2,1)S(1)}, u32[]{:S(2)}, u32[]{:S(2)}) collective-permute-start(bf16[352,512]{1,0:T(8,128)(2,1)S(1)} %get-tuple-element.302), channel_id=1, source_target_pairs={{0,8},{8,16},{16,24},{1,9},{9,17},{17,25},{2,10},{10,18},{18,26},{... | collective-permute-start | bytes 1081352 | tf_op jit(solution)/shard_map/ppermute | solution.py:84
  1489.9 60.4 %collective-permute-start.64 = (bf16[352,512]{1,0:T(8,128)(2,1)S(1)}, bf16[352,512]{1,0:T(8,128)(2,1)S(1)}, u32[]{:S(2)}, u32[]{:S(2)}) collective-permute-start(bf16[352,512]{1,0:T(8,128)(2,1)S(1)} %add_convert_fusion.32), channel_id=1, source_target_pairs={{8,0},{16,8},{24,16},{9,1},{17,9},{25,17},{10,2},{18,10},{26,18},{... | collective-permute-start | bytes 1081352 | tf_op jit(solution)/shard_map/ppermute | solution.py:85
  1550.3 233.7 %collective-permute-start.79 = (bf16[1408,512]{1,0:T(8,128)(2,1)}, bf16[1408,512]{1,0:T(8,128)(2,1)}, u32[]{:S(2)}, u32[]{:S(2)}) collective-permute-start(bf16[1408,512]{1,0:T(8,128)(2,1)} %get-tuple-element.233), channel_id=1, source_target_pairs={{0,8},{8,16},{16,24},{1,9},{9,17},{17,25},{2,10},{10,18},{18,26},{... | collective-permute-start | bytes 4325384 | tf_op jit(solution)/shard_map/ppermute | solution.py:84
  1567.6 124.0 %collective-permute-start.74 = (bf16[512,2816]{1,0:T(8,128)(2,1)}, bf16[512,2816]{1,0:T(8,128)(2,1)}, u32[]{:S(2)}, u32[]{:S(2)}) collective-permute-start(bf16[512,2816]{1,0:T(8,128)(2,1)} %get-tuple-element.220), channel_id=1, source_target_pairs={{24,16},{25,17},{26,18},{27,19},{28,20},{29,21},{30,22},{31,23}} | collective-permute-start | bytes 8650760 | tf_op jit(solution)/shard_map/ppermute | solution.py:85
  1574.1 118.9 %collective-permute-start.72 = (bf16[512,2816]{1,0:T(8,128)(2,1)S(1)}, bf16[512,2816]{1,0:T(8,128)(2,1)}, u32[]{:S(2)}, u32[]{:S(2)}) collective-permute-start(bf16[512,2816]{1,0:T(8,128)(2,1)S(1)} %add_convert_fusion.6), channel_id=1, source_target_pairs={{0,8},{8,16},{1,9},{9,17},{2,10},{10,18},{3,11},{11,19},{4,12},{12... | collective-permute-start | bytes 8650760 | tf_op jit(solution)/shard_map/ppermute | solution.py:84
  1593.4 85.1 %collective-permute-start.83 = (bf16[1408,512]{1,0:T(8,128)(2,1)}, bf16[1408,512]{1,0:T(8,128)(2,1)}, u32[]{:S(2)}, u32[]{:S(2)}) collective-permute-start(bf16[1408,512]{1,0:T(8,128)(2,1)} %get-tuple-element.239), channel_id=1, source_target_pairs={{0,8},{1,9},{2,10},{3,11},{4,12},{5,13},{6,14},{7,15}} | collective-permute-start | bytes 4325384 | tf_op jit(solution)/shard_map/ppermute | solution.py:84
  1599.5 78.2 %collective-permute-start.35 = (bf16[64,576]{0,1:T(8,128)(2,1)S(1)}, bf16[64,576]{0,1:T(8,128)(2,1)S(1)}, u32[]{:S(2)}, u32[]{:S(2)}) collective-permute-start(bf16[64,576]{0,1:T(8,128)(2,1)S(1)} %get-tuple-element.348), channel_id=1, source_target_pairs={{0,8},{1,9},{2,10},{3,11},{4,12},{5,13},{6,14},{7,15}} | collective-permute-start | bytes 221192 | tf_op jit(solution)/shard_map/ppermute | solution.py:84
  1691.7 155.6 %collective-permute-start.82 = (bf16[1408,512]{1,0:T(8,128)(2,1)}, bf16[1408,512]{1,0:T(8,128)(2,1)}, u32[]{:S(2)}, u32[]{:S(2)}) collective-permute-start(bf16[1408,512]{1,0:T(8,128)(2,1)} %add_convert_fusion.15), channel_id=1, source_target_pairs={{8,0},{16,8},{24,16},{9,1},{17,9},{25,17},{10,2},{18,10},{26,18},{... | collective-permute-start | bytes 4325384 | tf_op jit(solution)/shard_map/ppermute | solution.py:85
  1701.9 165.1 %collective-permute-start.75 = (bf16[512,2816]{1,0:T(8,128)(2,1)}, bf16[512,2816]{1,0:T(8,128)(2,1)}, u32[]{:S(2)}, u32[]{:S(2)}) collective-permute-start(bf16[512,2816]{1,0:T(8,128)(2,1)} %get-tuple-element.218), channel_id=1, source_target_pairs={{16,8},{24,16},{17,9},{25,17},{18,10},{26,18},{19,11},{27,19},{20,... | collective-permute-start | bytes 8650760 | tf_op jit(solution)/shard_map/ppermute | solution.py:85
  1740.5 95.0 %collective-permute-start.55 = (bf16[512,704]{0,1:T(8,128)(2,1)}, bf16[512,704]{0,1:T(8,128)(2,1)}, u32[]{:S(2)}, u32[]{:S(2)}) collective-permute-start(bf16[512,704]{0,1:T(8,128)(2,1)} %get-tuple-element.286), channel_id=1, source_target_pairs={{0,8},{8,16},{16,24},{1,9},{9,17},{17,25},{2,10},{10,18},{18,26},{... | collective-permute-start | bytes 2162696 | tf_op jit(solution)/shard_map/ppermute | solution.py:84
  1776.4 77.1 %collective-permute-start.58 = (bf16[512,704]{0,1:T(8,128)(2,1)}, bf16[512,704]{0,1:T(8,128)(2,1)}, u32[]{:S(2)}, u32[]{:S(2)}) collective-permute-start(bf16[512,704]{0,1:T(8,128)(2,1)} %add_convert_fusion.20), channel_id=1, source_target_pairs={{8,0},{16,8},{24,16},{9,1},{17,9},{25,17},{10,2},{18,10},{26,18},{... | collective-permute-start | bytes 2162696 | tf_op jit(solution)/shard_map/ppermute | solution.py:85
  1784.0 130.8 %collective-permute-start.67 = (bf16[512,2816]{1,0:T(8,128)(2,1)}, bf16[512,2816]{1,0:T(8,128)(2,1)}, u32[]{:S(2)}, u32[]{:S(2)}) collective-permute-start(bf16[512,2816]{1,0:T(8,128)(2,1)} %get-tuple-element.213), channel_id=1, source_target_pairs={{0,8},{8,16},{16,24},{1,9},{9,17},{17,25},{2,10},{10,18},{18,26},{... | collective-permute-start | bytes 8650760 | tf_op jit(solution)/shard_map/ppermute | solution.py:84
  1835.5 108.4 %collective-permute-start.70 = (bf16[512,2816]{1,0:T(8,128)(2,1)}, bf16[512,2816]{1,0:T(8,128)(2,1)}, u32[]{:S(2)}, u32[]{:S(2)}) collective-permute-start(bf16[512,2816]{1,0:T(8,128)(2,1)} %add_convert_fusion.7), channel_id=1, source_target_pairs={{8,0},{16,8},{24,16},{9,1},{17,9},{25,17},{10,2},{18,10},{26,18},{... | collective-permute-start | bytes 8650760 | tf_op jit(solution)/shard_map/ppermute | solution.py:85
  1847.2 451.3 %all-gather.38.cloned.1.call-start = ((), (), s32[]{:S(2)}) async-start(), calls=%async_computation.17 | async-start | bytes 5242880 | tf_op jit(solution)/shard_map/all_gather | solution.py:393
  1856.6 119.9 %collective-permute-start.85 = (bf16[1408,512]{1,0:T(8,128)(2,1)}, bf16[1408,512]{1,0:T(8,128)(2,1)}, u32[]{:S(2)}, u32[]{:S(2)}) collective-permute-start(bf16[1408,512]{1,0:T(8,128)(2,1)} %get-tuple-element.237), channel_id=1, source_target_pairs={{0,8},{8,16},{16,24},{1,9},{9,17},{17,25},{2,10},{10,18},{18,26},{... | collective-permute-start | bytes 4325384 | tf_op jit(solution)/shard_map/ppermute | solution.py:84
  1867.0 223.0 %collective-permute-start.73 = (bf16[512,2816]{1,0:T(8,128)(2,1)}, bf16[512,2816]{1,0:T(8,128)(2,1)S(1)}, u32[]{:S(2)}, u32[]{:S(2)}) collective-permute-start(bf16[512,2816]{1,0:T(8,128)(2,1)} %get-tuple-element.217), channel_id=1, source_target_pairs={{0,8},{8,16},{16,24},{1,9},{9,17},{17,25},{2,10},{10,18},{18,26},{... | collective-permute-start | bytes 8650760 | tf_op jit(solution)/shard_map/ppermute | solution.py:84
  1875.4 214.7 %collective-permute-start.76 = (bf16[512,2816]{1,0:T(8,128)(2,1)S(1)}, bf16[512,2816]{1,0:T(8,128)(2,1)S(1)}, u32[]{:S(2)}, u32[]{:S(2)}) collective-permute-start(bf16[512,2816]{1,0:T(8,128)(2,1)S(1)} %add_convert_fusion.3), channel_id=1, source_target_pairs={{8,0},{16,8},{24,16},{9,1},{17,9},{25,17},{10,2},{18,10},{26,18},{... | collective-permute-start | bytes 8650760 | tf_op jit(solution)/shard_map/ppermute | solution.py:85
  1914.7 170.0 %collective-permute-start.88 = (bf16[1408,512]{1,0:T(8,128)(2,1)S(1)}, bf16[1408,512]{1,0:T(8,128)(2,1)S(1)}, u32[]{:S(2)}, u32[]{:S(2)}) collective-permute-start(bf16[1408,512]{1,0:T(8,128)(2,1)S(1)} %add_convert_fusion.11), channel_id=1, source_target_pairs={{8,0},{16,8},{24,16},{9,1},{17,9},{25,17},{10,2},{18,10},{26,18},{... | collective-permute-start | bytes 4325384 | tf_op jit(solution)/shard_map/ppermute | solution.py:85
  2100.7 207.2 %all-gather.42.cloned.1.call-start = ((), (), s32[]{:S(2)}) async-start(), calls=%async_computation.22 | async-start | bytes 5242880 | tf_op jit(solution)/shard_map/all_gather | solution.py:459
  2180.7 51.2 %collective-permute-start.43 = (bf16[128,512]{1,0:T(8,128)(2,1)S(1)}, bf16[128,512]{1,0:T(8,128)(2,1)S(1)}, u32[]{:S(2)}, u32[]{:S(2)}) collective-permute-start(bf16[128,512]{1,0:T(8,128)(2,1)S(1)} %get-tuple-element.340), channel_id=1, source_target_pairs={{0,8},{8,16},{16,24},{1,9},{9,17},{17,25},{2,10},{10,18},{18,26},{... | collective-permute-start | bytes 393224 | tf_op jit(solution)/shard_map/ppermute | solution.py:84
  (245 other events, 7434.9 us)
Sparse Core Ops, SparseCore 0:
  9.6 83.4 all-gather.17
  94.7 26.4 all-gather.21
  122.7 81.4 all-gather.27
  205.6 35.9 all-gather.19
  243.6 208.2 all-gather.23
  453.4 104.9 all-gather.29
  560.5 57.3 all-gather.25
  619.5 33.6 all-gather.31
  654.8 199.9 all-gather.33
  856.2 104.8 all-gather.35
  1028.0 69.5 reduce-scatter.6
  1103.3 54.4 all-gather.39
  1205.0 42.4 reduce-scatter.10
  1254.8 28.3 all-gather.43
  1287.9 69.8 reduce-scatter.8
  1442.5 72.4 reduce-scatter.4
  1778.8 83.9 all-gather.45
  1867.1 146.9 all-gather.37
  2116.3 133.9 all-gather.41

commit v2 on v1

--- a/solution.py
+++ b/solution.py
@@ -67,23 +67,28 @@
     return lax.dot_general(left, right, (((0,), (0,)), ((), ())), preferred_element_type=F32)
 
 
-def line_scatter(value, axis):
+def line_gather(shard, axis):
     count = lax.axis_size("row")
     index = lax.axis_index("row")
-    width = value.shape[axis] // count
-
-    def block(j):
-        return lax.dynamic_slice_in_dim(value, jnp.clip(j, 0, count - 1) * width, width, axis)
-
-    right, left = None, None
+    width = shard.shape[axis]
+    right, left = shard, shard
+    rights, lefts = [], []
     for step in range(1, count):
-        right_out, left_out = block(index + count - step), block(index - count + step)
-        if right is not None:
-            right_out = (right_out.astype(F32) + right.astype(F32)).astype(BF16)
-            left_out = (left_out.astype(F32) + left.astype(F32)).astype(BF16)
-        right = lax.ppermute(right_out, "row", [(j, j + 1) for j in range(0, step)])
-        left = lax.ppermute(left_out, "row", [(j, j - 1) for j in range(count - step, count)])
-    return block(index).astype(F32) + right.astype(F32) + left.astype(F32)
+        right = lax.ppermute(right, "row", [(j, j + 1) for j in range(step - 1, count - 1)])
+        left = lax.ppermute(left, "row", [(j, j - 1) for j in range(1, count - step + 1)])
+        rights.append(right)
+        lefts.append(left)
+    shape = list(shard.shape)
+    shape[axis] = width * count
+    out = lax.dynamic_update_slice_in_dim(
+        jnp.zeros(shape, shard.dtype), shard, index * width, axis
+    )
+    for k in range(1, count):
+        piece = jnp.where(index >= k, rights[k - 1], lefts[count - k - 1])
+        out = lax.dynamic_update_slice_in_dim(
+            out, piece, lax.rem(index - k + count, count) * width, axis
+        )
+    return out
 
 
 def swap(value, bit):
@@ -165,12 +170,27 @@
     return out[: len(values)]
 
 
-def col_gather(value, axis=0):
-    return lax.all_gather(value, "col", axis=axis, tiled=True)
-
-
-def col_scatter(value):
-    return lax.psum_scatter(value, "col", scatter_dimension=0, tiled=True).astype(F32)
+def row_scatter(value, axis):
+    return lax.psum_scatter(
+        value.astype(BF16), "row", scatter_dimension=axis, tiled=True
+    ).astype(F32)
+
+
+def small_sum(value):
+    for bit in [1] + chip_bits():
+        value = value + swap(value, bit)
+    count = lax.axis_size("row")
+    total = value
+    for k in range(1, count):
+        total = total + lax.ppermute(value, "row", [(j, (j + k) % count) for j in range(count)])
+    return total
+
+
+def exchange(value, here, there):
+    count = lax.axis_size("row")
+    sent = dot(here, value).astype(BF16).reshape(count, -1, value.shape[1])
+    got = lax.all_to_all(sent, "row", split_axis=0, concat_axis=0, tiled=True)
+    return dot_tn(there, got.reshape(-1, value.shape[1])).astype(BF16)
 
 
 def body(
@@ -206,17 +226,45 @@
     def my_part(value):
         return lax.dynamic_slice_in_dim(value, col_index * part_rows, part_rows, 0)
 
-    my_order = lax.dynamic_slice_in_dim(dealing, row_index * group_rows, group_rows)
     token_ids = jnp.arange(group_rows, dtype=jnp.int32)
-    given_ids = row_index * group_rows + token_ids
-    my_inverse = jnp.sum(
-        jnp.where(
-            dealing[None, :] == given_ids[:, None],
-            jnp.arange(dealing.shape[0], dtype=jnp.int32)[None, :],
-            0,
+    room = max(16, 5 * group_rows // (16 * row_count) * 4)
+    lists = dealing.reshape(row_count, group_rows)
+    source = lists // group_rows
+    place_in = lists - source * group_rows
+    from_here = source == row_index
+    rank_here = jnp.where(from_here, jnp.cumsum(from_here.astype(jnp.int32), axis=1) - 1, -1)
+    my_source = lax.dynamic_index_in_dim(source, row_index, 0, False)
+    by_source = my_source[None, :] == jnp.arange(row_count, dtype=jnp.int32)[:, None]
+    count_in = jnp.cumsum(by_source.astype(jnp.int32), axis=1)
+    my_rank = jnp.sum(jnp.where(by_source, count_in, 0), axis=0) - 1
+    all_counts = jnp.sum(
+        (source[:, None, :] == jnp.arange(row_count, dtype=jnp.int32)[None, :, None]).astype(
+            jnp.int32
         ),
-        axis=1,
-    )
+        axis=2,
+    )
+    rounds = (jnp.max(all_counts) + room - 1) // room
+
+    def maps(step):
+        places = step * room + jnp.arange(room, dtype=jnp.int32)
+        hit = rank_here[:, None, :] == places[None, :, None]
+        token = jnp.sum(jnp.where(hit, place_in[:, None, :] + 1, 0), axis=2).reshape(-1) - 1
+        here = (token[:, None] == token_ids[None, :]).astype(BF16)
+        slot = my_rank - step * room
+        slot = jnp.where((slot >= 0) & (slot < room), my_source * room + slot, -1)
+        there = (jnp.arange(row_count * room, dtype=jnp.int32)[:, None] == slot[None, :]).astype(
+            BF16
+        )
+        return here, there
+
+    here, there = maps(0)
+
+    def more_dealt(carry):
+        step, total = carry
+        here_more, there_more = maps(step)
+        given = jnp.concatenate([tokens, cotangent], axis=1)
+        return step + 1, total + exchange(given, here_more, there_more)
+
     picks, weights = [], []
     slot_ids = jnp.arange(capacity, dtype=jnp.int32)
     for number in range(local_count):
@@ -232,48 +280,69 @@
 
     rows_in, dim = w_query.shape[0], w_query.shape[0] * row_count
     wide = attn_gain.shape[0]
-    lat_width = latent_gain.shape[0]
-    given_x = row_gather(tokens, 0)
-    dealt_x = jnp.take(given_x, my_order, axis=0)
-    gains = row_gather(jnp.concatenate([attn_gain, ffn_gain, latent_gain])[None], 0)
+    slice_width = tokens.shape[1]
+    more = lax.while_loop(
+        lambda carry: carry[0] < rounds,
+        more_dealt,
+        (jnp.int32(1), jnp.zeros((group_rows, 2 * slice_width), BF16)),
+    )[1]
+    dealt_x = exchange(tokens, here, there) + more[:, :slice_width]
+    full_x = cube_gather(dealt_x, 1)
+
+    query_width = w_query.shape[1]
+    lat_rows = rows_in // col_count
+    w_latent_s = lax.dynamic_slice_in_dim(w_latent, col_index * lat_rows, lat_rows, 0)
+    lat_wide = w_latent.shape[1]
+    first_s = jnp.concatenate(
+        [
+            w_query,
+            w_latent_s.reshape(-1, query_width),
+            jnp.concatenate([attn_gain, ffn_gain, latent_gain]).reshape(-1, query_width),
+        ],
+        axis=0,
+    )
+    first_s = jnp.pad(first_s, ((0, -first_s.shape[0] % 16), (0, 0)))
+    first_w = row_gather(first_s[None], 0)
+    query_w = first_w[:, :rows_in].reshape(dim, query_width)
+    lat_end = rows_in + lat_rows * lat_wide // query_width
+    latent_w = cube_gather(first_w[:, rows_in:lat_end].reshape(row_count * lat_rows, lat_wide), 0)
+    latent_w = latent_w.reshape(col_count, row_count, lat_rows, lat_wide).transpose(1, 0, 2, 3)
+    latent_w = latent_w.reshape(dim, lat_wide)
+    gains = first_w[:, lat_end:].reshape(row_count, -1)
     gain_one = gains[:, :wide].reshape(-1).astype(F32)
     gain_two = gains[:, wide : 2 * wide].reshape(-1).astype(F32)
-    latent_g = gains[:, 2 * wide :].reshape(-1).astype(F32)
-    lat_rows = rows_in // col_count
-    w_latent_s = lax.dynamic_slice_in_dim(w_latent, col_index * lat_rows, lat_rows, 0)
-    latent_w = cube_gather(row_gather(w_latent_s, 0), 0)
-    latent_w = latent_w.reshape(col_count, row_count, lat_rows, -1).transpose(1, 0, 2, 3)
-    latent_w = latent_w.reshape(dim, -1)
-    full_x = cube_gather(dealt_x, 1)
-
-    (w_query_s, w_output_s, w_expand_s) = after((w_query, w_output, w_expand), (given_x,))
-    query_w = row_gather(w_query_s, 0)
-    expand_w = row_gather(w_expand_s, 0)
-    output_w = row_gather(w_output_s, 1)
-    (cotangent_s,) = after((cotangent,), (given_x,))
-    given_dy = row_gather(cotangent_s, 0)
-    dealt_dy = jnp.take(given_dy, my_order, axis=0)
+    latent_g = gains[:, 2 * wide : 2 * wide + latent_gain.shape[0]].reshape(-1).astype(F32)
+
+    (cotangent_s,) = after((cotangent,), (dealt_x,))
+    dealt_dy = exchange(cotangent_s, here, there) + more[:, slice_width:]
     full_dy = cube_gather(dealt_dy, 1)
 
+    out_rows = w_output.shape[0]
+    rest_s = jnp.concatenate([w_output.reshape(-1, w_expand.shape[1]), w_expand])
+    (rest_s,) = after((rest_s,), (dealt_x,))
+    rest_w = row_gather(rest_s[None], 0)
+    out_count = w_output.size // w_expand.shape[1]
+    output_w = rest_w[:, :out_count].reshape(row_count, out_rows, -1)
+    output_w = output_w.transpose(1, 0, 2).reshape(out_rows, dim)
+    expand_w = rest_w[:, out_count:].reshape(-1, w_expand.shape[1])
+
     expert_w = []
-    earlier = [output_w, given_dy]
+    earlier = [first_w, rest_w]
     for number in range(local_count):
+        gather = row_gather if number % 2 == 0 else line_gather
         gu_s = jnp.concatenate([expert_gate[number], expert_up[number]], axis=1)
         (gu_s,) = after((gu_s,), (earlier[-2],))
-        gate_up_w = row_gather(gu_s, 0)
-        earlier.append(gate_up_w)
-        (d_s,) = after((expert_down[number],), (earlier[-2],))
-        down_w = row_gather(d_s, 1)
-        earlier.append(down_w)
+        gate_up_w = gather(gu_s, 0)
+        (d_s,) = after((expert_down[number],), (earlier[-1],))
+        down_w = gather(d_s, 1)
         expert_w.append((gate_up_w, down_w))
+        earlier += [gate_up_w, down_w]
         if number == 0:
             sgu_s = jnp.concatenate([shared_gate, shared_up], axis=1)
-            (sgu_s,) = after((sgu_s,), (earlier[-2],))
+            (sgu_s,) = after((sgu_s,), (gate_up_w,))
             shared_gu_w = row_gather(sgu_s, 0)
-            earlier.append(shared_gu_w)
-            (sd_s,) = after((shared_down,), (earlier[-2],))
+            (sd_s,) = after((shared_down,), (down_w,))
             shared_d_w = row_gather(sd_s, 1)
-            earlier.append(shared_d_w)
 
     head_count = query_w.shape[1] // (NOPE + ROPE)
     softmax_scale = (NOPE + ROPE) ** (-0.5)
@@ -359,41 +428,41 @@
         )
         result_rows = dot(hidden, down_w)
         grad_rows = dot_nt(grad_gate_up, gate_up_w)
-        grad_down = line_scatter(dot_tn(hidden, grad_result).astype(BF16), 1)
-        grad_gu = line_scatter(dot_tn(rows, grad_gate_up).astype(BF16), 0)
-        return result_rows, grad_rows, grad_gu[:, :width], grad_gu[:, width:], grad_down
-
-    moe_terms, grad_two, grad_shared_gate, grad_shared_up, grad_shared_down = branch(
-        normed_two, full_dy, shared_gu_w, shared_d_w
-    )
-    grad_gates, grad_ups, grad_downs = [], [], []
+        grad_down = dot_tn(hidden, grad_result).astype(BF16)
+        grad_gu = dot_tn(rows, grad_gate_up).astype(BF16)
+        return result_rows, grad_rows, grad_gu, grad_down
+
+    moe_terms, grad_two, grad_sgu, grad_sd = branch(normed_two, full_dy, shared_gu_w, shared_d_w)
+    grad_gus, grad_downs = [], []
     for number in range(local_count):
         gate_up_w, down_w = expert_w[number]
+        if number > 0:
+            gate_up_w, down_w = after((gate_up_w, down_w), (grad_gus[-1], grad_downs[-1]))
         pick, weight = picks[number], weights[number]
         rows = dot(pick, normed_two).astype(BF16)
         grad_result = (weight[:, None] * dot(pick, full_dy)).astype(BF16)
-        result_rows, grad_rows, grad_gate, grad_up, grad_down = branch(
-            rows, grad_result, gate_up_w, down_w
-        )
-        grad_gates.append(grad_gate)
-        grad_ups.append(grad_up)
+        result_rows, grad_rows, grad_gu, grad_down = branch(rows, grad_result, gate_up_w, down_w)
+        grad_gus.append(grad_gu)
         grad_downs.append(grad_down)
         moe_terms = moe_terms + dot_tn(pick, (weight[:, None] * result_rows).astype(BF16))
         grad_two = grad_two + dot_tn(pick, grad_rows.astype(BF16))
-
-    grad_two_part = col_scatter(grad_two.astype(BF16))
+    grad_gus = [row_scatter(item, 0) for item in grad_gus]
+    grad_downs = [row_scatter(item, 1) for item in grad_downs]
+    grad_sgu = row_scatter(grad_sgu, 0)
+    grad_sd = row_scatter(grad_sd, 1)
+
+    grad_two_part = cube_scatter(grad_two.astype(BF16))
     dy_part = my_part(full_dy).astype(F32)
     hidden_back, gain_two_grad = norm_back(grad_two_part, unit_two, scale_two, gain_two)
     grad_hidden_part = dy_part + hidden_back
-    grad_attn = col_gather(grad_hidden_part.astype(BF16))
-
-    moe_part = col_scatter(moe_terms.astype(BF16))
+    grad_attn = cube_gather(grad_hidden_part.astype(BF16), 0)
+
+    moe_part = cube_scatter(moe_terms.astype(BF16))
     result_part = (hidden_part + moe_part).astype(BF16)
     result_slice = lax.all_to_all(result_part, "col", split_axis=1, concat_axis=0, tiled=True)
-    back_result = lax.all_gather(result_slice, "row", axis=0, tiled=True)
-    result = jnp.take(back_result, my_inverse, axis=0)
-
-    grad_output_w = line_scatter(dot_tn(mixed, grad_attn).astype(BF16), 1)
+    result = exchange(result_slice, there, here)
+
+    grad_output_w = row_scatter(dot_tn(mixed, grad_attn), 1)
     grad_mixed = dot_nt(grad_attn, output_w).astype(BF16)
     grad_mixed = grad_mixed.reshape(group_rows, head_count, VDIM)
     grad_query_blocks = []
@@ -436,12 +505,12 @@
         .astype(BF16)
         .reshape(group_rows, head_count * (NOPE + ROPE))
     )
-    grad_one = col_scatter(dot_nt(grad_query_raw, query_w).astype(BF16))
+    grad_one = cube_scatter(dot_nt(grad_query_raw, query_w).astype(BF16))
     grad_expanded = jnp.concatenate([grad_keys[..., :NOPE], grad_values], axis=-1).astype(BF16)
     grad_expanded = grad_expanded.reshape(group_rows, head_count * (NOPE + VDIM))
     grad_compressed = dot_nt(grad_expanded, expand_w)
     grad_rope_key = rotate(jnp.sum(grad_keys[..., NOPE:], axis=1), position, -1.0)
-    grad_latent_part = col_scatter(
+    grad_latent_part = cube_scatter(
         jnp.concatenate([grad_compressed, grad_rope_key], axis=1).astype(BF16)
     )
     grad_front, latent_gain_grad = norm_back(
@@ -456,19 +525,30 @@
     )
     grad_input = (grad_hidden_part + input_back).astype(BF16)
     grad_slice = lax.all_to_all(grad_input, "col", split_axis=1, concat_axis=0, tiled=True)
-    back_grad = lax.all_gather(grad_slice, "row", axis=0, tiled=True)
-    tokens_grad = jnp.take(back_grad, my_inverse, axis=0)
-
-    grad_query_w = line_scatter(dot_tn(normed_one, grad_query_raw).astype(BF16), 0)
-    grad_expand_w = line_scatter(dot_tn(compressed, grad_expanded).astype(BF16), 0)
-    grad_latent = col_gather(grad_latent_part)
+    tokens_grad = exchange(grad_slice, there, here)
+
+    def more_back(carry):
+        step, total = carry
+        here_more, there_more = maps(step)
+        dealt = jnp.concatenate([result_slice, grad_slice], axis=1)
+        return step + 1, total + exchange(dealt, there_more, here_more)
+
+    more = lax.while_loop(
+        lambda carry: carry[0] < rounds,
+        more_back,
+        (jnp.int32(1), jnp.concatenate([result, tokens_grad], axis=1)),
+    )[1]
+    result, tokens_grad = more[:, :slice_width], more[:, slice_width:]
+
+    grad_query_w = row_scatter(dot_tn(normed_one, grad_query_raw), 0)
+    grad_expand_w = row_scatter(dot_tn(compressed, grad_expanded), 0)
+    grad_latent = cube_gather(grad_latent_part, 0)
     my_columns = lax.dynamic_index_in_dim(
         normed_one.reshape(group_rows, row_count, col_count, lat_rows), col_index, 2, False
     ).reshape(group_rows, row_count * lat_rows)
-    grad_latent_w = col_gather(line_scatter(dot_tn(my_columns, grad_latent).astype(BF16), 0))
-    gain_grads = lax.psum(
-        jnp.concatenate([gain_one_grad, gain_two_grad, latent_gain_grad]), ("row", "col")
-    )
+    grad_latent_w = cube_gather(row_scatter(dot_tn(my_columns, grad_latent), 0).astype(BF16), 0)
+    grad_latent_w = grad_latent_w.astype(F32)
+    gain_grads = small_sum(jnp.concatenate([gain_one_grad, gain_two_grad, latent_gain_grad]))
     width_two = gain_one_grad.shape[0]
     width_lat = latent_gain_grad.shape[0]
 
@@ -486,11 +566,11 @@
         grad_expand_w,
         grad_output_w,
         my_rows(gain_grads[width_two : 2 * width_two]),
-        grad_shared_gate,
-        grad_shared_up,
-        grad_shared_down,
-        jnp.stack(grad_gates),
-        jnp.stack(grad_ups),
+        grad_sgu[:, : shared_gate.shape[1]],
+        grad_sgu[:, shared_gate.shape[1] :],
+        grad_sd,
+        jnp.stack([item[:, : expert_gate.shape[2]] for item in grad_gus]),
+        jnp.stack([item[:, expert_gate.shape[2] :] for item in grad_gus]),
         jnp.stack(grad_downs),
     )
 

time: 2340 us -> 2100 us (0.90)
  starting transfers between devices: 354 us -> 139 us
  blocking collectives: 101 us -> 0 us
  waiting for transfers between devices: 1000 us -> 1080 us
  matrix products: 425 us -> 480 us
  local copies, waits for them, and re-layouts: 163 us -> 128 us
    reduce_scatter x4 -> x10, waiting for transfers between devices: 69.7 us -> 490 us  [row_scatter(): lax.psum_scatter(value.astype(BF16), 'row', scatter_dimension=axis, tiled...]
    all_gather x10 -> x6, waiting for transfers between devices: 376 us -> 40.9 us  [row_gather(): return lax.all_gather(shard, 'row', axis=axis, tiled=True)]
    ppermute x60 -> x15, starting transfers between devices: 321 us -> 36.2 us  [the longest x6 17.4 us: line_gather(): lax.ppermute(right, 'row', [(j, j + 1) for j in range(step - 1, count - 1)])]
    ppermute x60 -> x15, waiting for transfers between devices: 399 us -> 167 us  [the longest x6 165 us: line_gather(): lax.ppermute(left, 'row', [(j, j - 1) for j in range(1, count - step + 1)])]
    ppermute x29 -> x70, waiting for transfers between devices: 123 us -> 249 us  [swap(): lax.ppermute(value, 'col', [(j, j ^ bit) for j in range(lax.axis_size('co...]
    all_to_all x0 -> x4, waiting for transfers between devices: none -> 113 us  [exchange(): got = lax.all_to_all(sent, 'row', split_axis=0, concat_axis=0, tiled=True)]
    all_gather x3 -> x0, blocking collectives: 54.2 us -> none  [row_gather(): return lax.all_gather(shard, 'row', axis=axis, tiled=True)]
    convert_element_type x32 -> x12, other arithmetic: 62.2 us -> 14.9 us  [the longest x6 11.7 us: row_scatter(): return lax.psum_scatter(value.astype(BF16), 'row', scatter_dimension=axis...]
  transfers between devices with their start and end apart: 110 -> 107, of which waited for: 38 -> 48; matrix products, arithmetic and copies ran while one was open for 29% -> 32% of each run, Pallas kernels for 0% -> 0%
where the time goes in v2:
time: 2100 us; the launch traced here: 2080 us
  waiting for transfers between devices  1080 us (51%)
  matrix products  480 us (23%)
  other arithmetic  223 us (11%)
  starting transfers between devices  139 us (7%)
  local copies, waits for them, and re-layouts  128 us (6%)
  between operations  34.4 us (2%)
    reduce_scatter x10, waiting for transfers between devices, row_scatter(): lax.psum_scatter(value.astype(BF16), 'row', scatter_dimension=axis, tiled...  490 us
    ppermute x70, waiting for transfers between devices, swap(): lax.ppermute(value, 'col', [(j, j ^ bit) for j in range(lax.axis_size('co...  249 us
    dot_general x18, matrix products, dot(): return jnp.dot(left, right, preferred_element_type=F32)  169 us
    dot_general x18, matrix products, dot_tn(): lax.dot_general(left, right, (((0,), (0,)), ((), ())), preferred_element_...  166 us
    ppermute x6, waiting for transfers between devices, line_gather(): lax.ppermute(left, 'row', [(j, j - 1) for j in range(1, count - step + 1)])  165 us
    all_to_all x4, waiting for transfers between devices, exchange(): got = lax.all_to_all(sent, 'row', split_axis=0, concat_axis=0, tiled=True)  113 us
    dot_general x10, matrix products, dot_nt(): lax.dot_general(left, right, (((1,), (1,)), ((), ())), preferred_element_...  107 us
    ppermute x70, starting transfers between devices, swap(): lax.ppermute(value, 'col', [(j, j ^ bit) for j in range(lax.axis_size('co...  67.1 us
  transfers between devices with their start and end apart: 107, of which 48 were waited for; matrix products, arithmetic and copies ran while one was open for 32% of the time, Pallas kernels for 0%

profile of v2, /device:TPU:0, one launch (start us, length us, event | category | flops | bytes accessed | tf_op | source)
XLA Modules:
  0.0 2084.5 jit_solution(11680166197140867935)
XLA Ops:
  69.3 14.7 all-to-all-done.2
  116.6 20.4 collective-permute-done.6
  236.5 59.4 %all-to-all-done.3 = bf16[4,640,256]{2,1,0:T(8,128)(2,1)} async-done(((bf16[4,640,256]{2,1,0:T(8,128)(2,1)}), bf16[4,640,256]{2,1,0:T(8,128)(2,1)}, u32[]{:S(2)}, u32[]{:S(2)}) %all-to-all-start.3) | async-done | bytes 1310752 | tf_op jit(solution)/shard_map/all_to_all | solution.py:192
  326.2 15.9 collective-permute-done.39
  355.4 20.5 collective-permute-done.13
  392.7 11.8 collective-permute-done.16
  423.7 12.6 multiply_convert_fusion.2
  436.3 40.8 %all-gather.13.cloned.1.call-done = bf16[1408,2048]{1,0:T(8,128)(2,1)} async-done(((bf16[1408,512]{1,0:T(8,128)(2,1)}), bf16[1408,2048]{1,0:T(8,128)(2,1)}) %all-gather.13.cloned.1.call-update) | async-done | bytes 5767184 | tf_op jit(solution)/shard_map/all_gather | solution.py:165
  489.5 12.5 multiply_convert_fusion.4
  504.4 55.0 %collective-permute-done.30 = bf16[1408,512]{1,0:T(8,128)(2,1)} collective-permute-done((bf16[1408,512]{1,0:T(8,128)(2,1)}, bf16[1408,512]{1,0:T(8,128)(2,1)}, u32[]{:S(2)}, u32[]{:S(2)}) %collective-permute-start.30) | collective-permute-done | bytes 1441824 | tf_op jit(solution)/shard_map/ppermute | solution.py:78
  582.2 10.6 fusion.72
  592.8 24.5 %collective-permute-done.31 = bf16[1408,512]{1,0:T(8,128)(2,1)S(1)} collective-permute-done((bf16[1408,512]{1,0:T(8,128)(2,1)}, bf16[1408,512]{1,0:T(8,128)(2,1)S(1)}, u32[]{:S(2)}, u32[]{:S(2)}) %collective-permute-start.31) | collective-permute-done | bytes 1441824 | tf_op jit(solution)/shard_map/ppermute | solution.py:78
  630.4 20.6 collective-permute-done.32
  664.9 17.5 fusion.285
  682.5 15.2 multiply_convert_fusion.11
  697.7 18.6 convolution_convert_fusion.1
  716.3 18.1 fusion.74
  734.4 11.1 multiply_convert_fusion.5.clone.2
  755.5 14.2 fusion.40
  771.9 11.6 fusion.42
  790.2 27.4 %collective-permute-done.25 = bf16[512,2816]{1,0:T(8,128)(2,1)} collective-permute-done((bf16[512,2816]{1,0:T(8,128)(2,1)}, bf16[512,2816]{1,0:T(8,128)(2,1)}, u32[]{:S(2)}, u32[]{:S(2)}) %collective-permute-start.25) | collective-permute-done | bytes 2883616 | tf_op jit(solution)/shard_map/ppermute | solution.py:78
  818.9 11.2 fusion.284
  831.0 11.5 multiply_convert_fusion.16
  842.6 37.5 %collective-permute-done.26 = bf16[512,2816]{1,0:T(8,128)(2,1)} collective-permute-done((bf16[512,2816]{1,0:T(8,128)(2,1)}, bf16[512,2816]{1,0:T(8,128)(2,1)}, u32[]{:S(2)}, u32[]{:S(2)}) %collective-permute-start.26) | collective-permute-done | bytes 2883616 | tf_op jit(solution)/shard_map/ppermute | solution.py:78
  892.4 17.9 fusion.286
  910.4 13.6 multiply_convert_fusion.8
  934.1 16.2 fusion.73
  950.4 12.0 fusion.36
  962.4 11.7 fusion.38
  974.1 17.4 add_convert_fusion
  999.5 19.4 add_convert_fusion.1
  1036.4 17.7 collective-permute-done.47
  1056.5 19.7 collective-permute-done.42
  1079.9 14.7 collective-permute-done.44
  1106.3 12.3 collective-permute-done.45
  1144.0 16.3 collective-permute-done.52
  1165.5 11.8 convolution_convert_fusion.6
  1278.3 13.1 copy.272
  1303.1 10.7 convolution_convert_fusion.2
  1386.2 18.4 convolution_convert_fusion
  1413.6 39.0 %all-to-all-done.5 = bf16[4,640,256]{2,1,0:T(8,128)(2,1)} async-done(((bf16[4,640,256]{2,1,0:T(8,128)(2,1)}), bf16[4,640,256]{2,1,0:T(8,128)(2,1)}, u32[]{:S(2)}, u32[]{:S(2)}) %all-to-all-start.5) | async-done | bytes 1310752 | tf_op jit(solution)/shard_map/all_to_all | solution.py:192
  1469.6 111.1 %reduce-scatter.29.cloned.1.call-done = bf16[1408,512]{1,0:T(8,128)(2,1)} async-done(((bf16[1408,2048]{1,0:T(8,128)(2,1)}), bf16[1408,512]{1,0:T(8,128)(2,1)}) %reduce-scatter.29.cloned.1.call-update) | async-done | bytes 1441808 | tf_op jit(solution)/shard_map/reduce_scatter | solution.py:174
  1585.4 25.3 %reduce-scatter.17.cloned.1.call-done = bf16[256,512]{1,0:T(8,128)(2,1)} async-done(((bf16[256,2048]{1,0:T(8,128)(2,1)}), bf16[256,512]{1,0:T(8,128)(2,1)}) %reduce-scatter.17.cloned.1.call-update) | async-done | bytes 262160 | tf_op jit(solution)/shard_map/reduce_scatter | solution.py:174
  1612.5 34.4 %reduce-scatter.11.cloned.1.call-done = bf16[512,384]{1,0:T(8,128)(2,1)} async-done(((bf16[2048,384]{1,0:T(8,128)(2,1)}), bf16[512,384]{1,0:T(8,128)(2,1)}) %reduce-scatter.11.cloned.1.call-update) | async-done | bytes 393232 | tf_op jit(solution)/shard_map/reduce_scatter | solution.py:174
  1661.8 12.5 collective-permute-done.61
  1686.2 14.5 all-to-all-done.6
  1717.3 146.9 %reduce-scatter.23.cloned.1.call-done = bf16[512,2816]{1,0:T(8,128)(2,1)} async-done(((bf16[2048,2816]{1,0:T(8,128)(2,1)}), bf16[512,2816]{1,0:T(8,128)(2,1)}) %reduce-scatter.23.cloned.1.call-update) | async-done | bytes 2883600 | tf_op jit(solution)/shard_map/reduce_scatter | solution.py:174
  1897.0 170.8 %reduce-scatter.25.cloned.1.call-done = bf16[512,2816]{1,0:T(8,128)(2,1)} async-done(((bf16[2048,2816]{1,0:T(8,128)(2,1)}), bf16[512,2816]{1,0:T(8,128)(2,1)}) %reduce-scatter.25.cloned.1.call-update) | async-done | bytes 2883600 | tf_op jit(solution)/shard_map/reduce_scatter | solution.py:174
  (1005 shorter events, 739.5 us)
Async XLA Ops:
  7.2 103.9 %all-gather.17.cloned.1.call-start = ((), (), s32[]{:S(2)}) async-start(), calls=%async_computation.32 | async-start | bytes 2396160 | tf_op jit(solution)/shard_map/all_gather | solution.py:165
  37.1 46.9 %all-to-all-start.2 = ((bf16[4,640,256]{2,1,0:T(8,128)(2,1)}), bf16[4,640,256]{2,1,0:T(8,128)(2,1)}, u32[]{:S(2)}, u32[]{:S(2)}) async-start(bf16[4,640,256]{2,1,0:T(8,128)(2,1)} %bitcast.722), calls=%async_computation.2 | async-start | bytes 2621440 | tf_op jit(solution)/shard_map/all_to_all | solution.py:192
  43.7 128.5 %all-gather.19.cloned.1.call-start = ((), (), s32[]{:S(2)}) async-start(), calls=%async_computation.33 | async-start | bytes 1966080 | tf_op jit(solution)/shard_map/all_gather | solution.py:165
  91.3 330.9 %all-gather.9.cloned.1.call-start = ((), (), s32[]{:S(2)}) async-start(), calls=%async_computation.18 | async-start | bytes 14417920 | tf_op jit(solution)/shard_map/all_gather | solution.py:165
  106.4 45.0 %collective-permute-start.1 = (bf16[2,1024,256]{2,1,0:T(8,128)(2,1)}, bf16[2,1024,256]{2,1,0:T(8,128)(2,1)}, u32[]{:S(2)}, u32[]{:S(2)}) collective-permute-start(bf16[2,1024,256]{2,1,0:T(8,128)(2,1)} %pad_maximum_fusion.36), channel_id=1, source_target_pairs={{0,4},{1,5},{2,6},{3,7},{4,0},{5,1},{6,2},{7,3},{8,12},{9,13},{10,... | collective-permute-start | bytes 3145736 | tf_op jit(solution)/shard_map/ppermute | solution.py:95
  109.7 38.1 %collective-permute-start.4 = (bf16[2,1024,256]{2,1,0:T(8,128)(2,1)}, bf16[2,1024,256]{2,1,0:T(8,128)(2,1)}, u32[]{:S(2)}, u32[]{:S(2)}) collective-permute-start(bf16[2,1024,256]{2,1,0:T(8,128)(2,1)} %pad_maximum_fusion.37), channel_id=1, source_target_pairs={{0,2},{1,3},{2,0},{3,1},{4,6},{5,7},{6,4},{7,5},{8,10},{9,11},{10,... | collective-permute-start | bytes 3145736 | tf_op jit(solution)/shard_map/ppermute | solution.py:95
  221.2 74.7 %all-to-all-start.3 = ((bf16[4,640,256]{2,1,0:T(8,128)(2,1)}), bf16[4,640,256]{2,1,0:T(8,128)(2,1)}, u32[]{:S(2)}, u32[]{:S(2)}) async-start(bf16[4,640,256]{2,1,0:T(8,128)(2,1)} %bitcast.723), calls=%async_computation.3 | async-start | bytes 2621440 | tf_op jit(solution)/shard_map/all_to_all | solution.py:192
  225.9 251.2 %all-gather.13.cloned.1.call-start = ((), (), s32[]{:S(2)}) async-start(), calls=%async_computation.20 | async-start | bytes 7208960 | tf_op jit(solution)/shard_map/all_gather | solution.py:165
  235.9 110.7 %collective-permute-start.12 = (bf16[4,256,2048]{2,1,0:T(8,128)(2,1)}, bf16[4,256,2048]{2,1,0:T(8,128)(2,1)}, u32[]{:S(2)}, u32[]{:S(2)}) collective-permute-start(bf16[4,256,2048]{2,1,0:T(8,128)(2,1)} %pad_maximum_fusion.4), channel_id=1, source_target_pairs={{0,1},{1,0},{2,3},{3,2},{4,5},{5,4},{6,7},{7,6},{8,9},{9,8},{10,11... | collective-permute-start | bytes 12582920 | tf_op jit(solution)/shard_map/ppermute | solution.py:95
  324.4 494.5 %all-gather.11.cloned.1.call-start = ((), (), s32[]{:S(2)}) async-start(), calls=%async_computation.19 | async-start | bytes 3604480 | tf_op jit(solution)/shard_map/all_gather | solution.py:165
  421.1 65.1 %collective-permute-start.21 = (bf16[2,128,2048]{2,1,0:T(8,128)(2,1)}, bf16[2,128,2048]{2,1,0:T(8,128)(2,1)}, u32[]{:S(2)}, u32[]{:S(2)}) collective-permute-start(bf16[2,128,2048]{2,1,0:T(8,128)(2,1)} %pad_maximum_fusion.40), channel_id=1, source_target_pairs={{0,2},{1,3},{2,0},{3,1},{4,6},{5,7},{6,4},{7,5},{8,10},{9,11},{10,... | collective-permute-start | bytes 3145736 | tf_op jit(solution)/shard_map/ppermute | solution.py:95
  422.2 408.8 %all-gather.15.cloned.1.call-start = ((), (), s32[]{:S(2)}) async-start(), calls=%async_computation.21 | async-start | bytes 1802240 | tf_op jit(solution)/shard_map/all_gather | solution.py:165
  422.4 62.1 %collective-permute-start.18 = (bf16[2,128,2048]{2,1,0:T(8,128)(2,1)S(1)}, bf16[2,128,2048]{2,1,0:T(8,128)(2,1)}, u32[]{:S(2)}, u32[]{:S(2)}) collective-permute-start(bf16[2,128,2048]{2,1,0:T(8,128)(2,1)S(1)} %pad_maximum_fusion.39), channel_id=1, source_target_pairs={{0,4},{1,5},{2,6},{3,7},{4,0},{5,1},{6,2},{7,3},{8,12},{9,13},{10,... | collective-permute-start | bytes 3145736 | tf_op jit(solution)/shard_map/ppermute | solution.py:95
  477.1 82.2 %collective-permute-start.30 = (bf16[1408,512]{1,0:T(8,128)(2,1)}, bf16[1408,512]{1,0:T(8,128)(2,1)}, u32[]{:S(2)}, u32[]{:S(2)}) collective-permute-start(bf16[1408,512]{1,0:T(8,128)(2,1)} %get-tuple-element.398), channel_id=1, source_target_pairs={{8,0},{16,8},{24,16},{9,1},{17,9},{25,17},{10,2},{18,10},{26,18},{... | collective-permute-start | bytes 4325384 | tf_op jit(solution)/shard_map/ppermute | solution.py:78
  478.6 82.1 %collective-permute-start.29 = (bf16[1408,512]{1,0:T(8,128)(2,1)}, bf16[1408,512]{1,0:T(8,128)(2,1)}, u32[]{:S(2)}, u32[]{:S(2)}) collective-permute-start(bf16[1408,512]{1,0:T(8,128)(2,1)} %get-tuple-element.398), channel_id=1, source_target_pairs={{0,8},{8,16},{16,24},{1,9},{9,17},{17,25},{2,10},{10,18},{18,26},{... | collective-permute-start | bytes 4325384 | tf_op jit(solution)/shard_map/ppermute | solution.py:77
  486.2 75.5 %collective-permute-start.19 = (bf16[4,128,2048]{2,1,0:T(8,128)(2,1)S(1)}, bf16[4,128,2048]{2,1,0:T(8,128)(2,1)}, u32[]{:S(2)}, u32[]{:S(2)}) collective-permute-start(bf16[4,128,2048]{2,1,0:T(8,128)(2,1)S(1)} %pad_maximum_fusion.21), channel_id=1, source_target_pairs={{0,1},{1,0},{2,3},{3,2},{4,5},{5,4},{6,7},{7,6},{8,9},{9,8},{10,11... | collective-permute-start | bytes 6291464 | tf_op jit(solution)/shard_map/ppermute | solution.py:95
  489.1 73.8 %collective-permute-start.22 = (bf16[4,128,2048]{2,1,0:T(8,128)(2,1)}, bf16[4,128,2048]{2,1,0:T(8,128)(2,1)}, u32[]{:S(2)}, u32[]{:S(2)}) collective-permute-start(bf16[4,128,2048]{2,1,0:T(8,128)(2,1)} %pad_maximum_fusion.22), channel_id=1, source_target_pairs={{0,1},{1,0},{2,3},{3,2},{4,5},{5,4},{6,7},{7,6},{8,9},{9,8},{10,11... | collective-permute-start | bytes 6291464 | tf_op jit(solution)/shard_map/ppermute | solution.py:95
  502.1 861.8 %reduce-scatter.21.cloned.1.call-start = ((), (), s32[]{:S(2)}) async-start(), calls=%async_computation.27 | async-start | bytes 1802240 | tf_op jit(solution)/shard_map/reduce_scatter | solution.py:174
  559.4 58.0 %collective-permute-start.31 = (bf16[1408,512]{1,0:T(8,128)(2,1)}, bf16[1408,512]{1,0:T(8,128)(2,1)S(1)}, u32[]{:S(2)}, u32[]{:S(2)}) collective-permute-start(bf16[1408,512]{1,0:T(8,128)(2,1)} %collective-permute-done.30), channel_id=1, source_target_pairs={{8,0},{16,8},{9,1},{17,9},{10,2},{18,10},{11,3},{19,11},{12,4},{20... | collective-permute-start | bytes 4325384 | tf_op jit(solution)/shard_map/ppermute | solution.py:78
  560.7 58.0 %collective-permute-start.33 = (bf16[1408,512]{1,0:T(8,128)(2,1)}, bf16[1408,512]{1,0:T(8,128)(2,1)S(1)}, u32[]{:S(2)}, u32[]{:S(2)}) collective-permute-start(bf16[1408,512]{1,0:T(8,128)(2,1)} %collective-permute-done.29), channel_id=1, source_target_pairs={{8,16},{16,24},{9,17},{17,25},{10,18},{18,26},{11,19},{19,27},{12,... | collective-permute-start | bytes 4325384 | tf_op jit(solution)/shard_map/ppermute | solution.py:77
  617.3 33.7 %collective-permute-start.32 = (bf16[1408,512]{1,0:T(8,128)(2,1)S(1)}, bf16[1408,512]{1,0:T(8,128)(2,1)S(1)}, u32[]{:S(2)}, u32[]{:S(2)}) collective-permute-start(bf16[1408,512]{1,0:T(8,128)(2,1)S(1)} %collective-permute-done.31), channel_id=1, source_target_pairs={{8,0},{9,1},{10,2},{11,3},{12,4},{13,5},{14,6},{15,7}} | collective-permute-start | bytes 4325384 | tf_op jit(solution)/shard_map/ppermute | solution.py:78
  618.6 33.4 %collective-permute-start.34 = (bf16[1408,512]{1,0:T(8,128)(2,1)S(1)}, bf16[1408,512]{1,0:T(8,128)(2,1)S(1)}, u32[]{:S(2)}, u32[]{:S(2)}) collective-permute-start(bf16[1408,512]{1,0:T(8,128)(2,1)S(1)} %collective-permute-done.33), channel_id=1, source_target_pairs={{16,24},{17,25},{18,26},{19,27},{20,28},{21,29},{22,30},{23,31}} | collective-permute-start | bytes 4325384 | tf_op jit(solution)/shard_map/ppermute | solution.py:77
  657.2 96.8 %collective-permute-start.24 = (bf16[512,2816]{1,0:T(8,128)(2,1)S(1)}, bf16[512,2816]{1,0:T(8,128)(2,1)}, u32[]{:S(2)}, u32[]{:S(2)}) collective-permute-start(bf16[512,2816]{1,0:T(8,128)(2,1)S(1)} %copy-done.20), channel_id=1, source_target_pairs={{8,0},{16,8},{24,16},{9,1},{17,9},{25,17},{10,2},{18,10},{26,18},{... | collective-permute-start | bytes 8650760 | tf_op jit(solution)/shard_map/ppermute | solution.py:78
  658.6 111.1 %collective-permute-start.23 = (bf16[512,2816]{1,0:T(8,128)(2,1)S(1)}, bf16[512,2816]{1,0:T(8,128)(2,1)}, u32[]{:S(2)}, u32[]{:S(2)}) collective-permute-start(bf16[512,2816]{1,0:T(8,128)(2,1)S(1)} %copy-done.20), channel_id=1, source_target_pairs={{0,8},{8,16},{16,24},{1,9},{9,17},{17,25},{2,10},{10,18},{18,26},{... | collective-permute-start | bytes 8650760 | tf_op jit(solution)/shard_map/ppermute | solution.py:77
  754.0 63.7 %collective-permute-start.25 = (bf16[512,2816]{1,0:T(8,128)(2,1)}, bf16[512,2816]{1,0:T(8,128)(2,1)}, u32[]{:S(2)}, u32[]{:S(2)}) collective-permute-start(bf16[512,2816]{1,0:T(8,128)(2,1)} %collective-permute-done.24), channel_id=1, source_target_pairs={{8,0},{16,8},{9,1},{17,9},{10,2},{18,10},{11,3},{19,11},{12,4},{20... | collective-permute-start | bytes 8650760 | tf_op jit(solution)/shard_map/ppermute | solution.py:78
  769.7 60.4 %collective-permute-start.27 = (bf16[512,2816]{1,0:T(8,128)(2,1)}, bf16[512,2816]{1,0:T(8,128)(2,1)}, u32[]{:S(2)}, u32[]{:S(2)}) collective-permute-start(bf16[512,2816]{1,0:T(8,128)(2,1)} %collective-permute-done.23), channel_id=1, source_target_pairs={{8,16},{16,24},{9,17},{17,25},{10,18},{18,26},{11,19},{19,27},{12,... | collective-permute-start | bytes 8650760 | tf_op jit(solution)/shard_map/ppermute | solution.py:77
  817.6 62.5 %collective-permute-start.26 = (bf16[512,2816]{1,0:T(8,128)(2,1)}, bf16[512,2816]{1,0:T(8,128)(2,1)}, u32[]{:S(2)}, u32[]{:S(2)}) collective-permute-start(bf16[512,2816]{1,0:T(8,128)(2,1)} %collective-permute-done.25), channel_id=1, source_target_pairs={{8,0},{9,1},{10,2},{11,3},{12,4},{13,5},{14,6},{15,7}} | collective-permute-start | bytes 8650760 | tf_op jit(solution)/shard_map/ppermute | solution.py:78
  830.1 58.0 %collective-permute-start.28 = (bf16[512,2816]{1,0:T(8,128)(2,1)}, bf16[512,2816]{1,0:T(8,128)(2,1)S(1)}, u32[]{:S(2)}, u32[]{:S(2)}) collective-permute-start(bf16[512,2816]{1,0:T(8,128)(2,1)} %collective-permute-done.27), channel_id=1, source_target_pairs={{16,24},{17,25},{18,26},{19,27},{20,28},{21,29},{22,30},{23,31}} | collective-permute-start | bytes 8650760 | tf_op jit(solution)/shard_map/ppermute | solution.py:77
  1033.2 43.0 %collective-permute-start.42 = (bf16[2,128,2048]{2,1,0:T(8,128)(2,1)S(1)}, bf16[2,128,2048]{2,1,0:T(8,128)(2,1)S(1)}, u32[]{:S(2)}, u32[]{:S(2)}) collective-permute-start(bf16[2,128,2048]{2,1,0:T(8,128)(2,1)S(1)} %pad_maximum_fusion.43), channel_id=1, source_target_pairs={{0,2},{1,3},{2,0},{3,1},{4,6},{5,7},{6,4},{7,5},{8,10},{9,11},{10,... | collective-permute-start | bytes 3145736 | tf_op jit(solution)/shard_map/ppermute | solution.py:95
  1034.8 43.1 %collective-permute-start.49 = (bf16[2,128,2048]{2,1,0:T(8,128)(2,1)S(1)}, bf16[2,128,2048]{2,1,0:T(8,128)(2,1)S(1)}, u32[]{:S(2)}, u32[]{:S(2)}) collective-permute-start(bf16[2,128,2048]{2,1,0:T(8,128)(2,1)S(1)} %stack.294), channel_id=1, source_target_pairs={{0,4},{1,5},{2,6},{3,7},{4,0},{5,1},{6,2},{7,3},{8,12},{9,13},{10,... | collective-permute-start | bytes 3145736 | tf_op jit(solution)/shard_map/ppermute | solution.py:95
  1055.9 38.7 %collective-permute-start.44 = (bf16[2,128,2048]{2,1,0:T(8,128)(2,1)S(1)}, bf16[2,128,2048]{2,1,0:T(8,128)(2,1)S(1)}, u32[]{:S(2)}, u32[]{:S(2)}) collective-permute-start(bf16[2,128,2048]{2,1,0:T(8,128)(2,1)S(1)} %stack.293), channel_id=1, source_target_pairs={{0,4},{1,5},{2,6},{3,7},{4,0},{5,1},{6,2},{7,3},{8,12},{9,13},{10,... | collective-permute-start | bytes 3145736 | tf_op jit(solution)/shard_map/ppermute | solution.py:95
  1143.9 260.7 %reduce-scatter.19.cloned.1.call-start = ((), (), s32[]{:S(2)}) async-start(), calls=%async_computation.26 | async-start | bytes 3604480 | tf_op jit(solution)/shard_map/reduce_scatter | solution.py:174
  1177.4 281.9 %reduce-scatter.15.cloned.1.call-start = ((), (), s32[]{:S(2)}) async-start(), calls=%async_computation.24 | async-start | bytes 655360 | tf_op jit(solution)/shard_map/reduce_scatter | solution.py:174
  1298.2 162.8 %reduce-scatter.13.cloned.1.call-start = ((), (), s32[]{:S(2)}) async-start(), calls=%async_computation.23 | async-start | bytes 409600 | tf_op jit(solution)/shard_map/reduce_scatter | solution.py:174
  1301.3 168.3 %reduce-scatter.27.cloned.1.call-start = ((), (), s32[]{:S(2)}) async-start(), calls=%async_computation.30 | async-start | bytes 7208960 | tf_op jit(solution)/shard_map/reduce_scatter | solution.py:174
  1302.1 278.7 %reduce-scatter.29.cloned.1.call-start = ((), (), s32[]{:S(2)}) async-start(), calls=%async_computation.31 | async-start | bytes 7208960 | tf_op jit(solution)/shard_map/reduce_scatter | solution.py:174
  1313.8 296.9 %reduce-scatter.17.cloned.1.call-start = ((), (), s32[]{:S(2)}) async-start(), calls=%async_computation.25 | async-start | bytes 1310720 | tf_op jit(solution)/shard_map/reduce_scatter | solution.py:174
  1327.9 319.0 %reduce-scatter.11.cloned.1.call-start = ((), (), s32[]{:S(2)}) async-start(), calls=%async_computation.22 | async-start | bytes 1966080 | tf_op jit(solution)/shard_map/reduce_scatter | solution.py:174
  1340.6 523.6 %reduce-scatter.23.cloned.1.call-start = ((), (), s32[]{:S(2)}) async-start(), calls=%async_computation.28 | async-start | bytes 14417920 | tf_op jit(solution)/shard_map/reduce_scatter | solution.py:174
  1363.5 43.7 %collective-permute-start.57 = (bf16[4,256,2048]{2,1,0:T(8,128)(2,1)}, bf16[4,256,2048]{2,1,0:T(8,128)(2,1)}, u32[]{:S(2)}, u32[]{:S(2)}) collective-permute-start(bf16[4,256,2048]{2,1,0:T(8,128)(2,1)} %pad_maximum_fusion.7), channel_id=1, source_target_pairs={{0,1},{1,0},{2,3},{3,2},{4,5},{5,4},{6,7},{7,6},{8,9},{9,8},{10,11... | collective-permute-start | bytes 12582920 | tf_op jit(solution)/shard_map/ppermute | solution.py:95
  1377.2 75.4 %all-to-all-start.5 = ((bf16[4,640,256]{2,1,0:T(8,128)(2,1)}), bf16[4,640,256]{2,1,0:T(8,128)(2,1)}, u32[]{:S(2)}, u32[]{:S(2)}) async-start(bf16[4,640,256]{2,1,0:T(8,128)(2,1)} %bitcast.726), calls=%async_computation.5 | async-start | bytes 2621440 | tf_op jit(solution)/shard_map/all_to_all | solution.py:192
  1386.0 681.8 %reduce-scatter.25.cloned.1.call-start = ((), (), s32[]{:S(2)}) async-start(), calls=%async_computation.29 | async-start | bytes 14417920 | tf_op jit(solution)/shard_map/reduce_scatter | solution.py:174
  1413.1 53.3 %collective-permute-start.58 = (bf16[2,128,2048]{2,1,0:T(8,128)(2,1)S(1)}, bf16[2,128,2048]{2,1,0:T(8,128)(2,1)}, u32[]{:S(2)}, u32[]{:S(2)}) collective-permute-start(bf16[2,128,2048]{2,1,0:T(8,128)(2,1)S(1)} %pad_maximum_fusion.47), channel_id=1, source_target_pairs={{0,2},{1,3},{2,0},{3,1},{4,6},{5,7},{6,4},{7,5},{8,10},{9,11},{10,... | collective-permute-start | bytes 3145736 | tf_op jit(solution)/shard_map/ppermute | solution.py:95
  1461.7 188.6 %collective-permute-start.79 = (bf16[1,32,576]{2,1,0:T(8,128)(2,1)S(1)}, bf16[1,32,576]{2,1,0:T(8,128)(2,1)S(1)}, u32[]{:S(2)}, u32[]{:S(2)}) collective-permute-start(bf16[1,32,576]{2,1,0:T(8,128)(2,1)S(1)} %get-tuple-element.749), channel_id=1, source_target_pairs={{0,2},{1,3},{2,0},{3,1},{4,6},{5,7},{6,4},{7,5},{8,10},{9,11},{10,... | collective-permute-start | bytes 110600 | tf_op jit(solution)/shard_map/ppermute | solution.py:95
  1464.8 193.1 %collective-permute-start.60 = (bf16[2,128,2048]{2,1,0:T(8,128)(2,1)S(1)}, bf16[2,128,2048]{2,1,0:T(8,128)(2,1)}, u32[]{:S(2)}, u32[]{:S(2)}) collective-permute-start(bf16[2,128,2048]{2,1,0:T(8,128)(2,1)S(1)} %stack.295), channel_id=1, source_target_pairs={{0,4},{1,5},{2,6},{3,7},{4,0},{5,1},{6,2},{7,3},{8,12},{9,13},{10,... | collective-permute-start | bytes 3145736 | tf_op jit(solution)/shard_map/ppermute | solution.py:95
  1467.7 190.3 %collective-permute-start.59 = (bf16[1,128,2048]{2,1,0:T(8,128)(2,1)S(1)}, bf16[1,128,2048]{2,1,0:T(8,128)(2,1)S(1)}, u32[]{:S(2)}, u32[]{:S(2)}) collective-permute-start(bf16[1,128,2048]{2,1,0:T(8,128)(2,1)S(1)} %add_convert_fusion.9), channel_id=1, source_target_pairs={{0,4},{1,5},{2,6},{3,7},{4,0},{5,1},{6,2},{7,3},{8,12},{9,13},{10,... | collective-permute-start | bytes 1572872 | tf_op jit(solution)/shard_map/ppermute | solution.py:95
  1705.8 181.1 %all-to-all-start.7 = ((bf16[4,640,256]{2,1,0:T(8,128)(2,1)}), bf16[4,640,256]{2,1,0:T(8,128)(2,1)S(1)}, u32[]{:S(2)}, u32[]{:S(2)}) async-start(bf16[4,640,256]{2,1,0:T(8,128)(2,1)} %bitcast.725), calls=%async_computation.7 | async-start | bytes 2621440 | tf_op jit(solution)/shard_map/all_to_all | solution.py:192
  1713.8 152.7 %collective-permute-start.69 = (f32[4608]{0:T(1024)S(1)}, f32[4608]{0:T(1024)S(1)}, u32[]{:S(2)}, u32[]{:S(2)}) collective-permute-start(f32[4608]{0:T(1024)S(1)} %add.1553), channel_id=1, source_target_pairs={{0,4},{1,5},{2,6},{3,7},{4,0},{5,1},{6,2},{7,3},{8,12},{9,13},{10,... | collective-permute-start | bytes 55304 | tf_op jit(solution)/shard_map/ppermute | solution.py:95
  (252 other events, 3068.5 us)
Sparse Core Ops, SparseCore 0:
  10.6 56.8 all-gather.16
  91.4 35.7 all-gather.18
  143.8 226.4 all-gather.8
  372.2 104.8 all-gather.12
  479.1 81.5 all-gather.10
  562.2 46.9 all-gather.14
  1144.0 37.7 reduce-scatter.20
  1184.1 55.0 reduce-scatter.18
  1298.3 26.3 reduce-scatter.14
  1326.8 18.2 reduce-scatter.12
  1348.0 121.5 reduce-scatter.26
  1472.3 108.3 reduce-scatter.28
  1583.0 27.6 reduce-scatter.16
  1613.0 33.9 reduce-scatter.10
  1649.2 214.9 reduce-scatter.22
  1866.6 201.1 reduce-scatter.24

commit v3 on v2

--- a/solution.py
+++ b/solution.py
@@ -67,28 +67,32 @@
     return lax.dot_general(left, right, (((0,), (0,)), ((), ())), preferred_element_type=F32)
 
 
-def line_gather(shard, axis):
+def line_scatter(values):
     count = lax.axis_size("row")
     index = lax.axis_index("row")
-    width = shard.shape[axis]
-    right, left = shard, shard
-    rights, lefts = [], []
+
+    def block(j):
+        place = jnp.clip(j, 0, count - 1)
+        return jnp.concatenate(
+            [
+                lax.dynamic_slice_in_dim(
+                    value, place * (value.shape[0] // count), value.shape[0] // count, 0
+                )
+                for value in values
+            ],
+            axis=1,
+        )
+
+    right, left = None, None
     for step in range(1, count):
-        right = lax.ppermute(right, "row", [(j, j + 1) for j in range(step - 1, count - 1)])
-        left = lax.ppermute(left, "row", [(j, j - 1) for j in range(1, count - step + 1)])
-        rights.append(right)
-        lefts.append(left)
-    shape = list(shard.shape)
-    shape[axis] = width * count
-    out = lax.dynamic_update_slice_in_dim(
-        jnp.zeros(shape, shard.dtype), shard, index * width, axis
-    )
-    for k in range(1, count):
-        piece = jnp.where(index >= k, rights[k - 1], lefts[count - k - 1])
-        out = lax.dynamic_update_slice_in_dim(
-            out, piece, lax.rem(index - k + count, count) * width, axis
-        )
-    return out
+        right_out, left_out = block(index + count - step), block(index - count + step)
+        if right is not None:
+            right_out = (right_out.astype(F32) + right.astype(F32)).astype(BF16)
+            left_out = (left_out.astype(F32) + left.astype(F32)).astype(BF16)
+        yield right_out, left_out
+        right = lax.ppermute(right_out, "row", [(j, j + 1) for j in range(0, step)])
+        left = lax.ppermute(left_out, "row", [(j, j - 1) for j in range(count - step, count)])
+    yield block(index).astype(F32) + right.astype(F32) + left.astype(F32)
 
 
 def swap(value, bit):
@@ -97,68 +101,69 @@
 
 def chip_bits():
     return [1 << b for b in range(1, (lax.axis_size("col") - 1).bit_length())]
+
+
+def chip_swap(value, step):
+    bits = chip_bits()
+    other = bits[::-1]
+    return lax.ppermute(
+        value,
+        "col",
+        [(j, j ^ (other if j % 2 else bits)[step]) for j in range(lax.axis_size("col"))],
+    )
+
+
+def block_at(device, place):
+    bits = chip_bits()
+    even = sum(bit for n, bit in enumerate(bits) if place >> n & 1)
+    odd = sum(bit for n, bit in enumerate(bits[::-1]) if place >> n & 1)
+    return jnp.bitwise_xor(device, jnp.where(device % 2 == 0, even, odd))
 
 
 def cube_gather(block, axis):
     count = lax.axis_size("col")
     index = lax.axis_index("col")
-    bits = chip_bits()
-    half = block.shape[0] // 2
-    kept, swapped = [], []
-    for part, order in ((block[:half], bits), (block[half:], bits[::-1])):
-        held, keys = part[None], [0]
-        for bit in order:
-            held = jnp.concatenate([held, swap(held, bit)], axis=0)
-            keys = keys + [key ^ bit for key in keys]
-        order_of = [keys.index(key) for key in range(0, count, 2)]
-        kept.append((held, order_of))
-    swapped = [swap(held, 1) for held, order_of in kept]
-    out = []
-    for j in range(count):
-        rel = jnp.bitwise_xor(index, j)
-        halves = []
-        for (held, order_of), other in zip(kept, swapped):
-            place = jnp.array(order_of, jnp.int32)[rel // 2]
-            mine = lax.dynamic_index_in_dim(held, place, 0, False)
-            theirs = lax.dynamic_index_in_dim(other, place, 0, False)
-            halves.append(jnp.where(rel % 2 == 0, mine, theirs))
-        out.append(jnp.concatenate(halves, axis=0))
-    return jnp.concatenate(out, axis=axis)
+    width = block.shape[axis]
+    shape = list(block.shape)
+    shape[axis] = width * count
+    out = jnp.zeros(shape, block.dtype)
+    held = block[None]
+    sibling = jnp.bitwise_xor(index, 1)
+    done = 0
+    for step in range(len(chip_bits()) + 1):
+        theirs = swap(held[done:], 1)
+        for place in range(done, held.shape[0]):
+            for item, owner in ((held[place], index), (theirs[place - done], sibling)):
+                out = lax.dynamic_update_slice_in_dim(
+                    out, item, block_at(owner, place) * width, axis
+                )
+        done = held.shape[0]
+        if step < len(chip_bits()):
+            held = jnp.concatenate([held, chip_swap(held, step)], axis=0)
+    return out
 
 
 def cube_scatter(value):
     count = lax.axis_size("col")
     index = lax.axis_index("col")
-    bits = chip_bits()
     rows = value.shape[0] // count
-    half = rows // 2
-    evens = list(range(0, count, 2))
-
-    def blocks(me):
+
+    def blocks(device):
         return jnp.stack(
             [
-                lax.dynamic_slice_in_dim(value, jnp.bitwise_xor(me, key) * rows, rows, 0)
-                for key in evens
+                lax.dynamic_slice_in_dim(value, block_at(device, place) * rows, rows, 0)
+                for place in range(count // 2)
             ]
         )
 
     got = swap(blocks(jnp.bitwise_xor(index, 1)), 1)
-    total = (blocks(index).astype(F32) + got.astype(F32)).astype(BF16)
-    parts = []
-    for part, order in ((total[:, :half], bits), (total[:, half:], bits[::-1])):
-        held = {key: part[n] for n, key in enumerate(evens)}
-        for bit in order:
-            leaving = [key for key in held if key & bit]
-            arrived = swap(jnp.stack([held[key] for key in leaving]), bit)
-            held = {
-                key: (held[key].astype(F32) + arrived[leaving.index(key ^ bit)].astype(F32))
-                for key in held
-                if not key & bit
-            }
-            if len(held) > 1:
-                held = {key: item.astype(BF16) for key, item in held.items()}
-        parts.append(held[0])
-    return jnp.concatenate(parts, axis=0)
+    held = blocks(index).astype(F32) + got.astype(F32)
+    for step in range(len(chip_bits()) - 1, -1, -1):
+        held = held.astype(BF16)
+        half = held.shape[0] // 2
+        got = chip_swap(held[half:], step)
+        held = held[:half].astype(F32) + got.astype(F32)
+    return held[0]
 
 
 def row_gather(shard, axis):
@@ -171,9 +176,7 @@
 
 
 def row_scatter(value, axis):
-    return lax.psum_scatter(
-        value.astype(BF16), "row", scatter_dimension=axis, tiled=True
-    ).astype(F32)
+    return lax.psum_scatter(value, "row", scatter_dimension=axis, tiled=True)
 
 
 def small_sum(value):
@@ -326,23 +329,20 @@
     output_w = output_w.transpose(1, 0, 2).reshape(out_rows, dim)
     expand_w = rest_w[:, out_count:].reshape(-1, w_expand.shape[1])
 
+    queue = [first_w, rest_w]
+
+    def queued(shard, axis):
+        (shard,) = after((shard,), (queue[-2],))
+        queue.append(row_gather(shard, axis))
+        return queue[-1]
+
     expert_w = []
-    earlier = [first_w, rest_w]
     for number in range(local_count):
-        gather = row_gather if number % 2 == 0 else line_gather
-        gu_s = jnp.concatenate([expert_gate[number], expert_up[number]], axis=1)
-        (gu_s,) = after((gu_s,), (earlier[-2],))
-        gate_up_w = gather(gu_s, 0)
-        (d_s,) = after((expert_down[number],), (earlier[-1],))
-        down_w = gather(d_s, 1)
-        expert_w.append((gate_up_w, down_w))
-        earlier += [gate_up_w, down_w]
+        gate_up_s = jnp.concatenate([expert_gate[number], expert_up[number]], axis=1)
+        expert_w.append((queued(gate_up_s, 0), queued(expert_down[number], 1)))
         if number == 0:
-            sgu_s = jnp.concatenate([shared_gate, shared_up], axis=1)
-            (sgu_s,) = after((sgu_s,), (gate_up_w,))
-            shared_gu_w = row_gather(sgu_s, 0)
-            (sd_s,) = after((shared_down,), (down_w,))
-            shared_d_w = row_gather(sd_s, 1)
+            shared_gu_w = queued(jnp.concatenate([shared_gate, shared_up], axis=1), 0)
+            shared_d_w = queued(shared_down, 1)
 
     head_count = query_w.shape[1] // (NOPE + ROPE)
     softmax_scale = (NOPE + ROPE) ** (-0.5)
@@ -416,53 +416,83 @@
     unit_two = hidden_part * scale_two
     normed_two = cube_gather((unit_two * gain_two).astype(BF16), 0)
 
-    def branch(rows, grad_result, gate_up_w, down_w):
+    def forward(rows, gate_up_w):
         width = gate_up_w.shape[1] // 2
         gate_up = dot(rows, gate_up_w)
         gate_out, up_out = gate_up[:, :width], gate_up[:, width:]
         act, slope = silu_parts(gate_out)
         hidden = (act * up_out).astype(BF16)
-        grad_hidden = dot_nt(grad_result, down_w)
-        grad_gate_up = jnp.concatenate(
-            [(grad_hidden * up_out * slope).astype(BF16), (grad_hidden * act).astype(BF16)], axis=1
-        )
-        result_rows = dot(hidden, down_w)
-        grad_rows = dot_nt(grad_gate_up, gate_up_w)
-        grad_down = dot_tn(hidden, grad_result).astype(BF16)
-        grad_gu = dot_tn(rows, grad_gate_up).astype(BF16)
-        return result_rows, grad_rows, grad_gu, grad_down
-
-    moe_terms, grad_two, grad_sgu, grad_sd = branch(normed_two, full_dy, shared_gu_w, shared_d_w)
-    grad_gus, grad_downs = [], []
+        return hidden, act, up_out * slope
+
+    def backward(grad_hidden, act, up_slope):
+        return jnp.concatenate(
+            [(grad_hidden * up_slope).astype(BF16), (grad_hidden * act).astype(BF16)], axis=1
+        )
+
+    lines = []
+    grad_two, moe_terms = None, None
     for number in range(local_count):
         gate_up_w, down_w = expert_w[number]
-        if number > 0:
-            gate_up_w, down_w = after((gate_up_w, down_w), (grad_gus[-1], grad_downs[-1]))
         pick, weight = picks[number], weights[number]
         rows = dot(pick, normed_two).astype(BF16)
         grad_result = (weight[:, None] * dot(pick, full_dy)).astype(BF16)
-        result_rows, grad_rows, grad_gu, grad_down = branch(rows, grad_result, gate_up_w, down_w)
-        grad_gus.append(grad_gu)
-        grad_downs.append(grad_down)
-        moe_terms = moe_terms + dot_tn(pick, (weight[:, None] * result_rows).astype(BF16))
-        grad_two = grad_two + dot_tn(pick, grad_rows.astype(BF16))
-    grad_gus = [row_scatter(item, 0) for item in grad_gus]
-    grad_downs = [row_scatter(item, 1) for item in grad_downs]
-    grad_sgu = row_scatter(grad_sgu, 0)
-    grad_sd = row_scatter(grad_sd, 1)
-
-    grad_two_part = cube_scatter(grad_two.astype(BF16))
+        for line in lines:
+            (gate_up_w,) = after((gate_up_w,), next(line))
+        hidden, act, up_slope = forward(rows, gate_up_w)
+        grad_gate_up = backward(dot_nt(grad_result, down_w), act, up_slope)
+        for line in lines:
+            (grad_gate_up,) = after((grad_gate_up,), next(line))
+        grad_rows = dot_nt(grad_gate_up, gate_up_w).astype(BF16)
+        term = dot_tn(pick, grad_rows)
+        grad_two = term if grad_two is None else grad_two + term
+        if number + 1 < local_count:
+            grad_gu = dot_tn(rows, grad_gate_up).astype(BF16)
+            grad_down = dot_tn(grad_result, hidden).astype(BF16)
+            line = line_scatter([grad_gu, grad_down])
+            messages = next(line)
+            lines.append(line)
+            shared_in, full_dy_s = after((normed_two, full_dy), messages)
+            term = dot_tn(pick, (weight[:, None] * dot(hidden, down_w)).astype(BF16))
+            moe_terms = term if moe_terms is None else moe_terms + term
+        if number == 0:
+            shared_hidden, shared_act, shared_us = forward(shared_in, shared_gu_w)
+            grad_shared_gu = backward(dot_nt(full_dy_s, shared_d_w), shared_act, shared_us)
+            grad_two = grad_two + dot_nt(grad_shared_gu, shared_gu_w)
+            moe_terms = moe_terms + dot(shared_hidden, shared_d_w)
+            grad_sgu = dot_tn(shared_in, grad_shared_gu).astype(BF16)
+            grad_sd = dot_tn(shared_hidden, full_dy_s).astype(BF16)
+    ordered = []
+
+    def queued_sum(value, axis):
+        if len(ordered) > 1:
+            (value,) = after((value,), (ordered[-2],))
+        ordered.append(row_scatter(value.astype(BF16), axis))
+        return ordered[-1]
+
+    grad_sgu = queued_sum(grad_sgu, 0)
+    grad_sd = queued_sum(grad_sd, 1)
+    last_gu = queued_sum(dot_tn(rows, grad_gate_up), 0)
+    last_down = queued_sum(dot_tn(hidden, grad_result), 1)
+    grad_two = grad_two.astype(BF16)
+    (hidden_late, weight_late) = after((hidden, weight), (grad_two,))
+    term = dot_tn(pick, (weight_late[:, None] * dot(hidden_late, down_w)).astype(BF16))
+    moe_terms = (moe_terms + term).astype(BF16)
+
+    grad_two_part = cube_scatter(grad_two)
     dy_part = my_part(full_dy).astype(F32)
     hidden_back, gain_two_grad = norm_back(grad_two_part, unit_two, scale_two, gain_two)
     grad_hidden_part = dy_part + hidden_back
     grad_attn = cube_gather(grad_hidden_part.astype(BF16), 0)
 
-    moe_part = cube_scatter(moe_terms.astype(BF16))
+    (moe_terms,) = after((moe_terms,), (grad_attn,))
+    moe_part = cube_scatter(moe_terms)
     result_part = (hidden_part + moe_part).astype(BF16)
     result_slice = lax.all_to_all(result_part, "col", split_axis=1, concat_axis=0, tiled=True)
     result = exchange(result_slice, there, here)
 
-    grad_output_w = row_scatter(dot_tn(mixed, grad_attn), 1)
+    line_sums = [list(line)[-1] for line in lines]
+    grad_attn, *line_sums = after((grad_attn, *line_sums), ())
+    grad_output_w = queued_sum(dot_tn(mixed, grad_attn), 1)
     grad_mixed = dot_nt(grad_attn, output_w).astype(BF16)
     grad_mixed = grad_mixed.reshape(group_rows, head_count, VDIM)
     grad_query_blocks = []
@@ -540,15 +570,17 @@
     )[1]
     result, tokens_grad = more[:, :slice_width], more[:, slice_width:]
 
-    grad_query_w = row_scatter(dot_tn(normed_one, grad_query_raw), 0)
-    grad_expand_w = row_scatter(dot_tn(compressed, grad_expanded), 0)
+    grad_expand_w = queued_sum(dot_tn(compressed, grad_expanded), 0)
+    grad_query_w = queued_sum(dot_tn(normed_one, grad_query_raw), 0)
     grad_latent = cube_gather(grad_latent_part, 0)
     my_columns = lax.dynamic_index_in_dim(
         normed_one.reshape(group_rows, row_count, col_count, lat_rows), col_index, 2, False
     ).reshape(group_rows, row_count * lat_rows)
-    grad_latent_w = cube_gather(row_scatter(dot_tn(my_columns, grad_latent), 0).astype(BF16), 0)
-    grad_latent_w = grad_latent_w.astype(F32)
+    grad_latent_w = cube_gather(queued_sum(dot_tn(my_columns, grad_latent), 0), 0)
     gain_grads = small_sum(jnp.concatenate([gain_one_grad, gain_two_grad, latent_gain_grad]))
+    width_ff = expert_gate.shape[2]
+    grad_gus = line_sums + [last_gu]
+    grad_downs = [item[:, 2 * width_ff :].T for item in line_sums] + [last_down]
     width_two = gain_one_grad.shape[0]
     width_lat = latent_gain_grad.shape[0]
 
@@ -560,18 +592,18 @@
         result,
         tokens_grad,
         my_rows(gain_grads[:width_two]),
-        grad_query_w,
-        grad_latent_w,
+        grad_query_w.astype(F32),
+        grad_latent_w.astype(F32),
         my_rows(gain_grads[2 * width_two : 2 * width_two + width_lat]),
-        grad_expand_w,
-        grad_output_w,
+        grad_expand_w.astype(F32),
+        grad_output_w.astype(F32),
         my_rows(gain_grads[width_two : 2 * width_two]),
-        grad_sgu[:, : shared_gate.shape[1]],
-        grad_sgu[:, shared_gate.shape[1] :],
-        grad_sd,
-        jnp.stack([item[:, : expert_gate.shape[2]] for item in grad_gus]),
-        jnp.stack([item[:, expert_gate.shape[2] :] for item in grad_gus]),
-        jnp.stack(grad_downs),
+        grad_sgu[:, : shared_gate.shape[1]].astype(F32),
+        grad_sgu[:, shared_gate.shape[1] :].astype(F32),
+        grad_sd.astype(F32),
+        jnp.stack([item[:, :width_ff] for item in grad_gus]).astype(F32),
+        jnp.stack([item[:, width_ff : 2 * width_ff] for item in grad_gus]).astype(F32),
+        jnp.stack(grad_downs).astype(F32),
     )
 
 

time: 2100 us -> 1870 us (0.89)
  waiting for transfers between devices: 1080 us -> 741 us
  local copies, waits for them, and re-layouts: 128 us -> 346 us
  starting transfers between devices: 139 us -> 92 us
  other arithmetic: 223 us -> 177 us
    reduce_scatter x10 -> x7, waiting for transfers between devices: 490 us -> 55.1 us  [row_scatter(): return lax.psum_scatter(value, 'row', scatter_dimension=axis, tiled=True)]
    ppermute x70 -> x29, waiting for transfers between devices: 249 us -> 2.41 us  [swap(): lax.ppermute(value, 'col', [(j, j ^ bit) for j in range(lax.axis_size('co...]
    ppermute x12 -> x30, waiting for transfers between devices: 165 us -> 369 us  [the longest x3 260 us: line_scatter(): right = lax.ppermute(right_out, 'row', [(j, j + 1) for j in range(0, step)])]
    all_gather x6 -> x8, waiting for transfers between devices: 40.9 us -> 178 us  [row_gather(): return lax.all_gather(shard, 'row', axis=axis, tiled=True)]
    dynamic_slice x1 -> x29, local copies, waits for them, and re-layouts: 0.61 us -> 72 us  [the longest x27 56.4 us: blocks(): lax.dynamic_slice_in_dim(value, block_at(device, place) * rows, rows, 0)]
    dynamic_update_slice x2 -> x53, local copies, waits for them, and re-layouts: 3.27 us -> 73.2 us  [cube_gather(): lax.dynamic_update_slice_in_dim(out, item, block_at(owner, place) * width...]
    ppermute x70 -> x29, starting transfers between devices: 67.1 us -> 8.25 us  [swap(): lax.ppermute(value, 'col', [(j, j ^ bit) for j in range(lax.axis_size('co...]
    unnamed x96 -> x7, other arithmetic: 53.3 us -> 0.08 us
  transfers between devices with their start and end apart: 107 -> 84, of which waited for: 48 -> 27; matrix products, arithmetic and copies ran while one was open for 32% -> 47% of each run, Pallas kernels for 0% -> 0%
where the time goes in v3:
time: 1870 us; the launch traced here: 1860 us
  waiting for transfers between devices  741 us (40%)
  matrix products  486 us (26%)
  local copies, waits for them, and re-layouts  346 us (19%)
  other arithmetic  177 us (9%)
  starting transfers between devices  92 us (5%)
    ppermute x3, waiting for transfers between devices, line_scatter(): right = lax.ppermute(right_out, 'row', [(j, j + 1) for j in range(0, step)])  260 us
    all_gather x8, waiting for transfers between devices, row_gather(): return lax.all_gather(shard, 'row', axis=axis, tiled=True)  178 us
    dot_general x18, matrix products, dot(): return jnp.dot(left, right, preferred_element_type=F32)  172 us
    dot_general x18, matrix products, dot_tn(): lax.dot_general(left, right, (((0,), (0,)), ((), ())), preferred_element_...  168 us
    all_to_all x4, waiting for transfers between devices, exchange(): got = lax.all_to_all(sent, 'row', split_axis=0, concat_axis=0, tiled=True)  125 us
    dot_general x10, matrix products, dot_nt(): lax.dot_general(left, right, (((1,), (1,)), ((), ())), preferred_element_...  105 us
    ppermute x24, waiting for transfers between devices, chip_swap(): lax.ppermute(value, 'col', [(j, j ^ (other if j % 2 else bits)[step]) for...  102 us
    dynamic_update_slice x53, local copies, waits for them, and re-layouts, cube_gather(): lax.dynamic_update_slice_in_dim(out, item, block_at(owner, place) * width...  73.2 us
  transfers between devices with their start and end apart: 84, of which 27 were waited for; matrix products, arithmetic and copies ran while one was open for 47% of the time, Pallas kernels for 0%

profile of v3, /device:TPU:0, one launch (start us, length us, event | category | flops | bytes accessed | tf_op | source)
XLA Modules:
  0.0 1860.6 jit_solution(16013002213966477794)
XLA Ops:
  38.7 48.1 %all-to-all-done.2 = bf16[4,640,256]{2,1,0:T(8,128)(2,1)} async-done(((bf16[4,640,256]{2,1,0:T(8,128)(2,1)}), bf16[4,640,256]{2,1,0:T(8,128)(2,1)}, u32[]{:S(2)}, u32[]{:S(2)}) %all-to-all-start.2) | async-done | bytes 1310752 | tf_op jit(solution)/shard_map/all_to_all | solution.py:195
  158.9 49.2 %all-to-all-done.3 = bf16[4,640,256]{2,1,0:T(8,128)(2,1)} async-done(((bf16[4,640,256]{2,1,0:T(8,128)(2,1)}), bf16[4,640,256]{2,1,0:T(8,128)(2,1)}, u32[]{:S(2)}, u32[]{:S(2)}) %all-to-all-start.3) | async-done | bytes 1310752 | tf_op jit(solution)/shard_map/all_to_all | solution.py:195
  289.4 8.9 fusion.28
  318.9 38.1 %all-gather.11.cloned.1.call-done = bf16[2048,2816]{1,0:T(8,128)(2,1)} async-done(((bf16[512,2816]{1,0:T(8,128)(2,1)}), bf16[2048,2816]{1,0:T(8,128)(2,1)}) %all-gather.11.cloned.1.call-update) | async-done | bytes 11534352 | tf_op jit(solution)/shard_map/all_gather | solution.py:170
  373.8 89.8 %all-gather.13.cloned.1.call-done = bf16[1408,2048]{1,0:T(8,128)(2,1)} async-done(((bf16[1408,512]{1,0:T(8,128)(2,1)}), bf16[1408,2048]{1,0:T(8,128)(2,1)}) %all-gather.13.cloned.1.call-update) | async-done | bytes 5767184 | tf_op jit(solution)/shard_map/all_gather | solution.py:170
  472.4 50.6 %all-gather.15.cloned.1.call-done = bf16[2048,704]{0,1:T(8,128)(2,1)} async-done(((bf16[512,704]{0,1:T(8,128)(2,1)}), bf16[2048,704]{0,1:T(8,128)(2,1)}) %all-gather.15.cloned.1.call-update) | async-done | bytes 2883600 | tf_op jit(solution)/shard_map/all_gather | solution.py:170
  561.7 23.7 %collective-permute-done.11 = bf16[2,256,2048]{2,1,0:T(8,128)(2,1)} collective-permute-done((bf16[2,256,2048]{2,1,0:T(8,128)(2,1)}, bf16[2,256,2048]{2,1,0:T(8,128)(2,1)}, u32[]{:S(2)}, u32[]{:S(2)}) %collective-permute-start.11) | collective-permute-done | bytes 2097184 | tf_op jit(solution)/shard_map/ppermute | solution.py:109
  594.9 9.9 collective-permute-done.12
  627.2 12.8 multiply_convert_fusion.2
  639.9 12.5 multiply_convert_fusion.3
  675.0 13.2 fusion.75
  688.2 11.4 fusion.74
  701.7 14.9 fusion.250
  716.6 14.9 multiply_convert_fusion.10
  731.6 11.9 convolution_convert_fusion.3
  743.4 16.0 convolution_convert_fusion
  759.5 8.6 constant_dynamic-slice_fusion.9
  785.0 18.4 fusion.76
  803.4 14.3 fusion.43
  817.7 136.6 %collective-permute-done.23 = bf16[512,4224]{1,0:T(8,128)(2,1)S(1)} collective-permute-done((bf16[512,4224]{1,0:T(8,128)(2,1)}, bf16[512,4224]{1,0:T(8,128)(2,1)S(1)}, u32[]{:S(2)}, u32[]{:S(2)}) %collective-permute-start.23) | collective-permute-done | bytes 4325408 | tf_op jit(solution)/shard_map/ppermute | solution.py:93
  962.4 10.5 fusion.251
  972.9 11.9 multiply_convert_fusion.15
  984.8 67.7 %collective-permute-done.25 = bf16[512,4224]{1,0:T(8,128)(2,1)S(1)} collective-permute-done((bf16[512,4224]{1,0:T(8,128)(2,1)S(1)}, bf16[512,4224]{1,0:T(8,128)(2,1)S(1)}, u32[]{:S(2)}, u32[]{:S(2)}) %collective-permute-start.25) | collective-permute-done | bytes 4325408 | tf_op jit(solution)/shard_map/ppermute | solution.py:93
  1058.9 18.7 %fusion.252 = f32[1024,2816]{1,0:T(8,128)} fusion(bf16[1024,2048]{1,0:T(8,128)(2,1)} %fusion.75, bf16[2048,2816]{1,0:T(8,128)(2,1)} %all-gather.19.cloned.1.call-done), kind=kOutput, calls=%fused_computation.605 | convolution fusion | flops 11811160064 | bytes 27262976 | tf_op jit(solution)/shard_map/dot_general | solution.py:59
  1077.7 16.5 multiply_convert_fusion.7
  1094.7 18.5 fusion.362
  1113.1 14.7 fusion.40
  1127.9 13.6 add_convert_fusion.1
  1178.8 16.4 collective-permute-done.28
  1198.1 13.0 collective-permute-done.29
  1235.5 55.9 %collective-permute-done.38 = bf16[512,4224]{1,0:T(8,128)(2,1)} collective-permute-done((bf16[512,4224]{1,0:T(8,128)(2,1)}, bf16[512,4224]{1,0:T(8,128)(2,1)}, u32[]{:S(2)}, u32[]{:S(2)}) %collective-permute-start.38) | collective-permute-done | bytes 4325408 | tf_op jit(solution)/shard_map/ppermute | solution.py:93
  1306.6 8.0 fusion.257
  1314.7 8.3 copy.370
  1377.8 12.3 copy.361
  1399.5 23.3 %reduce-scatter.21.cloned.1.call-done = bf16[1408,512]{0,1:T(8,128)(2,1)} async-done(((bf16[1408,2048]{0,1:T(8,128)(2,1)}), bf16[1408,512]{0,1:T(8,128)(2,1)}) %reduce-scatter.21.cloned.1.call-update) | async-done | bytes 1441808 | tf_op jit(solution)/shard_map/reduce_scatter | solution.py:179
  1424.6 10.5 convolution_convert_fusion.4
  1439.1 8.7 multiply_convert_fusion.4.clone.2
  1449.5 11.6 fusion.45
  1477.4 18.6 fusion.255
  1496.0 9.1 reduce-scatter.11.cloned.1.call-done
  1505.1 9.6 multiply_convert_fusion.1.clone.5
  1514.7 12.0 fusion.39
  1554.0 19.5 %add_convert_fusion = bf16[2048,2048]{1,0:T(8,128)(2,1)} fusion(f32[2048,2048]{1,0:T(8,128)} %fusion.39, f32[2048,2048]{1,0:T(8,128)} %fusion.45, bf16[2048,352]{0,1:T(8,128)(2,1)} %get-tuple-element.687, bf16[352,2048]{1,0:T(8,128)(2,1)} %all-gather.17.cloned.1.call-done), kind=kOutput, calls=%fused_computation.47 | convolution fusion | flops 2965372928 | bytes 44826624 | tf_op jit(solution)/shard_map/dot_general | solution.py:59
  1621.2 8.4 collective-permute-done.41
  1641.9 21.3 %collective-permute-done.36 = bf16[2,256,2048]{2,1,0:T(8,128)(2,1)S(1)} collective-permute-done((bf16[2,256,2048]{2,1,0:T(8,128)(2,1)}, bf16[2,256,2048]{2,1,0:T(8,128)(2,1)S(1)}, u32[]{:S(2)}, u32[]{:S(2)}) %collective-permute-start.36) | collective-permute-done | bytes 2097184 | tf_op jit(solution)/shard_map/ppermute | solution.py:109
  1704.3 9.1 all-to-all-done.4
  1781.8 28.1 %all-to-all-done.5 = bf16[4,640,256]{2,1,0:T(8,128)(2,1)S(1)} async-done(((bf16[4,640,256]{2,1,0:T(8,128)(2,1)}), bf16[4,640,256]{2,1,0:T(8,128)(2,1)S(1)}, u32[]{:S(2)}, u32[]{:S(2)}) %all-to-all-start.5) | async-done | bytes 1310752 | tf_op jit(solution)/shard_map/all_to_all | solution.py:195
  1829.2 22.7 %reduce-scatter.17.cloned.1.call-done = bf16[512,384]{1,0:T(8,128)(2,1)} async-done(((bf16[2048,384]{1,0:T(8,128)(2,1)}), bf16[512,384]{1,0:T(8,128)(2,1)}) %reduce-scatter.17.cloned.1.call-update) | async-done | bytes 393232 | tf_op jit(solution)/shard_map/reduce_scatter | solution.py:179
  (930 shorter events, 739.8 us)
Async XLA Ops:
  26.7 60.1 %all-to-all-start.2 = ((bf16[4,640,256]{2,1,0:T(8,128)(2,1)}), bf16[4,640,256]{2,1,0:T(8,128)(2,1)}, u32[]{:S(2)}, u32[]{:S(2)}) async-start(bf16[4,640,256]{2,1,0:T(8,128)(2,1)} %bitcast.572), calls=%async_computation.2 | async-start | bytes 2621440 | tf_op jit(solution)/shard_map/all_to_all | solution.py:195
  33.1 65.8 %all-gather.23.cloned.1.call-start = ((), (), s32[]{:S(2)}) async-start(), calls=%async_computation.29 | async-start | bytes 2396160 | tf_op jit(solution)/shard_map/all_gather | solution.py:170
  35.4 195.8 %all-gather.25.cloned.1.call-start = ((), (), s32[]{:S(2)}) async-start(), calls=%async_computation.30 | async-start | bytes 1966080 | tf_op jit(solution)/shard_map/all_gather | solution.py:170
  93.5 263.4 %all-gather.11.cloned.1.call-start = ((), (), s32[]{:S(2)}) async-start(), calls=%async_computation.16 | async-start | bytes 14417920 | tf_op jit(solution)/shard_map/all_gather | solution.py:170
  112.8 29.9 %collective-permute-start.1 = (bf16[1,2048,256]{1,2,0:T(8,128)(2,1)}, bf16[1,2048,256]{1,2,0:T(8,128)(2,1)}, u32[]{:S(2)}, u32[]{:S(2)}) collective-permute-start(bf16[1,2048,256]{1,2,0:T(8,128)(2,1)} %bitcast.8), channel_id=1, source_target_pairs={{0,2},{1,5},{2,0},{3,7},{4,6},{5,1},{6,4},{7,3},{8,10},{9,13},{10,... | collective-permute-start | bytes 3145736 | tf_op jit(solution)/shard_map/ppermute | solution.py:109
  114.4 26.0 %collective-permute-start = (bf16[1,2048,256]{1,2,0:T(8,128)(2,1)}, bf16[1,2048,256]{1,2,0:T(8,128)(2,1)}, u32[]{:S(2)}, u32[]{:S(2)}) collective-permute-start(bf16[1,2048,256]{1,2,0:T(8,128)(2,1)} %bitcast.8), channel_id=1, source_target_pairs={{0,1},{1,0},{2,3},{3,2},{4,5},{5,4},{6,7},{7,6},{8,9},{9,8},{10,11... | collective-permute-start | bytes 3145736 | tf_op jit(solution)/shard_map/ppermute | solution.py:99
  129.3 27.9 %collective-permute-start.5 = (bf16[1,256,576]{2,1,0:T(8,128)(2,1)S(1)}, bf16[1,256,576]{2,1,0:T(8,128)(2,1)}, u32[]{:S(2)}, u32[]{:S(2)}) collective-permute-start(bf16[1,256,576]{2,1,0:T(8,128)(2,1)S(1)} %broadcast_in_dim_reshape.3), channel_id=1, source_target_pairs={{0,1},{1,0},{2,3},{3,2},{4,5},{5,4},{6,7},{7,6},{8,9},{9,8},{10,11... | collective-permute-start | bytes 884744 | tf_op jit(solution)/shard_map/ppermute | solution.py:99
  134.7 73.4 %all-to-all-start.3 = ((bf16[4,640,256]{2,1,0:T(8,128)(2,1)}), bf16[4,640,256]{2,1,0:T(8,128)(2,1)}, u32[]{:S(2)}, u32[]{:S(2)}) async-start(bf16[4,640,256]{2,1,0:T(8,128)(2,1)} %bitcast.573), calls=%async_computation.3 | async-start | bytes 2621440 | tf_op jit(solution)/shard_map/all_to_all | solution.py:195
  139.1 324.5 %all-gather.13.cloned.1.call-start = ((), (), s32[]{:S(2)}) async-start(), calls=%async_computation.17 | async-start | bytes 7208960 | tf_op jit(solution)/shard_map/all_gather | solution.py:170
  146.2 102.3 %collective-permute-start.3 = (bf16[2,2048,256]{1,2,0:T(8,128)(2,1)}, bf16[2,2048,256]{1,2,0:T(8,128)(2,1)}, u32[]{:S(2)}, u32[]{:S(2)}) collective-permute-start(bf16[2,2048,256]{1,2,0:T(8,128)(2,1)} %pad_maximum_fusion.20), channel_id=1, source_target_pairs={{0,4},{1,3},{2,6},{3,1},{4,0},{5,7},{6,2},{7,5},{8,12},{9,11},{10,... | collective-permute-start | bytes 6291464 | tf_op jit(solution)/shard_map/ppermute | solution.py:109
  150.0 76.6 %collective-permute-start.2 = (bf16[1,2048,256]{1,2,0:T(8,128)(2,1)}, bf16[1,2048,256]{1,2,0:T(8,128)(2,1)}, u32[]{:S(2)}, u32[]{:S(2)}) collective-permute-start(bf16[1,2048,256]{1,2,0:T(8,128)(2,1)} %collective-permute-done.1), channel_id=1, source_target_pairs={{0,1},{1,0},{2,3},{3,2},{4,5},{5,4},{6,7},{7,6},{8,9},{9,8},{10,11... | collective-permute-start | bytes 3145736 | tf_op jit(solution)/shard_map/ppermute | solution.py:99
  155.5 59.5 %collective-permute-start.8 = (bf16[2,256,576]{1,2,0:T(8,128)(2,1)}, bf16[2,256,576]{1,2,0:T(8,128)(2,1)}, u32[]{:S(2)}, u32[]{:S(2)}) collective-permute-start(bf16[2,256,576]{1,2,0:T(8,128)(2,1)} %copy.304), channel_id=1, source_target_pairs={{0,4},{1,3},{2,6},{3,1},{4,0},{5,7},{6,2},{7,5},{8,12},{9,11},{10,... | collective-permute-start | bytes 1769480 | tf_op jit(solution)/shard_map/ppermute | solution.py:109
  220.6 32.6 %collective-permute-start.18 = (bf16[1,2048,256]{1,2,0:T(8,128)(2,1)}, bf16[1,2048,256]{1,2,0:T(8,128)(2,1)}, u32[]{:S(2)}, u32[]{:S(2)}) collective-permute-start(bf16[1,2048,256]{1,2,0:T(8,128)(2,1)} %bitcast.73), channel_id=1, source_target_pairs={{0,1},{1,0},{2,3},{3,2},{4,5},{5,4},{6,7},{7,6},{8,9},{9,8},{10,11... | collective-permute-start | bytes 3145736 | tf_op jit(solution)/shard_map/ppermute | solution.py:99
  237.1 285.9 %all-gather.15.cloned.1.call-start = ((), (), s32[]{:S(2)}) async-start(), calls=%async_computation.18 | async-start | bytes 3604480 | tf_op jit(solution)/shard_map/all_gather | solution.py:170
  240.4 26.4 %collective-permute-start.21 = (bf16[2,2048,256]{1,2,0:T(8,128)(2,1)}, bf16[2,2048,256]{1,2,0:T(8,128)(2,1)}, u32[]{:S(2)}, u32[]{:S(2)}) collective-permute-start(bf16[2,2048,256]{1,2,0:T(8,128)(2,1)} %pad_maximum_fusion.22), channel_id=1, source_target_pairs={{0,4},{1,3},{2,6},{3,1},{4,0},{5,7},{6,2},{7,5},{8,12},{9,11},{10,... | collective-permute-start | bytes 6291464 | tf_op jit(solution)/shard_map/ppermute | solution.py:109
  356.9 301.7 %all-gather.17.cloned.1.call-start = ((), (), s32[]{:S(2)}) async-start(), calls=%async_computation.19 | async-start | bytes 1802240 | tf_op jit(solution)/shard_map/all_gather | solution.py:170
  463.6 595.3 %all-gather.19.cloned.1.call-start = ((), (), s32[]{:S(2)}) async-start(), calls=%async_computation.20 | async-start | bytes 14417920 | tf_op jit(solution)/shard_map/all_gather | solution.py:170
  523.0 554.7 %all-gather.21.cloned.1.call-start = ((), (), s32[]{:S(2)}) async-start(), calls=%async_computation.21 | async-start | bytes 7208960 | tf_op jit(solution)/shard_map/all_gather | solution.py:170
  559.1 26.4 %collective-permute-start.11 = (bf16[2,256,2048]{2,1,0:T(8,128)(2,1)}, bf16[2,256,2048]{2,1,0:T(8,128)(2,1)}, u32[]{:S(2)}, u32[]{:S(2)}) collective-permute-start(bf16[2,256,2048]{2,1,0:T(8,128)(2,1)} %slice.820), channel_id=1, source_target_pairs={{0,4},{1,3},{2,6},{3,1},{4,0},{5,7},{6,2},{7,5},{8,12},{9,11},{10,... | collective-permute-start | bytes 6291464 | tf_op jit(solution)/shard_map/ppermute | solution.py:109
  561.7 48.6 %collective-permute-start.22 = (bf16[2,2048,256]{1,2,0:T(8,128)(2,1)}, bf16[2,2048,256]{1,2,0:T(8,128)(2,1)}, u32[]{:S(2)}, u32[]{:S(2)}) collective-permute-start(bf16[2,2048,256]{1,2,0:T(8,128)(2,1)} %collective-permute-done.21), channel_id=1, source_target_pairs={{0,1},{1,0},{2,3},{3,2},{4,5},{5,4},{6,7},{7,6},{8,9},{9,8},{10,11... | collective-permute-start | bytes 6291464 | tf_op jit(solution)/shard_map/ppermute | solution.py:99
  625.6 27.4 %collective-permute-start.16 = (bf16[2,256,2048]{2,1,0:T(8,128)(2,1)S(1)}, bf16[2,256,2048]{2,1,0:T(8,128)(2,1)}, u32[]{:S(2)}, u32[]{:S(2)}) collective-permute-start(bf16[2,256,2048]{2,1,0:T(8,128)(2,1)S(1)} %pad_maximum_fusion.21), channel_id=1, source_target_pairs={{0,4},{1,3},{2,6},{3,1},{4,0},{5,7},{6,2},{7,5},{8,12},{9,11},{10,... | collective-permute-start | bytes 6291464 | tf_op jit(solution)/shard_map/ppermute | solution.py:109
  658.6 656.0 %reduce-scatter.19.cloned.1.call-start = ((), (), s32[]{:S(2)}) async-start(), calls=%async_computation.26 | async-start | bytes 1802240 | tf_op jit(solution)/shard_map/reduce_scatter | solution.py:179
  779.8 174.5 %collective-permute-start.23 = (bf16[512,4224]{1,0:T(8,128)(2,1)}, bf16[512,4224]{1,0:T(8,128)(2,1)S(1)}, u32[]{:S(2)}, u32[]{:S(2)}) collective-permute-start(bf16[512,4224]{1,0:T(8,128)(2,1)} %pad_maximum_fusion.5), channel_id=1, source_target_pairs={{0,8},{1,9},{2,10},{3,11},{4,12},{5,13},{6,14},{7,15}} | collective-permute-start | bytes 12976136 | tf_op jit(solution)/shard_map/ppermute | solution.py:93
  784.1 176.1 %collective-permute-start.24 = (bf16[512,4224]{1,0:T(8,128)(2,1)}, bf16[512,4224]{1,0:T(8,128)(2,1)S(1)}, u32[]{:S(2)}, u32[]{:S(2)}) collective-permute-start(bf16[512,4224]{1,0:T(8,128)(2,1)} %pad_maximum_fusion.6), channel_id=1, source_target_pairs={{24,16},{25,17},{26,18},{27,19},{28,20},{29,21},{30,22},{31,23}} | collective-permute-start | bytes 12976136 | tf_op jit(solution)/shard_map/ppermute | solution.py:94
  955.4 97.1 %collective-permute-start.25 = (bf16[512,4224]{1,0:T(8,128)(2,1)S(1)}, bf16[512,4224]{1,0:T(8,128)(2,1)S(1)}, u32[]{:S(2)}, u32[]{:S(2)}) collective-permute-start(bf16[512,4224]{1,0:T(8,128)(2,1)S(1)} %add_convert_fusion.5), channel_id=1, source_target_pairs={{0,8},{8,16},{1,9},{9,17},{2,10},{10,18},{3,11},{11,19},{4,12},{12... | collective-permute-start | bytes 12976136 | tf_op jit(solution)/shard_map/ppermute | solution.py:93
  961.3 94.1 %collective-permute-start.26 = (bf16[512,4224]{1,0:T(8,128)(2,1)S(1)}, bf16[512,4224]{1,0:T(8,128)(2,1)S(1)}, u32[]{:S(2)}, u32[]{:S(2)}) collective-permute-start(bf16[512,4224]{1,0:T(8,128)(2,1)S(1)} %add_convert_fusion.4), channel_id=1, source_target_pairs={{16,8},{24,16},{17,9},{25,17},{18,10},{26,18},{19,11},{27,19},{20,... | collective-permute-start | bytes 12976136 | tf_op jit(solution)/shard_map/ppermute | solution.py:94
  1169.1 26.1 %collective-permute-start.28 = (bf16[2,256,2048]{2,1,0:T(8,128)(2,1)S(1)}, bf16[2,256,2048]{2,1,0:T(8,128)(2,1)S(1)}, u32[]{:S(2)}, u32[]{:S(2)}) collective-permute-start(bf16[2,256,2048]{2,1,0:T(8,128)(2,1)S(1)} %slice.844), channel_id=1, source_target_pairs={{0,4},{1,3},{2,6},{3,1},{4,0},{5,7},{6,2},{7,5},{8,12},{9,11},{10,... | collective-permute-start | bytes 6291464 | tf_op jit(solution)/shard_map/ppermute | solution.py:109
  1170.9 120.5 %collective-permute-start.38 = (bf16[512,4224]{1,0:T(8,128)(2,1)}, bf16[512,4224]{1,0:T(8,128)(2,1)}, u32[]{:S(2)}, u32[]{:S(2)}) collective-permute-start(bf16[512,4224]{1,0:T(8,128)(2,1)} %add_convert_fusion.3), channel_id=1, source_target_pairs={{0,8},{8,16},{16,24},{1,9},{9,17},{17,25},{2,10},{10,18},{18,26},{... | collective-permute-start | bytes 12976136 | tf_op jit(solution)/shard_map/ppermute | solution.py:93
  1177.4 120.2 %collective-permute-start.39 = (bf16[512,4224]{1,0:T(8,128)(2,1)}, bf16[512,4224]{1,0:T(8,128)(2,1)}, u32[]{:S(2)}, u32[]{:S(2)}) collective-permute-start(bf16[512,4224]{1,0:T(8,128)(2,1)} %add_convert_fusion.2), channel_id=1, source_target_pairs={{8,0},{16,8},{24,16},{9,1},{17,9},{25,17},{10,2},{18,10},{26,18},{... | collective-permute-start | bytes 12976136 | tf_op jit(solution)/shard_map/ppermute | solution.py:94
  1225.0 197.8 %reduce-scatter.21.cloned.1.call-start = ((), (), s32[]{:S(2)}) async-start(), calls=%async_computation.27 | async-start | bytes 7208960 | tf_op jit(solution)/shard_map/reduce_scatter | solution.py:179
  1233.8 89.4 %collective-permute-start.33 = (bf16[2,256,2048]{2,1,0:T(8,128)(2,1)}, bf16[2,256,2048]{2,1,0:T(8,128)(2,1)}, u32[]{:S(2)}, u32[]{:S(2)}) collective-permute-start(bf16[2,256,2048]{2,1,0:T(8,128)(2,1)} %pad_maximum_fusion.23), channel_id=1, source_target_pairs={{0,4},{1,3},{2,6},{3,1},{4,0},{5,7},{6,2},{7,5},{8,12},{9,11},{10,... | collective-permute-start | bytes 6291464 | tf_op jit(solution)/shard_map/ppermute | solution.py:109
  1323.0 153.4 %reduce-scatter.23.cloned.1.call-start = ((), (), s32[]{:S(2)}) async-start(), calls=%async_computation.28 | async-start | bytes 655360 | tf_op jit(solution)/shard_map/reduce_scatter | solution.py:179
  1393.5 29.4 %collective-permute-start.44 = (bf16[2,256,576]{1,2,0:T(8,128)(2,1)S(1)}, bf16[2,256,576]{1,2,0:T(8,128)(2,1)S(1)}, u32[]{:S(2)}, u32[]{:S(2)}) collective-permute-start(bf16[2,256,576]{1,2,0:T(8,128)(2,1)S(1)} %slice.871), channel_id=1, source_target_pairs={{0,4},{1,3},{2,6},{3,1},{4,0},{5,7},{6,2},{7,5},{8,12},{9,11},{10,... | collective-permute-start | bytes 1769480 | tf_op jit(solution)/shard_map/ppermute | solution.py:109
  1422.8 82.2 %reduce-scatter.11.cloned.1.call-start = ((), (), s32[]{:S(2)}) async-start(), calls=%async_computation.22 | async-start | bytes 3604480 | tf_op jit(solution)/shard_map/reduce_scatter | solution.py:179
  1435.1 250.1 %reduce-scatter.25.cloned.1.call-start = ((), (), s32[]{:S(2)}) async-start(), calls=%async_computation.31 | async-start | bytes 409600
  1477.3 297.7 %reduce-scatter.13.cloned.1.call-start = ((), (), s32[]{:S(2)}) async-start(), calls=%async_computation.23 | async-start | bytes 14417920 | tf_op jit(solution)/shard_map/reduce_scatter | solution.py:179
  1554.0 43.5 %collective-permute-start.40 = (bf16[4,256,2048]{2,1,0:T(8,128)(2,1)}, bf16[4,256,2048]{2,1,0:T(8,128)(2,1)}, u32[]{:S(2)}, u32[]{:S(2)}) collective-permute-start(bf16[4,256,2048]{2,1,0:T(8,128)(2,1)} %pad_maximum_fusion.10), channel_id=1, source_target_pairs={{0,1},{1,0},{2,3},{3,2},{4,5},{5,4},{6,7},{7,6},{8,9},{9,8},{10,11... | collective-permute-start | bytes 12582920 | tf_op jit(solution)/shard_map/ppermute | solution.py:99
  1603.3 26.4 %collective-permute-start.41 = (bf16[2,256,2048]{2,1,0:T(8,128)(2,1)}, bf16[2,256,2048]{2,1,0:T(8,128)(2,1)}, u32[]{:S(2)}, u32[]{:S(2)}) collective-permute-start(bf16[2,256,2048]{2,1,0:T(8,128)(2,1)} %slice.861), channel_id=1, source_target_pairs={{0,4},{1,3},{2,6},{3,1},{4,0},{5,7},{6,2},{7,5},{8,12},{9,11},{10,... | collective-permute-start | bytes 6291464 | tf_op jit(solution)/shard_map/ppermute | solution.py:109
  1613.9 49.3 %collective-permute-start.36 = (bf16[2,256,2048]{2,1,0:T(8,128)(2,1)}, bf16[2,256,2048]{2,1,0:T(8,128)(2,1)S(1)}, u32[]{:S(2)}, u32[]{:S(2)}) collective-permute-start(bf16[2,256,2048]{2,1,0:T(8,128)(2,1)} %slice.852), channel_id=1, source_target_pairs={{0,4},{1,3},{2,6},{3,1},{4,0},{5,7},{6,2},{7,5},{8,12},{9,11},{10,... | collective-permute-start | bytes 6291464 | tf_op jit(solution)/shard_map/ppermute | solution.py:109
  1633.2 34.6 %collective-permute-start.42 = (bf16[1,256,2048]{2,1,0:T(8,128)(2,1)S(1)}, bf16[1,256,2048]{2,1,0:T(8,128)(2,1)S(1)}, u32[]{:S(2)}, u32[]{:S(2)}) collective-permute-start(bf16[1,256,2048]{2,1,0:T(8,128)(2,1)S(1)} %slice.863), channel_id=1, source_target_pairs={{0,2},{1,5},{2,0},{3,7},{4,6},{5,1},{6,4},{7,3},{8,10},{9,13},{10,... | collective-permute-start | bytes 3145736 | tf_op jit(solution)/shard_map/ppermute | solution.py:109
  1686.8 31.3 %collective-permute-start.58 = (bf16[1,64,576]{1,2,0:T(8,128)(2,1)}, bf16[1,64,576]{1,2,0:T(8,128)(2,1)}, u32[]{:S(2)}, u32[]{:S(2)}) collective-permute-start(bf16[1,64,576]{1,2,0:T(8,128)(2,1)} %bitcast.171), channel_id=1, source_target_pairs={{0,2},{1,5},{2,0},{3,7},{4,6},{5,1},{6,4},{7,3},{8,10},{9,13},{10,... | collective-permute-start | bytes 221192 | tf_op jit(solution)/shard_map/ppermute | solution.py:109
  1688.7 46.6 %collective-permute-start.57 = (bf16[1,64,576]{1,2,0:T(8,128)(2,1)}, bf16[1,64,576]{1,2,0:T(8,128)(2,1)}, u32[]{:S(2)}, u32[]{:S(2)}) collective-permute-start(bf16[1,64,576]{1,2,0:T(8,128)(2,1)} %bitcast.171), channel_id=1, source_target_pairs={{0,1},{1,0},{2,3},{3,2},{4,5},{5,4},{6,7},{7,6},{8,9},{9,8},{10,11... | collective-permute-start | bytes 221192 | tf_op jit(solution)/shard_map/ppermute | solution.py:99
  1688.7 31.7 %collective-permute-start.46 = (f32[4608]{0:T(1024)S(1)}, f32[4608]{0:T(1024)S(1)}, u32[]{:S(2)}, u32[]{:S(2)}) collective-permute-start(f32[4608]{0:T(1024)S(1)} %pad_maximum_fusion.44), channel_id=1, source_target_pairs={{0,1},{1,0},{2,3},{3,2},{4,5},{5,4},{6,7},{7,6},{8,9},{9,8},{10,11... | collective-permute-start | bytes 55304 | tf_op jit(solution)/shard_map/ppermute | solution.py:99
  1713.4 46.2 %all-to-all-start.7 = ((bf16[4,640,256]{2,1,0:T(8,128)(2,1)}), bf16[4,640,256]{2,1,0:T(8,128)(2,1)}, u32[]{:S(2)}, u32[]{:S(2)}) async-start(bf16[4,640,256]{2,1,0:T(8,128)(2,1)} %bitcast.571), calls=%async_computation.7 | async-start | bytes 2621440 | tf_op jit(solution)/shard_map/all_to_all | solution.py:195
  1719.9 25.3 %collective-permute-start.60 = (bf16[2,64,576]{1,2,0:T(8,128)(2,1)}, bf16[2,64,576]{1,2,0:T(8,128)(2,1)}, u32[]{:S(2)}, u32[]{:S(2)}) collective-permute-start(bf16[2,64,576]{1,2,0:T(8,128)(2,1)} %pad_maximum_fusion.42), channel_id=1, source_target_pairs={{0,4},{1,3},{2,6},{3,1},{4,0},{5,7},{6,2},{7,5},{8,12},{9,11},{10,... | collective-permute-start | bytes 442376 | tf_op jit(solution)/shard_map/ppermute | solution.py:109
  1759.6 50.3 %all-to-all-start.5 = ((bf16[4,640,256]{2,1,0:T(8,128)(2,1)}), bf16[4,640,256]{2,1,0:T(8,128)(2,1)S(1)}, u32[]{:S(2)}, u32[]{:S(2)}) async-start(bf16[4,640,256]{2,1,0:T(8,128)(2,1)} %bitcast.114), calls=%async_computation.5 | async-start | bytes 2621440 | tf_op jit(solution)/shard_map/all_to_all | solution.py:195
  1763.6 53.5 %reduce-scatter.15.cloned.1.call-start = ((), (), s32[]{:S(2)}) async-start(), calls=%async_computation.24 | async-start | bytes 1310720 | tf_op jit(solution)/shard_map/reduce_scatter | solution.py:179
  1775.1 76.8 %reduce-scatter.17.cloned.1.call-start = ((), (), s32[]{:S(2)}) async-start(), calls=%async_computation.25 | async-start | bytes 1966080 | tf_op jit(solution)/shard_map/reduce_scatter | solution.py:179
  (221 other events, 5463.9 us)
Sparse Core Ops, SparseCore 0:
  36.1 59.6 all-gather.22
  97.4 36.2 all-gather.24
  135.8 221.0 all-gather.10
  358.3 105.2 all-gather.12
  465.6 57.3 all-gather.14
  524.4 33.6 all-gather.16
  559.7 199.9 all-gather.18
  761.3 179.5 all-gather.20
  1225.1 54.6 reduce-scatter.18
  1323.1 99.6 reduce-scatter.20
  1425.7 22.1 reduce-scatter.22
  1450.6 54.4 reduce-scatter.10
  1507.9 19.9 reduce-scatter.24
  1530.1 195.5 reduce-scatter.12
  1775.2 36.2 reduce-scatter.14
  1817.2 34.6 reduce-scatter.16

commit v4 on v3

--- a/solution.py
+++ b/solution.py
@@ -1,6 +1,7 @@
 import jax
 import jax.numpy as jnp
 from jax import lax
+from jax.experimental.layout import Layout, with_layout_constraint
 from jax.sharding import PartitionSpec as P
 
 NOPE = 128
@@ -67,32 +68,62 @@
     return lax.dot_general(left, right, (((0,), (0,)), ((), ())), preferred_element_type=F32)
 
 
-def line_scatter(values):
+def row_major(value):
+    return with_layout_constraint(value, Layout(tuple(range(value.ndim))))
+
+
+def row_swap(value, bit):
+    return lax.ppermute(value, "row", [(j, j ^ bit) for j in range(lax.axis_size("row"))])
+
+
+def mate(value):
+    return row_swap(value, lax.axis_size("row") // 2)
+
+
+def half_bits():
+    return [1 << b for b in range((lax.axis_size("row") // 2).bit_length() - 1)]
+
+
+def expert_gather(kept, given, axis):
     count = lax.axis_size("row")
     index = lax.axis_index("row")
-
-    def block(j):
-        place = jnp.clip(j, 0, count - 1)
-        return jnp.concatenate(
-            [
-                lax.dynamic_slice_in_dim(
-                    value, place * (value.shape[0] // count), value.shape[0] // count, 0
-                )
-                for value in values
-            ],
-            axis=1,
-        )
-
-    right, left = None, None
-    for step in range(1, count):
-        right_out, left_out = block(index + count - step), block(index - count + step)
-        if right is not None:
-            right_out = (right_out.astype(F32) + right.astype(F32)).astype(BF16)
-            left_out = (left_out.astype(F32) + left.astype(F32)).astype(BF16)
-        yield right_out, left_out
-        right = lax.ppermute(right_out, "row", [(j, j + 1) for j in range(0, step)])
-        left = lax.ppermute(left_out, "row", [(j, j - 1) for j in range(count - step, count)])
-    yield block(index).astype(F32) + right.astype(F32) + left.astype(F32)
+    width = kept.shape[axis]
+    shape = list(kept.shape)
+    shape[axis] = width * count
+    out = jnp.zeros(shape, kept.dtype)
+    for first, item in ((0, kept), (count // 2, mate(given))):
+        items = {first: item}
+        for bit in half_bits():
+            items.update({key ^ bit: row_swap(items[key], bit) for key in list(items)})
+        for key, piece in items.items():
+            out = lax.dynamic_update_slice_in_dim(
+                out, piece, jnp.bitwise_xor(index, key) * width, axis
+            )
+    return out
+
+
+def expert_scatter(value, axis):
+    count = lax.axis_size("row")
+    index = lax.axis_index("row")
+    width = value.shape[axis] // count
+    sums = []
+    for first in (count // 2, 0):
+        items = {
+            key: lax.dynamic_slice_in_dim(
+                value, jnp.bitwise_xor(index, key ^ first) * width, width, axis
+            )
+            for key in range(count // 2)
+        }
+        for bit in half_bits()[::-1]:
+            items = {
+                key: (
+                    items[key].astype(F32) + row_swap(items[key ^ bit], bit).astype(F32)
+                ).astype(BF16)
+                for key in items
+                if key < bit
+            }
+        sums.append(items[0])
+    return sums[1], sums[0]
 
 
 def swap(value, bit):
@@ -127,7 +158,7 @@
     shape = list(block.shape)
     shape[axis] = width * count
     out = jnp.zeros(shape, block.dtype)
-    held = block[None]
+    held = row_major(block)[None]
     sibling = jnp.bitwise_xor(index, 1)
     done = 0
     for step in range(len(chip_bits()) + 1):
@@ -147,6 +178,7 @@
     count = lax.axis_size("col")
     index = lax.axis_index("col")
     rows = value.shape[0] // count
+    value = row_major(value)
 
     def blocks(device):
         return jnp.stack(
@@ -189,11 +221,17 @@
     return total
 
 
-def exchange(value, here, there):
+def onehot(index, width):
+    return (index[:, None] == jnp.arange(width, dtype=jnp.int32)[None, :]).astype(BF16)
+
+
+def exchange(value, sent_of, slot_of):
     count = lax.axis_size("row")
-    sent = dot(here, value).astype(BF16).reshape(count, -1, value.shape[1])
+    sent = row_major(dot(onehot(sent_of, value.shape[0]), value).astype(BF16))
+    sent = sent.reshape(count, -1, value.shape[1])
     got = lax.all_to_all(sent, "row", split_axis=0, concat_axis=0, tiled=True)
-    return dot_tn(there, got.reshape(-1, value.shape[1])).astype(BF16)
+    got = got.reshape(-1, value.shape[1])
+    return row_major(dot(onehot(slot_of, got.shape[0]), got).astype(BF16))
 
 
 def body(
@@ -248,37 +286,51 @@
     )
     rounds = (jnp.max(all_counts) + room - 1) // room
 
+    inverse_group = jnp.arange(row_count, dtype=jnp.int32)[:, None, None]
+    here_hit = (place_in[:, :, None] == token_ids[None, None, :]) & from_here[:, :, None]
+    rank_of = jnp.sum(jnp.where(here_hit, rank_here[:, :, None], 0), axis=(0, 1))
+    group_of = jnp.sum(jnp.where(here_hit, inverse_group, 0), axis=(0, 1))
+
     def maps(step):
         places = step * room + jnp.arange(room, dtype=jnp.int32)
+
+        def listed(row_of, rank):
+            hit = (rank[None, None, :] == places[None, :, None]) & (
+                row_of[None, None, :] == jnp.arange(row_count, dtype=jnp.int32)[:, None, None]
+            )
+            return jnp.sum(jnp.where(hit, token_ids[None, None, :] + 1, 0), axis=2).reshape(-1) - 1
+
+        def slots(row_of, rank):
+            inside = (rank >= places[0]) & (rank < places[0] + room)
+            return jnp.where(inside, row_of * room + rank - places[0], -1)
+
         hit = rank_here[:, None, :] == places[None, :, None]
-        token = jnp.sum(jnp.where(hit, place_in[:, None, :] + 1, 0), axis=2).reshape(-1) - 1
-        here = (token[:, None] == token_ids[None, :]).astype(BF16)
-        slot = my_rank - step * room
-        slot = jnp.where((slot >= 0) & (slot < room), my_source * room + slot, -1)
-        there = (jnp.arange(row_count * room, dtype=jnp.int32)[:, None] == slot[None, :]).astype(
-            BF16
-        )
-        return here, there
-
-    here, there = maps(0)
+        out_tokens = jnp.sum(jnp.where(hit, place_in[:, None, :] + 1, 0), axis=2).reshape(-1) - 1
+        dealt = (my_source, my_rank)
+        return out_tokens, slots(*dealt), listed(*dealt), slots(group_of, rank_of)
+
+    out_list, in_slots, back_list, back_slots = maps(0)
 
     def more_dealt(carry):
         step, total = carry
-        here_more, there_more = maps(step)
+        out_more, in_more, _, _ = maps(step)
         given = jnp.concatenate([tokens, cotangent], axis=1)
-        return step + 1, total + exchange(given, here_more, there_more)
-
-    picks, weights = [], []
-    slot_ids = jnp.arange(capacity, dtype=jnp.int32)
-    for number in range(local_count):
-        named = routes == (col_index * local_count + number)
+        return step + 1, total + exchange(given, out_more, in_more)
+
+    host = row_index // (row_count // 2)
+    expert = col_index * local_count + host
+
+    def chosen(group_routes, group_gates):
+        named = group_routes == expert
         named_any = jnp.any(named, axis=1)
         running = jnp.cumsum(named_any.astype(jnp.int32))
         place = jnp.where(named_any, running - 1, -1)
-        pick = place[None, :] == slot_ids[:, None]
-        token_weight = jnp.sum(jnp.where(named, gate_weights, 0.0), axis=1)
-        picks.append(pick.astype(BF16))
-        weights.append(jnp.sum(jnp.where(pick, token_weight[None, :], 0.0), axis=1))
+        pick = place[None, :] == jnp.arange(capacity, dtype=jnp.int32)[:, None]
+        token_weight = jnp.sum(jnp.where(named, group_gates, 0.0), axis=1)
+        return pick.astype(BF16), jnp.sum(jnp.where(pick, token_weight[None, :], 0.0), axis=1)
+
+    pick, weight = chosen(routes, gate_weights)
+    mate_pick, mate_weight = chosen(mate(routes), mate(gate_weights))
     document, position = documents(doc_lengths[0], group_rows)
 
     rows_in, dim = w_query.shape[0], w_query.shape[0] * row_count
@@ -289,7 +341,7 @@
         more_dealt,
         (jnp.int32(1), jnp.zeros((group_rows, 2 * slice_width), BF16)),
     )[1]
-    dealt_x = exchange(tokens, here, there) + more[:, :slice_width]
+    dealt_x = exchange(tokens, out_list, in_slots) + more[:, :slice_width]
     full_x = cube_gather(dealt_x, 1)
 
     query_width = w_query.shape[1]
@@ -305,6 +357,7 @@
         axis=0,
     )
     first_s = jnp.pad(first_s, ((0, -first_s.shape[0] % 16), (0, 0)))
+    (first_s,) = after((first_s,), (dealt_x,))
     first_w = row_gather(first_s[None], 0)
     query_w = first_w[:, :rows_in].reshape(dim, query_width)
     lat_end = rows_in + lat_rows * lat_wide // query_width
@@ -317,8 +370,9 @@
     latent_g = gains[:, 2 * wide : 2 * wide + latent_gain.shape[0]].reshape(-1).astype(F32)
 
     (cotangent_s,) = after((cotangent,), (dealt_x,))
-    dealt_dy = exchange(cotangent_s, here, there) + more[:, slice_width:]
-    full_dy = cube_gather(dealt_dy, 1)
+    dealt_dy = exchange(cotangent_s, out_list, in_slots) + more[:, slice_width:]
+    both_dy = cube_gather(jnp.concatenate([dealt_dy, mate(dealt_dy)], axis=0), 1)
+    full_dy, mate_dy = both_dy[:group_rows], both_dy[group_rows:]
 
     out_rows = w_output.shape[0]
     rest_s = jnp.concatenate([w_output.reshape(-1, w_expand.shape[1]), w_expand])
@@ -329,20 +383,21 @@
     output_w = output_w.transpose(1, 0, 2).reshape(out_rows, dim)
     expand_w = rest_w[:, out_count:].reshape(-1, w_expand.shape[1])
 
-    queue = [first_w, rest_w]
-
-    def queued(shard, axis):
-        (shard,) = after((shard,), (queue[-2],))
-        queue.append(row_gather(shard, axis))
-        return queue[-1]
-
-    expert_w = []
-    for number in range(local_count):
-        gate_up_s = jnp.concatenate([expert_gate[number], expert_up[number]], axis=1)
-        expert_w.append((queued(gate_up_s, 0), queued(expert_down[number], 1)))
-        if number == 0:
-            shared_gu_w = queued(jnp.concatenate([shared_gate, shared_up], axis=1), 0)
-            shared_d_w = queued(shared_down, 1)
+    (shared_gu_s,) = after((jnp.concatenate([shared_gate, shared_up], axis=1),), (first_w,))
+    shared_gu_w = row_gather(shared_gu_s, 0)
+    (shared_d_s,) = after((shared_down,), (rest_w,))
+    shared_d_w = row_gather(shared_d_s, 1)
+
+    def of_expert(value, number):
+        return lax.dynamic_index_in_dim(value, number, 0, False)
+
+    def both_parts(number):
+        return jnp.concatenate([of_expert(expert_gate, number), of_expert(expert_up, number)], 1)
+
+    kept, given = after((both_parts(host), both_parts(1 - host)), (dealt_dy,))
+    gate_up_w = expert_gather(kept, given, 0)
+    kept, given = after((of_expert(expert_down, host), of_expert(expert_down, 1 - host)), (dealt_dy,))
+    down_w = expert_gather(kept, given, 1)
 
     head_count = query_w.shape[1] // (NOPE + ROPE)
     softmax_scale = (NOPE + ROPE) ** (-0.5)
@@ -414,7 +469,11 @@
     hidden_part = x_part + attn_part
     scale_two = lax.rsqrt(jnp.mean(hidden_part * hidden_part, axis=-1, keepdims=True) + EPSILON)
     unit_two = hidden_part * scale_two
-    normed_two = cube_gather((unit_two * gain_two).astype(BF16), 0)
+    normed_part = (unit_two * gain_two).astype(BF16)
+    mate_part = mate(normed_part)
+    normed_two = cube_gather(normed_part, 0)
+    (mate_part,) = after((mate_part,), (normed_two,))
+    mate_two = cube_gather(mate_part, 0)
 
     def forward(rows, gate_up_w):
         width = gate_up_w.shape[1] // 2
@@ -429,38 +488,6 @@
             [(grad_hidden * up_slope).astype(BF16), (grad_hidden * act).astype(BF16)], axis=1
         )
 
-    lines = []
-    grad_two, moe_terms = None, None
-    for number in range(local_count):
-        gate_up_w, down_w = expert_w[number]
-        pick, weight = picks[number], weights[number]
-        rows = dot(pick, normed_two).astype(BF16)
-        grad_result = (weight[:, None] * dot(pick, full_dy)).astype(BF16)
-        for line in lines:
-            (gate_up_w,) = after((gate_up_w,), next(line))
-        hidden, act, up_slope = forward(rows, gate_up_w)
-        grad_gate_up = backward(dot_nt(grad_result, down_w), act, up_slope)
-        for line in lines:
-            (grad_gate_up,) = after((grad_gate_up,), next(line))
-        grad_rows = dot_nt(grad_gate_up, gate_up_w).astype(BF16)
-        term = dot_tn(pick, grad_rows)
-        grad_two = term if grad_two is None else grad_two + term
-        if number + 1 < local_count:
-            grad_gu = dot_tn(rows, grad_gate_up).astype(BF16)
-            grad_down = dot_tn(grad_result, hidden).astype(BF16)
-            line = line_scatter([grad_gu, grad_down])
-            messages = next(line)
-            lines.append(line)
-            shared_in, full_dy_s = after((normed_two, full_dy), messages)
-            term = dot_tn(pick, (weight[:, None] * dot(hidden, down_w)).astype(BF16))
-            moe_terms = term if moe_terms is None else moe_terms + term
-        if number == 0:
-            shared_hidden, shared_act, shared_us = forward(shared_in, shared_gu_w)
-            grad_shared_gu = backward(dot_nt(full_dy_s, shared_d_w), shared_act, shared_us)
-            grad_two = grad_two + dot_nt(grad_shared_gu, shared_gu_w)
-            moe_terms = moe_terms + dot(shared_hidden, shared_d_w)
-            grad_sgu = dot_tn(shared_in, grad_shared_gu).astype(BF16)
-            grad_sd = dot_tn(shared_hidden, full_dy_s).astype(BF16)
     ordered = []
 
     def queued_sum(value, axis):
@@ -469,29 +496,52 @@
         ordered.append(row_scatter(value.astype(BF16), axis))
         return ordered[-1]
 
-    grad_sgu = queued_sum(grad_sgu, 0)
-    grad_sd = queued_sum(grad_sd, 1)
-    last_gu = queued_sum(dot_tn(rows, grad_gate_up), 0)
-    last_down = queued_sum(dot_tn(hidden, grad_result), 1)
-    grad_two = grad_two.astype(BF16)
-    (hidden_late, weight_late) = after((hidden, weight), (grad_two,))
-    term = dot_tn(pick, (weight_late[:, None] * dot(hidden_late, down_w)).astype(BF16))
-    moe_terms = (moe_terms + term).astype(BF16)
-
-    grad_two_part = cube_scatter(grad_two)
+    shared_hidden, shared_act, shared_us = forward(normed_two, shared_gu_w)
+    grad_shared_gu = backward(dot_nt(full_dy, shared_d_w), shared_act, shared_us)
+    grad_two = dot_nt(grad_shared_gu, shared_gu_w)
+    moe_terms = dot(shared_hidden, shared_d_w)
+    grad_sgu = queued_sum(dot_tn(normed_two, grad_shared_gu), 0)
+    grad_sd = queued_sum(dot_tn(shared_hidden, full_dy), 1)
+
+    rows = jnp.concatenate(
+        [dot(pick, normed_two).astype(BF16), dot(mate_pick, mate_two).astype(BF16)], axis=0
+    )
+    grad_result = jnp.concatenate(
+        [
+            (weight[:, None] * dot(pick, full_dy)).astype(BF16),
+            (mate_weight[:, None] * dot(mate_pick, mate_dy)).astype(BF16),
+        ],
+        axis=0,
+    )
+    hidden, act, up_slope = forward(rows, gate_up_w)
+    grad_gate_up = backward(dot_nt(grad_result, down_w), act, up_slope)
+    mate_rows = dot_nt(grad_gate_up[capacity:], gate_up_w).astype(BF16)
+    mate_grad = dot_tn(mate_pick, mate_rows).astype(BF16)
+    (own_gate_up,) = after((grad_gate_up[:capacity],), (mate_grad,))
+    own_rows = dot_nt(own_gate_up, gate_up_w).astype(BF16)
+    grad_two = (grad_two + dot_tn(pick, own_rows)).astype(BF16)
+    mate_grad = mate(cube_scatter(mate_grad).astype(BF16))
+    grad_gu = dot_tn(rows, grad_gate_up).astype(BF16)
+    grad_down = dot_tn(hidden, grad_result).astype(BF16)
+
+    grad_two_part = cube_scatter(grad_two) + mate_grad.astype(F32)
     dy_part = my_part(full_dy).astype(F32)
     hidden_back, gain_two_grad = norm_back(grad_two_part, unit_two, scale_two, gain_two)
     grad_hidden_part = dy_part + hidden_back
     grad_attn = cube_gather(grad_hidden_part.astype(BF16), 0)
 
-    (moe_terms,) = after((moe_terms,), (grad_attn,))
-    moe_part = cube_scatter(moe_terms)
+    (hidden_late,) = after((hidden,), (grad_two,))
+    weights = jnp.concatenate([weight, mate_weight])
+    result_rows = (weights[:, None] * dot(hidden_late, down_w)).astype(BF16)
+    mate_terms = dot_tn(mate_pick, result_rows[capacity:]).astype(BF16)
+    moe_terms = (moe_terms + dot_tn(pick, result_rows[:capacity])).astype(BF16)
+    mate_terms, moe_terms = after((mate_terms, moe_terms), (grad_attn,))
+    mate_terms = mate(cube_scatter(mate_terms).astype(BF16))
+    moe_part = cube_scatter(moe_terms) + mate_terms.astype(F32)
     result_part = (hidden_part + moe_part).astype(BF16)
     result_slice = lax.all_to_all(result_part, "col", split_axis=1, concat_axis=0, tiled=True)
-    result = exchange(result_slice, there, here)
-
-    line_sums = [list(line)[-1] for line in lines]
-    grad_attn, *line_sums = after((grad_attn, *line_sums), ())
+    result = exchange(result_slice, back_list, back_slots)
+
     grad_output_w = queued_sum(dot_tn(mixed, grad_attn), 1)
     grad_mixed = dot_nt(grad_attn, output_w).astype(BF16)
     grad_mixed = grad_mixed.reshape(group_rows, head_count, VDIM)
@@ -535,6 +585,9 @@
         .astype(BF16)
         .reshape(group_rows, head_count * (NOPE + ROPE))
     )
+    own_gu, mate_gu = expert_scatter(grad_gu, 0)
+    own_down, mate_down = expert_scatter(grad_down, 1)
+    grad_query_raw, mate_gu = after((grad_query_raw, mate_gu), ())
     grad_one = cube_scatter(dot_nt(grad_query_raw, query_w).astype(BF16))
     grad_expanded = jnp.concatenate([grad_keys[..., :NOPE], grad_values], axis=-1).astype(BF16)
     grad_expanded = grad_expanded.reshape(group_rows, head_count * (NOPE + VDIM))
@@ -555,13 +608,13 @@
     )
     grad_input = (grad_hidden_part + input_back).astype(BF16)
     grad_slice = lax.all_to_all(grad_input, "col", split_axis=1, concat_axis=0, tiled=True)
-    tokens_grad = exchange(grad_slice, there, here)
+    tokens_grad = exchange(grad_slice, back_list, back_slots)
 
     def more_back(carry):
         step, total = carry
-        here_more, there_more = maps(step)
+        _, _, back_more, slots_more = maps(step)
         dealt = jnp.concatenate([result_slice, grad_slice], axis=1)
-        return step + 1, total + exchange(dealt, there_more, here_more)
+        return step + 1, total + exchange(dealt, back_more, slots_more)
 
     more = lax.while_loop(
         lambda carry: carry[0] < rounds,
@@ -579,8 +632,11 @@
     grad_latent_w = cube_gather(queued_sum(dot_tn(my_columns, grad_latent), 0), 0)
     gain_grads = small_sum(jnp.concatenate([gain_one_grad, gain_two_grad, latent_gain_grad]))
     width_ff = expert_gate.shape[2]
-    grad_gus = line_sums + [last_gu]
-    grad_downs = [item[:, 2 * width_ff :].T for item in line_sums] + [last_down]
+    other_gu, other_down = mate(mate_gu), mate(mate_down)
+
+    def in_order(own, other):
+        return jnp.stack([jnp.where(host == 0, own, other), jnp.where(host == 0, other, own)])
+
     width_two = gain_one_grad.shape[0]
     width_lat = latent_gain_grad.shape[0]
 
@@ -601,9 +657,9 @@
         grad_sgu[:, : shared_gate.shape[1]].astype(F32),
         grad_sgu[:, shared_gate.shape[1] :].astype(F32),
         grad_sd.astype(F32),
-        jnp.stack([item[:, :width_ff] for item in grad_gus]).astype(F32),
-        jnp.stack([item[:, width_ff : 2 * width_ff] for item in grad_gus]).astype(F32),
-        jnp.stack(grad_downs).astype(F32),
+        in_order(own_gu[:, :width_ff], other_gu[:, :width_ff]).astype(F32),
+        in_order(own_gu[:, width_ff:], other_gu[:, width_ff:]).astype(F32),
+        in_order(own_down, other_down).astype(F32),
     )
 
 

time: 1870 us -> 1730 us (0.925)
  waiting for transfers between devices: 741 us -> 614 us
  other arithmetic: 177 us -> 247 us
  local copies, waits for them, and re-layouts: 346 us -> 293 us
  matrix products: 486 us -> 457 us
    all_gather x8 -> x4, waiting for transfers between devices: 178 us -> 36.1 us  [row_gather(): return lax.all_gather(shard, 'row', axis=axis, tiled=True)]
    ppermute x6 -> x18, waiting for transfers between devices: 266 us -> 364 us  [row_swap(): lax.ppermute(value, 'row', [(j, j ^ bit) for j in range(lax.axis_size('ro...]
    all_to_all x4, waiting for transfers between devices: 125 us -> 53.9 us  [exchange(): got = lax.all_to_all(sent, 'row', split_axis=0, concat_axis=0, tiled=True)]
    dynamic_slice x27 -> x4, local copies, waits for them, and re-layouts: 56.4 us -> 1.35 us  [blocks(): lax.dynamic_slice_in_dim(value, block_at(device, place) * rows, rows, 0)]
    dot_general x18 -> x12, matrix products: 168 us -> 133 us  [dot_tn(): lax.dot_general(left, right, (((0,), (0,)), ((), ())), preferred_element_...]
    reduce_sum x3 -> x6, other arithmetic: 1.87 us -> 30.4 us  [the longest x1 23.2 us: body(): group_of = jnp.sum(jnp.where(here_hit, inverse_group, 0), axis=(0, 1))]
    dynamic_update_slice x0 -> x8, local copies, waits for them, and re-layouts: none -> 23.2 us  [expert_gather(): lax.dynamic_update_slice_in_dim(out, piece, jnp.bitwise_xor(index, key) *...]
    squeeze x16 -> x5, local copies, waits for them, and re-layouts: 25 us -> 2.35 us  [cube_gather(): theirs[place - done]]
  transfers between devices with their start and end apart: 84 -> 101, of which waited for: 27 -> 34; matrix products, arithmetic and copies ran while one was open for 47% -> 52% of each run, Pallas kernels for 0% -> 0%
where the time goes in v4:
time: 1730 us; the launch traced here: 1720 us
  waiting for transfers between devices  614 us (35%)
  matrix products  457 us (26%)
  local copies, waits for them, and re-layouts  293 us (17%)
  other arithmetic  247 us (14%)
  starting transfers between devices  89.1 us (5%)
  between operations  18.9 us (1%)
    ppermute x18, waiting for transfers between devices, row_swap(): lax.ppermute(value, 'row', [(j, j ^ bit) for j in range(lax.axis_size('ro...  364 us
    dot_general x20, matrix products, dot(): return jnp.dot(left, right, preferred_element_type=F32)  187 us
    dot_general x12, matrix products, dot_tn(): lax.dot_general(left, right, (((0,), (0,)), ((), ())), preferred_element_...  133 us
    dot_general x9, matrix products, dot_nt(): lax.dot_general(left, right, (((1,), (1,)), ((), ())), preferred_element_...  96.3 us
    dynamic_update_slice x59, local copies, waits for them, and re-layouts, cube_gather(): lax.dynamic_update_slice_in_dim(out, item, block_at(owner, place) * width...  83.6 us
    ppermute x30, waiting for transfers between devices, chip_swap(): lax.ppermute(value, 'col', [(j, j ^ (other if j % 2 else bits)[step]) for...  83 us
    reduce_scatter x6, waiting for transfers between devices, row_scatter(): return lax.psum_scatter(value, 'row', scatter_dimension=axis, tiled=True)  63.6 us
    all_to_all x4, waiting for transfers between devices, exchange(): got = lax.all_to_all(sent, 'row', split_axis=0, concat_axis=0, tiled=True)  53.9 us
  transfers between devices with their start and end apart: 101, of which 34 were waited for; matrix products, arithmetic and copies ran while one was open for 52% of the time, Pallas kernels for 0%

profile of v4, /device:TPU:0, one launch (start us, length us, event | category | flops | bytes accessed | tf_op | source)
XLA Modules:
  0.0 1719.5 jit_solution(16491108000991818785)
XLA Ops:
  38.4 23.2 %select_reduce_fusion.2 = (s32[2048]{0:T(1024)S(1)}, s32[2048]{0:T(1024)S(1)}) fusion(s32[4,2048]{1,0:T(4,128)S(1)} %get-tuple-element.810, pred[4,2048]{1,0:T(4,128)(4,1)S(1)} %get-tuple-element.546, s32[4,2048]{1,0:T(4,128)S(1)} %get-tuple-element.809), kind=kLoop, calls=%fused_computation.31 | loop fusion | flops 100659200 | bytes 90112 | tf_op jit(solution)/shard_map/reduce_sum | solution.py:292
  78.6 21.6 %all-to-all-done.2 = bf16[4,640,256]{2,1,0:T(8,128)(2,1)S(1)} async-done(((bf16[4,640,256]{2,1,0:T(8,128)(2,1)}), bf16[4,640,256]{2,1,0:T(8,128)(2,1)S(1)}, u32[]{:S(2)}, u32[]{:S(2)}) %all-to-all-start.2) | async-done | bytes 1310752 | tf_op jit(solution)/shard_map/all_to_all | solution.py:232
  139.9 22.0 %all-gather.11.cloned.1.call-done = bf16[2496,384]{1,0:T(8,128)(2,1)} async-done(((bf16[624,384]{1,0:T(8,128)(2,1)}), bf16[2496,384]{1,0:T(8,128)(2,1)}) %all-gather.11.cloned.1.call-update) | async-done | bytes 1916944 | tf_op jit(solution)/shard_map/all_gather | solution.py:202
  172.2 20.1 %all-to-all-done.3 = bf16[4,640,256]{2,1,0:T(8,128)(2,1)S(1)} async-done(((bf16[4,640,256]{2,1,0:T(8,128)(2,1)}), bf16[4,640,256]{2,1,0:T(8,128)(2,1)S(1)}, u32[]{:S(2)}, u32[]{:S(2)}) %all-to-all-start.3) | async-done | bytes 1310752 | tf_op jit(solution)/shard_map/all_to_all | solution.py:232
  216.6 14.1 all-gather.13.cloned.1.call-done
  242.8 17.1 collective-permute-done.29
  307.5 8.8 fusion.27
  316.3 9.1 fusion.282
  376.3 65.5 %collective-permute-done.35 = bf16[1408,512]{1,0:T(8,128)(2,1)} collective-permute-done((bf16[1408,512]{1,0:T(8,128)(2,1)}, bf16[1408,512]{1,0:T(8,128)(2,1)}, u32[]{:S(2)}, u32[]{:S(2)}) %collective-permute-start.35) | collective-permute-done | bytes 1441824 | tf_op jit(solution)/shard_map/ppermute | solution.py:76
  441.8 71.3 %collective-permute-done.36 = bf16[1408,512]{1,0:T(8,128)(2,1)} collective-permute-done((bf16[1408,512]{1,0:T(8,128)(2,1)}, bf16[1408,512]{1,0:T(8,128)(2,1)}, u32[]{:S(2)}, u32[]{:S(2)}) %collective-permute-start.36) | collective-permute-done | bytes 1441824 | tf_op jit(solution)/shard_map/ppermute | solution.py:76
  533.0 17.2 %collective-permute-done.37 = bf16[1408,512]{1,0:T(8,128)(2,1)S(1)} collective-permute-done((bf16[1408,512]{1,0:T(8,128)(2,1)}, bf16[1408,512]{1,0:T(8,128)(2,1)S(1)}, u32[]{:S(2)}, u32[]{:S(2)}) %collective-permute-start.37) | collective-permute-done | bytes 1441824 | tf_op jit(solution)/shard_map/ppermute | solution.py:76
  556.1 12.3 copy.352
  583.9 15.8 collective-permute-done.11
  601.8 10.0 collective-permute-done.28
  628.4 8.3 collective-permute-done.16
  639.7 12.9 multiply_convert_fusion.6
  652.6 10.5 collective-permute-done.18
  663.2 12.6 multiply_convert_fusion.5
  675.8 8.3 slice.913
  697.8 11.2 fusion.283
  709.0 11.1 multiply_convert_fusion.12
  731.8 13.8 fusion.86
  745.6 8.5 convolution_convert_fusion.3
  779.3 11.6 fusion.85
  792.8 34.6 %fusion.60 = f32[2048,2816]{1,0:T(8,128)} fusion(bf16[2048,2816]{1,0:T(8,128)(2,1)} %constant_dynamic-update-slice_fusion.4, bf16[1024,2048]{1,0:T(8,128)(2,1)S(1)} %fusion.85, bf16[1024,2048]{1,0:T(8,128)(2,1)S(1)} %copy-done.179), kind=kOutput, calls=%fused_computation.129 | convolution fusion | flops 23639097344 | bytes 42991616 | tf_op jit(solution)/shard_map/dot_general | solution.py:60
  827.4 26.8 %multiply_convert_fusion.1 = (bf16[2048,1408]{1,0:T(8,128)(2,1)}, bf16[2048,1408]{1,0:T(8,128)(2,1)}, bf16[2048,1408]{1,0:T(8,128)(2,1)}) fusion(f32[2048,2816]{1,0:T(8,128)} %fusion.60, bf16[1408,2048]{1,0:T(8,128)(2,1)} %constant_dynamic-update-slice_fusion, bf16[1024,2048]{1,0:T(8,128)(2,1)} %multiply_convert_fusion.5, ...), kind=kOutput, calls=%fused_computation.64 | convolution fusion | flops 11871191040 | bytes 54525952 | tf_op jit(solution)/shard_map/dot_general | solution.py:64
  860.5 17.3 %fusion.56 = bf16[1024,2048]{1,0:T(8,128)(2,1)} fusion(bf16[2048,2816]{1,0:T(8,128)(2,1)} %constant_dynamic-update-slice_fusion.4, bf16[2048,1408]{1,0:T(8,128)(2,1)} %get-tuple-element.551, bf16[2048,1408]{1,0:T(8,128)(2,1)S(1)} %copy-done.41), kind=kOutput, calls=%fused_computation.124 | convolution fusion | flops 11822694400 | bytes 27262976 | tf_op jit(solution)/shard_map/dot_general | solution.py:64
  877.8 17.7 %convolution_convert_fusion.2 = bf16[1408,2048]{1,0:T(8,128)(2,1)} fusion(bf16[2048,1408]{1,0:T(8,128)(2,1)} %get-tuple-element.463, bf16[1024,2048]{1,0:T(8,128)(2,1)} %multiply_convert_fusion.5, bf16[1024,2048]{1,0:T(8,128)(2,1)S(1)} %copy-done.176), kind=kOutput, calls=%fused_computation.113 | convolution fusion | flops 11830820864 | bytes 19922944 | tf_op jit(solution)/shard_map/dot_general | solution.py:68
  895.5 10.9 fusion.50
  909.5 15.2 fusion.284
  924.7 11.9 fusion.44
  936.7 11.8 add_convert_fusion.1
  957.8 30.9 %fusion.30 = bf16[2048,2816]{1,0:T(8,128)(2,1)} fusion(bf16[2048,1408]{1,0:T(8,128)(2,1)S(1)} %bitcast.584, bf16[2048,1408]{1,0:T(8,128)(2,1)} %get-tuple-element.551, bf16[1024,2048]{1,0:T(8,128)(2,1)} %copy-done.180, bf16[1024,2048]{1,0:T(8,128)(2,1)} %fusion.86), kind=kOutput, calls=%fused_computation.69 | convolution fusion | flops 23667933184 | bytes 31457280 | tf_op jit(solution)/shard_map/dot_general | solution.py:68
  1004.8 17.5 %multiply_convert_fusion = bf16[2048,2048]{1,0:T(8,128)(2,1)} fusion(bf16[2048,1408]{1,0:T(8,128)(2,1)S(1)} %bitcast.665, bf16[1408,2048]{1,0:T(8,128)(2,1)} %constant_dynamic-update-slice_fusion, f32[2048]{0:T(1024)S(1)} %copy-done.164), kind=kOutput, calls=%fused_computation.56 | convolution fusion | flops 11819548672 | bytes 19931136 | tf_op jit(solution)/shard_map/dot_general | solution.py:60
  1032.0 14.2 fusion.43
  1046.3 17.1 collective-permute-done.39
  1067.8 13.3 fusion.51
  1081.6 57.7 %collective-permute-done.44 = bf16[256,2048]{1,0:T(8,128)(2,1)S(1)} collective-permute-done((bf16[256,2048]{1,0:T(8,128)(2,1)S(1)}, bf16[256,2048]{1,0:T(8,128)(2,1)S(1)}, u32[]{:S(2)}, u32[]{:S(2)}) %collective-permute-start.44) | collective-permute-done | bytes 1048608 | tf_op jit(solution)/shard_map/ppermute | solution.py:76
  1144.7 10.6 add_convert_fusion
  1166.4 67.4 %collective-permute-done.80 = bf16[512,2816]{1,0:T(8,128)(2,1)} collective-permute-done((bf16[512,2816]{1,0:T(8,128)(2,1)}, bf16[512,2816]{1,0:T(8,128)(2,1)}, u32[]{:S(2)}, u32[]{:S(2)}) %collective-permute-start.80) | collective-permute-done | bytes 2883616 | tf_op jit(solution)/shard_map/ppermute | solution.py:76
  1233.9 8.3 add_convert_fusion.8
  1436.2 41.5 %reduce-scatter.9.cloned.1.call-done = bf16[256,512]{1,0:T(8,128)(2,1)} async-done(((bf16[256,2048]{1,0:T(8,128)(2,1)}), bf16[256,512]{1,0:T(8,128)(2,1)}) %reduce-scatter.9.cloned.1.call-update) | async-done | bytes 262160 | tf_op jit(solution)/shard_map/reduce_scatter | solution.py:211
  1479.5 22.1 %reduce-scatter.17.cloned.1.call-done = bf16[64,576]{1,0:T(8,128)(2,1)} async-done(((bf16[256,576]{1,0:T(8,128)(2,1)}), bf16[64,576]{1,0:T(8,128)(2,1)}) %reduce-scatter.17.cloned.1.call-update) | async-done | bytes 73744 | tf_op jit(solution)/shard_map/reduce_scatter | solution.py:211
  1522.5 9.3 collective-permute-done.60
  1541.9 43.8 %collective-permute-done.81 = bf16[512,2816]{1,0:T(8,128)(2,1)} collective-permute-done((bf16[512,2816]{1,0:T(8,128)(2,1)}, bf16[512,2816]{1,0:T(8,128)(2,1)}, u32[]{:S(2)}, u32[]{:S(2)}) %collective-permute-start.81) | collective-permute-done | bytes 2883616 | tf_op jit(solution)/shard_map/ppermute | solution.py:76
  1594.0 14.1 collective-permute-done.56
  1622.0 9.1 all-to-all-done.4
  1691.5 12.2 all-to-all-done.5
  (991 shorter events, 728.6 us)
Async XLA Ops:
  7.2 120.0 %collective-permute-start.13 = (s32[2048,6]{0,1:T(8,128)}, s32[2048,6]{0,1:T(8,128)}, u32[]{:S(2)}, u32[]{:S(2)}) collective-permute-start(s32[2048,6]{0,1:T(8,128)} %param.47), channel_id=1, source_target_pairs={{0,16},{8,24},{16,0},{24,8},{1,17},{9,25},{17,1},{25,9},{2,18},{10... | collective-permute-start | bytes 147464 | tf_op jit(solution)/shard_map/ppermute | solution.py:76
  11.3 150.8 %collective-permute-start.14 = (f32[2048,6]{0,1:T(8,128)}, f32[2048,6]{0,1:T(8,128)}, u32[]{:S(2)}, u32[]{:S(2)}) collective-permute-start(f32[2048,6]{0,1:T(8,128)} %param.48), channel_id=1, source_target_pairs={{0,16},{8,24},{16,0},{24,8},{1,17},{9,25},{17,1},{25,9},{2,18},{10... | collective-permute-start | bytes 147464 | tf_op jit(solution)/shard_map/ppermute | solution.py:76
  69.4 92.5 %all-gather.11.cloned.1.call-start = ((), (), s32[]{:S(2)}) async-start(), calls=%async_computation.22 | async-start | bytes 2396160 | tf_op jit(solution)/shard_map/all_gather | solution.py:202
  109.4 121.4 %all-gather.13.cloned.1.call-start = ((), (), s32[]{:S(2)}) async-start(), calls=%async_computation.23 | async-start | bytes 1966080 | tf_op jit(solution)/shard_map/all_gather | solution.py:202
  136.2 56.1 %all-to-all-start.3 = ((bf16[4,640,256]{2,1,0:T(8,128)(2,1)}), bf16[4,640,256]{2,1,0:T(8,128)(2,1)S(1)}, u32[]{:S(2)}, u32[]{:S(2)}) async-start(bf16[4,640,256]{2,1,0:T(8,128)(2,1)} %bitcast.626), calls=%async_computation.3 | async-start | bytes 2621440 | tf_op jit(solution)/shard_map/all_to_all | solution.py:232
  139.8 558.1 %all-gather.9.cloned.1.call-start = ((), (), s32[]{:S(2)}) async-start(), calls=%async_computation.15 | async-start | bytes 3604480 | tf_op jit(solution)/shard_map/all_gather | solution.py:202
  161.9 547.1 %all-gather.7.cloned.1.call-start = ((), (), s32[]{:S(2)}) async-start(), calls=%async_computation.14 | async-start | bytes 1802240 | tf_op jit(solution)/shard_map/all_gather | solution.py:202
  167.3 104.3 %collective-permute-start.3 = (bf16[2,2048,256]{2,1,0:T(8,128)(2,1)}, bf16[2,2048,256]{2,1,0:T(8,128)(2,1)}, u32[]{:S(2)}, u32[]{:S(2)}) collective-permute-start(bf16[2,2048,256]{2,1,0:T(8,128)(2,1)} %pad_maximum_fusion.24), channel_id=1, source_target_pairs={{0,4},{1,3},{2,6},{3,1},{4,0},{5,7},{6,2},{7,5},{8,12},{9,11},{10,... | collective-permute-start | bytes 6291464 | tf_op jit(solution)/shard_map/ppermute | solution.py:140
  197.9 62.0 %collective-permute-start.29 = (bf16[2048,256]{1,0:T(8,128)(2,1)}, bf16[2048,256]{1,0:T(8,128)(2,1)}, u32[]{:S(2)}, u32[]{:S(2)}) collective-permute-start(bf16[2048,256]{1,0:T(8,128)(2,1)} %fusion.119), channel_id=1, source_target_pairs={{0,16},{8,24},{16,0},{24,8},{1,17},{9,25},{17,1},{25,9},{2,18},{10... | collective-permute-start | bytes 3145736 | tf_op jit(solution)/shard_map/ppermute | solution.py:76
  197.9 317.8 %collective-permute-start.26 = (bf16[512,2816]{1,0:T(8,128)(2,1)}, bf16[512,2816]{1,0:T(8,128)(2,1)}, u32[]{:S(2)}, u32[]{:S(2)}) collective-permute-start(bf16[512,2816]{1,0:T(8,128)(2,1)} %pad_maximum_fusion.18), channel_id=1, source_target_pairs={{0,8},{8,0},{16,24},{24,16},{1,9},{9,1},{17,25},{25,17},{2,10},{10... | collective-permute-start | bytes 8650760 | tf_op jit(solution)/shard_map/ppermute | solution.py:76
  198.9 242.8 %collective-permute-start.35 = (bf16[1408,512]{1,0:T(8,128)(2,1)}, bf16[1408,512]{1,0:T(8,128)(2,1)}, u32[]{:S(2)}, u32[]{:S(2)}) collective-permute-start(bf16[1408,512]{1,0:T(8,128)(2,1)} %get-tuple-element.460), channel_id=1, source_target_pairs={{0,8},{8,0},{16,24},{24,16},{1,9},{9,1},{17,25},{25,17},{2,10},{10... | collective-permute-start | bytes 4325384 | tf_op jit(solution)/shard_map/ppermute | solution.py:76
  235.2 532.8 %reduce-scatter.13.cloned.1.call-start = ((), (), s32[]{:S(2)}) async-start(), calls=%async_computation.19 | async-start | bytes 1802240 | tf_op jit(solution)/shard_map/reduce_scatter | solution.py:211
  280.1 238.2 %collective-permute-start.27 = (bf16[512,2816]{1,0:T(8,128)(2,1)}, bf16[512,2816]{1,0:T(8,128)(2,1)}, u32[]{:S(2)}, u32[]{:S(2)}) collective-permute-start(bf16[512,2816]{1,0:T(8,128)(2,1)} %pad_maximum_fusion.19), channel_id=1, source_target_pairs={{0,16},{8,24},{16,0},{24,8},{1,17},{9,25},{17,1},{25,9},{2,18},{10... | collective-permute-start | bytes 8650760 | tf_op jit(solution)/shard_map/ppermute | solution.py:76
  288.2 224.9 %collective-permute-start.36 = (bf16[1408,512]{1,0:T(8,128)(2,1)}, bf16[1408,512]{1,0:T(8,128)(2,1)}, u32[]{:S(2)}, u32[]{:S(2)}) collective-permute-start(bf16[1408,512]{1,0:T(8,128)(2,1)} %get-tuple-element.461), channel_id=1, source_target_pairs={{0,16},{8,24},{16,0},{24,8},{1,17},{9,25},{17,1},{25,9},{2,18},{10... | collective-permute-start | bytes 4325384 | tf_op jit(solution)/shard_map/ppermute | solution.py:76
  295.1 228.8 %collective-permute-start.31 = (bf16[1,4096,256]{2,1,0:T(8,128)(2,1)}, bf16[1,4096,256]{2,1,0:T(8,128)(2,1)}, u32[]{:S(2)}, u32[]{:S(2)}) collective-permute-start(bf16[1,4096,256]{2,1,0:T(8,128)(2,1)} %get-tuple-element.638), channel_id=1, source_target_pairs={{0,2},{1,5},{2,0},{3,7},{4,6},{5,1},{6,4},{7,3},{8,10},{9,13},{10,... | collective-permute-start | bytes 6291464 | tf_op jit(solution)/shard_map/ppermute | solution.py:140
  441.8 109.7 %collective-permute-start.30 = (bf16[1,4096,256]{2,1,0:T(8,128)(2,1)}, bf16[1,4096,256]{2,1,0:T(8,128)(2,1)S(1)}, u32[]{:S(2)}, u32[]{:S(2)}) collective-permute-start(bf16[1,4096,256]{2,1,0:T(8,128)(2,1)} %get-tuple-element.638), channel_id=1, source_target_pairs={{0,1},{1,0},{2,3},{3,2},{4,5},{5,4},{6,7},{7,6},{8,9},{9,8},{10,11... | collective-permute-start | bytes 6291464 | tf_op jit(solution)/shard_map/ppermute | solution.py:130
  513.1 55.9 %collective-permute-start.10 = (bf16[4,256,2048]{2,1,0:T(8,128)(2,1)}, bf16[4,256,2048]{2,1,0:T(8,128)(2,1)}, u32[]{:S(2)}, u32[]{:S(2)}) collective-permute-start(bf16[4,256,2048]{2,1,0:T(8,128)(2,1)} %pad_maximum_fusion.10), channel_id=1, source_target_pairs={{0,1},{1,0},{2,3},{3,2},{4,5},{5,4},{6,7},{7,6},{8,9},{9,8},{10,11... | collective-permute-start | bytes 12582920 | tf_op jit(solution)/shard_map/ppermute | solution.py:130
  518.3 93.5 %collective-permute-start.28 = (bf16[512,2816]{1,0:T(8,128)(2,1)}, bf16[512,2816]{1,0:T(8,128)(2,1)}, u32[]{:S(2)}, u32[]{:S(2)}) collective-permute-start(bf16[512,2816]{1,0:T(8,128)(2,1)} %collective-permute-done.27), channel_id=1, source_target_pairs={{0,8},{8,0},{16,24},{24,16},{1,9},{9,1},{17,25},{25,17},{2,10},{10... | collective-permute-start | bytes 8650760 | tf_op jit(solution)/shard_map/ppermute | solution.py:76
  528.5 50.1 %collective-permute-start.33 = (bf16[2,4096,256]{2,1,0:T(8,128)(2,1)}, bf16[2,4096,256]{2,1,0:T(8,128)(2,1)}, u32[]{:S(2)}, u32[]{:S(2)}) collective-permute-start(bf16[2,4096,256]{2,1,0:T(8,128)(2,1)} %pad_maximum_fusion.11), channel_id=1, source_target_pairs={{0,4},{1,3},{2,6},{3,1},{4,0},{5,7},{6,2},{7,5},{8,12},{9,11},{10,... | collective-permute-start | bytes 12582920 | tf_op jit(solution)/shard_map/ppermute | solution.py:140
  623.0 61.0 %collective-permute-start.15 = (bf16[1,256,2048]{2,1,0:T(8,128)(2,1)S(1)}, bf16[1,256,2048]{2,1,0:T(8,128)(2,1)S(1)}, u32[]{:S(2)}, u32[]{:S(2)}) collective-permute-start(bf16[1,256,2048]{2,1,0:T(8,128)(2,1)S(1)} %bitcast.588), channel_id=1, source_target_pairs={{0,1},{1,0},{2,3},{3,2},{4,5},{5,4},{6,7},{7,6},{8,9},{9,8},{10,11... | collective-permute-start | bytes 3145736 | tf_op jit(solution)/shard_map/ppermute | solution.py:130
  623.0 73.5 %collective-permute-start.20 = (bf16[256,2048]{1,0:T(8,128)(2,1)S(1)}, bf16[256,2048]{1,0:T(8,128)(2,1)S(1)}, u32[]{:S(2)}, u32[]{:S(2)}) collective-permute-start(bf16[256,2048]{1,0:T(8,128)(2,1)S(1)} %get-tuple-element.538), channel_id=1, source_target_pairs={{0,16},{8,24},{16,0},{24,8},{1,17},{9,25},{17,1},{25,9},{2,18},{10... | collective-permute-start | bytes 3145736 | tf_op jit(solution)/shard_map/ppermute | solution.py:76
  697.6 64.7 %collective-permute-start.21 = (bf16[1,256,2048]{2,1,0:T(8,128)(2,1)S(1)}, bf16[1,256,2048]{2,1,0:T(8,128)(2,1)}, u32[]{:S(2)}, u32[]{:S(2)}) collective-permute-start(bf16[1,256,2048]{2,1,0:T(8,128)(2,1)S(1)} %bitcast.592), channel_id=1, source_target_pairs={{0,1},{1,0},{2,3},{3,2},{4,5},{5,4},{6,7},{7,6},{8,9},{9,8},{10,11... | collective-permute-start | bytes 3145736 | tf_op jit(solution)/shard_map/ppermute | solution.py:130
  728.9 435.1 %reduce-scatter.7.cloned.1.call-start = ((), (), s32[]{:S(2)}) async-start(), calls=%async_computation.16 | async-start | bytes 3604480 | tf_op jit(solution)/shard_map/reduce_scatter | solution.py:211
  762.3 642.3 %reduce-scatter.15.cloned.1.call-start = ((), (), s32[]{:S(2)}) async-start(), calls=%async_computation.20 | async-start | bytes 655360 | tf_op jit(solution)/shard_map/reduce_scatter | solution.py:211
  953.6 68.7 %collective-permute-start.38 = (bf16[4,256,2048]{2,1,0:T(8,128)(2,1)}, bf16[4,256,2048]{2,1,0:T(8,128)(2,1)}, u32[]{:S(2)}, u32[]{:S(2)}) collective-permute-start(bf16[4,256,2048]{2,1,0:T(8,128)(2,1)} %pad_maximum_fusion.12), channel_id=1, source_target_pairs={{0,1},{1,0},{2,3},{3,2},{4,5},{5,4},{6,7},{7,6},{8,9},{9,8},{10,11... | collective-permute-start | bytes 12582920 | tf_op jit(solution)/shard_map/ppermute | solution.py:130
  991.9 163.4 %collective-permute-start.83 = (bf16[1408,512]{1,0:T(8,128)(2,1)S(1)}, bf16[1408,512]{1,0:T(8,128)(2,1)S(1)}, u32[]{:S(2)}, u32[]{:S(2)}) collective-permute-start(bf16[1408,512]{1,0:T(8,128)(2,1)S(1)} %get-tuple-element.610), channel_id=1, source_target_pairs={{0,8},{8,0},{16,24},{24,16},{1,9},{9,1},{17,25},{25,17},{2,10},{10... | collective-permute-start | bytes 4325384 | tf_op jit(solution)/shard_map/ppermute | solution.py:76
  992.2 249.9 %collective-permute-start.82 = (bf16[1408,512]{1,0:T(8,128)(2,1)}, bf16[1408,512]{1,0:T(8,128)(2,1)}, u32[]{:S(2)}, u32[]{:S(2)}) collective-permute-start(bf16[1408,512]{1,0:T(8,128)(2,1)} %get-tuple-element.609), channel_id=1, source_target_pairs={{0,8},{8,0},{16,24},{24,16},{1,9},{9,1},{17,25},{25,17},{2,10},{10... | collective-permute-start | bytes 4325384 | tf_op jit(solution)/shard_map/ppermute | solution.py:76
  999.7 166.7 %collective-permute-start.57 = (bf16[512,2816]{1,0:T(8,128)(2,1)}, bf16[512,2816]{1,0:T(8,128)(2,1)}, u32[]{:S(2)}, u32[]{:S(2)}) collective-permute-start(bf16[512,2816]{1,0:T(8,128)(2,1)} %get-tuple-element.556), channel_id=1, source_target_pairs={{0,8},{8,0},{16,24},{24,16},{1,9},{9,1},{17,25},{25,17},{2,10},{10... | collective-permute-start | bytes 8650760 | tf_op jit(solution)/shard_map/ppermute | solution.py:76
  1066.3 73.0 %collective-permute-start.44 = (bf16[256,2048]{1,0:T(8,128)(2,1)S(1)}, bf16[256,2048]{1,0:T(8,128)(2,1)S(1)}, u32[]{:S(2)}, u32[]{:S(2)}) collective-permute-start(bf16[256,2048]{1,0:T(8,128)(2,1)S(1)} %fusion.178), channel_id=1, source_target_pairs={{0,16},{8,24},{16,0},{24,8},{1,17},{9,25},{17,1},{25,9},{2,18},{10... | collective-permute-start | bytes 3145736 | tf_op jit(solution)/shard_map/ppermute | solution.py:76
  1081.1 152.8 %collective-permute-start.80 = (bf16[512,2816]{1,0:T(8,128)(2,1)}, bf16[512,2816]{1,0:T(8,128)(2,1)}, u32[]{:S(2)}, u32[]{:S(2)}) collective-permute-start(bf16[512,2816]{1,0:T(8,128)(2,1)} %get-tuple-element.555), channel_id=1, source_target_pairs={{0,8},{8,0},{16,24},{24,16},{1,9},{9,1},{17,25},{25,17},{2,10},{10... | collective-permute-start | bytes 8650760 | tf_op jit(solution)/shard_map/ppermute | solution.py:76
  1158.2 83.9 %collective-permute-start.84 = (bf16[1408,512]{1,0:T(8,128)(2,1)}, bf16[1408,512]{1,0:T(8,128)(2,1)}, u32[]{:S(2)}, u32[]{:S(2)}) collective-permute-start(bf16[1408,512]{1,0:T(8,128)(2,1)} %add_convert_fusion.16), channel_id=1, source_target_pairs={{0,16},{8,24},{16,0},{24,8},{1,17},{9,25},{17,1},{25,9},{2,18},{10... | collective-permute-start | bytes 4325384 | tf_op jit(solution)/shard_map/ppermute | solution.py:76
  1163.3 85.2 %collective-permute-start.48 = (bf16[2,256,2048]{2,1,0:T(8,128)(2,1)}, bf16[2,256,2048]{2,1,0:T(8,128)(2,1)}, u32[]{:S(2)}, u32[]{:S(2)}) collective-permute-start(bf16[2,256,2048]{2,1,0:T(8,128)(2,1)} %pad_maximum_fusion.28), channel_id=1, source_target_pairs={{0,4},{1,3},{2,6},{3,1},{4,0},{5,7},{6,2},{7,5},{8,12},{9,11},{10,... | collective-permute-start | bytes 6291464 | tf_op jit(solution)/shard_map/ppermute | solution.py:140
  1323.7 154.0 %reduce-scatter.9.cloned.1.call-start = ((), (), s32[]{:S(2)}) async-start(), calls=%async_computation.17 | async-start | bytes 1310720 | tf_op jit(solution)/shard_map/reduce_scatter | solution.py:211
  1353.2 58.5 %collective-permute-start.58 = (bf16[4,256,2048]{2,1,0:T(8,128)(2,1)}, bf16[4,256,2048]{2,1,0:T(8,128)(2,1)}, u32[]{:S(2)}, u32[]{:S(2)}) collective-permute-start(bf16[4,256,2048]{2,1,0:T(8,128)(2,1)} %pad_maximum_fusion.16), channel_id=1, source_target_pairs={{0,1},{1,0},{2,3},{3,2},{4,5},{5,4},{6,7},{7,6},{8,9},{9,8},{10,11... | collective-permute-start | bytes 12582920 | tf_op jit(solution)/shard_map/ppermute | solution.py:130
  1356.3 49.4 %collective-permute-start.53 = (bf16[4,256,2048]{2,1,0:T(8,128)(2,1)}, bf16[4,256,2048]{2,1,0:T(8,128)(2,1)}, u32[]{:S(2)}, u32[]{:S(2)}) collective-permute-start(bf16[4,256,2048]{2,1,0:T(8,128)(2,1)} %pad_maximum_fusion.15), channel_id=1, source_target_pairs={{0,1},{1,0},{2,3},{3,2},{4,5},{5,4},{6,7},{7,6},{8,9},{9,8},{10,11... | collective-permute-start | bytes 12582920 | tf_op jit(solution)/shard_map/ppermute | solution.py:130
  1387.5 114.1 %reduce-scatter.17.cloned.1.call-start = ((), (), s32[]{:S(2)}) async-start(), calls=%async_computation.21 | async-start | bytes 409600 | tf_op jit(solution)/shard_map/reduce_scatter | solution.py:211
  1389.3 196.5 %collective-permute-start.81 = (bf16[512,2816]{1,0:T(8,128)(2,1)}, bf16[512,2816]{1,0:T(8,128)(2,1)}, u32[]{:S(2)}, u32[]{:S(2)}) collective-permute-start(bf16[512,2816]{1,0:T(8,128)(2,1)} %get-tuple-element.472), channel_id=1, source_target_pairs={{0,16},{8,24},{16,0},{24,8},{1,17},{9,25},{17,1},{25,9},{2,18},{10... | collective-permute-start | bytes 8650760 | tf_op jit(solution)/shard_map/ppermute | solution.py:76
  1405.5 274.0 %reduce-scatter.11.cloned.1.call-start = ((), (), s32[]{:S(2)}) async-start(), calls=%async_computation.18 | async-start | bytes 1966080 | tf_op jit(solution)/shard_map/reduce_scatter | solution.py:211
  1410.9 92.3 %collective-permute-start.54 = (bf16[2,256,2048]{2,1,0:T(8,128)(2,1)}, bf16[2,256,2048]{2,1,0:T(8,128)(2,1)S(1)}, u32[]{:S(2)}, u32[]{:S(2)}) collective-permute-start(bf16[2,256,2048]{2,1,0:T(8,128)(2,1)} %slice.940), channel_id=1, source_target_pairs={{0,4},{1,3},{2,6},{3,1},{4,0},{5,7},{6,2},{7,5},{8,12},{9,11},{10,... | collective-permute-start | bytes 6291464 | tf_op jit(solution)/shard_map/ppermute | solution.py:140
  1420.7 85.6 %collective-permute-start.59 = (bf16[2,256,2048]{2,1,0:T(8,128)(2,1)}, bf16[2,256,2048]{2,1,0:T(8,128)(2,1)}, u32[]{:S(2)}, u32[]{:S(2)}) collective-permute-start(bf16[2,256,2048]{2,1,0:T(8,128)(2,1)} %slice.949), channel_id=1, source_target_pairs={{0,4},{1,3},{2,6},{3,1},{4,0},{5,7},{6,2},{7,5},{8,12},{9,11},{10,... | collective-permute-start | bytes 6291464 | tf_op jit(solution)/shard_map/ppermute | solution.py:140
  1429.1 81.3 %collective-permute-start.51 = (bf16[2,256,2048]{2,1,0:T(8,128)(2,1)}, bf16[2,256,2048]{2,1,0:T(8,128)(2,1)}, u32[]{:S(2)}, u32[]{:S(2)}) collective-permute-start(bf16[2,256,2048]{2,1,0:T(8,128)(2,1)} %slice.936), channel_id=1, source_target_pairs={{0,4},{1,3},{2,6},{3,1},{4,0},{5,7},{6,2},{7,5},{8,12},{9,11},{10,... | collective-permute-start | bytes 6291464 | tf_op jit(solution)/shard_map/ppermute | solution.py:140
  1501.6 89.0 %collective-permute-start.76 = (bf16[1,64,576]{2,1,0:T(8,128)(2,1)}, bf16[1,64,576]{2,1,0:T(8,128)(2,1)}, u32[]{:S(2)}, u32[]{:S(2)}) collective-permute-start(bf16[1,64,576]{2,1,0:T(8,128)(2,1)} %bitcast.639), channel_id=1, source_target_pairs={{0,2},{1,5},{2,0},{3,7},{4,6},{5,1},{6,4},{7,3},{8,10},{9,13},{10,... | collective-permute-start | bytes 221192 | tf_op jit(solution)/shard_map/ppermute | solution.py:140
  1513.9 79.5 %collective-permute-start.52 = (bf16[1,256,2048]{2,1,0:T(8,128)(2,1)}, bf16[1,256,2048]{2,1,0:T(8,128)(2,1)}, u32[]{:S(2)}, u32[]{:S(2)}) collective-permute-start(bf16[1,256,2048]{2,1,0:T(8,128)(2,1)} %slice.938), channel_id=1, source_target_pairs={{0,2},{1,5},{2,0},{3,7},{4,6},{5,1},{6,4},{7,3},{8,10},{9,13},{10,... | collective-permute-start | bytes 3145736 | tf_op jit(solution)/shard_map/ppermute | solution.py:140
  1522.0 86.2 %collective-permute-start.56 = (bf16[256,2048]{1,0:T(8,128)(2,1)}, bf16[256,2048]{1,0:T(8,128)(2,1)}, u32[]{:S(2)}, u32[]{:S(2)}) collective-permute-start(bf16[256,2048]{1,0:T(8,128)(2,1)} %fusion.179), channel_id=1, source_target_pairs={{0,16},{8,24},{16,0},{24,8},{1,17},{9,25},{17,1},{25,9},{2,18},{10... | collective-permute-start | bytes 3145736 | tf_op jit(solution)/shard_map/ppermute | solution.py:76
  1537.5 73.9 %all-to-all-start.6 = ((bf16[256,8,256]{2,0,1:T(8,128)(2,1)}), bf16[256,8,256]{2,0,1:T(8,128)(2,1)}, u32[]{:S(2)}, u32[]{:S(2)}) async-start(bf16[256,8,256]{2,0,1:T(8,128)(2,1)} %bitcast.590), calls=%async_computation.6 | async-start | bytes 2097152 | tf_op jit(solution)/shard_map/all_to_all | solution.py:610
  1590.5 53.5 %collective-permute-start.75 = (bf16[1,64,576]{2,1,0:T(8,128)(2,1)S(1)}, bf16[1,64,576]{2,1,0:T(8,128)(2,1)}, u32[]{:S(2)}, u32[]{:S(2)}) collective-permute-start(bf16[1,64,576]{2,1,0:T(8,128)(2,1)S(1)} %bitcast.640), channel_id=1, source_target_pairs={{0,1},{1,0},{2,3},{3,2},{4,5},{5,4},{6,7},{7,6},{8,9},{9,8},{10,11... | collective-permute-start | bytes 221192 | tf_op jit(solution)/shard_map/ppermute | solution.py:130
  1592.1 61.7 %collective-permute-start.78 = (bf16[2,64,576]{2,1,0:T(8,128)(2,1)}, bf16[2,64,576]{2,1,0:T(8,128)(2,1)}, u32[]{:S(2)}, u32[]{:S(2)}) collective-permute-start(bf16[2,64,576]{2,1,0:T(8,128)(2,1)} %pad_maximum_fusion.48), channel_id=1, source_target_pairs={{0,4},{1,3},{2,6},{3,1},{4,0},{5,7},{6,2},{7,5},{8,12},{9,11},{10,... | collective-permute-start | bytes 442376 | tf_op jit(solution)/shard_map/ppermute | solution.py:140
  1593.4 56.1 %collective-permute-start.77 = (bf16[1,64,576]{2,1,0:T(8,128)(2,1)}, bf16[1,64,576]{2,1,0:T(8,128)(2,1)}, u32[]{:S(2)}, u32[]{:S(2)}) collective-permute-start(bf16[1,64,576]{2,1,0:T(8,128)(2,1)} %collective-permute-done.76), channel_id=1, source_target_pairs={{0,1},{1,0},{2,3},{3,2},{4,5},{5,4},{6,7},{7,6},{8,9},{9,8},{10,11... | collective-permute-start | bytes 221192 | tf_op jit(solution)/shard_map/ppermute | solution.py:130
  (252 other events, 4298.8 us)
Sparse Core Ops, SparseCore 0:
  109.5 52.3 all-gather.10
  164.0 66.7 all-gather.12
  232.9 145.9 all-gather.8
  380.3 111.4 all-gather.6
  729.1 30.9 reduce-scatter.12
  762.4 54.9 reduce-scatter.6
  1323.8 19.5 reduce-scatter.14
  1387.6 89.9 reduce-scatter.8
  1480.6 20.8 reduce-scatter.16
  1503.8 64.9 reduce-scatter.10

commit v5 on v4

--- a/solution.py
+++ b/solution.py
@@ -84,17 +84,19 @@
     return [1 << b for b in range((lax.axis_size("row") // 2).bit_length() - 1)]
 
 
-def expert_gather(kept, given, axis):
+def expert_gather(kept, given, axis, hold):
     count = lax.axis_size("row")
     index = lax.axis_index("row")
     width = kept.shape[axis]
     shape = list(kept.shape)
     shape[axis] = width * count
     out = jnp.zeros(shape, kept.dtype)
-    for first, item in ((0, kept), (count // 2, mate(given))):
+    (arrived,) = after((mate(given),), hold)
+    for first, item in ((count // 2, arrived), (0, kept)):
         items = {first: item}
         for bit in half_bits():
-            items.update({key ^ bit: row_swap(items[key], bit) for key in list(items)})
+            new = after([row_swap(items[key], bit) for key in items], hold)
+            items.update({key ^ bit: piece for key, piece in zip(list(items), new)})
         for key, piece in items.items():
             out = lax.dynamic_update_slice_in_dim(
                 out, piece, jnp.bitwise_xor(index, key) * width, axis
@@ -102,12 +104,12 @@
     return out
 
 
-def expert_scatter(value, axis):
+def expert_scatter(value, axis, holds):
     count = lax.axis_size("row")
     index = lax.axis_index("row")
     width = value.shape[axis] // count
     sums = []
-    for first in (count // 2, 0):
+    for first, hold in zip((count // 2, 0), holds):
         items = {
             key: lax.dynamic_slice_in_dim(
                 value, jnp.bitwise_xor(index, key ^ first) * width, width, axis
@@ -115,12 +117,11 @@
             for key in range(count // 2)
         }
         for bit in half_bits()[::-1]:
+            keys = [key for key in items if key < bit]
+            new = after([row_swap(items[key ^ bit], bit) for key in keys], hold)
             items = {
-                key: (
-                    items[key].astype(F32) + row_swap(items[key ^ bit], bit).astype(F32)
-                ).astype(BF16)
-                for key in items
-                if key < bit
+                key: (items[key].astype(F32) + piece.astype(F32)).astype(BF16)
+                for key, piece in zip(keys, new)
             }
         sums.append(items[0])
     return sums[1], sums[0]
@@ -225,12 +226,12 @@
     return (index[:, None] == jnp.arange(width, dtype=jnp.int32)[None, :]).astype(BF16)
 
 
-def exchange(value, sent_of, slot_of):
+def exchange(value, sent_of, slot_of, hold=()):
     count = lax.axis_size("row")
     sent = row_major(dot(onehot(sent_of, value.shape[0]), value).astype(BF16))
     sent = sent.reshape(count, -1, value.shape[1])
     got = lax.all_to_all(sent, "row", split_axis=0, concat_axis=0, tiled=True)
-    got = got.reshape(-1, value.shape[1])
+    (got,) = after((got.reshape(-1, value.shape[1]),), hold)
     return row_major(dot(onehot(slot_of, got.shape[0]), got).astype(BF16))
 
 
@@ -286,34 +287,19 @@
     )
     rounds = (jnp.max(all_counts) + room - 1) // room
 
-    inverse_group = jnp.arange(row_count, dtype=jnp.int32)[:, None, None]
-    here_hit = (place_in[:, :, None] == token_ids[None, None, :]) & from_here[:, :, None]
-    rank_of = jnp.sum(jnp.where(here_hit, rank_here[:, :, None], 0), axis=(0, 1))
-    group_of = jnp.sum(jnp.where(here_hit, inverse_group, 0), axis=(0, 1))
-
-    def maps(step):
+    def maps_out(step):
         places = step * room + jnp.arange(room, dtype=jnp.int32)
-
-        def listed(row_of, rank):
-            hit = (rank[None, None, :] == places[None, :, None]) & (
-                row_of[None, None, :] == jnp.arange(row_count, dtype=jnp.int32)[:, None, None]
-            )
-            return jnp.sum(jnp.where(hit, token_ids[None, None, :] + 1, 0), axis=2).reshape(-1) - 1
-
-        def slots(row_of, rank):
-            inside = (rank >= places[0]) & (rank < places[0] + room)
-            return jnp.where(inside, row_of * room + rank - places[0], -1)
-
         hit = rank_here[:, None, :] == places[None, :, None]
-        out_tokens = jnp.sum(jnp.where(hit, place_in[:, None, :] + 1, 0), axis=2).reshape(-1) - 1
-        dealt = (my_source, my_rank)
-        return out_tokens, slots(*dealt), listed(*dealt), slots(group_of, rank_of)
-
-    out_list, in_slots, back_list, back_slots = maps(0)
+        listed = jnp.sum(jnp.where(hit, place_in[:, None, :] + 1, 0), axis=2).reshape(-1) - 1
+        slot = my_rank - step * room
+        inside = (slot >= 0) & (slot < room)
+        return listed, jnp.where(inside, my_source * room + slot, -1)
+
+    out_list, in_slots = maps_out(0)
 
     def more_dealt(carry):
         step, total = carry
-        out_more, in_more, _, _ = maps(step)
+        out_more, in_more = maps_out(step)
         given = jnp.concatenate([tokens, cotangent], axis=1)
         return step + 1, total + exchange(given, out_more, in_more)
 
@@ -329,8 +315,6 @@
         token_weight = jnp.sum(jnp.where(named, group_gates, 0.0), axis=1)
         return pick.astype(BF16), jnp.sum(jnp.where(pick, token_weight[None, :], 0.0), axis=1)
 
-    pick, weight = chosen(routes, gate_weights)
-    mate_pick, mate_weight = chosen(mate(routes), mate(gate_weights))
     document, position = documents(doc_lengths[0], group_rows)
 
     rows_in, dim = w_query.shape[0], w_query.shape[0] * row_count
@@ -342,6 +326,9 @@
         (jnp.int32(1), jnp.zeros((group_rows, 2 * slice_width), BF16)),
     )[1]
     dealt_x = exchange(tokens, out_list, in_slots) + more[:, :slice_width]
+    routes_late, gates_late = after((routes, gate_weights), (dealt_x,))
+    pick, weight = chosen(routes_late, gates_late)
+    mate_pick, mate_weight = chosen(mate(routes_late), mate(gates_late))
     full_x = cube_gather(dealt_x, 1)
 
     query_width = w_query.shape[1]
@@ -369,11 +356,6 @@
     gain_two = gains[:, wide : 2 * wide].reshape(-1).astype(F32)
     latent_g = gains[:, 2 * wide : 2 * wide + latent_gain.shape[0]].reshape(-1).astype(F32)
 
-    (cotangent_s,) = after((cotangent,), (dealt_x,))
-    dealt_dy = exchange(cotangent_s, out_list, in_slots) + more[:, slice_width:]
-    both_dy = cube_gather(jnp.concatenate([dealt_dy, mate(dealt_dy)], axis=0), 1)
-    full_dy, mate_dy = both_dy[:group_rows], both_dy[group_rows:]
-
     out_rows = w_output.shape[0]
     rest_s = jnp.concatenate([w_output.reshape(-1, w_expand.shape[1]), w_expand])
     (rest_s,) = after((rest_s,), (dealt_x,))
@@ -383,21 +365,16 @@
     output_w = output_w.transpose(1, 0, 2).reshape(out_rows, dim)
     expand_w = rest_w[:, out_count:].reshape(-1, w_expand.shape[1])
 
-    (shared_gu_s,) = after((jnp.concatenate([shared_gate, shared_up], axis=1),), (first_w,))
-    shared_gu_w = row_gather(shared_gu_s, 0)
-    (shared_d_s,) = after((shared_down,), (rest_w,))
-    shared_d_w = row_gather(shared_d_s, 1)
-
     def of_expert(value, number):
         return lax.dynamic_index_in_dim(value, number, 0, False)
 
     def both_parts(number):
         return jnp.concatenate([of_expert(expert_gate, number), of_expert(expert_up, number)], 1)
 
-    kept, given = after((both_parts(host), both_parts(1 - host)), (dealt_dy,))
-    gate_up_w = expert_gather(kept, given, 0)
-    kept, given = after((of_expert(expert_down, host), of_expert(expert_down, 1 - host)), (dealt_dy,))
-    down_w = expert_gather(kept, given, 1)
+    gate_up_parts = after((both_parts(host), both_parts(1 - host)), (first_w,))
+    down_parts = after(
+        (of_expert(expert_down, host), of_expert(expert_down, 1 - host)), (first_w, rest_w)
+    )
 
     head_count = query_w.shape[1] // (NOPE + ROPE)
     softmax_scale = (NOPE + ROPE) ** (-0.5)
@@ -406,6 +383,7 @@
     residual = full_x.astype(F32)
     scale_one = lax.rsqrt(jnp.mean(residual * residual, axis=-1, keepdims=True) + EPSILON)
     normed_one = (residual * scale_one * gain_one).astype(BF16)
+    (cotangent_s,) = after((cotangent,), (normed_one,))
     query_raw = dot(normed_one, query_w)
     query_raw = query_raw.reshape(group_rows, head_count, NOPE + ROPE)
     query_heads = jnp.concatenate(
@@ -427,6 +405,8 @@
         axis=-1,
     )
     value_heads = expanded[..., NOPE:]
+    dealt_dy = exchange(cotangent_s, out_list, in_slots, (expanded,)) + more[:, slice_width:]
+    full_dy = cube_gather(dealt_dy, 1)
 
     def block_scores(first_row, last_row):
         raw_scores = (
@@ -474,6 +454,36 @@
     normed_two = cube_gather(normed_part, 0)
     (mate_part,) = after((mate_part,), (normed_two,))
     mate_two = cube_gather(mate_part, 0)
+    (dealt_mate_dy,) = after((mate(dealt_dy),), (normed_part,))
+    mate_dy = cube_gather(dealt_mate_dy, 1)
+    gate_up_w = expert_gather(*gate_up_parts, 0, (normed_part,))
+    down_w = expert_gather(*down_parts, 1, (normed_part,))
+    shared_gu_s, shared_d_s = after(
+        (jnp.concatenate([shared_gate, shared_up], axis=1), shared_down), (normed_part,)
+    )
+    shared_gu_w = row_gather(shared_gu_s, 0)
+    shared_d_w = row_gather(shared_d_s, 1)
+
+    place_late, rank_late, here_late, source_late, my_rank_late = after(
+        (place_in, rank_here, from_here, my_source, my_rank), (normed_part,)
+    )
+    hit = (place_late[:, :, None] == token_ids[None, None, :]) & here_late[:, :, None]
+    rank_of = jnp.sum(jnp.where(hit, rank_late[:, :, None], 0), axis=(0, 1))
+    groups = jnp.arange(row_count, dtype=jnp.int32)
+    group_of = jnp.sum(jnp.where(hit, groups[:, None, None], 0), axis=(0, 1))
+
+    def maps_back(step):
+        places = step * room + jnp.arange(room, dtype=jnp.int32)
+        hit = (my_rank_late[None, None, :] == places[None, :, None]) & (
+            source_late[None, None, :] == groups[:, None, None]
+        )
+        listed = jnp.sum(jnp.where(hit, token_ids[None, None, :] + 1, 0), axis=2).reshape(-1) - 1
+        slot = rank_of - step * room
+        inside = (slot >= 0) & (slot < room)
+        return listed, jnp.where(inside, group_of * room + slot, -1)
+
+    back_list, back_slots = maps_back(0)
+    gate_up_w, back_list, back_slots = after((gate_up_w, back_list, back_slots), ())
 
     def forward(rows, gate_up_w):
         width = gate_up_w.shape[1] // 2
@@ -488,20 +498,8 @@
             [(grad_hidden * up_slope).astype(BF16), (grad_hidden * act).astype(BF16)], axis=1
         )
 
-    ordered = []
-
     def queued_sum(value, axis):
-        if len(ordered) > 1:
-            (value,) = after((value,), (ordered[-2],))
-        ordered.append(row_scatter(value.astype(BF16), axis))
-        return ordered[-1]
-
-    shared_hidden, shared_act, shared_us = forward(normed_two, shared_gu_w)
-    grad_shared_gu = backward(dot_nt(full_dy, shared_d_w), shared_act, shared_us)
-    grad_two = dot_nt(grad_shared_gu, shared_gu_w)
-    moe_terms = dot(shared_hidden, shared_d_w)
-    grad_sgu = queued_sum(dot_tn(normed_two, grad_shared_gu), 0)
-    grad_sd = queued_sum(dot_tn(shared_hidden, full_dy), 1)
+        return row_scatter(value.astype(BF16), axis)
 
     rows = jnp.concatenate(
         [dot(pick, normed_two).astype(BF16), dot(mate_pick, mate_two).astype(BF16)], axis=0
@@ -517,30 +515,38 @@
     grad_gate_up = backward(dot_nt(grad_result, down_w), act, up_slope)
     mate_rows = dot_nt(grad_gate_up[capacity:], gate_up_w).astype(BF16)
     mate_grad = dot_tn(mate_pick, mate_rows).astype(BF16)
-    (own_gate_up,) = after((grad_gate_up[:capacity],), (mate_grad,))
+    mate_grad_part = mate(cube_scatter(mate_grad).astype(BF16))
+    own_gate_up, normed_s, dy_s = after(
+        (grad_gate_up[:capacity], normed_two, full_dy), (mate_grad,)
+    )
     own_rows = dot_nt(own_gate_up, gate_up_w).astype(BF16)
+    shared_hidden, shared_act, shared_us = forward(normed_s, shared_gu_w)
+    grad_shared_gu = backward(dot_nt(dy_s, shared_d_w), shared_act, shared_us)
+    grad_two = dot_nt(grad_shared_gu, shared_gu_w)
     grad_two = (grad_two + dot_tn(pick, own_rows)).astype(BF16)
-    mate_grad = mate(cube_scatter(mate_grad).astype(BF16))
-    grad_gu = dot_tn(rows, grad_gate_up).astype(BF16)
-    grad_down = dot_tn(hidden, grad_result).astype(BF16)
-
-    grad_two_part = cube_scatter(grad_two) + mate_grad.astype(F32)
+    grad_two_part = cube_scatter(grad_two)
+    late = after((rows, grad_gate_up, hidden, grad_result), (grad_two,))
+    grad_gu = dot_tn(late[0], late[1]).astype(BF16)
+    grad_down = dot_tn(late[2], late[3]).astype(BF16)
+    late = after((normed_two, grad_shared_gu, shared_hidden, full_dy), (grad_two,))
+    grad_sgu = queued_sum(dot_tn(late[0], late[1]), 0)
+    grad_sd = queued_sum(dot_tn(late[2], late[3]), 1)
+
+    (mate_grad_part,) = after((mate_grad_part,), (grad_two_part,))
+    grad_two_part = grad_two_part + mate_grad_part.astype(F32)
     dy_part = my_part(full_dy).astype(F32)
     hidden_back, gain_two_grad = norm_back(grad_two_part, unit_two, scale_two, gain_two)
     grad_hidden_part = dy_part + hidden_back
     grad_attn = cube_gather(grad_hidden_part.astype(BF16), 0)
 
-    (hidden_late,) = after((hidden,), (grad_two,))
+    hidden_late, shared_late = after((hidden, shared_hidden), (grad_hidden_part,))
     weights = jnp.concatenate([weight, mate_weight])
     result_rows = (weights[:, None] * dot(hidden_late, down_w)).astype(BF16)
     mate_terms = dot_tn(mate_pick, result_rows[capacity:]).astype(BF16)
-    moe_terms = (moe_terms + dot_tn(pick, result_rows[:capacity])).astype(BF16)
-    mate_terms, moe_terms = after((mate_terms, moe_terms), (grad_attn,))
+    moe_terms = dot(shared_late, shared_d_w) + dot_tn(pick, result_rows[:capacity])
+    mate_terms, moe_terms = after((mate_terms, moe_terms.astype(BF16)), (grad_attn,))
     mate_terms = mate(cube_scatter(mate_terms).astype(BF16))
-    moe_part = cube_scatter(moe_terms) + mate_terms.astype(F32)
-    result_part = (hidden_part + moe_part).astype(BF16)
-    result_slice = lax.all_to_all(result_part, "col", split_axis=1, concat_axis=0, tiled=True)
-    result = exchange(result_slice, back_list, back_slots)
+    moe_part = cube_scatter(moe_terms)
 
     grad_output_w = queued_sum(dot_tn(mixed, grad_attn), 1)
     grad_mixed = dot_nt(grad_attn, output_w).astype(BF16)
@@ -585,10 +591,15 @@
         .astype(BF16)
         .reshape(group_rows, head_count * (NOPE + ROPE))
     )
-    own_gu, mate_gu = expert_scatter(grad_gu, 0)
-    own_down, mate_down = expert_scatter(grad_down, 1)
-    grad_query_raw, mate_gu = after((grad_query_raw, mate_gu), ())
-    grad_one = cube_scatter(dot_nt(grad_query_raw, query_w).astype(BF16))
+    grad_one = dot_nt(grad_query_raw, query_w).astype(BF16)
+
+    mate_terms, moe_part = after((mate_terms, moe_part), (grad_one,))
+    result_part = (hidden_part + (moe_part + mate_terms.astype(F32))).astype(BF16)
+    result_slice = lax.all_to_all(result_part, "col", split_axis=1, concat_axis=0, tiled=True)
+
+    grad_one = cube_scatter(grad_one)
+    own_gu, mate_gu = expert_scatter(grad_gu, 0, ((grad_attn,), (grad_one,)))
+    own_down, mate_down = expert_scatter(grad_down, 1, ((grad_attn,), (grad_one,)))
     grad_expanded = jnp.concatenate([grad_keys[..., :NOPE], grad_values], axis=-1).astype(BF16)
     grad_expanded = grad_expanded.reshape(group_rows, head_count * (NOPE + VDIM))
     grad_compressed = dot_nt(grad_expanded, expand_w)
@@ -608,11 +619,12 @@
     )
     grad_input = (grad_hidden_part + input_back).astype(BF16)
     grad_slice = lax.all_to_all(grad_input, "col", split_axis=1, concat_axis=0, tiled=True)
+    result = exchange(result_slice, back_list, back_slots, (grad_input,))
     tokens_grad = exchange(grad_slice, back_list, back_slots)
 
     def more_back(carry):
         step, total = carry
-        _, _, back_more, slots_more = maps(step)
+        back_more, slots_more = maps_back(step)
         dealt = jnp.concatenate([result_slice, grad_slice], axis=1)
         return step + 1, total + exchange(dealt, back_more, slots_more)
 
@@ -632,7 +644,7 @@
     grad_latent_w = cube_gather(queued_sum(dot_tn(my_columns, grad_latent), 0), 0)
     gain_grads = small_sum(jnp.concatenate([gain_one_grad, gain_two_grad, latent_gain_grad]))
     width_ff = expert_gate.shape[2]
-    other_gu, other_down = mate(mate_gu), mate(mate_down)
+    other_gu, other_down = after((mate(mate_gu), mate(mate_down)), (grad_input,))
 
     def in_order(own, other):
         return jnp.stack([jnp.where(host == 0, own, other), jnp.where(host == 0, other, own)])

time: 1730 us -> 1950 us (1.13)
  waiting for transfers between devices: 614 us -> 827 us
  other arithmetic: 247 us -> 273 us
  matrix products: 457 us -> 437 us
    ppermute x3, waiting for transfers between devices: 0.01 us -> 130 us  [small_sum(): lax.ppermute(value, 'row', [(j, (j + k) % count) for j in range(count)])]
    ppermute x18, waiting for transfers between devices: 364 us -> 459 us  [row_swap(): lax.ppermute(value, 'row', [(j, j ^ bit) for j in range(lax.axis_size('ro...]
    reduce_scatter x6, waiting for transfers between devices: 63.6 us -> 0.01 us  [row_scatter(): return lax.psum_scatter(value, 'row', scatter_dimension=axis, tiled=True)]
    ppermute x30 -> x32, waiting for transfers between devices: 83 us -> 125 us  [chip_swap(): lax.ppermute(value, 'col', [(j, j ^ (other if j % 2 else bits)[step]) for...]
    dynamic_update_slice x59 -> x67, local copies, waits for them, and re-layouts: 83.6 us -> 75.7 us  [cube_gather(): lax.dynamic_update_slice_in_dim(out, item, block_at(owner, place) * width...]
    unnamed x408 -> x432, local copies, waits for them, and re-layouts: 39.6 us -> 46.3 us
    ppermute x30 -> x32, starting transfers between devices: 34.4 us -> 39.5 us  [chip_swap(): lax.ppermute(value, 'col', [(j, j ^ (other if j % 2 else bits)[step]) for...]
  transfers between devices with their start and end apart: 101 -> 106, of which waited for: 34 -> 36; matrix products, arithmetic and copies ran while one was open for 52% -> 43% of each run, Pallas kernels for 0% -> 0%
where the time goes in v5:
time: 1950 us; the launch traced here: 1940 us
  waiting for transfers between devices  827 us (42%)
  matrix products  437 us (22%)
  local copies, waits for them, and re-layouts  278 us (14%)
  other arithmetic  273 us (14%)
  starting transfers between devices  102 us (5%)
    ppermute x18, waiting for transfers between devices, row_swap(): lax.ppermute(value, 'row', [(j, j ^ bit) for j in range(lax.axis_size('ro...  459 us
    dot_general x20, matrix products, dot(): return jnp.dot(left, right, preferred_element_type=F32)  176 us
    ppermute x3, waiting for transfers between devices, small_sum(): lax.ppermute(value, 'row', [(j, (j + k) % count) for j in range(count)])  130 us
    dot_general x12, matrix products, dot_tn(): lax.dot_general(left, right, (((0,), (0,)), ((), ())), preferred_element_...  127 us
    ppermute x32, waiting for transfers between devices, chip_swap(): lax.ppermute(value, 'col', [(j, j ^ (other if j % 2 else bits)[step]) for...  125 us
    dot_general x9, matrix products, dot_nt(): lax.dot_general(left, right, (((1,), (1,)), ((), ())), preferred_element_...  97.1 us
    dynamic_update_slice x67, local copies, waits for them, and re-layouts, cube_gather(): lax.dynamic_update_slice_in_dim(out, item, block_at(owner, place) * width...  75.7 us
    all_to_all x4, waiting for transfers between devices, exchange(): got = lax.all_to_all(sent, 'row', split_axis=0, concat_axis=0, tiled=True)  47.7 us
  transfers between devices with their start and end apart: 106, of which 36 were waited for; matrix products, arithmetic and copies ran while one was open for 43% of the time, Pallas kernels for 0%

profile of v5, /device:TPU:0, one launch (start us, length us, event | category | flops | bytes accessed | tf_op | source)
XLA Modules:
  0.0 1936.4 jit_solution(719402761131069417)
XLA Ops:
  40.8 25.3 %all-to-all-done.2 = bf16[4,640,256]{2,1,0:T(8,128)(2,1)S(1)} async-done(((bf16[4,640,256]{2,1,0:T(8,128)(2,1)}), bf16[4,640,256]{2,1,0:T(8,128)(2,1)S(1)}, u32[]{:S(2)}, u32[]{:S(2)}) %all-to-all-start.2) | async-done | bytes 1310752 | tf_op jit(solution)/shard_map/all_to_all | solution.py:233
  119.1 38.9 %all-gather.11.cloned.1.call-done = bf16[2496,384]{1,0:T(8,128)(2,1)} async-done(((bf16[624,384]{1,0:T(8,128)(2,1)}), bf16[2496,384]{1,0:T(8,128)(2,1)}) %all-gather.11.cloned.1.call-update) | async-done | bytes 1916944 | tf_op jit(solution)/shard_map/all_gather | solution.py:203
  203.5 8.8 fusion.29
  212.2 9.1 fusion.269
  291.0 27.8 %collective-permute-done.16 = s32[2048,6]{0,1:T(8,128)S(1)} collective-permute-done((s32[2048,6]{0,1:T(8,128)S(1)}, s32[2048,6]{0,1:T(8,128)S(1)}, u32[]{:S(2)}, u32[]{:S(2)}) %collective-permute-start.16) | collective-permute-done | bytes 49184 | tf_op jit(solution)/shard_map/ppermute | solution.py:76
  333.0 9.1 collective-permute-done.30
  355.2 12.2 copy.346
  379.4 14.6 collective-permute-done.12
  426.9 13.1 multiply_convert_fusion.6
  440.9 83.9 %collective-permute-done = bf16[512,2816]{1,0:T(8,128)(2,1)} collective-permute-done((bf16[512,2816]{1,0:T(8,128)(2,1)}, bf16[512,2816]{1,0:T(8,128)(2,1)}, u32[]{:S(2)}, u32[]{:S(2)}) %collective-permute-start) | collective-permute-done | bytes 2883616 | tf_op jit(solution)/shard_map/ppermute | solution.py:76
  528.6 78.3 %collective-permute-done.40 = bf16[1408,512]{1,0:T(8,128)(2,1)} collective-permute-done((bf16[1408,512]{1,0:T(8,128)(2,1)}, bf16[1408,512]{1,0:T(8,128)(2,1)}, u32[]{:S(2)}, u32[]{:S(2)}) %collective-permute-start.40) | collective-permute-done | bytes 1441824 | tf_op jit(solution)/shard_map/ppermute | solution.py:76
  609.2 22.1 %collective-permute-done.34 = bf16[2048,256]{1,0:T(8,128)(2,1)} collective-permute-done((bf16[2048,256]{1,0:T(8,128)(2,1)}, bf16[2048,256]{1,0:T(8,128)(2,1)}, u32[]{:S(2)}, u32[]{:S(2)}) %collective-permute-start.34) | collective-permute-done | bytes 1048608 | tf_op jit(solution)/shard_map/ppermute | solution.py:76
  631.3 23.4 %select_reduce_fusion.2 = (s32[2048]{0:T(1024)S(1)}, s32[2048]{0:T(1024)S(1)}) fusion(s32[4,2048]{1,0:T(4,128)S(1)} %copy-done.116, pred[4,2048]{1,0:T(4,128)(4,1)S(1)} %copy-done.173, s32[4,2048]{1,0:T(4,128)S(1)} %copy-done.104), kind=kLoop, calls=%fused_computation.32 | loop fusion | flops 100659200 | bytes 90112 | tf_op jit(solution)/shard_map/reduce_sum | solution.py:473
  682.8 14.6 collective-permute-done.36
  700.1 38.4 %collective-permute-done.41 = bf16[1408,512]{1,0:T(8,128)(2,1)} collective-permute-done((bf16[1408,512]{1,0:T(8,128)(2,1)}, bf16[1408,512]{1,0:T(8,128)(2,1)}, u32[]{:S(2)}, u32[]{:S(2)}) %collective-permute-start.41) | collective-permute-done | bytes 1441824 | tf_op jit(solution)/shard_map/ppermute | solution.py:76
  751.6 18.0 collective-permute-done.38
  777.1 9.6 collective-permute-done.25
  788.8 12.9 multiply_convert_fusion.5
  801.8 10.6 fusion.81
  824.8 10.8 fusion.80
  835.6 30.4 %fusion.251 = f32[2048,2816]{1,0:T(8,128)} fusion(bf16[2048,2816]{1,0:T(8,128)(2,1)S(1)} %constant_dynamic-update-slice_fusion.8, bf16[1024,2048]{1,0:T(8,128)(2,1)} %fusion.80, bf16[1024,2048]{1,0:T(8,128)(2,1)} %fusion.81), kind=kOutput, calls=%fused_computation.647 | convolution fusion | flops 23639097344 | bytes 42991616 | tf_op jit(solution)/shard_map/dot_general | solution.py:60
  866.1 26.3 %multiply_convert_fusion.1 = (bf16[2048,1408]{1,0:T(8,128)(2,1)}, bf16[2048,1408]{1,0:T(8,128)(2,1)}, bf16[2048,1408]{1,0:T(8,128)(2,1)}) fusion(f32[2048,2816]{1,0:T(8,128)} %fusion.251, bf16[1408,2048]{1,0:T(8,128)(2,1)} %copy-done.48, bf16[1024,2048]{1,0:T(8,128)(2,1)} %multiply_convert_fusion.5, bf16[1024,2048]{1,0:T(8,128)(2,1)} %multiply_convert_fusion.6), kind=kOutput, calls=%fused_computation.64 | convolution fusion | flops 11871191040 | bytes 54525952 | tf_op jit(solution)/shard_map/dot_general | solution.py:64
  892.3 18.2 fusion.55
  916.2 10.1 fusion.49
  934.5 14.1 fusion.356
  948.7 12.1 fusion.42
  960.8 11.2 fusion.270
  972.0 10.7 multiply_convert_fusion.11
  982.7 11.9 add_convert_fusion.1
  1036.6 11.2 pad_maximum_fusion
  1056.2 15.2 convolution_convert_fusion.3
  1073.4 15.4 collective-permute-done.44
  1103.1 77.2 %collective-permute-done.49 = bf16[256,2048]{1,0:T(8,128)(2,1)} collective-permute-done((bf16[256,2048]{1,0:T(8,128)(2,1)}, bf16[256,2048]{1,0:T(8,128)(2,1)}, u32[]{:S(2)}, u32[]{:S(2)}) %collective-permute-start.49) | collective-permute-done | bytes 1048608 | tf_op jit(solution)/shard_map/ppermute | solution.py:76
  1187.8 15.4 multiply_convert_fusion
  1203.3 11.2 fusion.50
  1216.1 11.6 fusion.41
  1227.8 11.0 add_convert_fusion
  1350.9 12.0 dynamic-slice_bitcast_fusion.21
  1396.9 30.0 %convolution_convert_fusion = bf16[2048,2816]{1,0:T(8,128)(2,1)S(1)} fusion(bf16[2048,2048]{1,0:T(8,128)(2,1)} %pad_maximum_fusion.1, bf16[2048,2816]{1,0:T(8,128)(2,1)} %pad_maximum_fusion), kind=kOutput, calls=%fused_computation.69 | convolution fusion | flops 23628087296 | bytes 31457280 | tf_op jit(solution)/shard_map/dot_general | solution.py:68
  1433.6 9.2 convolution_convert_fusion.7
  1472.0 61.8 %collective-permute-done.85 = bf16[512,2816]{1,0:T(8,128)(2,1)} collective-permute-done((bf16[512,2816]{1,0:T(8,128)(2,1)}, bf16[512,2816]{1,0:T(8,128)(2,1)}, u32[]{:S(2)}, u32[]{:S(2)}) %collective-permute-start.85) | collective-permute-done | bytes 2883616 | tf_op jit(solution)/shard_map/ppermute | solution.py:76
  1577.2 8.8 collective-permute-done.64
  1592.3 44.8 %collective-permute-done.84 = bf16[512,2816]{1,0:T(8,128)(2,1)} collective-permute-done((bf16[512,2816]{1,0:T(8,128)(2,1)}, bf16[512,2816]{1,0:T(8,128)(2,1)}, u32[]{:S(2)}, u32[]{:S(2)}) %collective-permute-start.84) | collective-permute-done | bytes 2883616 | tf_op jit(solution)/shard_map/ppermute | solution.py:76
  1685.3 8.6 all-to-all-done.4
  1710.3 17.9 collective-permute-done.73
  1728.2 112.3 %collective-permute-done.72 = f32[4608]{0:T(1024)} collective-permute-done((f32[4608]{0:T(1024)S(1)}, f32[4608]{0:T(1024)}, u32[]{:S(2)}, u32[]{:S(2)}) %collective-permute-start.72) | collective-permute-done | bytes 18464 | tf_op jit(solution)/shard_map/ppermute | solution.py:221
  1860.3 25.0 %collective-permute-done.88 = bf16[1408,512]{1,0:T(8,128)(2,1)} collective-permute-done((bf16[1408,512]{1,0:T(8,128)(2,1)S(1)}, bf16[1408,512]{1,0:T(8,128)(2,1)}, u32[]{:S(2)}, u32[]{:S(2)}) %collective-permute-start.88) | collective-permute-done | bytes 1441824 | tf_op jit(solution)/shard_map/ppermute | solution.py:76
  1902.1 18.8 all-to-all-done.5
  (1036 shorter events, 774.0 us)
Async XLA Ops:
  34.7 79.5 %all-gather.13.cloned.1.call-start = ((), (), s32[]{:S(2)}) async-start(), calls=%async_computation.23 | async-start | bytes 1966080 | tf_op jit(solution)/shard_map/all_gather | solution.py:203
  77.9 80.2 %all-gather.11.cloned.1.call-start = ((), (), s32[]{:S(2)}) async-start(), calls=%async_computation.22 | async-start | bytes 2396160 | tf_op jit(solution)/shard_map/all_gather | solution.py:203
  102.3 65.6 %collective-permute-start.4 = (bf16[2,2048,256]{2,1,0:T(8,128)(2,1)}, bf16[2,2048,256]{2,1,0:T(8,128)(2,1)}, u32[]{:S(2)}, u32[]{:S(2)}) collective-permute-start(bf16[2,2048,256]{2,1,0:T(8,128)(2,1)} %pad_maximum_fusion.16), channel_id=1, source_target_pairs={{0,4},{1,3},{2,6},{3,1},{4,0},{5,7},{6,2},{7,5},{8,12},{9,11},{10,... | collective-permute-start | bytes 6291464 | tf_op jit(solution)/shard_map/ppermute | solution.py:141
  282.0 678.8 %all-gather.7.cloned.1.call-start = ((), (), s32[]{:S(2)}) async-start(), calls=%async_computation.14 | async-start | bytes 3604480 | tf_op jit(solution)/shard_map/all_gather | solution.py:203
  286.0 60.6 %collective-permute-start.11 = (bf16[4,256,2048]{2,1,0:T(8,128)(2,1)}, bf16[4,256,2048]{2,1,0:T(8,128)(2,1)}, u32[]{:S(2)}, u32[]{:S(2)}) collective-permute-start(bf16[4,256,2048]{2,1,0:T(8,128)(2,1)} %pad_maximum_fusion.3), channel_id=1, source_target_pairs={{0,1},{1,0},{2,3},{3,2},{4,5},{5,4},{6,7},{7,6},{8,9},{9,8},{10,11... | collective-permute-start | bytes 12582920 | tf_op jit(solution)/shard_map/ppermute | solution.py:131
  330.3 194.6 %collective-permute-start = (bf16[512,2816]{1,0:T(8,128)(2,1)}, bf16[512,2816]{1,0:T(8,128)(2,1)}, u32[]{:S(2)}, u32[]{:S(2)}) collective-permute-start(bf16[512,2816]{1,0:T(8,128)(2,1)} %pad_maximum_fusion.11), channel_id=1, source_target_pairs={{0,16},{8,24},{16,0},{24,8},{1,17},{9,25},{17,1},{25,9},{2,18},{10... | collective-permute-start | bytes 8650760 | tf_op jit(solution)/shard_map/ppermute | solution.py:76
  330.3 194.6 %collective-permute-start.15 = (bf16[512,2816]{1,0:T(8,128)(2,1)S(1)}, bf16[512,2816]{1,0:T(8,128)(2,1)}, u32[]{:S(2)}, u32[]{:S(2)}) collective-permute-start(bf16[512,2816]{1,0:T(8,128)(2,1)S(1)} %copy-done.32), channel_id=1, source_target_pairs={{0,8},{8,0},{16,24},{24,16},{1,9},{9,1},{17,25},{25,17},{2,10},{10... | collective-permute-start | bytes 8650760 | tf_op jit(solution)/shard_map/ppermute | solution.py:76
  394.0 212.9 %collective-permute-start.40 = (bf16[1408,512]{1,0:T(8,128)(2,1)}, bf16[1408,512]{1,0:T(8,128)(2,1)}, u32[]{:S(2)}, u32[]{:S(2)}) collective-permute-start(bf16[1408,512]{1,0:T(8,128)(2,1)} %get-tuple-element.456), channel_id=1, source_target_pairs={{0,16},{8,24},{16,0},{24,8},{1,17},{9,25},{17,1},{25,9},{2,18},{10... | collective-permute-start | bytes 4325384 | tf_op jit(solution)/shard_map/ppermute | solution.py:76
  401.5 207.7 %collective-permute-start.42 = (bf16[1408,512]{1,0:T(8,128)(2,1)}, bf16[1408,512]{1,0:T(8,128)(2,1)}, u32[]{:S(2)}, u32[]{:S(2)}) collective-permute-start(bf16[1408,512]{1,0:T(8,128)(2,1)} %get-tuple-element.459), channel_id=1, source_target_pairs={{0,8},{8,0},{16,24},{24,16},{1,9},{9,1},{17,25},{25,17},{2,10},{10... | collective-permute-start | bytes 4325384 | tf_op jit(solution)/shard_map/ppermute | solution.py:76
  411.4 219.9 %collective-permute-start.34 = (bf16[2048,256]{1,0:T(8,128)(2,1)}, bf16[2048,256]{1,0:T(8,128)(2,1)}, u32[]{:S(2)}, u32[]{:S(2)}) collective-permute-start(bf16[2048,256]{1,0:T(8,128)(2,1)} %get-tuple-element.701), channel_id=1, source_target_pairs={{0,16},{8,24},{16,0},{24,8},{1,17},{9,25},{17,1},{25,9},{2,18},{10... | collective-permute-start | bytes 3145736 | tf_op jit(solution)/shard_map/ppermute | solution.py:76
  422.1 549.9 %all-gather.9.cloned.1.call-start = ((), (), s32[]{:S(2)}) async-start(), calls=%async_computation.15 | async-start | bytes 1802240 | tf_op jit(solution)/shard_map/all_gather | solution.py:203
  524.9 246.2 %collective-permute-start.23 = (bf16[256,2048]{1,0:T(8,128)(2,1)}, bf16[256,2048]{1,0:T(8,128)(2,1)}, u32[]{:S(2)}, u32[]{:S(2)}) collective-permute-start(bf16[256,2048]{1,0:T(8,128)(2,1)} %get-tuple-element.555), channel_id=1, source_target_pairs={{0,16},{8,24},{16,0},{24,8},{1,17},{9,25},{17,1},{25,9},{2,18},{10... | collective-permute-start | bytes 3145736 | tf_op jit(solution)/shard_map/ppermute | solution.py:76
  528.6 144.2 %collective-permute-start.18 = (bf16[1,256,2048]{2,1,0:T(8,128)(2,1)}, bf16[1,256,2048]{2,1,0:T(8,128)(2,1)}, u32[]{:S(2)}, u32[]{:S(2)}) collective-permute-start(bf16[1,256,2048]{2,1,0:T(8,128)(2,1)} %bitcast.66), channel_id=1, source_target_pairs={{0,1},{1,0},{2,3},{3,2},{4,5},{5,4},{6,7},{7,6},{8,9},{9,8},{10,11... | collective-permute-start | bytes 3145736 | tf_op jit(solution)/shard_map/ppermute | solution.py:131
  606.9 68.3 %collective-permute-start.19 = (bf16[1,256,2048]{2,1,0:T(8,128)(2,1)}, bf16[1,256,2048]{2,1,0:T(8,128)(2,1)}, u32[]{:S(2)}, u32[]{:S(2)}) collective-permute-start(bf16[1,256,2048]{2,1,0:T(8,128)(2,1)} %bitcast.66), channel_id=1, source_target_pairs={{0,2},{1,5},{2,0},{3,7},{4,6},{5,1},{6,4},{7,3},{8,10},{9,13},{10,... | collective-permute-start | bytes 3145736 | tf_op jit(solution)/shard_map/ppermute | solution.py:141
  609.2 136.8 %collective-permute-start.14 = (bf16[512,2816]{1,0:T(8,128)(2,1)}, bf16[512,2816]{1,0:T(8,128)(2,1)}, u32[]{:S(2)}, u32[]{:S(2)}) collective-permute-start(bf16[512,2816]{1,0:T(8,128)(2,1)} %collective-permute-done), channel_id=1, source_target_pairs={{0,8},{8,0},{16,24},{24,16},{1,9},{9,1},{17,25},{25,17},{2,10},{10... | collective-permute-start | bytes 8650760 | tf_op jit(solution)/shard_map/ppermute | solution.py:76
  631.2 107.2 %collective-permute-start.41 = (bf16[1408,512]{1,0:T(8,128)(2,1)}, bf16[1408,512]{1,0:T(8,128)(2,1)}, u32[]{:S(2)}, u32[]{:S(2)}) collective-permute-start(bf16[1408,512]{1,0:T(8,128)(2,1)} %collective-permute-done.40), channel_id=1, source_target_pairs={{0,8},{8,0},{16,24},{24,16},{1,9},{9,1},{17,25},{25,17},{2,10},{10... | collective-permute-start | bytes 4325384 | tf_op jit(solution)/shard_map/ppermute | solution.py:76
  631.3 812.3 %reduce-scatter.17.cloned.1.call-start = ((), (), s32[]{:S(2)}) async-start(), calls=%async_computation.21 | async-start | bytes 1802240 | tf_op jit(solution)/shard_map/reduce_scatter | solution.py:212
  680.8 65.2 %collective-permute-start.21 = (bf16[2,256,2048]{2,1,0:T(8,128)(2,1)S(1)}, bf16[2,256,2048]{2,1,0:T(8,128)(2,1)S(1)}, u32[]{:S(2)}, u32[]{:S(2)}) collective-permute-start(bf16[2,256,2048]{2,1,0:T(8,128)(2,1)S(1)} %pad_maximum_fusion.17), channel_id=1, source_target_pairs={{0,4},{1,3},{2,6},{3,1},{4,0},{5,7},{6,2},{7,5},{8,12},{9,11},{10,... | collective-permute-start | bytes 6291464 | tf_op jit(solution)/shard_map/ppermute | solution.py:141
  933.6 86.1 %collective-permute-start.46 = (bf16[4,256,2048]{2,1,0:T(8,128)(2,1)}, bf16[4,256,2048]{2,1,0:T(8,128)(2,1)}, u32[]{:S(2)}, u32[]{:S(2)}) collective-permute-start(bf16[4,256,2048]{2,1,0:T(8,128)(2,1)} %pad_maximum_fusion.5), channel_id=1, source_target_pairs={{0,1},{1,0},{2,3},{3,2},{4,5},{5,4},{6,7},{7,6},{8,9},{9,8},{10,11... | collective-permute-start | bytes 12582920 | tf_op jit(solution)/shard_map/ppermute | solution.py:131
  999.8 48.0 %collective-permute-start.43 = (bf16[4,256,2048]{2,1,0:T(8,128)(2,1)}, bf16[4,256,2048]{2,1,0:T(8,128)(2,1)}, u32[]{:S(2)}, u32[]{:S(2)}) collective-permute-start(bf16[4,256,2048]{2,1,0:T(8,128)(2,1)} %pad_maximum_fusion.4), channel_id=1, source_target_pairs={{0,1},{1,0},{2,3},{3,2},{4,5},{5,4},{6,7},{7,6},{8,9},{9,8},{10,11... | collective-permute-start | bytes 12582920 | tf_op jit(solution)/shard_map/ppermute | solution.py:131
  1019.7 425.9 %reduce-scatter.15.cloned.1.call-start = ((), (), s32[]{:S(2)}) async-start(), calls=%async_computation.20 | async-start | bytes 3604480 | tf_op jit(solution)/shard_map/reduce_scatter | solution.py:212
  1073.4 374.5 %collective-permute-start.87 = (bf16[1408,512]{1,0:T(8,128)(2,1)}, bf16[1408,512]{1,0:T(8,128)(2,1)}, u32[]{:S(2)}, u32[]{:S(2)}) collective-permute-start(bf16[1408,512]{1,0:T(8,128)(2,1)} %get-tuple-element.627), channel_id=1, source_target_pairs={{0,8},{8,0},{16,24},{24,16},{1,9},{9,1},{17,25},{25,17},{2,10},{10... | collective-permute-start | bytes 4325384 | tf_op jit(solution)/shard_map/ppermute | solution.py:76
  1092.0 88.3 %collective-permute-start.45 = (bf16[1,256,2048]{2,1,0:T(8,128)(2,1)}, bf16[1,256,2048]{2,1,0:T(8,128)(2,1)}, u32[]{:S(2)}, u32[]{:S(2)}) collective-permute-start(bf16[1,256,2048]{2,1,0:T(8,128)(2,1)} %slice.899), channel_id=1, source_target_pairs={{0,2},{1,5},{2,0},{3,7},{4,6},{5,1},{6,4},{7,3},{8,10},{9,13},{10,... | collective-permute-start | bytes 3145736 | tf_op jit(solution)/shard_map/ppermute | solution.py:141
  1094.8 85.5 %collective-permute-start.49 = (bf16[256,2048]{1,0:T(8,128)(2,1)}, bf16[256,2048]{1,0:T(8,128)(2,1)}, u32[]{:S(2)}, u32[]{:S(2)}) collective-permute-start(bf16[256,2048]{1,0:T(8,128)(2,1)} %fusion.165), channel_id=1, source_target_pairs={{0,16},{8,24},{16,0},{24,8},{1,17},{9,25},{17,1},{25,9},{2,18},{10... | collective-permute-start | bytes 3145736 | tf_op jit(solution)/shard_map/ppermute | solution.py:76
  1103.0 344.9 %reduce-scatter.9.cloned.1.call-start = ((), (), s32[]{:S(2)}) async-start(), calls=%async_computation.17 | async-start | bytes 409600 | tf_op jit(solution)/shard_map/reduce_scatter | solution.py:212
  1187.0 55.1 %collective-permute-start.50 = (bf16[1,256,2048]{2,1,0:T(8,128)(2,1)S(1)}, bf16[1,256,2048]{2,1,0:T(8,128)(2,1)}, u32[]{:S(2)}, u32[]{:S(2)}) collective-permute-start(bf16[1,256,2048]{2,1,0:T(8,128)(2,1)S(1)} %get-tuple-element.552), channel_id=1, source_target_pairs={{0,1},{1,0},{2,3},{3,2},{4,5},{5,4},{6,7},{7,6},{8,9},{9,8},{10,11... | collective-permute-start | bytes 3145736 | tf_op jit(solution)/shard_map/ppermute | solution.py:131
  1344.1 111.2 %collective-permute-start.62 = (bf16[4,256,2048]{2,1,0:T(8,128)(2,1)}, bf16[4,256,2048]{2,1,0:T(8,128)(2,1)}, u32[]{:S(2)}, u32[]{:S(2)}) collective-permute-start(bf16[4,256,2048]{2,1,0:T(8,128)(2,1)} %pad_maximum_fusion.8), channel_id=1, source_target_pairs={{0,1},{1,0},{2,3},{3,2},{4,5},{5,4},{6,7},{7,6},{8,9},{9,8},{10,11... | collective-permute-start | bytes 12582920 | tf_op jit(solution)/shard_map/ppermute | solution.py:131
  1378.3 160.3 %reduce-scatter.11.cloned.1.call-start = ((), (), s32[]{:S(2)}) async-start(), calls=%async_computation.18 | async-start | bytes 655360 | tf_op jit(solution)/shard_map/reduce_scatter | solution.py:212
  1382.4 65.7 %collective-permute-start.55 = (bf16[4,256,2048]{2,1,0:T(8,128)(2,1)}, bf16[4,256,2048]{2,1,0:T(8,128)(2,1)}, u32[]{:S(2)}, u32[]{:S(2)}) collective-permute-start(bf16[4,256,2048]{2,1,0:T(8,128)(2,1)} %pad_maximum_fusion.6), channel_id=1, source_target_pairs={{0,1},{1,0},{2,3},{3,2},{4,5},{5,4},{6,7},{7,6},{8,9},{9,8},{10,11... | collective-permute-start | bytes 12582920 | tf_op jit(solution)/shard_map/ppermute | solution.py:131
  1386.1 154.1 %reduce-scatter.13.cloned.1.call-start = ((), (), s32[]{:S(2)}) async-start(), calls=%async_computation.19 | async-start | bytes 1310720 | tf_op jit(solution)/shard_map/reduce_scatter | solution.py:212
  1390.0 71.7 %collective-permute-start.59 = (bf16[4,256,2048]{2,1,0:T(8,128)(2,1)}, bf16[4,256,2048]{2,1,0:T(8,128)(2,1)}, u32[]{:S(2)}, u32[]{:S(2)}) collective-permute-start(bf16[4,256,2048]{2,1,0:T(8,128)(2,1)} %pad_maximum_fusion.7), channel_id=1, source_target_pairs={{0,1},{1,0},{2,3},{3,2},{4,5},{5,4},{6,7},{7,6},{8,9},{9,8},{10,11... | collective-permute-start | bytes 12582920 | tf_op jit(solution)/shard_map/ppermute | solution.py:131
  1396.9 145.2 %reduce-scatter.7.cloned.1.call-start = ((), (), s32[]{:S(2)}) async-start(), calls=%async_computation.16 | async-start | bytes 1966080 | tf_op jit(solution)/shard_map/reduce_scatter | solution.py:212
  1433.1 100.7 %collective-permute-start.85 = (bf16[512,2816]{1,0:T(8,128)(2,1)}, bf16[512,2816]{1,0:T(8,128)(2,1)}, u32[]{:S(2)}, u32[]{:S(2)}) collective-permute-start(bf16[512,2816]{1,0:T(8,128)(2,1)} %get-tuple-element.572), channel_id=1, source_target_pairs={{0,8},{8,0},{16,24},{24,16},{1,9},{9,1},{17,25},{25,17},{2,10},{10... | collective-permute-start | bytes 8650760 | tf_op jit(solution)/shard_map/ppermute | solution.py:76
  1447.9 87.4 %collective-permute-start.79 = (bf16[1,64,576]{2,1,0:T(8,128)(2,1)}, bf16[1,64,576]{2,1,0:T(8,128)(2,1)S(1)}, u32[]{:S(2)}, u32[]{:S(2)}) collective-permute-start(bf16[1,64,576]{2,1,0:T(8,128)(2,1)} %bitcast.671), channel_id=1, source_target_pairs={{0,1},{1,0},{2,3},{3,2},{4,5},{5,4},{6,7},{7,6},{8,9},{9,8},{10,11... | collective-permute-start | bytes 221192 | tf_op jit(solution)/shard_map/ppermute | solution.py:131
  1455.3 100.3 %collective-permute-start.56 = (bf16[2,256,2048]{2,1,0:T(8,128)(2,1)}, bf16[2,256,2048]{2,1,0:T(8,128)(2,1)}, u32[]{:S(2)}, u32[]{:S(2)}) collective-permute-start(bf16[2,256,2048]{2,1,0:T(8,128)(2,1)} %slice.911), channel_id=1, source_target_pairs={{0,4},{1,3},{2,6},{3,1},{4,0},{5,7},{6,2},{7,5},{8,12},{9,11},{10,... | collective-permute-start | bytes 6291464 | tf_op jit(solution)/shard_map/ppermute | solution.py:141
  1461.7 98.2 %collective-permute-start.63 = (bf16[2,256,2048]{2,1,0:T(8,128)(2,1)}, bf16[2,256,2048]{2,1,0:T(8,128)(2,1)S(1)}, u32[]{:S(2)}, u32[]{:S(2)}) collective-permute-start(bf16[2,256,2048]{2,1,0:T(8,128)(2,1)} %slice.924), channel_id=1, source_target_pairs={{0,4},{1,3},{2,6},{3,1},{4,0},{5,7},{6,2},{7,5},{8,12},{9,11},{10,... | collective-permute-start | bytes 6291464 | tf_op jit(solution)/shard_map/ppermute | solution.py:141
  1470.4 91.7 %collective-permute-start.60 = (bf16[2,256,2048]{2,1,0:T(8,128)(2,1)}, bf16[2,256,2048]{2,1,0:T(8,128)(2,1)}, u32[]{:S(2)}, u32[]{:S(2)}) collective-permute-start(bf16[2,256,2048]{2,1,0:T(8,128)(2,1)} %slice.915), channel_id=1, source_target_pairs={{0,4},{1,3},{2,6},{3,1},{4,0},{5,7},{6,2},{7,5},{8,12},{9,11},{10,... | collective-permute-start | bytes 6291464 | tf_op jit(solution)/shard_map/ppermute | solution.py:141
  1549.1 87.9 %collective-permute-start.84 = (bf16[512,2816]{1,0:T(8,128)(2,1)}, bf16[512,2816]{1,0:T(8,128)(2,1)}, u32[]{:S(2)}, u32[]{:S(2)}) collective-permute-start(bf16[512,2816]{1,0:T(8,128)(2,1)} %get-tuple-element.573), channel_id=1, source_target_pairs={{0,8},{8,0},{16,24},{24,16},{1,9},{9,1},{17,25},{25,17},{2,10},{10... | collective-permute-start | bytes 8650760 | tf_op jit(solution)/shard_map/ppermute | solution.py:76
  1552.0 155.4 %collective-permute-start.89 = (bf16[1408,512]{1,0:T(8,128)(2,1)}, bf16[1408,512]{1,0:T(8,128)(2,1)}, u32[]{:S(2)}, u32[]{:S(2)}) collective-permute-start(bf16[1408,512]{1,0:T(8,128)(2,1)} %get-tuple-element.626), channel_id=1, source_target_pairs={{0,8},{8,0},{16,24},{24,16},{1,9},{9,1},{17,25},{25,17},{2,10},{10... | collective-permute-start | bytes 4325384 | tf_op jit(solution)/shard_map/ppermute | solution.py:76
  1555.6 129.1 %collective-permute-start.83 = (bf16[2,64,576]{2,1,0:T(8,128)(2,1)}, bf16[2,64,576]{2,1,0:T(8,128)(2,1)}, u32[]{:S(2)}, u32[]{:S(2)}) collective-permute-start(bf16[2,64,576]{2,1,0:T(8,128)(2,1)} %copy-done.145), channel_id=1, source_target_pairs={{0,1},{1,0},{2,3},{3,2},{4,5},{5,4},{6,7},{7,6},{8,9},{9,8},{10,11... | collective-permute-start | bytes 442376 | tf_op jit(solution)/shard_map/ppermute | solution.py:131
  1574.8 79.4 %collective-permute-start.61 = (bf16[1,256,2048]{2,1,0:T(8,128)(2,1)}, bf16[1,256,2048]{2,1,0:T(8,128)(2,1)}, u32[]{:S(2)}, u32[]{:S(2)}) collective-permute-start(bf16[1,256,2048]{2,1,0:T(8,128)(2,1)} %slice.917), channel_id=1, source_target_pairs={{0,2},{1,5},{2,0},{3,7},{4,6},{5,1},{6,4},{7,3},{8,10},{9,13},{10,... | collective-permute-start | bytes 3145736 | tf_op jit(solution)/shard_map/ppermute | solution.py:141
  1586.0 82.1 %collective-permute-start.58 = (bf16[256,2048]{1,0:T(8,128)(2,1)}, bf16[256,2048]{1,0:T(8,128)(2,1)}, u32[]{:S(2)}, u32[]{:S(2)}) collective-permute-start(bf16[256,2048]{1,0:T(8,128)(2,1)} %fusion.166), channel_id=1, source_target_pairs={{0,16},{8,24},{16,0},{24,8},{1,17},{9,25},{17,1},{25,9},{2,18},{10... | collective-permute-start | bytes 3145736 | tf_op jit(solution)/shard_map/ppermute | solution.py:76
  1649.5 235.8 %collective-permute-start.86 = (bf16[512,2816]{1,0:T(8,128)(2,1)}, bf16[512,2816]{1,0:T(8,128)(2,1)}, u32[]{:S(2)}, u32[]{:S(2)}) collective-permute-start(bf16[512,2816]{1,0:T(8,128)(2,1)} %get-tuple-element.570), channel_id=1, source_target_pairs={{0,16},{8,24},{16,0},{24,8},{1,17},{9,25},{17,1},{25,9},{2,18},{10... | collective-permute-start | bytes 8650760 | tf_op jit(solution)/shard_map/ppermute | solution.py:76
  1666.2 62.0 %collective-permute-start.73 = (f32[4608]{0:T(1024)S(1)}, f32[4608]{0:T(1024)}, u32[]{:S(2)}, u32[]{:S(2)}) collective-permute-start(f32[4608]{0:T(1024)S(1)} %add.909), channel_id=1, source_target_pairs={{0,24},{8,0},{16,8},{24,16},{1,25},{9,1},{17,9},{25,17},{2,26},{10... | collective-permute-start | bytes 55304 | tf_op jit(solution)/shard_map/ppermute | solution.py:221
  1668.1 172.3 %collective-permute-start.72 = (f32[4608]{0:T(1024)S(1)}, f32[4608]{0:T(1024)}, u32[]{:S(2)}, u32[]{:S(2)}) collective-permute-start(f32[4608]{0:T(1024)S(1)} %add.909), channel_id=1, source_target_pairs={{0,16},{8,24},{16,0},{24,8},{1,17},{9,25},{17,1},{25,9},{2,18},{10... | collective-permute-start | bytes 55304 | tf_op jit(solution)/shard_map/ppermute | solution.py:221
  1684.7 155.8 %collective-permute-start.71 = (f32[4608]{0:T(1024)S(1)}, f32[4608]{0:T(1024)}, u32[]{:S(2)}, u32[]{:S(2)}) collective-permute-start(f32[4608]{0:T(1024)S(1)} %add.909), channel_id=1, source_target_pairs={{0,8},{8,16},{16,24},{24,0},{1,9},{9,17},{17,25},{25,1},{2,10},{10... | collective-permute-start | bytes 55304 | tf_op jit(solution)/shard_map/ppermute | solution.py:221
  1693.9 160.6 %all-to-all-start.7 = ((bf16[4,640,256]{2,1,0:T(8,128)(2,1)}), bf16[4,640,256]{2,1,0:T(8,128)(2,1)}, u32[]{:S(2)}, u32[]{:S(2)}) async-start(bf16[4,640,256]{2,1,0:T(8,128)(2,1)} %bitcast.657), calls=%async_computation.7 | async-start | bytes 2621440 | tf_op jit(solution)/shard_map/all_to_all | solution.py:233
  1707.4 177.9 %collective-permute-start.88 = (bf16[1408,512]{1,0:T(8,128)(2,1)S(1)}, bf16[1408,512]{1,0:T(8,128)(2,1)}, u32[]{:S(2)}, u32[]{:S(2)}) collective-permute-start(bf16[1408,512]{1,0:T(8,128)(2,1)S(1)} %copy-done.107), channel_id=1, source_target_pairs={{0,16},{8,24},{16,0},{24,8},{1,17},{9,25},{17,1},{25,9},{2,18},{10... | collective-permute-start | bytes 4325384 | tf_op jit(solution)/shard_map/ppermute | solution.py:76
  (267 other events, 5456.6 us)
Sparse Core Ops, SparseCore 0:
  78.0 36.2 all-gather.12
  116.4 41.5 all-gather.10
  422.2 110.7 all-gather.6
  631.4 59.8 all-gather.8
  1019.8 32.2 reduce-scatter.16
  1103.1 82.6 reduce-scatter.14
  1378.4 20.0 reduce-scatter.8
  1401.3 19.8 reduce-scatter.10
  1423.5 35.2 reduce-scatter.12
  1461.0 59.7 reduce-scatter.6

commit v6 on v5

--- a/solution.py
+++ b/solution.py
@@ -72,59 +72,33 @@
     return with_layout_constraint(value, Layout(tuple(range(value.ndim))))
 
 
-def row_swap(value, bit):
-    return lax.ppermute(value, "row", [(j, j ^ bit) for j in range(lax.axis_size("row"))])
-
-
 def mate(value):
-    return row_swap(value, lax.axis_size("row") // 2)
-
-
-def half_bits():
-    return [1 << b for b in range((lax.axis_size("row") // 2).bit_length() - 1)]
-
-
-def expert_gather(kept, given, axis, hold):
     count = lax.axis_size("row")
-    index = lax.axis_index("row")
-    width = kept.shape[axis]
-    shape = list(kept.shape)
-    shape[axis] = width * count
-    out = jnp.zeros(shape, kept.dtype)
-    (arrived,) = after((mate(given),), hold)
-    for first, item in ((count // 2, arrived), (0, kept)):
-        items = {first: item}
-        for bit in half_bits():
-            new = after([row_swap(items[key], bit) for key in items], hold)
-            items.update({key ^ bit: piece for key, piece in zip(list(items), new)})
-        for key, piece in items.items():
-            out = lax.dynamic_update_slice_in_dim(
-                out, piece, jnp.bitwise_xor(index, key) * width, axis
-            )
-    return out
-
-
-def expert_scatter(value, axis, holds):
-    count = lax.axis_size("row")
-    index = lax.axis_index("row")
-    width = value.shape[axis] // count
-    sums = []
-    for first, hold in zip((count // 2, 0), holds):
-        items = {
-            key: lax.dynamic_slice_in_dim(
-                value, jnp.bitwise_xor(index, key ^ first) * width, width, axis
-            )
-            for key in range(count // 2)
-        }
-        for bit in half_bits()[::-1]:
-            keys = [key for key in items if key < bit]
-            new = after([row_swap(items[key ^ bit], bit) for key in keys], hold)
-            items = {
-                key: (items[key].astype(F32) + piece.astype(F32)).astype(BF16)
-                for key, piece in zip(keys, new)
-            }
-        sums.append(items[0])
-    return sums[1], sums[0]
+    return lax.ppermute(value, "row", [(j, j ^ (count // 2)) for j in range(count)])
+
+
+def mates():
+    half = lax.axis_size("row") // 2
+    return [[j, j + half] for j in range(half)]
+
+
+def halves():
+    half = lax.axis_size("row") // 2
+    return [list(range(half)), list(range(half, 2 * half))]
+
+
+def mate_exchange(value):
+    return lax.all_to_all(
+        value, "row", split_axis=0, concat_axis=0, axis_index_groups=mates(), tiled=True
+    )
+
+
+def half_gather(value, axis):
+    return lax.all_gather(value, "row", axis=axis, axis_index_groups=halves())
+
+
+def half_sum(value, axis):
+    return lax.psum_scatter(value, "row", scatter_dimension=axis, axis_index_groups=halves())
 
 
 def swap(value, bit):
@@ -175,16 +149,16 @@
     return out
 
 
-def cube_scatter(value):
+def cube_scatter(value, axis=0):
     count = lax.axis_size("col")
     index = lax.axis_index("col")
-    rows = value.shape[0] // count
+    rows = value.shape[axis] // count
     value = row_major(value)
 
     def blocks(device):
         return jnp.stack(
             [
-                lax.dynamic_slice_in_dim(value, block_at(device, place) * rows, rows, 0)
+                lax.dynamic_slice_in_dim(value, block_at(device, place) * rows, rows, axis)
                 for place in range(count // 2)
             ]
         )
@@ -334,47 +308,35 @@
     query_width = w_query.shape[1]
     lat_rows = rows_in // col_count
     w_latent_s = lax.dynamic_slice_in_dim(w_latent, col_index * lat_rows, lat_rows, 0)
-    lat_wide = w_latent.shape[1]
-    first_s = jnp.concatenate(
-        [
-            w_query,
-            w_latent_s.reshape(-1, query_width),
-            jnp.concatenate([attn_gain, ffn_gain, latent_gain]).reshape(-1, query_width),
-        ],
-        axis=0,
-    )
+    parts = [
+        w_query,
+        w_latent_s.reshape(-1, query_width),
+        jnp.concatenate([w_output, w_expand], axis=0).reshape(-1, query_width),
+        jnp.concatenate([attn_gain, ffn_gain, latent_gain]).reshape(-1, query_width),
+    ]
+    first_s = jnp.concatenate(parts, axis=0)
     first_s = jnp.pad(first_s, ((0, -first_s.shape[0] % 16), (0, 0)))
     (first_s,) = after((first_s,), (dealt_x,))
     first_w = row_gather(first_s[None], 0)
-    query_w = first_w[:, :rows_in].reshape(dim, query_width)
-    lat_end = rows_in + lat_rows * lat_wide // query_width
-    latent_w = cube_gather(first_w[:, rows_in:lat_end].reshape(row_count * lat_rows, lat_wide), 0)
-    latent_w = latent_w.reshape(col_count, row_count, lat_rows, lat_wide).transpose(1, 0, 2, 3)
-    latent_w = latent_w.reshape(dim, lat_wide)
-    gains = first_w[:, lat_end:].reshape(row_count, -1)
+    pieces, start = [], 0
+    for part in parts:
+        pieces.append(first_w[:, start : start + part.shape[0]])
+        start += part.shape[0]
+    query_w = pieces[0].reshape(dim, query_width)
+    latent_w = cube_gather(pieces[1].reshape(row_count * lat_rows, w_latent.shape[1]), 0)
+    latent_w = latent_w.reshape(col_count, row_count, lat_rows, -1).transpose(1, 0, 2, 3)
+    latent_w = latent_w.reshape(dim, w_latent.shape[1])
+    out_rows, out_width = w_output.shape
+    rest_w = pieces[2].reshape(row_count, -1, out_width)
+    output_w = rest_w[:, :out_rows].transpose(1, 0, 2).reshape(out_rows, dim)
+    expand_w = rest_w[:, out_rows:].reshape(-1, out_width)
+    gains = pieces[3].reshape(row_count, -1)
     gain_one = gains[:, :wide].reshape(-1).astype(F32)
     gain_two = gains[:, wide : 2 * wide].reshape(-1).astype(F32)
-    latent_g = gains[:, 2 * wide : 2 * wide + latent_gain.shape[0]].reshape(-1).astype(F32)
-
-    out_rows = w_output.shape[0]
-    rest_s = jnp.concatenate([w_output.reshape(-1, w_expand.shape[1]), w_expand])
-    (rest_s,) = after((rest_s,), (dealt_x,))
-    rest_w = row_gather(rest_s[None], 0)
-    out_count = w_output.size // w_expand.shape[1]
-    output_w = rest_w[:, :out_count].reshape(row_count, out_rows, -1)
-    output_w = output_w.transpose(1, 0, 2).reshape(out_rows, dim)
-    expand_w = rest_w[:, out_count:].reshape(-1, w_expand.shape[1])
-
-    def of_expert(value, number):
-        return lax.dynamic_index_in_dim(value, number, 0, False)
-
-    def both_parts(number):
-        return jnp.concatenate([of_expert(expert_gate, number), of_expert(expert_up, number)], 1)
-
-    gate_up_parts = after((both_parts(host), both_parts(1 - host)), (first_w,))
-    down_parts = after(
-        (of_expert(expert_down, host), of_expert(expert_down, 1 - host)), (first_w, rest_w)
-    )
+    latent_g = gains[:, 2 * wide :].reshape(-1).astype(F32)
+
+    (gate_s, up_s, down_s) = after((expert_gate, expert_up, expert_down), (first_w,))
+    gate_s, up_s, down_s = mate_exchange(gate_s), mate_exchange(up_s), mate_exchange(down_s)
 
     head_count = query_w.shape[1] // (NOPE + ROPE)
     softmax_scale = (NOPE + ROPE) ** (-0.5)
@@ -406,7 +368,8 @@
     )
     value_heads = expanded[..., NOPE:]
     dealt_dy = exchange(cotangent_s, out_list, in_slots, (expanded,)) + more[:, slice_width:]
-    full_dy = cube_gather(dealt_dy, 1)
+    (gate_s,) = after((gate_s,), (query_heads,))
+    gate_w = half_gather(gate_s, 1).reshape(dim, -1)
 
     def block_scores(first_row, last_row):
         raw_scores = (
@@ -444,24 +407,25 @@
     mixed = (
         jnp.concatenate(mixed_blocks, axis=0).reshape(group_rows, head_count * VDIM).astype(BF16)
     )
+    mate_dy = mate(dealt_dy)
+    (up_s,) = after((up_s,), (mixed,))
+    up_w = half_gather(up_s, 1).reshape(dim, -1)
     attn_part = cube_scatter(dot(mixed, output_w).astype(BF16))
+    mate_dy, down_s = after((mate_dy, down_s), (attn_part,))
+    both_dy = cube_gather(jnp.stack([dealt_dy, mate_dy]), 2)
+    full_dy = both_dy[0]
+    down_w = half_gather(down_s.transpose(1, 0, 2), 2).reshape(down_s.shape[1], dim)
     x_part = my_part(full_x).astype(F32)
     hidden_part = x_part + attn_part
     scale_two = lax.rsqrt(jnp.mean(hidden_part * hidden_part, axis=-1, keepdims=True) + EPSILON)
     unit_two = hidden_part * scale_two
     normed_part = (unit_two * gain_two).astype(BF16)
-    mate_part = mate(normed_part)
-    normed_two = cube_gather(normed_part, 0)
-    (mate_part,) = after((mate_part,), (normed_two,))
-    mate_two = cube_gather(mate_part, 0)
-    (dealt_mate_dy,) = after((mate(dealt_dy),), (normed_part,))
-    mate_dy = cube_gather(dealt_mate_dy, 1)
-    gate_up_w = expert_gather(*gate_up_parts, 0, (normed_part,))
-    down_w = expert_gather(*down_parts, 1, (normed_part,))
-    shared_gu_s, shared_d_s = after(
+    both_normed = cube_gather(jnp.stack([normed_part, mate(normed_part)]), 1)
+    normed_two = both_normed[0]
+    shared_g_s, shared_d_s = after(
         (jnp.concatenate([shared_gate, shared_up], axis=1), shared_down), (normed_part,)
     )
-    shared_gu_w = row_gather(shared_gu_s, 0)
+    shared_gu_w = row_gather(shared_g_s, 0)
     shared_d_w = row_gather(shared_d_s, 1)
 
     place_late, rank_late, here_late, source_late, my_rank_late = after(
@@ -483,54 +447,63 @@
         return listed, jnp.where(inside, group_of * room + slot, -1)
 
     back_list, back_slots = maps_back(0)
-    gate_up_w, back_list, back_slots = after((gate_up_w, back_list, back_slots), ())
-
-    def forward(rows, gate_up_w):
-        width = gate_up_w.shape[1] // 2
-        gate_up = dot(rows, gate_up_w)
-        gate_out, up_out = gate_up[:, :width], gate_up[:, width:]
+    gate_w, back_list, back_slots = after((gate_w, back_list, back_slots), ())
+
+    def forward(gate_out, up_out):
         act, slope = silu_parts(gate_out)
-        hidden = (act * up_out).astype(BF16)
-        return hidden, act, up_out * slope
+        return (act * up_out).astype(BF16), act, up_out * slope
 
     def backward(grad_hidden, act, up_slope):
-        return jnp.concatenate(
-            [(grad_hidden * up_slope).astype(BF16), (grad_hidden * act).astype(BF16)], axis=1
-        )
-
-    def queued_sum(value, axis):
-        return row_scatter(value.astype(BF16), axis)
-
-    rows = jnp.concatenate(
-        [dot(pick, normed_two).astype(BF16), dot(mate_pick, mate_two).astype(BF16)], axis=0
-    )
-    grad_result = jnp.concatenate(
-        [
-            (weight[:, None] * dot(pick, full_dy)).astype(BF16),
-            (mate_weight[:, None] * dot(mate_pick, mate_dy)).astype(BF16),
-        ],
-        axis=0,
-    )
-    hidden, act, up_slope = forward(rows, gate_up_w)
-    grad_gate_up = backward(dot_nt(grad_result, down_w), act, up_slope)
-    mate_rows = dot_nt(grad_gate_up[capacity:], gate_up_w).astype(BF16)
+        return (grad_hidden * up_slope).astype(BF16), (grad_hidden * act).astype(BF16)
+
+    def picked(values):
+        return lax.dot_general(
+            both_picks, values, (((2,), (1,)), ((0,), (0,))), preferred_element_type=F32
+        )
+
+    both_picks = jnp.stack([pick, mate_pick])
+    weights = jnp.concatenate([weight, mate_weight])[:, None]
+    rows = picked(both_normed).astype(BF16).reshape(2 * capacity, dim)
+    grad_result = (weights * picked(both_dy).reshape(2 * capacity, dim)).astype(BF16)
+    hidden, act, up_slope = forward(dot(rows, gate_w), dot(rows, up_w))
+    grad_gate, grad_up = backward(dot_nt(grad_result, down_w), act, up_slope)
+
+    def row_grads(gate_part, up_part):
+        return (dot_nt(gate_part, gate_w) + dot_nt(up_part, up_w)).astype(BF16)
+
+    mate_rows = row_grads(grad_gate[capacity:], grad_up[capacity:])
     mate_grad = dot_tn(mate_pick, mate_rows).astype(BF16)
     mate_grad_part = mate(cube_scatter(mate_grad).astype(BF16))
-    own_gate_up, normed_s, dy_s = after(
-        (grad_gate_up[:capacity], normed_two, full_dy), (mate_grad,)
-    )
-    own_rows = dot_nt(own_gate_up, gate_up_w).astype(BF16)
-    shared_hidden, shared_act, shared_us = forward(normed_s, shared_gu_w)
-    grad_shared_gu = backward(dot_nt(dy_s, shared_d_w), shared_act, shared_us)
+    own_gate, own_up, normed_s, dy_s = after(
+        (grad_gate[:capacity], grad_up[:capacity], normed_two, full_dy), (mate_grad,)
+    )
+    own_rows = row_grads(own_gate, own_up)
+    shared_width = shared_gate.shape[1]
+    shared_out = dot(normed_s, shared_gu_w)
+    shared_hidden, shared_act, shared_us = forward(
+        shared_out[:, :shared_width], shared_out[:, shared_width:]
+    )
+    grad_shared_gu = jnp.concatenate(
+        backward(dot_nt(dy_s, shared_d_w), shared_act, shared_us), axis=1
+    )
     grad_two = dot_nt(grad_shared_gu, shared_gu_w)
     grad_two = (grad_two + dot_tn(pick, own_rows)).astype(BF16)
     grad_two_part = cube_scatter(grad_two)
-    late = after((rows, grad_gate_up, hidden, grad_result), (grad_two,))
-    grad_gu = dot_tn(late[0], late[1]).astype(BF16)
-    grad_down = dot_tn(late[2], late[3]).astype(BF16)
+
+    def row_sum(value, axis):
+        return row_scatter(value.astype(BF16), axis)
+
+    def half_rows(value, axis):
+        shape = value.shape[:axis] + (2, row_count // 2, -1) + value.shape[axis + 1 :]
+        return half_sum(value.astype(BF16).reshape(shape), axis + 1)
+
+    late_rows, late_result, late_hidden = after((rows, grad_result, hidden), (grad_two,))
+    sum_down = half_rows(dot_tn(late_hidden, late_result), 1).transpose(1, 0, 2)
+    sum_gate = half_rows(dot_tn(late_rows, grad_gate), 0)
+    sum_up = half_rows(dot_tn(late_rows, grad_up), 0)
     late = after((normed_two, grad_shared_gu, shared_hidden, full_dy), (grad_two,))
-    grad_sgu = queued_sum(dot_tn(late[0], late[1]), 0)
-    grad_sd = queued_sum(dot_tn(late[2], late[3]), 1)
+    grad_sgu = row_sum(dot_tn(late[0], late[1]), 0)
+    grad_sd = row_sum(dot_tn(late[2], late[3]), 1)
 
     (mate_grad_part,) = after((mate_grad_part,), (grad_two_part,))
     grad_two_part = grad_two_part + mate_grad_part.astype(F32)
@@ -540,15 +513,16 @@
     grad_attn = cube_gather(grad_hidden_part.astype(BF16), 0)
 
     hidden_late, shared_late = after((hidden, shared_hidden), (grad_hidden_part,))
-    weights = jnp.concatenate([weight, mate_weight])
-    result_rows = (weights[:, None] * dot(hidden_late, down_w)).astype(BF16)
-    mate_terms = dot_tn(mate_pick, result_rows[capacity:]).astype(BF16)
+    result_rows = (weights * dot(hidden_late, down_w)).astype(BF16)
+    mate_terms = dot_tn(mate_pick, result_rows[capacity:])
     moe_terms = dot(shared_late, shared_d_w) + dot_tn(pick, result_rows[:capacity])
-    mate_terms, moe_terms = after((mate_terms, moe_terms.astype(BF16)), (grad_attn,))
-    mate_terms = mate(cube_scatter(mate_terms).astype(BF16))
-    moe_part = cube_scatter(moe_terms)
-
-    grad_output_w = queued_sum(dot_tn(mixed, grad_attn), 1)
+    (both_terms,) = after((jnp.stack([moe_terms.astype(BF16), mate_terms.astype(BF16)]),), (grad_attn,))
+    both_terms = cube_scatter(both_terms, 1)
+    moe_part, mate_terms = both_terms[0], mate(both_terms[1].astype(BF16))
+    sum_down, sum_gate = after((sum_down, sum_gate), (grad_attn,))
+    grad_down, grad_gate = mate_exchange(sum_down), mate_exchange(sum_gate)
+
+    grad_output_w = row_sum(dot_tn(mixed, grad_attn), 1)
     grad_mixed = dot_nt(grad_attn, output_w).astype(BF16)
     grad_mixed = grad_mixed.reshape(group_rows, head_count, VDIM)
     grad_query_blocks = []
@@ -598,8 +572,8 @@
     result_slice = lax.all_to_all(result_part, "col", split_axis=1, concat_axis=0, tiled=True)
 
     grad_one = cube_scatter(grad_one)
-    own_gu, mate_gu = expert_scatter(grad_gu, 0, ((grad_attn,), (grad_one,)))
-    own_down, mate_down = expert_scatter(grad_down, 1, ((grad_attn,), (grad_one,)))
+    (sum_up,) = after((sum_up,), (grad_one,))
+    grad_up = mate_exchange(sum_up)
     grad_expanded = jnp.concatenate([grad_keys[..., :NOPE], grad_values], axis=-1).astype(BF16)
     grad_expanded = grad_expanded.reshape(group_rows, head_count * (NOPE + VDIM))
     grad_compressed = dot_nt(grad_expanded, expand_w)
@@ -635,20 +609,14 @@
     )[1]
     result, tokens_grad = more[:, :slice_width], more[:, slice_width:]
 
-    grad_expand_w = queued_sum(dot_tn(compressed, grad_expanded), 0)
-    grad_query_w = queued_sum(dot_tn(normed_one, grad_query_raw), 0)
+    grad_expand_w = row_sum(dot_tn(compressed, grad_expanded), 0)
+    grad_query_w = row_sum(dot_tn(normed_one, grad_query_raw), 0)
     grad_latent = cube_gather(grad_latent_part, 0)
     my_columns = lax.dynamic_index_in_dim(
         normed_one.reshape(group_rows, row_count, col_count, lat_rows), col_index, 2, False
     ).reshape(group_rows, row_count * lat_rows)
-    grad_latent_w = cube_gather(queued_sum(dot_tn(my_columns, grad_latent), 0), 0)
+    grad_latent_w = cube_gather(row_sum(dot_tn(my_columns, grad_latent), 0), 0)
     gain_grads = small_sum(jnp.concatenate([gain_one_grad, gain_two_grad, latent_gain_grad]))
-    width_ff = expert_gate.shape[2]
-    other_gu, other_down = after((mate(mate_gu), mate(mate_down)), (grad_input,))
-
-    def in_order(own, other):
-        return jnp.stack([jnp.where(host == 0, own, other), jnp.where(host == 0, other, own)])
-
     width_two = gain_one_grad.shape[0]
     width_lat = latent_gain_grad.shape[0]
 
@@ -669,9 +637,9 @@
         grad_sgu[:, : shared_gate.shape[1]].astype(F32),
         grad_sgu[:, shared_gate.shape[1] :].astype(F32),
         grad_sd.astype(F32),
-        in_order(own_gu[:, :width_ff], other_gu[:, :width_ff]).astype(F32),
-        in_order(own_gu[:, width_ff:], other_gu[:, width_ff:]).astype(F32),
-        in_order(own_down, other_down).astype(F32),
+        grad_gate.astype(F32),
+        grad_up.astype(F32),
+        grad_down.astype(F32),
     )
 
 

time: 1950 us -> 1990 us (1.021)
  matrix products: 437 us -> 483 us
  other arithmetic: 273 us -> 250 us
    all_to_all x0 -> x6, waiting for transfers between devices: none -> 348 us  [mate_exchange(): lax.all_to_all(value, 'row', split_axis=0, concat_axis=0, axis_index_grou...]
    ppermute x18 -> x6, waiting for transfers between devices: 459 us -> 206 us  [mate(): lax.ppermute(value, 'row', [(j, j ^ count // 2) for j in range(count)])]
    ppermute x3, waiting for transfers between devices: 130 us -> 0.01 us  [small_sum(): lax.ppermute(value, 'row', [(j, (j + k) % count) for j in range(count)])]
    dot_general x0 -> x2, matrix products: none -> 45 us  [picked(): lax.dot_general(both_picks, values, (((2,), (1,)), ((0,), (0,))), preferr...]
    concatenate x10 -> x4, other arithmetic: 42.8 us -> 2.8 us  [the longest x1 1.78 us: body(): jnp.concatenate(backward(dot_nt(dy_s, shared_d_w), shared_act, shared_us)...]
    all_to_all x0 -> x6, starting transfers between devices: none -> 27.4 us  [mate_exchange(): lax.all_to_all(value, 'row', split_axis=0, concat_axis=0, axis_index_grou...]
    reshape x2 -> x8, local copies, waits for them, and re-layouts: 2.8 us -> 29.6 us  [the longest x4 22.6 us: half_rows(): return half_sum(value.astype(BF16).reshape(shape), axis + 1)]
    all_gather x4 -> x3, waiting for transfers between devices: 46 us -> 20.7 us  [row_gather(): return lax.all_gather(shard, 'row', axis=axis, tiled=True)]
  transfers between devices with their start and end apart: 106 -> 92, of which waited for: 36 -> 31; matrix products, arithmetic and copies ran while one was open for 43% -> 45% of each run, Pallas kernels for 0% -> 0%
where the time goes in v6:
time: 1990 us; the launch traced here: 1980 us
  waiting for transfers between devices  816 us (41%)
  matrix products  483 us (24%)
  local copies, waits for them, and re-layouts  295 us (15%)
  other arithmetic  250 us (13%)
  starting transfers between devices  111 us (6%)
    all_to_all x6, waiting for transfers between devices, mate_exchange(): lax.all_to_all(value, 'row', split_axis=0, concat_axis=0, axis_index_grou...  348 us
    ppermute x6, waiting for transfers between devices, mate(): lax.ppermute(value, 'row', [(j, j ^ count // 2) for j in range(count)])  206 us
    dot_general x17, matrix products, dot(): return jnp.dot(left, right, preferred_element_type=F32)  153 us
    dot_general x13, matrix products, dot_tn(): lax.dot_general(left, right, (((0,), (0,)), ((), ())), preferred_element_...  150 us
    ppermute x26, waiting for transfers between devices, chip_swap(): lax.ppermute(value, 'col', [(j, j ^ (other if j % 2 else bits)[step]) for...  147 us
    dot_general x10, matrix products, dot_nt(): lax.dot_general(left, right, (((1,), (1,)), ((), ())), preferred_element_...  88.1 us
    dynamic_update_slice x51, local copies, waits for them, and re-layouts, cube_gather(): lax.dynamic_update_slice_in_dim(out, item, block_at(owner, place) * width...  82.1 us
    all_to_all x4, waiting for transfers between devices, exchange(): got = lax.all_to_all(sent, 'row', split_axis=0, concat_axis=0, tiled=True)  71.3 us
  transfers between devices with their start and end apart: 92, of which 31 were waited for; matrix products, arithmetic and copies ran while one was open for 45% of the time, Pallas kernels for 0%

profile of v6, /device:TPU:0, one launch (start us, length us, event | category | flops | bytes accessed | tf_op | source)
XLA Modules:
  0.0 1980.5 jit_solution(3794830858430509899)
XLA Ops:
  34.8 24.6 %all-to-all-done.2 = bf16[4,640,256]{2,1,0:T(8,128)(2,1)S(1)} async-done(((bf16[4,640,256]{2,1,0:T(8,128)(2,1)}), bf16[4,640,256]{2,1,0:T(8,128)(2,1)S(1)}, u32[]{:S(2)}, u32[]{:S(2)}) %all-to-all-start.2) | async-done | bytes 1310752 | tf_op jit(solution)/shard_map/all_to_all | solution.py:207
  82.0 11.1 collective-permute-done.1
  105.2 17.0 collective-permute-done.3
  125.7 20.7 %all-gather.15.cloned.1.call-done = bf16[4544,384]{1,0:T(8,128)(2,1)} async-done(((bf16[1136,384]{1,0:T(8,128)(2,1)}), bf16[4544,384]{1,0:T(8,128)(2,1)}) %all-gather.15.cloned.1.call-update) | async-done | bytes 3489808 | tf_op jit(solution)/shard_map/all_gather | solution.py:177
  217.1 9.9 fusion.258
  255.4 47.0 %all-to-all-done.3 = bf16[2,512,1408]{2,1,0:T(8,128)(2,1)S(1)} async-done(((bf16[2,512,1408]{2,1,0:T(8,128)(2,1)}), bf16[2,512,1408]{2,1,0:T(8,128)(2,1)S(1)}, u32[]{:S(2)}, u32[]{:S(2)}) %all-to-all-start.3) | async-done | bytes 2883616 | tf_op jit(solution)/shard_map/all_to_all | solution.py:91
  329.6 32.6 %all-to-all-done.5 = bf16[4,640,256]{2,1,0:T(8,128)(2,1)} async-done(((bf16[4,640,256]{2,1,0:T(8,128)(2,1)}), bf16[4,640,256]{2,1,0:T(8,128)(2,1)}, u32[]{:S(2)}, u32[]{:S(2)}) %all-to-all-start.5) | async-done | bytes 1310752 | tf_op jit(solution)/shard_map/all_to_all | solution.py:207
  381.7 75.2 %all-to-all-done.6 = bf16[2,1408,512]{1,2,0:T(8,128)(2,1)} async-done(((bf16[2,1408,512]{1,2,0:T(8,128)(2,1)}), bf16[2,1408,512]{1,2,0:T(8,128)(2,1)}, u32[]{:S(2)}, u32[]{:S(2)}) %all-to-all-start.6) | async-done | bytes 2883616 | tf_op jit(solution)/shard_map/all_to_all | solution.py:91
  456.9 21.3 %collective-permute-done.21 = bf16[2048,256]{1,0:T(8,128)(2,1)} collective-permute-done((bf16[2048,256]{1,0:T(8,128)(2,1)}, bf16[2048,256]{1,0:T(8,128)(2,1)}, u32[]{:S(2)}, u32[]{:S(2)}) %collective-permute-start.21) | collective-permute-done | bytes 1048608 | tf_op jit(solution)/shard_map/ppermute | solution.py:77
  502.8 60.3 %collective-permute-done.13 = s32[2048,6]{0,1:T(8,128)S(1)} collective-permute-done((s32[2048,6]{0,1:T(8,128)S(1)}, s32[2048,6]{0,1:T(8,128)S(1)}, u32[]{:S(2)}, u32[]{:S(2)}) %collective-permute-start.13) | collective-permute-done | bytes 49184 | tf_op jit(solution)/shard_map/ppermute | solution.py:77
  592.4 30.1 %collective-permute-done.23 = bf16[1,2,2048,256]{3,2,1,0:T(8,128)(2,1)} collective-permute-done((bf16[1,2,2048,256]{3,2,1,0:T(8,128)(2,1)S(1)}, bf16[1,2,2048,256]{3,2,1,0:T(8,128)(2,1)}, u32[]{:S(2)}, u32[]{:S(2)}) %collective-permute-start.23) | collective-permute-done | bytes 2097184 | tf_op jit(solution)/shard_map/ppermute | solution.py:115
  640.2 19.3 collective-permute-done.12
  664.0 23.2 %select_reduce_fusion.2 = (s32[2048]{0:T(1024)S(1)}, s32[2048]{0:T(1024)S(1)}) fusion(s32[4,2048]{1,0:T(4,128)S(1)} %copy-done.96, pred[4,2048]{1,0:T(4,128)(4,1)S(1)} %copy-done.162, s32[4,2048]{1,0:T(4,128)S(1)} %copy-done.79), kind=kLoop, calls=%fused_computation.32 | loop fusion | flops 100659200 | bytes 90112 | tf_op jit(solution)/shard_map/reduce_sum | solution.py:437
  688.5 67.4 %collective-permute-done.14 = bf16[256,2048]{1,0:T(8,128)(2,1)} collective-permute-done((bf16[256,2048]{1,0:T(8,128)(2,1)}, bf16[256,2048]{1,0:T(8,128)(2,1)}, u32[]{:S(2)}, u32[]{:S(2)}) %collective-permute-start.14) | collective-permute-done | bytes 1048608 | tf_op jit(solution)/shard_map/ppermute | solution.py:77
  774.4 16.9 collective-permute-done.16
  810.6 23.1 %multiply_convert_fusion.1 = (bf16[2,1024,2048]{2,1,0:T(8,128)(2,1)}, f32[2,1024,2048]{2,1,0:T(8,128)}) fusion(f32[2,1024]{1,0:T(2,128)S(1)} %mul.691, bf16[2,2048,2048]{2,1,0:T(8,128)(2,1)} %fusion.118, pred[1,1024,2048]{2,1,0:T(32,128)(4,1)S(1)} %copy-done.46, pred[1,1024,2048]{2,1,0:T(32,128)(4,1)S(1)} %copy-done.47), kind=kOutput, calls=%fused_computation.63 | convolution fusion | flops 17192452096 | bytes 46145536 | tf_op jit(solution)/shard_map/dot_general | solution.py:460
  841.9 18.6 fusion.260
  860.5 10.8 fusion.243
  895.8 21.9 %convolution_convert_fusion.5 = bf16[2,1024,2048]{2,1,0:T(8,128)(2,1)} fusion(bf16[2,2048,2048]{2,1,0:T(8,128)(2,1)} %fusion.122, pred[1,1024,2048]{2,1,0:T(32,128)(4,1)S(1)} %copy-done.46, pred[1,1024,2048]{2,1,0:T(32,128)(4,1)S(1)} %copy-done.48), kind=kOutput, calls=%fused_computation.122 | convolution fusion | flops 17188257792 | bytes 29360128 | tf_op jit(solution)/shard_map/dot_general | solution.py:460
  917.7 16.9 fusion.259
  934.6 29.7 %multiply_convert_fusion.4 = (bf16[2048,1408]{1,0:T(8,128)(2,1)}, bf16[2048,1408]{1,0:T(8,128)(2,1)}, bf16[2048,1408]{1,0:T(8,128)(2,1)}) fusion(f32[2048,1408]{1,0:T(8,128)} %fusion.259, f32[2048,1408]{1,0:T(8,128)} %fusion.260, bf16[2048,2048]{1,0:T(8,128)(2,1)} %bitcast.658, bf16[2048,1408]{1,0:T(8,128)(2,1)} %bitcast.653), kind=kOutput, calls=%fused_computation.67 | convolution fusion | flops 11854413824 | bytes 54525952 | tf_op jit(solution)/shard_map/dot_general | solution.py:60
  964.3 11.9 fusion.83
  986.8 10.9 add_convert_fusion.27
  997.7 11.8 fusion.47
  1018.5 22.7 %fusion.46 = f32[2048,2048]{1,0:T(8,128)} fusion(f32[1024,2048]{1,0:T(8,128)} %fusion.262, bf16[1024,1408]{1,0:T(8,128)(2,1)S(1)} %slice.841, bf16[2048,1408]{1,0:T(8,128)(2,1)} %bitcast.655, pred[1024,2048]{1,0:T(32,128)(4,1)} %iota_compare_fusion.81), kind=kOutput, calls=%fused_computation.100 | convolution fusion | flops 14499708928 | bytes 35913728 | tf_op jit(solution)/shard_map/dot_general | solution.py:68
  1041.2 11.3 fusion.261
  1052.6 10.8 multiply_convert_fusion.10
  1063.5 13.4 add_convert_fusion.2
  1076.9 15.5 convolution_convert_fusion.2
  1095.5 17.6 convolution_convert_fusion.3
  1134.7 16.7 convolution_convert_fusion.4
  1151.4 10.5 reshape.1356
  1180.9 18.2 collective-permute-done.31
  1203.3 12.0 copy.356
  1215.4 17.4 collective-permute-done.28
  1247.9 39.1 %collective-permute-done.33 = bf16[256,2048]{1,0:T(8,128)(2,1)} collective-permute-done((bf16[256,2048]{1,0:T(8,128)(2,1)}, bf16[256,2048]{1,0:T(8,128)(2,1)}, u32[]{:S(2)}, u32[]{:S(2)}) %collective-permute-start.33) | collective-permute-done | bytes 1048608 | tf_op jit(solution)/shard_map/ppermute | solution.py:77
  1312.6 17.2 multiply_convert_fusion
  1333.1 11.7 fusion.45
  1396.1 13.3 convert_bitcast_fusion
  1414.2 14.5 fusion.40
  1482.4 10.9 convolution_convert_fusion.6
  1538.9 80.7 %all-to-all-done.12 = bf16[2,512,1408]{2,1,0:T(8,128)(2,1)S(1)} async-done(((bf16[2,512,1408]{2,1,0:T(8,128)(2,1)}), bf16[2,512,1408]{2,1,0:T(8,128)(2,1)S(1)}, u32[]{:S(2)}, u32[]{:S(2)}) %all-to-all-start.12) | async-done | bytes 2883616 | tf_op jit(solution)/shard_map/all_to_all | solution.py:91
  1654.6 59.7 %all-to-all-done.11 = bf16[2,512,1408]{2,1,0:T(8,128)(2,1)} async-done(((bf16[2,512,1408]{2,1,0:T(8,128)(2,1)}), bf16[2,512,1408]{2,1,0:T(8,128)(2,1)}, u32[]{:S(2)}, u32[]{:S(2)}) %all-to-all-start.11) | async-done | bytes 2883616 | tf_op jit(solution)/shard_map/all_to_all | solution.py:91
  1719.7 9.5 convolution_convert_fusion.9
  1744.2 85.0 %all-to-all-done.13 = bf16[2,1408,512]{2,1,0:T(8,128)(2,1)} async-done(((bf16[2,1408,512]{2,1,0:T(8,128)(2,1)}), bf16[2,1408,512]{2,1,0:T(8,128)(2,1)}, u32[]{:S(2)}, u32[]{:S(2)}) %all-to-all-start.13) | async-done | bytes 2883616 | tf_op jit(solution)/shard_map/all_to_all | solution.py:91
  1835.3 16.3 collective-permute-done.42
  1864.8 9.2 all-to-all-done.7
  1950.9 14.1 all-to-all-done.8
  (940 shorter events, 782.3 us)
Async XLA Ops:
  28.0 118.3 %all-gather.15.cloned.1.call-start = ((), (), s32[]{:S(2)}) async-start(), calls=%async_computation.34 | async-start | bytes 4362240 | tf_op jit(solution)/shard_map/all_gather | solution.py:177
  122.2 46.6 %collective-permute-start.4 = (bf16[2,2048,256]{2,1,0:T(8,128)(2,1)}, bf16[2,2048,256]{2,1,0:T(8,128)(2,1)}, u32[]{:S(2)}, u32[]{:S(2)}) collective-permute-start(bf16[2,2048,256]{2,1,0:T(8,128)(2,1)} %collective-permute-done.3), channel_id=1, source_target_pairs={{0,1},{1,0},{2,3},{3,2},{4,5},{5,4},{6,7},{7,6},{8,9},{9,8},{10,11... | collective-permute-start | bytes 6291464 | tf_op jit(solution)/shard_map/ppermute | solution.py:105
  148.8 58.0 %collective-permute-start.5 = (bf16[1,256,576]{2,1,0:T(8,128)(2,1)S(1)}, bf16[1,256,576]{2,1,0:T(8,128)(2,1)}, u32[]{:S(2)}, u32[]{:S(2)}) collective-permute-start(bf16[1,256,576]{2,1,0:T(8,128)(2,1)S(1)} %broadcast_in_dim.231), channel_id=1, source_target_pairs={{0,1},{1,0},{2,3},{3,2},{4,5},{5,4},{6,7},{7,6},{8,9},{9,8},{10,11... | collective-permute-start | bytes 884744 | tf_op jit(solution)/shard_map/ppermute | solution.py:105
  148.9 45.7 %collective-permute-start.6 = (bf16[1,256,576]{2,1,0:T(8,128)(2,1)S(1)}, bf16[1,256,576]{2,1,0:T(8,128)(2,1)S(1)}, u32[]{:S(2)}, u32[]{:S(2)}) collective-permute-start(bf16[1,256,576]{2,1,0:T(8,128)(2,1)S(1)} %broadcast_in_dim.231), channel_id=1, source_target_pairs={{0,2},{1,5},{2,0},{3,7},{4,6},{5,1},{6,4},{7,3},{8,10},{9,13},{10,... | collective-permute-start | bytes 884744 | tf_op jit(solution)/shard_map/ppermute | solution.py:115
  234.3 68.1 %all-to-all-start.3 = ((bf16[2,512,1408]{2,1,0:T(8,128)(2,1)}), bf16[2,512,1408]{2,1,0:T(8,128)(2,1)S(1)}, u32[]{:S(2)}, u32[]{:S(2)}) async-start(bf16[2,512,1408]{2,1,0:T(8,128)(2,1)} %param.59), calls=%async_computation.3 | async-start | bytes 5767168 | tf_op jit(solution)/shard_map/all_to_all | solution.py:91
  238.2 532.8 %all-gather.17.cloned.1.call-start = ((), (), s32[]{:S(2)}) async-start(), calls=%async_computation.35 | async-start | bytes 8650752 | tf_op jit(solution)/shard_map/all_gather | solution.py:97
  314.5 47.7 %all-to-all-start.5 = ((bf16[4,640,256]{2,1,0:T(8,128)(2,1)}), bf16[4,640,256]{2,1,0:T(8,128)(2,1)}, u32[]{:S(2)}, u32[]{:S(2)}) async-start(bf16[4,640,256]{2,1,0:T(8,128)(2,1)} %bitcast.75), calls=%async_computation.5 | async-start | bytes 2621440 | tf_op jit(solution)/shard_map/all_to_all | solution.py:207
  362.2 94.7 %all-to-all-start.6 = ((bf16[2,1408,512]{1,2,0:T(8,128)(2,1)}), bf16[2,1408,512]{1,2,0:T(8,128)(2,1)}, u32[]{:S(2)}, u32[]{:S(2)}) async-start(bf16[2,1408,512]{1,2,0:T(8,128)(2,1)} %copy.331), calls=%async_computation.6 | async-start | bytes 5767168 | tf_op jit(solution)/shard_map/all_to_all | solution.py:91
  367.4 474.6 %all-gather.21.cloned.1.call-start = ((), (), s32[]{:S(2)}) async-start(), calls=%async_computation.37 | async-start | bytes 8650752 | tf_op jit(solution)/shard_map/all_gather | solution.py:97
  375.5 102.7 %collective-permute-start.21 = (bf16[2048,256]{1,0:T(8,128)(2,1)}, bf16[2048,256]{1,0:T(8,128)(2,1)}, u32[]{:S(2)}, u32[]{:S(2)}) collective-permute-start(bf16[2048,256]{1,0:T(8,128)(2,1)} %fusion.108), channel_id=1, source_target_pairs={{0,16},{8,24},{16,0},{24,8},{1,17},{9,25},{17,1},{25,9},{2,18},{10... | collective-permute-start | bytes 3145736 | tf_op jit(solution)/shard_map/ppermute | solution.py:77
  489.8 90.3 %collective-permute-start.10 = (bf16[4,256,2048]{2,1,0:T(8,128)(2,1)}, bf16[4,256,2048]{2,1,0:T(8,128)(2,1)}, u32[]{:S(2)}, u32[]{:S(2)}) collective-permute-start(bf16[4,256,2048]{2,1,0:T(8,128)(2,1)} %pad_maximum_fusion.2), channel_id=1, source_target_pairs={{0,1},{1,0},{2,3},{3,2},{4,5},{5,4},{6,7},{7,6},{8,9},{9,8},{10,11... | collective-permute-start | bytes 12582920 | tf_op jit(solution)/shard_map/ppermute | solution.py:105
  489.8 78.4 %all-to-all-start.4 = ((bf16[2,512,1408]{2,1,0:T(8,128)(2,1)}), bf16[2,512,1408]{2,1,0:T(8,128)(2,1)S(1)}, u32[]{:S(2)}, u32[]{:S(2)}) async-start(bf16[2,512,1408]{2,1,0:T(8,128)(2,1)} %param.60), calls=%async_computation.4 | async-start | bytes 5767168 | tf_op jit(solution)/shard_map/all_to_all | solution.py:91
  493.9 440.7 %all-gather.19.cloned.1.call-start = ((), (), s32[]{:S(2)}) async-start(), calls=%async_computation.36 | async-start | bytes 8650752 | tf_op jit(solution)/shard_map/all_gather | solution.py:97
  496.1 67.1 %collective-permute-start.13 = (s32[2048,6]{0,1:T(8,128)S(1)}, s32[2048,6]{0,1:T(8,128)S(1)}, u32[]{:S(2)}, u32[]{:S(2)}) collective-permute-start(s32[2048,6]{0,1:T(8,128)S(1)} %copy-done.131), channel_id=1, source_target_pairs={{0,16},{8,24},{16,0},{24,8},{1,17},{9,25},{17,1},{25,9},{2,18},{10... | collective-permute-start | bytes 147464 | tf_op jit(solution)/shard_map/ppermute | solution.py:77
  499.0 66.2 %collective-permute-start.20 = (f32[2048,6]{0,1:T(8,128)S(1)}, f32[2048,6]{0,1:T(8,128)S(1)}, u32[]{:S(2)}, u32[]{:S(2)}) collective-permute-start(f32[2048,6]{0,1:T(8,128)S(1)} %copy-done.132), channel_id=1, source_target_pairs={{0,16},{8,24},{16,0},{24,8},{1,17},{9,25},{17,1},{25,9},{2,18},{10... | collective-permute-start | bytes 147464 | tf_op jit(solution)/shard_map/ppermute | solution.py:77
  569.8 471.4 %all-gather.11.cloned.1.call-start = ((), (), s32[]{:S(2)}) async-start(), calls=%async_computation.23 | async-start | bytes 3604480 | tf_op jit(solution)/shard_map/all_gather | solution.py:177
  580.0 47.7 %collective-permute-start.22 = (bf16[1,2,2048,256]{3,2,1,0:T(8,128)(2,1)S(1)}, bf16[1,2,2048,256]{3,2,1,0:T(8,128)(2,1)}, u32[]{:S(2)}, u32[]{:S(2)}) collective-permute-start(bf16[1,2,2048,256]{3,2,1,0:T(8,128)(2,1)S(1)} %get-tuple-element.613), channel_id=1, source_target_pairs={{0,1},{1,0},{2,3},{3,2},{4,5},{5,4},{6,7},{7,6},{8,9},{9,8},{10,11... | collective-permute-start | bytes 6291464 | tf_op jit(solution)/shard_map/ppermute | solution.py:105
  585.0 45.9 %collective-permute-start.11 = (bf16[2,256,2048]{2,1,0:T(8,128)(2,1)}, bf16[2,256,2048]{2,1,0:T(8,128)(2,1)}, u32[]{:S(2)}, u32[]{:S(2)}) collective-permute-start(bf16[2,256,2048]{2,1,0:T(8,128)(2,1)} %slice.824), channel_id=1, source_target_pairs={{0,4},{1,3},{2,6},{3,1},{4,0},{5,7},{6,2},{7,5},{8,12},{9,11},{10,... | collective-permute-start | bytes 6291464 | tf_op jit(solution)/shard_map/ppermute | solution.py:115
  626.5 61.0 %collective-permute-start.25 = (bf16[2,2,2048,256]{3,2,1,0:T(8,128)(2,1)}, bf16[2,2,2048,256]{3,2,1,0:T(8,128)(2,1)}, u32[]{:S(2)}, u32[]{:S(2)}) collective-permute-start(bf16[2,2,2048,256]{3,2,1,0:T(8,128)(2,1)} %pad_maximum_fusion.4), channel_id=1, source_target_pairs={{0,4},{1,3},{2,6},{3,1},{4,0},{5,7},{6,2},{7,5},{8,12},{9,11},{10,... | collective-permute-start | bytes 12582920 | tf_op jit(solution)/shard_map/ppermute | solution.py:115
  662.8 93.1 %collective-permute-start.14 = (bf16[256,2048]{1,0:T(8,128)(2,1)}, bf16[256,2048]{1,0:T(8,128)(2,1)}, u32[]{:S(2)}, u32[]{:S(2)}) collective-permute-start(bf16[256,2048]{1,0:T(8,128)(2,1)} %multiply_convert_fusion.13), channel_id=1, source_target_pairs={{0,16},{8,24},{16,0},{24,8},{1,17},{9,25},{17,1},{25,9},{2,18},{10... | collective-permute-start | bytes 3145736 | tf_op jit(solution)/shard_map/ppermute | solution.py:77
  663.5 389.1 %all-gather.13.cloned.1.call-start = ((), (), s32[]{:S(2)}) async-start(), calls=%async_computation.24 | async-start | bytes 1802240 | tf_op jit(solution)/shard_map/all_gather | solution.py:177
  687.5 113.4 %collective-permute-start.26 = (bf16[2,2,2048,256]{3,2,1,0:T(8,128)(2,1)}, bf16[2,2,2048,256]{3,2,1,0:T(8,128)(2,1)}, u32[]{:S(2)}, u32[]{:S(2)}) collective-permute-start(bf16[2,2,2048,256]{3,2,1,0:T(8,128)(2,1)} %collective-permute-done.25), channel_id=1, source_target_pairs={{0,1},{1,0},{2,3},{3,2},{4,5},{5,4},{6,7},{7,6},{8,9},{9,8},{10,11... | collective-permute-start | bytes 12582920 | tf_op jit(solution)/shard_map/ppermute | solution.py:105
  771.1 742.1 %reduce-scatter.26.cloned.1.call-start = ((), (), s32[]{:S(2)}) async-start(), calls=%async_computation.33 | async-start | bytes 8650752 | tf_op jit(solution)/shard_map/reduce_scatter | solution.py:101
  793.3 48.7 %collective-permute-start.18 = (bf16[2,2,256,2048]{3,2,1,0:T(8,128)(2,1)S(1)}, bf16[2,2,256,2048]{3,2,1,0:T(8,128)(2,1)}, u32[]{:S(2)}, u32[]{:S(2)}) collective-permute-start(bf16[2,2,256,2048]{3,2,1,0:T(8,128)(2,1)S(1)} %pad_maximum_fusion.3), channel_id=1, source_target_pairs={{0,4},{1,3},{2,6},{3,1},{4,0},{5,7},{6,2},{7,5},{8,12},{9,11},{10,... | collective-permute-start | bytes 12582920 | tf_op jit(solution)/shard_map/ppermute | solution.py:115
  794.6 85.1 %collective-permute-start.17 = (bf16[1,2,256,2048]{3,2,1,0:T(8,128)(2,1)}, bf16[1,2,256,2048]{3,2,1,0:T(8,128)(2,1)}, u32[]{:S(2)}, u32[]{:S(2)}) collective-permute-start(bf16[1,2,256,2048]{3,2,1,0:T(8,128)(2,1)} %collective-permute-done.16), channel_id=1, source_target_pairs={{0,1},{1,0},{2,3},{3,2},{4,5},{5,4},{6,7},{7,6},{8,9},{9,8},{10,11... | collective-permute-start | bytes 6291464 | tf_op jit(solution)/shard_map/ppermute | solution.py:105
  1095.4 434.4 %reduce-scatter.24.cloned.1.call-start = ((), (), s32[]{:S(2)}) async-start(), calls=%async_computation.32 | async-start | bytes 8650752 | tf_op jit(solution)/shard_map/reduce_scatter | solution.py:101
  1116.1 413.8 %reduce-scatter.22.cloned.1.call-start = ((), (), s32[]{:S(2)}) async-start(), calls=%async_computation.31 | async-start | bytes 8650752 | tf_op jit(solution)/shard_map/reduce_scatter | solution.py:101
  1124.6 49.7 %collective-permute-start.27 = (bf16[4,256,2048]{2,1,0:T(8,128)(2,1)}, bf16[4,256,2048]{2,1,0:T(8,128)(2,1)}, u32[]{:S(2)}, u32[]{:S(2)}) collective-permute-start(bf16[4,256,2048]{2,1,0:T(8,128)(2,1)} %pad_maximum_fusion.5), channel_id=1, source_target_pairs={{0,1},{1,0},{2,3},{3,2},{4,5},{5,4},{6,7},{7,6},{8,9},{9,8},{10,11... | collective-permute-start | bytes 12582920 | tf_op jit(solution)/shard_map/ppermute | solution.py:105
  1168.1 484.6 %reduce-scatter.20.cloned.1.call-start = ((), (), s32[]{:S(2)}) async-start(), calls=%async_computation.30 | async-start | bytes 1802240 | tf_op jit(solution)/shard_map/reduce_scatter | solution.py:186
  1179.6 53.2 %collective-permute-start.28 = (bf16[2,256,2048]{2,1,0:T(8,128)(2,1)}, bf16[2,256,2048]{2,1,0:T(8,128)(2,1)S(1)}, u32[]{:S(2)}, u32[]{:S(2)}) collective-permute-start(bf16[2,256,2048]{2,1,0:T(8,128)(2,1)} %slice.849), channel_id=1, source_target_pairs={{0,4},{1,3},{2,6},{3,1},{4,0},{5,7},{6,2},{7,5},{8,12},{9,11},{10,... | collective-permute-start | bytes 6291464 | tf_op jit(solution)/shard_map/ppermute | solution.py:115
  1237.6 49.4 %collective-permute-start.29 = (bf16[1,256,2048]{2,1,0:T(8,128)(2,1)}, bf16[1,256,2048]{2,1,0:T(8,128)(2,1)}, u32[]{:S(2)}, u32[]{:S(2)}) collective-permute-start(bf16[1,256,2048]{2,1,0:T(8,128)(2,1)} %slice.851), channel_id=1, source_target_pairs={{0,2},{1,5},{2,0},{3,7},{4,6},{5,1},{6,4},{7,3},{8,10},{9,13},{10,... | collective-permute-start | bytes 3145736 | tf_op jit(solution)/shard_map/ppermute | solution.py:115
  1301.8 427.5 %reduce-scatter.12.cloned.1.call-start = ((), (), s32[]{:S(2)}) async-start(), calls=%async_computation.26 | async-start | bytes 409600 | tf_op jit(solution)/shard_map/reduce_scatter | solution.py:186
  1460.5 56.7 %collective-permute-start.39 = (bf16[4,2,256,2048]{3,2,1,0:T(8,128)(2,1)}, bf16[4,2,256,2048]{3,2,1,0:T(8,128)(2,1)}, u32[]{:S(2)}, u32[]{:S(2)}) collective-permute-start(bf16[4,2,256,2048]{3,2,1,0:T(8,128)(2,1)} %pad_maximum_fusion.1), channel_id=1, source_target_pairs={{0,1},{1,0},{2,3},{3,2},{4,5},{5,4},{6,7},{7,6},{8,9},{9,8},{10,11... | collective-permute-start | bytes 25165832 | tf_op jit(solution)/shard_map/ppermute | solution.py:105
  1482.3 400.8 %reduce-scatter.18.cloned.1.call-start = ((), (), s32[]{:S(2)}) async-start(), calls=%async_computation.29 | async-start | bytes 3604480 | tf_op jit(solution)/shard_map/reduce_scatter | solution.py:186
  1513.2 106.4 %all-to-all-start.12 = ((bf16[2,512,1408]{2,1,0:T(8,128)(2,1)}), bf16[2,512,1408]{2,1,0:T(8,128)(2,1)S(1)}, u32[]{:S(2)}, u32[]{:S(2)}) async-start(bf16[2,512,1408]{2,1,0:T(8,128)(2,1)} %bitcast.583), calls=%async_computation.21 | async-start | bytes 5767168 | tf_op jit(solution)/shard_map/all_to_all | solution.py:91
  1529.2 108.0 %collective-permute-start.40 = (bf16[2,2,256,2048]{3,2,1,0:T(8,128)(2,1)}, bf16[2,2,256,2048]{3,2,1,0:T(8,128)(2,1)}, u32[]{:S(2)}, u32[]{:S(2)}) collective-permute-start(bf16[2,2,256,2048]{3,2,1,0:T(8,128)(2,1)} %slice.863), channel_id=1, source_target_pairs={{0,4},{1,3},{2,6},{3,1},{4,0},{5,7},{6,2},{7,5},{8,12},{9,11},{10,... | collective-permute-start | bytes 12582920 | tf_op jit(solution)/shard_map/ppermute | solution.py:115
  1537.5 108.1 %collective-permute-start.44 = (bf16[2,256,2048]{2,1,0:T(8,128)(2,1)}, bf16[2,256,2048]{2,1,0:T(8,128)(2,1)}, u32[]{:S(2)}, u32[]{:S(2)}) collective-permute-start(bf16[2,256,2048]{2,1,0:T(8,128)(2,1)} %slice.874), channel_id=1, source_target_pairs={{0,4},{1,3},{2,6},{3,1},{4,0},{5,7},{6,2},{7,5},{8,12},{9,11},{10,... | collective-permute-start | bytes 6291464 | tf_op jit(solution)/shard_map/ppermute | solution.py:115
  1619.6 94.7 %all-to-all-start.11 = ((bf16[2,512,1408]{2,1,0:T(8,128)(2,1)}), bf16[2,512,1408]{2,1,0:T(8,128)(2,1)}, u32[]{:S(2)}, u32[]{:S(2)}) async-start(bf16[2,512,1408]{2,1,0:T(8,128)(2,1)} %bitcast.582), calls=%async_computation.19 | async-start | bytes 5767168 | tf_op jit(solution)/shard_map/all_to_all | solution.py:91
  1624.7 263.7 %reduce-scatter.14.cloned.1.call-start = ((), (), s32[]{:S(2)}) async-start(), calls=%async_computation.27 | async-start | bytes 655360 | tf_op jit(solution)/shard_map/reduce_scatter | solution.py:186
  1630.1 259.9 %reduce-scatter.16.cloned.1.call-start = ((), (), s32[]{:S(2)}) async-start(), calls=%async_computation.28 | async-start | bytes 1310720 | tf_op jit(solution)/shard_map/reduce_scatter | solution.py:186
  1644.1 90.4 %collective-permute-start.41 = (bf16[1,2,256,2048]{3,2,1,0:T(8,128)(2,1)}, bf16[1,2,256,2048]{3,2,1,0:T(8,128)(2,1)}, u32[]{:S(2)}, u32[]{:S(2)}) collective-permute-start(bf16[1,2,256,2048]{3,2,1,0:T(8,128)(2,1)} %slice.865), channel_id=1, source_target_pairs={{0,2},{1,5},{2,0},{3,7},{4,6},{5,1},{6,4},{7,3},{8,10},{9,13},{10,... | collective-permute-start | bytes 6291464 | tf_op jit(solution)/shard_map/ppermute | solution.py:115
  1650.5 80.4 %collective-permute-start.45 = (bf16[1,256,2048]{2,1,0:T(8,128)(2,1)}, bf16[1,256,2048]{2,1,0:T(8,128)(2,1)}, u32[]{:S(2)}, u32[]{:S(2)}) collective-permute-start(bf16[1,256,2048]{2,1,0:T(8,128)(2,1)} %slice.876), channel_id=1, source_target_pairs={{0,2},{1,5},{2,0},{3,7},{4,6},{5,1},{6,4},{7,3},{8,10},{9,13},{10,... | collective-permute-start | bytes 3145736 | tf_op jit(solution)/shard_map/ppermute | solution.py:115
  1714.3 114.9 %all-to-all-start.13 = ((bf16[2,1408,512]{2,1,0:T(8,128)(2,1)}), bf16[2,1408,512]{2,1,0:T(8,128)(2,1)}, u32[]{:S(2)}, u32[]{:S(2)}) async-start(bf16[2,1408,512]{2,1,0:T(8,128)(2,1)} %bitcast.581), calls=%async_computation.22 | async-start | bytes 5767168 | tf_op jit(solution)/shard_map/all_to_all | solution.py:91
  1719.4 182.3 %reduce-scatter.10.cloned.1.call-start = ((), (), s32[]{:S(2)}) async-start(), calls=%async_computation.25 | async-start | bytes 1966080 | tf_op jit(solution)/shard_map/reduce_scatter | solution.py:186
  1729.3 149.4 %collective-permute-start.61 = (bf16[1,64,576]{2,1,0:T(8,128)(2,1)}, bf16[1,64,576]{2,1,0:T(8,128)(2,1)}, u32[]{:S(2)}, u32[]{:S(2)}) collective-permute-start(bf16[1,64,576]{2,1,0:T(8,128)(2,1)} %bitcast.619), channel_id=1, source_target_pairs={{0,2},{1,5},{2,0},{3,7},{4,6},{5,1},{6,4},{7,3},{8,10},{9,13},{10,... | collective-permute-start | bytes 221192 | tf_op jit(solution)/shard_map/ppermute | solution.py:115
  1730.8 174.3 %collective-permute-start.60 = (bf16[1,64,576]{2,1,0:T(8,128)(2,1)}, bf16[1,64,576]{2,1,0:T(8,128)(2,1)}, u32[]{:S(2)}, u32[]{:S(2)}) collective-permute-start(bf16[1,64,576]{2,1,0:T(8,128)(2,1)} %bitcast.620), channel_id=1, source_target_pairs={{0,1},{1,0},{2,3},{3,2},{4,5},{5,4},{6,7},{7,6},{8,9},{9,8},{10,11... | collective-permute-start | bytes 221192 | tf_op jit(solution)/shard_map/ppermute | solution.py:105
  1738.4 113.1 %collective-permute-start.42 = (bf16[256,2048]{1,0:T(8,128)(2,1)}, bf16[256,2048]{1,0:T(8,128)(2,1)}, u32[]{:S(2)}, u32[]{:S(2)}) collective-permute-start(bf16[256,2048]{1,0:T(8,128)(2,1)} %fusion.176), channel_id=1, source_target_pairs={{0,16},{8,24},{16,0},{24,8},{1,17},{9,25},{17,1},{25,9},{2,18},{10... | collective-permute-start | bytes 3145736 | tf_op jit(solution)/shard_map/ppermute | solution.py:77
  1874.0 56.3 %all-to-all-start.10 = ((bf16[4,640,256]{2,1,0:T(8,128)(2,1)}), bf16[4,640,256]{2,1,0:T(8,128)(2,1)}, u32[]{:S(2)}, u32[]{:S(2)}) async-start(bf16[4,640,256]{2,1,0:T(8,128)(2,1)} %bitcast.607), calls=%async_computation.10 | async-start | bytes 2621440 | tf_op jit(solution)/shard_map/all_to_all | solution.py:207
  (233 other events, 4613.0 us)
Sparse Core Ops, SparseCore 0:
  78.0 68.2 all-gather.14
  304.1 119.6 all-gather.16
  478.3 106.9 all-gather.20
  586.7 74.4 all-gather.18
  663.6 93.1 all-gather.10
  771.2 32.1 all-gather.12
  1095.5 69.5 reduce-scatter.25
  1168.1 71.3 reduce-scatter.23
  1241.8 93.7 reduce-scatter.21
  1337.9 31.3 reduce-scatter.19
  1482.4 19.4 reduce-scatter.11
  1504.2 93.6 reduce-scatter.17
  1630.2 42.0 reduce-scatter.13
  1675.2 34.5 reduce-scatter.15
  1729.4 79.5 reduce-scatter.9

commit v7 on v6

--- a/solution.py
+++ b/solution.py
@@ -87,10 +87,21 @@
     return [list(range(half)), list(range(half, 2 * half))]
 
 
-def mate_exchange(value):
-    return lax.all_to_all(
-        value, "row", split_axis=0, concat_axis=0, axis_index_groups=mates(), tiled=True
-    )
+def mate_swap(value):
+    host = lax.axis_index("row") // (lax.axis_size("row") // 2)
+    slot = jnp.arange(2, dtype=jnp.int32).reshape((2,) + (1,) * (value.ndim - 1))
+    masked = jnp.where(slot == host, jnp.zeros((), value.dtype), value)
+    return lax.psum_scatter(masked, "row", scatter_dimension=0, axis_index_groups=mates())
+
+
+def in_order(own, other):
+    first = lax.axis_index("row") // (lax.axis_size("row") // 2) == 0
+    return jnp.stack([jnp.where(first, own, other), jnp.where(first, other, own)])
+
+
+def own_slot(value):
+    host = lax.axis_index("row") // (lax.axis_size("row") // 2)
+    return lax.dynamic_index_in_dim(value, host, 0, False)
 
 
 def half_gather(value, axis):
@@ -300,9 +311,10 @@
         (jnp.int32(1), jnp.zeros((group_rows, 2 * slice_width), BF16)),
     )[1]
     dealt_x = exchange(tokens, out_list, in_slots) + more[:, :slice_width]
+    dealt_x, mate_routes, mate_gates = after((dealt_x, mate(routes), mate(gate_weights)), ())
     routes_late, gates_late = after((routes, gate_weights), (dealt_x,))
     pick, weight = chosen(routes_late, gates_late)
-    mate_pick, mate_weight = chosen(mate(routes_late), mate(gates_late))
+    mate_pick, mate_weight = chosen(mate_routes, mate_gates)
     full_x = cube_gather(dealt_x, 1)
 
     query_width = w_query.shape[1]
@@ -336,7 +348,8 @@
     latent_g = gains[:, 2 * wide :].reshape(-1).astype(F32)
 
     (gate_s, up_s, down_s) = after((expert_gate, expert_up, expert_down), (first_w,))
-    gate_s, up_s, down_s = mate_exchange(gate_s), mate_exchange(up_s), mate_exchange(down_s)
+    gate_m, up_m, down_m = mate_swap(gate_s), mate_swap(up_s), mate_swap(down_s)
+    gate_s, up_s, down_s = own_slot(gate_s), own_slot(up_s), own_slot(down_s)
 
     head_count = query_w.shape[1] // (NOPE + ROPE)
     softmax_scale = (NOPE + ROPE) ** (-0.5)
@@ -368,8 +381,6 @@
     )
     value_heads = expanded[..., NOPE:]
     dealt_dy = exchange(cotangent_s, out_list, in_slots, (expanded,)) + more[:, slice_width:]
-    (gate_s,) = after((gate_s,), (query_heads,))
-    gate_w = half_gather(gate_s, 1).reshape(dim, -1)
 
     def block_scores(first_row, last_row):
         raw_scores = (
@@ -408,22 +419,25 @@
         jnp.concatenate(mixed_blocks, axis=0).reshape(group_rows, head_count * VDIM).astype(BF16)
     )
     mate_dy = mate(dealt_dy)
-    (up_s,) = after((up_s,), (mixed,))
-    up_w = half_gather(up_s, 1).reshape(dim, -1)
+    (gate_m,) = after((gate_m,), (mixed,))
+    gate_w = half_gather(in_order(gate_s, gate_m), 1).reshape(dim, -1)
     attn_part = cube_scatter(dot(mixed, output_w).astype(BF16))
-    mate_dy, down_s = after((mate_dy, down_s), (attn_part,))
+    mate_dy, up_m = after((mate_dy, up_m), (attn_part,))
+    up_w = half_gather(in_order(up_s, up_m), 1).reshape(dim, -1)
     both_dy = cube_gather(jnp.stack([dealt_dy, mate_dy]), 2)
     full_dy = both_dy[0]
-    down_w = half_gather(down_s.transpose(1, 0, 2), 2).reshape(down_s.shape[1], dim)
     x_part = my_part(full_x).astype(F32)
     hidden_part = x_part + attn_part
     scale_two = lax.rsqrt(jnp.mean(hidden_part * hidden_part, axis=-1, keepdims=True) + EPSILON)
     unit_two = hidden_part * scale_two
     normed_part = (unit_two * gain_two).astype(BF16)
+    (down_m,) = after((down_m,), (normed_part,))
+    down_w = half_gather(in_order(down_s, down_m), 1)
+    down_w = down_w.transpose(2, 0, 1, 3).reshape(down_s.shape[0], dim)
     both_normed = cube_gather(jnp.stack([normed_part, mate(normed_part)]), 1)
     normed_two = both_normed[0]
     shared_g_s, shared_d_s = after(
-        (jnp.concatenate([shared_gate, shared_up], axis=1), shared_down), (normed_part,)
+        (jnp.concatenate([shared_gate, shared_up], axis=1), shared_down), (both_normed,)
     )
     shared_gu_w = row_gather(shared_g_s, 0)
     shared_d_w = row_gather(shared_d_s, 1)
@@ -493,14 +507,13 @@
     def row_sum(value, axis):
         return row_scatter(value.astype(BF16), axis)
 
-    def half_rows(value, axis):
-        shape = value.shape[:axis] + (2, row_count // 2, -1) + value.shape[axis + 1 :]
-        return half_sum(value.astype(BF16).reshape(shape), axis + 1)
+    def half_rows(value):
+        return half_sum(value.astype(BF16).reshape(2, row_count // 2, -1, value.shape[1]), 1)
 
     late_rows, late_result, late_hidden = after((rows, grad_result, hidden), (grad_two,))
-    sum_down = half_rows(dot_tn(late_hidden, late_result), 1).transpose(1, 0, 2)
-    sum_gate = half_rows(dot_tn(late_rows, grad_gate), 0)
-    sum_up = half_rows(dot_tn(late_rows, grad_up), 0)
+    sum_down = half_rows(dot_tn(late_result, late_hidden))
+    sum_gate = half_rows(dot_tn(late_rows, grad_gate))
+    sum_up = half_rows(dot_tn(late_rows, grad_up))
     late = after((normed_two, grad_shared_gu, shared_hidden, full_dy), (grad_two,))
     grad_sgu = row_sum(dot_tn(late[0], late[1]), 0)
     grad_sd = row_sum(dot_tn(late[2], late[3]), 1)
@@ -520,7 +533,8 @@
     both_terms = cube_scatter(both_terms, 1)
     moe_part, mate_terms = both_terms[0], mate(both_terms[1].astype(BF16))
     sum_down, sum_gate = after((sum_down, sum_gate), (grad_attn,))
-    grad_down, grad_gate = mate_exchange(sum_down), mate_exchange(sum_gate)
+    grad_down = in_order(own_slot(sum_down), mate_swap(sum_down)).transpose(0, 2, 1)
+    grad_gate = in_order(own_slot(sum_gate), mate_swap(sum_gate))
 
     grad_output_w = row_sum(dot_tn(mixed, grad_attn), 1)
     grad_mixed = dot_nt(grad_attn, output_w).astype(BF16)
@@ -573,7 +587,7 @@
 
     grad_one = cube_scatter(grad_one)
     (sum_up,) = after((sum_up,), (grad_one,))
-    grad_up = mate_exchange(sum_up)
+    grad_up = in_order(own_slot(sum_up), mate_swap(sum_up))
     grad_expanded = jnp.concatenate([grad_keys[..., :NOPE], grad_values], axis=-1).astype(BF16)
     grad_expanded = grad_expanded.reshape(group_rows, head_count * (NOPE + VDIM))
     grad_compressed = dot_nt(grad_expanded, expand_w)

time: 1990 us -> 1830 us (0.920)
  waiting for transfers between devices: 816 us -> 655 us
  starting transfers between devices: 111 us -> 81.8 us
  other arithmetic: 250 us -> 276 us
    all_to_all x6 -> x0, waiting for transfers between devices: 348 us -> none  [mate_exchange(): lax.all_to_all(value, 'row', split_axis=0, concat_axis=0, axis_index_grou...]
    reduce_scatter x0 -> x6, waiting for transfers between devices: none -> 122 us  [mate_swap(): lax.psum_scatter(masked, 'row', scatter_dimension=0, axis_index_groups=ma...]
    all_gather x3, waiting for transfers between devices: 20.7 us -> 79.2 us  [row_gather(): return lax.all_gather(shard, 'row', axis=axis, tiled=True)]
    ppermute x26, waiting for transfers between devices: 147 us -> 205 us  [chip_swap(): lax.ppermute(value, 'col', [(j, j ^ (other if j % 2 else bits)[step]) for...]
    ppermute x6, waiting for transfers between devices: 206 us -> 159 us  [mate(): lax.ppermute(value, 'row', [(j, j ^ count // 2) for j in range(count)])]
    all_to_all x6 -> x0, starting transfers between devices: 27.4 us -> none  [mate_exchange(): lax.all_to_all(value, 'row', split_axis=0, concat_axis=0, axis_index_grou...]
    select_n x0 -> x6, other arithmetic: none -> 24.4 us  [the longest x3 14.1 us: mate_swap(): masked = jnp.where(slot == host, jnp.zeros((), value.dtype), value)]
    unnamed x392 -> x427, local copies, waits for them, and re-layouts: 35.8 us -> 50 us
  transfers between devices with their start and end apart: 92 -> 92, of which waited for: 31 -> 35; matrix products, arithmetic and copies ran while one was open for 45% -> 51% of each run, Pallas kernels for 0% -> 0%
where the time goes in v7:
time: 1830 us; the launch traced here: 1820 us
  waiting for transfers between devices  655 us (36%)
  matrix products  472 us (26%)
  local copies, waits for them, and re-layouts  311 us (17%)
  other arithmetic  276 us (15%)
  starting transfers between devices  81.8 us (4%)
  between operations  18.8 us (1%)
    ppermute x26, waiting for transfers between devices, chip_swap(): lax.ppermute(value, 'col', [(j, j ^ (other if j % 2 else bits)[step]) for...  205 us
    ppermute x6, waiting for transfers between devices, mate(): lax.ppermute(value, 'row', [(j, j ^ count // 2) for j in range(count)])  159 us
    dot_general x17, matrix products, dot(): return jnp.dot(left, right, preferred_element_type=F32)  155 us
    dot_general x13, matrix products, dot_tn(): lax.dot_general(left, right, (((0,), (0,)), ((), ())), preferred_element_...  146 us
    reduce_scatter x6, waiting for transfers between devices, mate_swap(): lax.psum_scatter(masked, 'row', scatter_dimension=0, axis_index_groups=ma...  122 us
    dynamic_update_slice x52, local copies, waits for them, and re-layouts, cube_gather(): lax.dynamic_update_slice_in_dim(out, item, block_at(owner, place) * width...  92.8 us
    dot_general x10, matrix products, dot_nt(): lax.dot_general(left, right, (((1,), (1,)), ((), ())), preferred_element_...  87.8 us
    all_gather x3, waiting for transfers between devices, row_gather(): return lax.all_gather(shard, 'row', axis=axis, tiled=True)  79.2 us
  transfers between devices with their start and end apart: 92, of which 35 were waited for; matrix products, arithmetic and copies ran while one was open for 51% of the time, Pallas kernels for 0%

profile of v7, /device:TPU:0, one launch (start us, length us, event | category | flops | bytes accessed | tf_op | source)
XLA Modules:
  0.0 1815.3 jit_solution(8304942595097186214)
XLA Ops:
  37.5 24.2 %all-to-all-done.2 = bf16[4,640,256]{2,1,0:T(8,128)(2,1)S(1)} async-done(((bf16[4,640,256]{2,1,0:T(8,128)(2,1)}), bf16[4,640,256]{2,1,0:T(8,128)(2,1)S(1)}, u32[]{:S(2)}, u32[]{:S(2)}) %all-to-all-start.2) | async-done | bytes 1310752 | tf_op jit(solution)/shard_map/all_to_all | solution.py:218
  74.6 65.4 %all-gather.15.cloned.1.call-done = bf16[4544,384]{1,0:T(8,128)(2,1)} async-done(((bf16[1136,384]{1,0:T(8,128)(2,1)}), bf16[4544,384]{1,0:T(8,128)(2,1)}) %all-gather.15.cloned.1.call-update) | async-done | bytes 3489808 | tf_op jit(solution)/shard_map/all_gather | solution.py:188
  149.2 10.9 collective-permute-done.3
  172.0 14.5 collective-permute-done.5
  257.4 10.0 fusion.264
  332.0 20.6 %collective-permute-done.13 = bf16[2,256,2048]{2,1,0:T(8,128)(2,1)} collective-permute-done((bf16[2,256,2048]{2,1,0:T(8,128)(2,1)}, bf16[2,256,2048]{2,1,0:T(8,128)(2,1)}, u32[]{:S(2)}, u32[]{:S(2)}) %collective-permute-start.13) | collective-permute-done | bytes 2097184 | tf_op jit(solution)/shard_map/ppermute | solution.py:126
  385.5 23.9 %all-to-all-done.3 = bf16[4,640,256]{2,1,0:T(8,128)(2,1)} async-done(((bf16[4,640,256]{2,1,0:T(8,128)(2,1)}), bf16[4,640,256]{2,1,0:T(8,128)(2,1)}, u32[]{:S(2)}, u32[]{:S(2)}) %all-to-all-start.3) | async-done | bytes 1310752 | tf_op jit(solution)/shard_map/all_to_all | solution.py:218
  421.4 40.8 %collective-permute-done.21 = bf16[2048,256]{1,0:T(8,128)(2,1)} collective-permute-done((bf16[2048,256]{1,0:T(8,128)(2,1)S(1)}, bf16[2048,256]{1,0:T(8,128)(2,1)}, u32[]{:S(2)}, u32[]{:S(2)}) %collective-permute-start.21) | collective-permute-done | bytes 1048608 | tf_op jit(solution)/shard_map/ppermute | solution.py:77
  483.2 15.2 collective-permute-done.23
  511.7 43.4 %collective-permute-done.15 = bf16[256,2048]{1,0:T(8,128)(2,1)S(1)} collective-permute-done((bf16[256,2048]{1,0:T(8,128)(2,1)S(1)}, bf16[256,2048]{1,0:T(8,128)(2,1)S(1)}, u32[]{:S(2)}, u32[]{:S(2)}) %collective-permute-start.15) | collective-permute-done | bytes 1048608 | tf_op jit(solution)/shard_map/ppermute | solution.py:77
  565.0 23.2 %select_reduce_fusion.2 = (s32[2048]{0:T(1024)S(1)}, s32[2048]{0:T(1024)S(1)}) fusion(s32[4,2048]{1,0:T(4,128)S(1)} %copy-done.101, pred[4,2048]{1,0:T(4,128)(4,1)S(1)} %copy-done.172, s32[4,2048]{1,0:T(4,128)S(1)} %copy-done.89), kind=kLoop, calls=%fused_computation.32 | loop fusion | flops 100659200 | bytes 90112 | tf_op jit(solution)/shard_map/reduce_sum | solution.py:451
  620.4 20.4 %collective-permute-done.19 = bf16[2,2,256,2048]{3,2,1,0:T(8,128)(2,1)} collective-permute-done((bf16[2,2,256,2048]{3,2,1,0:T(8,128)(2,1)}, bf16[2,2,256,2048]{3,2,1,0:T(8,128)(2,1)}, u32[]{:S(2)}, u32[]{:S(2)}) %collective-permute-start.19) | collective-permute-done | bytes 4194336 | tf_op jit(solution)/shard_map/ppermute | solution.py:126
  653.4 22.8 %multiply_convert_fusion.1 = (bf16[2,1024,2048]{2,1,0:T(8,128)(2,1)S(1)}, f32[2,1024,2048]{2,1,0:T(8,128)}) fusion(f32[2,1024]{1,0:T(2,128)S(1)} %mul.691, bf16[2,2048,2048]{2,1,0:T(8,128)(2,1)} %fusion.118, pred[1,1024,2048]{2,1,0:T(32,128)(4,1)S(1)} %copy-done.35, pred[1,1024,2048]{2,1,0:T(32,128)(4,1)S(1)} %copy-done.34), kind=kOutput, calls=%fused_computation.63 | convolution fusion | flops 17192452096 | bytes 46145536 | tf_op jit(solution)/shard_map/dot_general | solution.py:474
  676.3 9.3 fusion.30
  685.5 10.1 fusion.249
  695.6 17.1 fusion.266
  722.2 21.8 %convolution_convert_fusion.5 = bf16[2,1024,2048]{2,1,0:T(8,128)(2,1)} fusion(bf16[2,2048,2048]{2,1,0:T(8,128)(2,1)} %fusion.122, pred[1,1024,2048]{2,1,0:T(32,128)(4,1)S(1)} %copy-done.35, pred[1,1024,2048]{2,1,0:T(32,128)(4,1)S(1)} %copy-done.34), kind=kOutput, calls=%fused_computation.123 | convolution fusion | flops 17188257792 | bytes 29360128 | tf_op jit(solution)/shard_map/dot_general | solution.py:474
  744.0 18.5 %fusion.265 = f32[2048,1408]{1,0:T(8,128)} fusion(bf16[2048,2048]{1,0:T(8,128)(2,1)} %bitcast.710, bf16[2048,1408]{1,0:T(8,128)(2,1)} %bitcast.701), kind=kOutput, calls=%fused_computation.628 | convolution fusion | flops 11811160064 | bytes 25690112 | tf_op jit(solution)/shard_map/dot_general | solution.py:60
  762.6 29.7 %multiply_convert_fusion.4 = (bf16[2048,1408]{1,0:T(8,128)(2,1)}, bf16[2048,1408]{1,0:T(8,128)(2,1)}, bf16[2048,1408]{1,0:T(8,128)(2,1)}) fusion(f32[2048,1408]{1,0:T(8,128)} %fusion.265, f32[2048,1408]{1,0:T(8,128)} %fusion.266, bf16[2048,2048]{1,0:T(8,128)(2,1)} %bitcast.711, bf16[2048,1408]{1,0:T(8,128)(2,1)} %bitcast.706), kind=kOutput, calls=%fused_computation.67 | convolution fusion | flops 11854413824 | bytes 54525952 | tf_op jit(solution)/shard_map/dot_general | solution.py:60
  792.3 11.8 fusion.83
  804.1 12.6 add_convert_fusion.27
  829.0 11.5 fusion.47
  849.5 23.1 %fusion.46 = f32[2048,2048]{1,0:T(8,128)} fusion(f32[1024,2048]{1,0:T(8,128)} %fusion.268, bf16[1024,1408]{1,0:T(8,128)(2,1)S(1)} %slice.841, bf16[2048,1408]{1,0:T(8,128)(2,1)} %bitcast.708, pred[1024,2048]{1,0:T(32,128)(4,1)} %iota_compare_fusion.82), kind=kOutput, calls=%fused_computation.100 | convolution fusion | flops 14499708928 | bytes 35913728 | tf_op jit(solution)/shard_map/dot_general | solution.py:68
  872.6 11.2 fusion.267
  883.9 13.7 all-gather.13.cloned.1.call-done
  897.7 10.8 multiply_convert_fusion.10
  908.5 13.4 add_convert_fusion.2
  921.9 15.5 convolution_convert_fusion.2
  957.7 15.6 convolution_convert_fusion.3
  987.4 19.1 %collective-permute-done.31 = bf16[2,256,2048]{2,1,0:T(8,128)(2,1)S(1)} collective-permute-done((bf16[2,256,2048]{2,1,0:T(8,128)(2,1)S(1)}, bf16[2,256,2048]{2,1,0:T(8,128)(2,1)S(1)}, u32[]{:S(2)}, u32[]{:S(2)}) %collective-permute-start.31) | collective-permute-done | bytes 2097184 | tf_op jit(solution)/shard_map/ppermute | solution.py:126
  1009.0 24.6 %collective-permute-done.32 = bf16[1,256,2048]{2,1,0:T(8,128)(2,1)S(1)} collective-permute-done((bf16[1,256,2048]{2,1,0:T(8,128)(2,1)S(1)}, bf16[1,256,2048]{2,1,0:T(8,128)(2,1)S(1)}, u32[]{:S(2)}, u32[]{:S(2)}) %collective-permute-start.32) | collective-permute-done | bytes 1048608 | tf_op jit(solution)/shard_map/ppermute | solution.py:126
  1042.8 38.1 %collective-permute-done.33 = bf16[256,2048]{1,0:T(8,128)(2,1)S(1)} collective-permute-done((bf16[256,2048]{1,0:T(8,128)(2,1)S(1)}, bf16[256,2048]{1,0:T(8,128)(2,1)S(1)}, u32[]{:S(2)}, u32[]{:S(2)}) %collective-permute-start.33) | collective-permute-done | bytes 1048608 | tf_op jit(solution)/shard_map/ppermute | solution.py:77
  1087.7 13.3 collective-permute-done.35
  1105.6 14.3 convolution_convert_fusion.4
  1228.1 12.3 copy.366
  1261.2 10.8 convolution_convert_fusion.6
  1272.1 17.5 multiply_convert_fusion
  1289.7 11.7 fusion.45
  1324.1 9.3 convolution_convert_fusion.9
  1333.5 10.3 fusion.40
  1343.8 13.4 convert_bitcast_fusion
  1451.3 33.0 %collective-permute-done.63 = bf16[2,64,576]{2,1,0:T(8,128)(2,1)} collective-permute-done((bf16[2,64,576]{2,1,0:T(8,128)(2,1)}, bf16[2,64,576]{2,1,0:T(8,128)(2,1)}, u32[]{:S(2)}, u32[]{:S(2)}) %collective-permute-start.63) | collective-permute-done | bytes 147488 | tf_op jit(solution)/shard_map/ppermute | solution.py:126
  1523.1 51.9 %reduce-scatter.42.cloned.1.call-done = bf16[1,512,1408]{2,1,0:T(8,128)(2,1)} async-done(((bf16[2,512,1408]{2,1,0:T(8,128)(2,1)}), bf16[1,512,1408]{2,1,0:T(8,128)(2,1)}) %reduce-scatter.42.cloned.1.call-update) | async-done | bytes 1441808 | tf_op jit(solution)/shard_map/reduce_scatter | solution.py:94
  1578.3 70.4 %reduce-scatter.38.cloned.1.call-done = bf16[1,512,1408]{2,1,0:T(8,128)(2,1)} async-done(((bf16[2,512,1408]{2,1,0:T(8,128)(2,1)}), bf16[1,512,1408]{2,1,0:T(8,128)(2,1)}) %reduce-scatter.38.cloned.1.call-update) | async-done | bytes 1441808 | tf_op jit(solution)/shard_map/reduce_scatter | solution.py:94
  1670.3 36.7 %collective-permute-done.42 = bf16[256,2048]{1,0:T(8,128)(2,1)} collective-permute-done((bf16[256,2048]{1,0:T(8,128)(2,1)}, bf16[256,2048]{1,0:T(8,128)(2,1)}, u32[]{:S(2)}, u32[]{:S(2)}) %collective-permute-start.42) | collective-permute-done | bytes 1048608 | tf_op jit(solution)/shard_map/ppermute | solution.py:77
  1720.3 9.1 all-to-all-done.4
  1753.6 10.1 all-to-all-done.7
  1787.1 11.3 all-to-all-done.5
  (997 shorter events, 798.3 us)
Async XLA Ops:
  7.2 64.3 %collective-permute-start = (s32[2048,6]{0,1:T(8,128)}, s32[2048,6]{0,1:T(8,128)S(1)}, u32[]{:S(2)}, u32[]{:S(2)}) collective-permute-start(s32[2048,6]{0,1:T(8,128)} %param.47), channel_id=1, source_target_pairs={{0,16},{8,24},{16,0},{24,8},{1,17},{9,25},{17,1},{25,9},{2,18},{10... | collective-permute-start | bytes 147464 | tf_op jit(solution)/shard_map/ppermute | solution.py:77
  11.3 60.2 %collective-permute-start.1 = (f32[2048,6]{0,1:T(8,128)}, f32[2048,6]{0,1:T(8,128)}, u32[]{:S(2)}, u32[]{:S(2)}) collective-permute-start(f32[2048,6]{0,1:T(8,128)} %param.48), channel_id=1, source_target_pairs={{0,16},{8,24},{16,0},{24,8},{1,17},{9,25},{17,1},{25,9},{2,18},{10... | collective-permute-start | bytes 147464 | tf_op jit(solution)/shard_map/ppermute | solution.py:77
  25.6 36.1 %all-to-all-start.2 = ((bf16[4,640,256]{2,1,0:T(8,128)(2,1)}), bf16[4,640,256]{2,1,0:T(8,128)(2,1)S(1)}, u32[]{:S(2)}, u32[]{:S(2)}) async-start(bf16[4,640,256]{2,1,0:T(8,128)(2,1)} %bitcast.663), calls=%async_computation.2 | async-start | bytes 2621440 | tf_op jit(solution)/shard_map/all_to_all | solution.py:218
  30.9 109.1 %all-gather.15.cloned.1.call-start = ((), (), s32[]{:S(2)}) async-start(), calls=%async_computation.40 | async-start | bytes 4362240 | tf_op jit(solution)/shard_map/all_gather | solution.py:188
  71.6 255.8 %reduce-scatter.16.cloned.1.call-start = ((), (), s32[]{:S(2)}) async-start(), calls=%async_computation.23 | async-start | bytes 4325376 | tf_op jit(solution)/shard_map/reduce_scatter | solution.py:94
  144.9 235.0 %reduce-scatter.20.cloned.1.call-start = ((), (), s32[]{:S(2)}) async-start(), calls=%async_computation.25 | async-start | bytes 4325376 | tf_op jit(solution)/shard_map/reduce_scatter | solution.py:94
  192.0 55.2 %collective-permute-start.7 = (bf16[1,256,576]{2,1,0:T(8,128)(2,1)}, bf16[1,256,576]{2,1,0:T(8,128)(2,1)}, u32[]{:S(2)}, u32[]{:S(2)}) collective-permute-start(bf16[1,256,576]{2,1,0:T(8,128)(2,1)} %broadcast_in_dim.274), channel_id=1, source_target_pairs={{0,1},{1,0},{2,3},{3,2},{4,5},{5,4},{6,7},{7,6},{8,9},{9,8},{10,11... | collective-permute-start | bytes 884744 | tf_op jit(solution)/shard_map/ppermute | solution.py:116
  192.5 41.7 %collective-permute-start.8 = (bf16[1,256,576]{2,1,0:T(8,128)(2,1)}, bf16[1,256,576]{2,1,0:T(8,128)(2,1)S(1)}, u32[]{:S(2)}, u32[]{:S(2)}) collective-permute-start(bf16[1,256,576]{2,1,0:T(8,128)(2,1)} %broadcast_in_dim.274), channel_id=1, source_target_pairs={{0,2},{1,5},{2,0},{3,7},{4,6},{5,1},{6,4},{7,3},{8,10},{9,13},{10,... | collective-permute-start | bytes 884744 | tf_op jit(solution)/shard_map/ppermute | solution.py:126
  212.1 250.1 %reduce-scatter.18.cloned.1.call-start = ((), (), s32[]{:S(2)}) async-start(), calls=%async_computation.24 | async-start | bytes 4325376 | tf_op jit(solution)/shard_map/reduce_scatter | solution.py:94
  312.0 288.4 %all-gather.17.cloned.1.call-start = ((), (), s32[]{:S(2)}) async-start(), calls=%async_computation.41 | async-start | bytes 8650752 | tf_op jit(solution)/shard_map/all_gather | solution.py:108
  374.2 35.1 %all-to-all-start.3 = ((bf16[4,640,256]{2,1,0:T(8,128)(2,1)}), bf16[4,640,256]{2,1,0:T(8,128)(2,1)}, u32[]{:S(2)}, u32[]{:S(2)}) async-start(bf16[4,640,256]{2,1,0:T(8,128)(2,1)} %bitcast.662), calls=%async_computation.4 | async-start | bytes 2621440 | tf_op jit(solution)/shard_map/all_to_all | solution.py:218
  378.7 233.3 %all-gather.21.cloned.1.call-start = ((), (), s32[]{:S(2)}) async-start(), calls=%async_computation.43 | async-start | bytes 8650752 | tf_op jit(solution)/shard_map/all_gather | solution.py:108
  383.8 378.7 %all-gather.19.cloned.1.call-start = ((), (), s32[]{:S(2)}) async-start(), calls=%async_computation.42 | async-start | bytes 8650752 | tf_op jit(solution)/shard_map/all_gather | solution.py:108
  415.5 46.7 %collective-permute-start.21 = (bf16[2048,256]{1,0:T(8,128)(2,1)S(1)}, bf16[2048,256]{1,0:T(8,128)(2,1)}, u32[]{:S(2)}, u32[]{:S(2)}) collective-permute-start(bf16[2048,256]{1,0:T(8,128)(2,1)S(1)} %fusion.108), channel_id=1, source_target_pairs={{0,16},{8,24},{16,0},{24,8},{1,17},{9,25},{17,1},{25,9},{2,18},{10... | collective-permute-start | bytes 3145736 | tf_op jit(solution)/shard_map/ppermute | solution.py:77
  483.0 389.7 %all-gather.11.cloned.1.call-start = ((), (), s32[]{:S(2)}) async-start(), calls=%async_computation.26 | async-start | bytes 3604480 | tf_op jit(solution)/shard_map/all_gather | solution.py:188
  501.1 91.3 %collective-permute-start.25 = (bf16[2,2,2048,256]{3,2,1,0:T(8,128)(2,1)S(1)}, bf16[2,2,2048,256]{3,2,1,0:T(8,128)(2,1)}, u32[]{:S(2)}, u32[]{:S(2)}) collective-permute-start(bf16[2,2,2048,256]{3,2,1,0:T(8,128)(2,1)S(1)} %pad_maximum_fusion.4), channel_id=1, source_target_pairs={{0,4},{1,3},{2,6},{3,1},{4,0},{5,7},{6,2},{7,5},{8,12},{9,11},{10,... | collective-permute-start | bytes 12582920 | tf_op jit(solution)/shard_map/ppermute | solution.py:126
  502.8 94.5 %collective-permute-start.24 = (bf16[1,2,2048,256]{3,2,1,0:T(8,128)(2,1)}, bf16[1,2,2048,256]{3,2,1,0:T(8,128)(2,1)}, u32[]{:S(2)}, u32[]{:S(2)}) collective-permute-start(bf16[1,2,2048,256]{3,2,1,0:T(8,128)(2,1)} %collective-permute-done.23), channel_id=1, source_target_pairs={{0,1},{1,0},{2,3},{3,2},{4,5},{5,4},{6,7},{7,6},{8,9},{9,8},{10,11... | collective-permute-start | bytes 6291464 | tf_op jit(solution)/shard_map/ppermute | solution.py:116
  506.3 48.9 %collective-permute-start.15 = (bf16[256,2048]{1,0:T(8,128)(2,1)S(1)}, bf16[256,2048]{1,0:T(8,128)(2,1)S(1)}, u32[]{:S(2)}, u32[]{:S(2)}) collective-permute-start(bf16[256,2048]{1,0:T(8,128)(2,1)S(1)} %copy-done.111), channel_id=1, source_target_pairs={{0,16},{8,24},{16,0},{24,8},{1,17},{9,25},{17,1},{25,9},{2,18},{10... | collective-permute-start | bytes 3145736 | tf_op jit(solution)/shard_map/ppermute | solution.py:77
  592.0 48.8 %collective-permute-start.19 = (bf16[2,2,256,2048]{3,2,1,0:T(8,128)(2,1)}, bf16[2,2,256,2048]{3,2,1,0:T(8,128)(2,1)}, u32[]{:S(2)}, u32[]{:S(2)}) collective-permute-start(bf16[2,2,256,2048]{3,2,1,0:T(8,128)(2,1)} %pad_maximum_fusion.3), channel_id=1, source_target_pairs={{0,4},{1,3},{2,6},{3,1},{4,0},{5,7},{6,2},{7,5},{8,12},{9,11},{10,... | collective-permute-start | bytes 12582920 | tf_op jit(solution)/shard_map/ppermute | solution.py:126
  592.4 51.6 %collective-permute-start.26 = (bf16[2,2,2048,256]{3,2,1,0:T(8,128)(2,1)}, bf16[2,2,2048,256]{3,2,1,0:T(8,128)(2,1)}, u32[]{:S(2)}, u32[]{:S(2)}) collective-permute-start(bf16[2,2,2048,256]{3,2,1,0:T(8,128)(2,1)} %collective-permute-done.25), channel_id=1, source_target_pairs={{0,1},{1,0},{2,3},{3,2},{4,5},{5,4},{6,7},{7,6},{8,9},{9,8},{10,11... | collective-permute-start | bytes 12582920 | tf_op jit(solution)/shard_map/ppermute | solution.py:116
  640.8 72.0 %collective-permute-start.20 = (bf16[2,2,256,2048]{3,2,1,0:T(8,128)(2,1)}, bf16[2,2,256,2048]{3,2,1,0:T(8,128)(2,1)}, u32[]{:S(2)}, u32[]{:S(2)}) collective-permute-start(bf16[2,2,256,2048]{3,2,1,0:T(8,128)(2,1)} %collective-permute-done.19), channel_id=1, source_target_pairs={{0,1},{1,0},{2,3},{3,2},{4,5},{5,4},{6,7},{7,6},{8,9},{9,8},{10,11... | collective-permute-start | bytes 12582920 | tf_op jit(solution)/shard_map/ppermute | solution.py:116
  804.1 93.6 %all-gather.13.cloned.1.call-start = ((), (), s32[]{:S(2)}) async-start(), calls=%async_computation.27 | async-start | bytes 1802240 | tf_op jit(solution)/shard_map/all_gather | solution.py:188
  849.5 507.6 %reduce-scatter.40.cloned.1.call-start = ((), (), s32[]{:S(2)}) async-start(), calls=%async_computation.37 | async-start | bytes 8650752 | tf_op jit(solution)/shard_map/reduce_scatter | solution.py:112
  940.3 416.8 %reduce-scatter.36.cloned.1.call-start = ((), (), s32[]{:S(2)}) async-start(), calls=%async_computation.35 | async-start | bytes 8650752 | tf_op jit(solution)/shard_map/reduce_scatter | solution.py:112
  976.4 380.7 %reduce-scatter.34.cloned.1.call-start = ((), (), s32[]{:S(2)}) async-start(), calls=%async_computation.34 | async-start | bytes 8650752 | tf_op jit(solution)/shard_map/reduce_scatter | solution.py:112
  985.8 54.4 %collective-permute-start.28 = (bf16[2,256,2048]{2,1,0:T(8,128)(2,1)S(1)}, bf16[2,256,2048]{2,1,0:T(8,128)(2,1)S(1)}, u32[]{:S(2)}, u32[]{:S(2)}) collective-permute-start(bf16[2,256,2048]{2,1,0:T(8,128)(2,1)S(1)} %slice.849), channel_id=1, source_target_pairs={{0,4},{1,3},{2,6},{3,1},{4,0},{5,7},{6,2},{7,5},{8,12},{9,11},{10,... | collective-permute-start | bytes 6291464 | tf_op jit(solution)/shard_map/ppermute | solution.py:126
  1034.0 46.9 %collective-permute-start.33 = (bf16[256,2048]{1,0:T(8,128)(2,1)S(1)}, bf16[256,2048]{1,0:T(8,128)(2,1)S(1)}, u32[]{:S(2)}, u32[]{:S(2)}) collective-permute-start(bf16[256,2048]{1,0:T(8,128)(2,1)S(1)} %fusion.181), channel_id=1, source_target_pairs={{0,16},{8,24},{16,0},{24,8},{1,17},{9,25},{17,1},{25,9},{2,18},{10... | collective-permute-start | bytes 3145736 | tf_op jit(solution)/shard_map/ppermute | solution.py:77
  1041.2 39.6 %collective-permute-start.29 = (bf16[1,256,2048]{2,1,0:T(8,128)(2,1)S(1)}, bf16[1,256,2048]{2,1,0:T(8,128)(2,1)S(1)}, u32[]{:S(2)}, u32[]{:S(2)}) collective-permute-start(bf16[1,256,2048]{2,1,0:T(8,128)(2,1)S(1)} %slice.851), channel_id=1, source_target_pairs={{0,2},{1,5},{2,0},{3,7},{4,6},{5,1},{6,4},{7,3},{8,10},{9,13},{10,... | collective-permute-start | bytes 3145736 | tf_op jit(solution)/shard_map/ppermute | solution.py:126
  1087.6 44.1 %collective-permute-start.34 = (bf16[1,256,2048]{2,1,0:T(8,128)(2,1)}, bf16[1,256,2048]{2,1,0:T(8,128)(2,1)}, u32[]{:S(2)}, u32[]{:S(2)}) collective-permute-start(bf16[1,256,2048]{2,1,0:T(8,128)(2,1)} %get-tuple-element.643), channel_id=1, source_target_pairs={{0,1},{1,0},{2,3},{3,2},{4,5},{5,4},{6,7},{7,6},{8,9},{9,8},{10,11... | collective-permute-start | bytes 3145736 | tf_op jit(solution)/shard_map/ppermute | solution.py:116
  1122.9 290.2 %reduce-scatter.32.cloned.1.call-start = ((), (), s32[]{:S(2)}) async-start(), calls=%async_computation.33 | async-start | bytes 1802240 | tf_op jit(solution)/shard_map/reduce_scatter | solution.py:197
  1228.0 187.1 %reduce-scatter.24.cloned.1.call-start = ((), (), s32[]{:S(2)}) async-start(), calls=%async_computation.29 | async-start | bytes 409600 | tf_op jit(solution)/shard_map/reduce_scatter | solution.py:197
  1261.2 165.4 %reduce-scatter.30.cloned.1.call-start = ((), (), s32[]{:S(2)}) async-start(), calls=%async_computation.32 | async-start | bytes 3604480 | tf_op jit(solution)/shard_map/reduce_scatter | solution.py:197
  1272.1 156.9 %reduce-scatter.26.cloned.1.call-start = ((), (), s32[]{:S(2)}) async-start(), calls=%async_computation.30 | async-start | bytes 655360 | tf_op jit(solution)/shard_map/reduce_scatter | solution.py:197
  1311.2 119.4 %reduce-scatter.28.cloned.1.call-start = ((), (), s32[]{:S(2)}) async-start(), calls=%async_computation.31 | async-start | bytes 1310720 | tf_op jit(solution)/shard_map/reduce_scatter | solution.py:197
  1321.1 111.4 %reduce-scatter.22.cloned.1.call-start = ((), (), s32[]{:S(2)}) async-start(), calls=%async_computation.28 | async-start | bytes 1966080 | tf_op jit(solution)/shard_map/reduce_scatter | solution.py:197
  1333.4 170.9 %reduce-scatter.44.cloned.1.call-start = ((), (), s32[]{:S(2)}) async-start(), calls=%async_computation.39 | async-start | bytes 4325376 | tf_op jit(solution)/shard_map/reduce_scatter | solution.py:94
  1364.5 210.5 %reduce-scatter.42.cloned.1.call-start = ((), (), s32[]{:S(2)}) async-start(), calls=%async_computation.38 | async-start | bytes 4325376 | tf_op jit(solution)/shard_map/reduce_scatter | solution.py:94
  1385.9 262.8 %reduce-scatter.38.cloned.1.call-start = ((), (), s32[]{:S(2)}) async-start(), calls=%async_computation.36 | async-start | bytes 4325376 | tf_op jit(solution)/shard_map/reduce_scatter | solution.py:94
  1410.3 97.2 %collective-permute-start.40 = (bf16[2,2,256,2048]{3,2,1,0:T(8,128)(2,1)}, bf16[2,2,256,2048]{3,2,1,0:T(8,128)(2,1)}, u32[]{:S(2)}, u32[]{:S(2)}) collective-permute-start(bf16[2,2,256,2048]{3,2,1,0:T(8,128)(2,1)} %slice.863), channel_id=1, source_target_pairs={{0,4},{1,3},{2,6},{3,1},{4,0},{5,7},{6,2},{7,5},{8,12},{9,11},{10,... | collective-permute-start | bytes 12582920 | tf_op jit(solution)/shard_map/ppermute | solution.py:126
  1423.0 93.2 %collective-permute-start.44 = (bf16[2,256,2048]{2,1,0:T(8,128)(2,1)}, bf16[2,256,2048]{2,1,0:T(8,128)(2,1)}, u32[]{:S(2)}, u32[]{:S(2)}) collective-permute-start(bf16[2,256,2048]{2,1,0:T(8,128)(2,1)} %slice.874), channel_id=1, source_target_pairs={{0,4},{1,3},{2,6},{3,1},{4,0},{5,7},{6,2},{7,5},{8,12},{9,11},{10,... | collective-permute-start | bytes 6291464 | tf_op jit(solution)/shard_map/ppermute | solution.py:126
  1425.1 59.2 %collective-permute-start.63 = (bf16[2,64,576]{2,1,0:T(8,128)(2,1)}, bf16[2,64,576]{2,1,0:T(8,128)(2,1)}, u32[]{:S(2)}, u32[]{:S(2)}) collective-permute-start(bf16[2,64,576]{2,1,0:T(8,128)(2,1)} %pad_maximum_fusion.36), channel_id=1, source_target_pairs={{0,4},{1,3},{2,6},{3,1},{4,0},{5,7},{6,2},{7,5},{8,12},{9,11},{10,... | collective-permute-start | bytes 442376 | tf_op jit(solution)/shard_map/ppermute | solution.py:126
  1515.4 140.3 %collective-permute-start.41 = (bf16[1,2,256,2048]{3,2,1,0:T(8,128)(2,1)}, bf16[1,2,256,2048]{3,2,1,0:T(8,128)(2,1)}, u32[]{:S(2)}, u32[]{:S(2)}) collective-permute-start(bf16[1,2,256,2048]{3,2,1,0:T(8,128)(2,1)} %slice.865), channel_id=1, source_target_pairs={{0,2},{1,5},{2,0},{3,7},{4,6},{5,1},{6,4},{7,3},{8,10},{9,13},{10,... | collective-permute-start | bytes 6291464 | tf_op jit(solution)/shard_map/ppermute | solution.py:126
  1522.4 130.2 %collective-permute-start.45 = (bf16[1,256,2048]{2,1,0:T(8,128)(2,1)}, bf16[1,256,2048]{2,1,0:T(8,128)(2,1)}, u32[]{:S(2)}, u32[]{:S(2)}) collective-permute-start(bf16[1,256,2048]{2,1,0:T(8,128)(2,1)} %slice.876), channel_id=1, source_target_pairs={{0,2},{1,5},{2,0},{3,7},{4,6},{5,1},{6,4},{7,3},{8,10},{9,13},{10,... | collective-permute-start | bytes 3145736 | tf_op jit(solution)/shard_map/ppermute | solution.py:126
  1655.6 78.1 %collective-permute-start.49 = (f32[4608]{0:T(1024)S(1)}, f32[4608]{0:T(1024)S(1)}, u32[]{:S(2)}, u32[]{:S(2)}) collective-permute-start(f32[4608]{0:T(1024)S(1)} %pad_maximum_fusion.38), channel_id=1, source_target_pairs={{0,1},{1,0},{2,3},{3,2},{4,5},{5,4},{6,7},{7,6},{8,9},{9,8},{10,11... | collective-permute-start | bytes 55304 | tf_op jit(solution)/shard_map/ppermute | solution.py:116
  1659.2 47.8 %collective-permute-start.42 = (bf16[256,2048]{1,0:T(8,128)(2,1)}, bf16[256,2048]{1,0:T(8,128)(2,1)}, u32[]{:S(2)}, u32[]{:S(2)}) collective-permute-start(bf16[256,2048]{1,0:T(8,128)(2,1)} %fusion.182), channel_id=1, source_target_pairs={{0,16},{8,24},{16,0},{24,8},{1,17},{9,25},{17,1},{25,9},{2,18},{10... | collective-permute-start | bytes 3145736 | tf_op jit(solution)/shard_map/ppermute | solution.py:77
  1664.1 45.7 %all-to-all-start.6 = ((bf16[256,8,256]{2,0,1:T(8,128)(2,1)}), bf16[256,8,256]{2,0,1:T(8,128)(2,1)}, u32[]{:S(2)}, u32[]{:S(2)}) async-start(bf16[256,8,256]{2,0,1:T(8,128)(2,1)} %bitcast.622), calls=%async_computation.9 | async-start | bytes 2097152 | tf_op jit(solution)/shard_map/all_to_all | solution.py:609
  1741.4 35.8 %collective-permute-start.52 = (f32[4608]{0:T(1024)S(1)}, f32[4608]{0:T(1024)S(1)}, u32[]{:S(2)}, u32[]{:S(2)}) collective-permute-start(f32[4608]{0:T(1024)S(1)} %add.833), channel_id=1, source_target_pairs={{0,8},{8,16},{16,24},{24,0},{1,9},{9,17},{17,25},{25,1},{2,10},{10... | collective-permute-start | bytes 55304 | tf_op jit(solution)/shard_map/ppermute | solution.py:206
  1763.7 34.8 %all-to-all-start.5 = ((bf16[4,640,256]{2,1,0:T(8,128)(2,1)}), bf16[4,640,256]{2,1,0:T(8,128)(2,1)}, u32[]{:S(2)}, u32[]{:S(2)}) async-start(bf16[4,640,256]{2,1,0:T(8,128)(2,1)} %bitcast.665), calls=%async_computation.8 | async-start | bytes 2621440 | tf_op jit(solution)/shard_map/all_to_all | solution.py:218
  (251 other events, 4087.6 us)
Sparse Core Ops, SparseCore 0:
  71.7 68.2 all-gather.14
  145.1 70.8 reduce-scatter.15
  218.3 71.2 reduce-scatter.19
  312.1 70.6 reduce-scatter.17
  384.9 108.5 all-gather.16
  495.5 96.1 all-gather.20
  593.3 74.4 all-gather.18
  804.2 58.0 all-gather.10
  864.0 33.6 all-gather.12
  940.5 70.2 reduce-scatter.39
  1013.0 93.8 reduce-scatter.35
  1123.1 71.4 reduce-scatter.33
  1228.2 32.8 reduce-scatter.31
  1263.7 18.9 reduce-scatter.23
  1284.9 54.4 reduce-scatter.29
  1342.0 21.4 reduce-scatter.25
  1365.7 25.4 reduce-scatter.27
  1393.4 33.9 reduce-scatter.21
  1430.3 71.2 reduce-scatter.43
  1503.7 71.2 reduce-scatter.41
  1577.4 71.3 reduce-scatter.37

commit v8 on v7

--- a/solution.py
+++ b/solution.py
@@ -160,7 +160,7 @@
     return out
 
 
-def cube_scatter(value, axis=0):
+def scatter_stages(value, axis=0):
     count = lax.axis_size("col")
     index = lax.axis_index("col")
     rows = value.shape[axis] // count
@@ -178,10 +178,15 @@
     held = blocks(index).astype(F32) + got.astype(F32)
     for step in range(len(chip_bits()) - 1, -1, -1):
         held = held.astype(BF16)
+        yield held
         half = held.shape[0] // 2
         got = chip_swap(held[half:], step)
         held = held[:half].astype(F32) + got.astype(F32)
-    return held[0]
+    yield held[0]
+
+
+def cube_scatter(value, axis=0):
+    return list(scatter_stages(value, axis))[-1]
 
 
 def row_gather(shard, axis):
@@ -329,7 +334,7 @@
     first_s = jnp.concatenate(parts, axis=0)
     first_s = jnp.pad(first_s, ((0, -first_s.shape[0] % 16), (0, 0)))
     (first_s,) = after((first_s,), (dealt_x,))
-    first_w = row_gather(first_s[None], 0)
+    (first_w,) = after((row_gather(first_s[None], 0),), (full_x,))
     pieces, start = [], 0
     for part in parts:
         pieces.append(first_w[:, start : start + part.shape[0]])
@@ -358,7 +363,6 @@
     residual = full_x.astype(F32)
     scale_one = lax.rsqrt(jnp.mean(residual * residual, axis=-1, keepdims=True) + EPSILON)
     normed_one = (residual * scale_one * gain_one).astype(BF16)
-    (cotangent_s,) = after((cotangent,), (normed_one,))
     query_raw = dot(normed_one, query_w)
     query_raw = query_raw.reshape(group_rows, head_count, NOPE + ROPE)
     query_heads = jnp.concatenate(
@@ -380,7 +384,6 @@
         axis=-1,
     )
     value_heads = expanded[..., NOPE:]
-    dealt_dy = exchange(cotangent_s, out_list, in_slots, (expanded,)) + more[:, slice_width:]
 
     def block_scores(first_row, last_row):
         raw_scores = (
@@ -418,32 +421,35 @@
     mixed = (
         jnp.concatenate(mixed_blocks, axis=0).reshape(group_rows, head_count * VDIM).astype(BF16)
     )
-    mate_dy = mate(dealt_dy)
     (gate_m,) = after((gate_m,), (mixed,))
     gate_w = half_gather(in_order(gate_s, gate_m), 1).reshape(dim, -1)
-    attn_part = cube_scatter(dot(mixed, output_w).astype(BF16))
-    mate_dy, up_m = after((mate_dy, up_m), (attn_part,))
-    up_w = half_gather(in_order(up_s, up_m), 1).reshape(dim, -1)
-    both_dy = cube_gather(jnp.stack([dealt_dy, mate_dy]), 2)
-    full_dy = both_dy[0]
+    attn_terms = dot(mixed, output_w).astype(BF16)
+    (cotangent_s,) = after((cotangent,), (attn_terms,))
+    attn_part = cube_scatter(attn_terms)
     x_part = my_part(full_x).astype(F32)
     hidden_part = x_part + attn_part
     scale_two = lax.rsqrt(jnp.mean(hidden_part * hidden_part, axis=-1, keepdims=True) + EPSILON)
     unit_two = hidden_part * scale_two
     normed_part = (unit_two * gain_two).astype(BF16)
-    (down_m,) = after((down_m,), (normed_part,))
+    mate_normed, up_m = after((mate(normed_part), up_m), (normed_part,))
+    up_w = half_gather(in_order(up_s, up_m), 1).reshape(dim, -1)
+    (down_m,) = after((down_m,), (mate_normed,))
     down_w = half_gather(in_order(down_s, down_m), 1)
     down_w = down_w.transpose(2, 0, 1, 3).reshape(down_s.shape[0], dim)
-    both_normed = cube_gather(jnp.stack([normed_part, mate(normed_part)]), 1)
+    both_normed = cube_gather(jnp.stack([normed_part, mate_normed]), 1)
     normed_two = both_normed[0]
+    dealt_dy = exchange(cotangent_s, out_list, in_slots, (mate_normed,)) + more[:, slice_width:]
+    (mate_dy,) = after((mate(dealt_dy),), (both_normed,))
+    both_dy = cube_gather(jnp.stack([dealt_dy, mate_dy]), 2)
+    full_dy = both_dy[0]
     shared_g_s, shared_d_s = after(
-        (jnp.concatenate([shared_gate, shared_up], axis=1), shared_down), (both_normed,)
+        (jnp.concatenate([shared_gate, shared_up], axis=1), shared_down), (mate_normed,)
     )
     shared_gu_w = row_gather(shared_g_s, 0)
     shared_d_w = row_gather(shared_d_s, 1)
 
     place_late, rank_late, here_late, source_late, my_rank_late = after(
-        (place_in, rank_here, from_here, my_source, my_rank), (normed_part,)
+        (place_in, rank_here, from_here, my_source, my_rank), (both_normed,)
     )
     hit = (place_late[:, :, None] == token_ids[None, None, :]) & here_late[:, :, None]
     rank_of = jnp.sum(jnp.where(hit, rank_late[:, :, None], 0), axis=(0, 1))
@@ -485,35 +491,44 @@
     def row_grads(gate_part, up_part):
         return (dot_nt(gate_part, gate_w) + dot_nt(up_part, up_w)).astype(BF16)
 
-    mate_rows = row_grads(grad_gate[capacity:], grad_up[capacity:])
+    def row_sum(value, axis):
+        return row_scatter(value.astype(BF16), axis)
+
+    def half_rows(value):
+        return half_sum(value.reshape(2, row_count // 2, -1, value.shape[1]), 1)
+
+    expert_grads = [
+        dot_tn(grad_result, hidden).astype(BF16),
+        dot_tn(rows, grad_gate).astype(BF16),
+        dot_tn(rows, grad_up).astype(BF16),
+    ]
+    sum_down, sum_gate, sum_up = [half_rows(value) for value in expert_grads]
+    gate_late, up_late = after((grad_gate, grad_up), expert_grads)
+    mate_rows = row_grads(gate_late[capacity:], up_late[capacity:])
     mate_grad = dot_tn(mate_pick, mate_rows).astype(BF16)
-    mate_grad_part = mate(cube_scatter(mate_grad).astype(BF16))
-    own_gate, own_up, normed_s, dy_s = after(
-        (grad_gate[:capacity], grad_up[:capacity], normed_two, full_dy), (mate_grad,)
-    )
+    stages = scatter_stages(mate_grad)
+    own_gate, own_up = after((gate_late[:capacity], up_late[:capacity]), (mate_grad,))
     own_rows = row_grads(own_gate, own_up)
+    normed_s, dy_s = after((normed_two, full_dy), (own_rows, next(stages)))
     shared_width = shared_gate.shape[1]
     shared_out = dot(normed_s, shared_gu_w)
     shared_hidden, shared_act, shared_us = forward(
         shared_out[:, :shared_width], shared_out[:, shared_width:]
     )
+    stage = next(stages)
+    shared_grad_hidden, stage = after((dot_nt(dy_s, shared_d_w), stage), ())
     grad_shared_gu = jnp.concatenate(
-        backward(dot_nt(dy_s, shared_d_w), shared_act, shared_us), axis=1
-    )
+        backward(shared_grad_hidden, shared_act, shared_us), axis=1
+    )
+    *_, mate_sum = stages
     grad_two = dot_nt(grad_shared_gu, shared_gu_w)
     grad_two = (grad_two + dot_tn(pick, own_rows)).astype(BF16)
+    grad_two, mate_sum, sum_down = after((grad_two, mate_sum, sum_down), ())
+    mate_grad_part = mate(mate_sum.astype(BF16))
     grad_two_part = cube_scatter(grad_two)
-
-    def row_sum(value, axis):
-        return row_scatter(value.astype(BF16), axis)
-
-    def half_rows(value):
-        return half_sum(value.astype(BF16).reshape(2, row_count // 2, -1, value.shape[1]), 1)
-
-    late_rows, late_result, late_hidden = after((rows, grad_result, hidden), (grad_two,))
-    sum_down = half_rows(dot_tn(late_result, late_hidden))
-    sum_gate = half_rows(dot_tn(late_rows, grad_gate))
-    sum_up = half_rows(dot_tn(late_rows, grad_up))
+    swap_down = mate_swap(sum_down)
+    (sum_gate,) = after((sum_gate,), (grad_two_part,))
+    swap_gate = mate_swap(sum_gate)
     late = after((normed_two, grad_shared_gu, shared_hidden, full_dy), (grad_two,))
     grad_sgu = row_sum(dot_tn(late[0], late[1]), 0)
     grad_sd = row_sum(dot_tn(late[2], late[3]), 1)
@@ -529,12 +544,10 @@
     result_rows = (weights * dot(hidden_late, down_w)).astype(BF16)
     mate_terms = dot_tn(mate_pick, result_rows[capacity:])
     moe_terms = dot(shared_late, shared_d_w) + dot_tn(pick, result_rows[:capacity])
-    (both_terms,) = after((jnp.stack([moe_terms.astype(BF16), mate_terms.astype(BF16)]),), (grad_attn,))
-    both_terms = cube_scatter(both_terms, 1)
-    moe_part, mate_terms = both_terms[0], mate(both_terms[1].astype(BF16))
-    sum_down, sum_gate = after((sum_down, sum_gate), (grad_attn,))
-    grad_down = in_order(own_slot(sum_down), mate_swap(sum_down)).transpose(0, 2, 1)
-    grad_gate = in_order(own_slot(sum_gate), mate_swap(sum_gate))
+    both_terms = jnp.stack([moe_terms.astype(BF16), mate_terms.astype(BF16)])
+    grad_attn, both_terms, sum_up = after((grad_attn, both_terms, sum_up), ())
+    swap_up = mate_swap(sum_up)
+    term_stages = scatter_stages(both_terms, 1)
 
     grad_output_w = row_sum(dot_tn(mixed, grad_attn), 1)
     grad_mixed = dot_nt(grad_attn, output_w).astype(BF16)
@@ -579,15 +592,16 @@
         .astype(BF16)
         .reshape(group_rows, head_count * (NOPE + ROPE))
     )
+    grad_query_raw, _ = after((grad_query_raw, next(term_stages)), ())
     grad_one = dot_nt(grad_query_raw, query_w).astype(BF16)
-
-    mate_terms, moe_part = after((mate_terms, moe_part), (grad_one,))
+    *_, both_terms = term_stages
+    moe_part, mate_terms = both_terms[0], mate(both_terms[1].astype(BF16))
+
+    grad_one_part = cube_scatter(grad_one)
+    mate_terms, moe_part = after((mate_terms, moe_part), (grad_one_part,))
     result_part = (hidden_part + (moe_part + mate_terms.astype(F32))).astype(BF16)
     result_slice = lax.all_to_all(result_part, "col", split_axis=1, concat_axis=0, tiled=True)
 
-    grad_one = cube_scatter(grad_one)
-    (sum_up,) = after((sum_up,), (grad_one,))
-    grad_up = in_order(own_slot(sum_up), mate_swap(sum_up))
     grad_expanded = jnp.concatenate([grad_keys[..., :NOPE], grad_values], axis=-1).astype(BF16)
     grad_expanded = grad_expanded.reshape(group_rows, head_count * (NOPE + VDIM))
     grad_compressed = dot_nt(grad_expanded, expand_w)
@@ -600,14 +614,14 @@
     )
     grad_latent_part = jnp.concatenate([grad_front, grad_latent_part[:, LAT:]], axis=1).astype(BF16)
     latent_term = dot_nt(grad_latent_part, latent_w)
-    grad_one = grad_one + latent_term
+    grad_one = grad_one_part + latent_term
     scale_one_part = my_part(scale_one)
     input_back, gain_one_grad = norm_back(
         grad_one, x_part * scale_one_part, scale_one_part, gain_one
     )
     grad_input = (grad_hidden_part + input_back).astype(BF16)
     grad_slice = lax.all_to_all(grad_input, "col", split_axis=1, concat_axis=0, tiled=True)
-    result = exchange(result_slice, back_list, back_slots, (grad_input,))
+    result = exchange(result_slice, back_list, back_slots)
     tokens_grad = exchange(grad_slice, back_list, back_slots)
 
     def more_back(carry):
@@ -629,7 +643,16 @@
     my_columns = lax.dynamic_index_in_dim(
         normed_one.reshape(group_rows, row_count, col_count, lat_rows), col_index, 2, False
     ).reshape(group_rows, row_count * lat_rows)
-    grad_latent_w = cube_gather(row_sum(dot_tn(my_columns, grad_latent), 0), 0)
+    (grad_latent_w,) = after((row_sum(dot_tn(my_columns, grad_latent), 0),), (grad_one_part,))
+    grad_latent_w = cube_gather(grad_latent_w, 0)
+    sums = after(
+        (swap_down, swap_gate, swap_up, grad_sgu, grad_sd, grad_query_w, grad_expand_w, grad_output_w),
+        (grad_slice,),
+    )
+    swap_down, swap_gate, swap_up, grad_sgu, grad_sd, grad_query_w, grad_expand_w, grad_output_w = sums
+    grad_down = in_order(own_slot(sum_down), swap_down).transpose(0, 2, 1)
+    grad_gate = in_order(own_slot(sum_gate), swap_gate)
+    grad_up = in_order(own_slot(sum_up), swap_up)
     gain_grads = small_sum(jnp.concatenate([gain_one_grad, gain_two_grad, latent_gain_grad]))
     width_two = gain_one_grad.shape[0]
     width_lat = latent_gain_grad.shape[0]

time: 1830 us -> 1930 us (1.055)
  waiting for transfers between devices: 655 us -> 761 us
    ppermute x26, waiting for transfers between devices: 205 us -> 275 us  [chip_swap(): lax.ppermute(value, 'col', [(j, j ^ (other if j % 2 else bits)[step]) for...]
    ppermute x6, waiting for transfers between devices: 159 us -> 202 us  [mate(): lax.ppermute(value, 'row', [(j, j ^ count // 2) for j in range(count)])]
    all_gather x3, waiting for transfers between devices: 79.2 us -> 36.5 us  [row_gather(): return lax.all_gather(shard, 'row', axis=axis, tiled=True)]
    reduce_scatter x6, waiting for transfers between devices: 0.01 us -> 36.7 us  [row_scatter(): return lax.psum_scatter(value, 'row', scatter_dimension=axis, tiled=True)]
    dot_general x10 -> x11, matrix products: 87.8 us -> 98.3 us  [dot_nt(): lax.dot_general(left, right, (((1,), (1,)), ((), ())), preferred_element_...]
    unnamed x427 -> x413, local copies, waits for them, and re-layouts: 50 us -> 41.6 us
  transfers between devices with their start and end apart: 92 -> 92, of which waited for: 35 -> 40; matrix products, arithmetic and copies ran while one was open for 51% -> 52% of each run, Pallas kernels for 0% -> 0%
where the time goes in v8:
time: 1930 us; the launch traced here: 1920 us
  waiting for transfers between devices  761 us (39%)
  matrix products  489 us (25%)
  local copies, waits for them, and re-layouts  296 us (15%)
  other arithmetic  262 us (14%)
  starting transfers between devices  81.4 us (4%)
    ppermute x26, waiting for transfers between devices, chip_swap(): lax.ppermute(value, 'col', [(j, j ^ (other if j % 2 else bits)[step]) for...  275 us
    ppermute x6, waiting for transfers between devices, mate(): lax.ppermute(value, 'row', [(j, j ^ count // 2) for j in range(count)])  202 us
    dot_general x17, matrix products, dot(): return jnp.dot(left, right, preferred_element_type=F32)  156 us
    dot_general x13, matrix products, dot_tn(): lax.dot_general(left, right, (((0,), (0,)), ((), ())), preferred_element_...  146 us
    reduce_scatter x6, waiting for transfers between devices, mate_swap(): lax.psum_scatter(masked, 'row', scatter_dimension=0, axis_index_groups=ma...  132 us
    dot_general x11, matrix products, dot_nt(): lax.dot_general(left, right, (((1,), (1,)), ((), ())), preferred_element_...  98.3 us
    dynamic_update_slice x52, local copies, waits for them, and re-layouts, cube_gather(): lax.dynamic_update_slice_in_dim(out, item, block_at(owner, place) * width...  84.5 us
    all_to_all x4, waiting for transfers between devices, exchange(): got = lax.all_to_all(sent, 'row', split_axis=0, concat_axis=0, tiled=True)  54.5 us
  transfers between devices with their start and end apart: 92, of which 40 were waited for; matrix products, arithmetic and copies ran while one was open for 52% of the time, Pallas kernels for 0%

profile of v8, /device:TPU:0, one launch (start us, length us, event | category | flops | bytes accessed | tf_op | source)
XLA Modules:
  0.0 1916.7 jit_solution(17714016517044915234)
XLA Ops:
  35.6 24.6 %all-to-all-done.2 = bf16[4,640,256]{2,1,0:T(8,128)(2,1)S(1)} async-done(((bf16[4,640,256]{2,1,0:T(8,128)(2,1)}), bf16[4,640,256]{2,1,0:T(8,128)(2,1)S(1)}, u32[]{:S(2)}, u32[]{:S(2)}) %all-to-all-start.2) | async-done | bytes 1310752 | tf_op jit(solution)/shard_map/all_to_all | solution.py:223
  78.0 12.0 collective-permute-done.3
  101.5 16.3 collective-permute-done.5
  128.8 36.5 %all-gather.15.cloned.1.call-done = bf16[4544,384]{1,0:T(8,128)(2,1)} async-done(((bf16[1136,384]{1,0:T(8,128)(2,1)}), bf16[4544,384]{1,0:T(8,128)(2,1)}) %all-gather.15.cloned.1.call-update) | async-done | bytes 3489808 | tf_op jit(solution)/shard_map/all_gather | solution.py:193
  225.1 10.0 fusion.267
  295.9 24.6 %collective-permute-done.13 = bf16[2,256,2048]{2,1,0:T(8,128)(2,1)S(1)} collective-permute-done((bf16[2,256,2048]{2,1,0:T(8,128)(2,1)}, bf16[2,256,2048]{2,1,0:T(8,128)(2,1)S(1)}, u32[]{:S(2)}, u32[]{:S(2)}) %collective-permute-start.13) | collective-permute-done | bytes 2097184 | tf_op jit(solution)/shard_map/ppermute | solution.py:126
  324.3 13.5 collective-permute-done.14
  342.9 85.6 %collective-permute-done.15 = bf16[256,2048]{1,0:T(8,128)(2,1)} collective-permute-done((bf16[256,2048]{1,0:T(8,128)(2,1)}, bf16[256,2048]{1,0:T(8,128)(2,1)}, u32[]{:S(2)}, u32[]{:S(2)}) %collective-permute-start.15) | collective-permute-done | bytes 1048608 | tf_op jit(solution)/shard_map/ppermute | solution.py:77
  433.5 25.8 %reduce-scatter.16.cloned.1.call-done = bf16[1,512,1408]{2,1,0:T(8,128)(2,1)} async-done(((bf16[2,512,1408]{2,1,0:T(8,128)(2,1)}), bf16[1,512,1408]{2,1,0:T(8,128)(2,1)}) %reduce-scatter.16.cloned.1.call-update) | async-done | bytes 1441808 | tf_op jit(solution)/shard_map/reduce_scatter | solution.py:94
  478.9 22.6 %collective-permute-done.17 = bf16[1,2,256,2048]{3,2,1,0:T(8,128)(2,1)S(1)} collective-permute-done((bf16[1,2,256,2048]{3,2,1,0:T(8,128)(2,1)}, bf16[1,2,256,2048]{3,2,1,0:T(8,128)(2,1)S(1)}, u32[]{:S(2)}, u32[]{:S(2)}) %collective-permute-start.17) | collective-permute-done | bytes 2097184 | tf_op jit(solution)/shard_map/ppermute | solution.py:126
  522.5 32.6 %collective-permute-done.19 = bf16[2,2,256,2048]{3,2,1,0:T(8,128)(2,1)} collective-permute-done((bf16[2,2,256,2048]{3,2,1,0:T(8,128)(2,1)}, bf16[2,2,256,2048]{3,2,1,0:T(8,128)(2,1)}, u32[]{:S(2)}, u32[]{:S(2)}) %collective-permute-start.19) | collective-permute-done | bytes 4194336 | tf_op jit(solution)/shard_map/ppermute | solution.py:126
  596.3 17.1 collective-permute-done.21
  625.8 23.2 %select_reduce_fusion.2 = (s32[2048]{0:T(1024)S(1)}, s32[2048]{0:T(1024)S(1)}) fusion(s32[4,2048]{1,0:T(4,128)S(1)} %copy-done.98, pred[4,2048]{1,0:T(4,128)(4,1)S(1)} %copy-done.170, s32[4,2048]{1,0:T(4,128)S(1)} %copy-done.87), kind=kLoop, calls=%fused_computation.32 | loop fusion | flops 100659200 | bytes 90112 | tf_op jit(solution)/shard_map/reduce_sum | solution.py:457
  660.2 23.5 %convolution_convert_fusion.5 = bf16[2,1024,2048]{2,1,0:T(8,128)(2,1)} fusion(bf16[2,2048,2048]{2,1,0:T(8,128)(2,1)} %fusion.120, pred[1,1024,2048]{2,1,0:T(32,128)(4,1)} %iota_compare_fusion.35, pred[1,1024,2048]{2,1,0:T(32,128)(4,1)S(1)} %iota_compare_fusion.36), kind=kOutput, calls=%fused_computation.123 | convolution fusion | flops 17188257792 | bytes 29360128 | tf_op jit(solution)/shard_map/dot_general | solution.py:480
  683.7 19.4 %collective-permute-done.25 = bf16[2,2,2048,256]{3,2,1,0:T(8,128)(2,1)} collective-permute-done((bf16[2,2,2048,256]{3,2,1,0:T(8,128)(2,1)}, bf16[2,2,2048,256]{3,2,1,0:T(8,128)(2,1)}, u32[]{:S(2)}, u32[]{:S(2)}) %collective-permute-start.25) | collective-permute-done | bytes 4194336 | tf_op jit(solution)/shard_map/ppermute | solution.py:126
  703.1 17.0 fusion.269
  749.6 22.7 %multiply_convert_fusion.1 = (bf16[2,1024,2048]{2,1,0:T(8,128)(2,1)S(1)}, f32[2,1024,2048]{2,1,0:T(8,128)}) fusion(f32[2,1024]{1,0:T(2,128)S(1)} %mul.689, bf16[2,2048,2048]{2,1,0:T(8,128)(2,1)} %fusion.116, pred[1,1024,2048]{2,1,0:T(32,128)(4,1)S(1)} %copy-done.39, pred[1,1024,2048]{2,1,0:T(32,128)(4,1)S(1)} %iota_compare_fusion.36), kind=kOutput, calls=%fused_computation.63 | convolution fusion | flops 17192452096 | bytes 46145536 | tf_op jit(solution)/shard_map/dot_general | solution.py:480
  781.9 17.2 fusion.268
  799.1 29.8 %multiply_convert_fusion.2 = (bf16[2048,1408]{1,0:T(8,128)(2,1)}, bf16[2048,1408]{1,0:T(8,128)(2,1)}, bf16[2048,1408]{1,0:T(8,128)(2,1)}) fusion(f32[2048,1408]{1,0:T(8,128)} %fusion.269, f32[2048,1408]{1,0:T(8,128)} %fusion.268, bf16[2048,2048]{1,0:T(8,128)(2,1)} %bitcast.742, bf16[2048,1408]{1,0:T(8,128)(2,1)} %bitcast.735), kind=kOutput, calls=%fused_computation.65 | convolution fusion | flops 11854413824 | bytes 54525952 | tf_op jit(solution)/shard_map/dot_general | solution.py:60
  828.9 17.2 convolution_convert_fusion.4
  849.0 19.5 %convolution_convert_fusion.2 = bf16[2048,1408]{1,0:T(8,128)(2,1)} fusion(bf16[2048,2048]{1,0:T(8,128)(2,1)} %bitcast.743, bf16[2048,1408]{1,0:T(8,128)(2,1)} %get-tuple-element.468), kind=kOutput, calls=%fused_computation.110 | convolution fusion | flops 11814043648 | bytes 19922944 | tf_op jit(solution)/shard_map/dot_general | solution.py:68
  868.5 19.4 %convolution_convert_fusion.3 = bf16[2048,1408]{1,0:T(8,128)(2,1)} fusion(bf16[2048,2048]{1,0:T(8,128)(2,1)} %bitcast.744, bf16[2048,1408]{1,0:T(8,128)(2,1)} %get-tuple-element.467), kind=kOutput, calls=%fused_computation.111 | convolution fusion | flops 11814043648 | bytes 19922944 | tf_op jit(solution)/shard_map/dot_general | solution.py:68
  893.4 12.5 fusion.82
  905.8 10.6 add_convert_fusion.23
  916.4 11.2 fusion.47
  936.3 10.2 fusion.252
  946.5 10.7 fusion.270
  957.4 11.2 add_convert_fusion.7
  968.6 12.0 fusion.46
  995.3 9.7 fusion.272
  1020.2 14.2 add_convert_fusion.2
  1051.4 24.6 %collective-permute-done.31 = bf16[2,256,2048]{2,1,0:T(8,128)(2,1)S(1)} collective-permute-done((bf16[2,256,2048]{2,1,0:T(8,128)(2,1)S(1)}, bf16[2,256,2048]{2,1,0:T(8,128)(2,1)S(1)}, u32[]{:S(2)}, u32[]{:S(2)}) %collective-permute-start.31) | collective-permute-done | bytes 2097184 | tf_op jit(solution)/shard_map/ppermute | solution.py:126
  1094.4 34.1 %collective-permute-done.33 = bf16[256,2048]{1,0:T(8,128)(2,1)} collective-permute-done((bf16[256,2048]{1,0:T(8,128)(2,1)}, bf16[256,2048]{1,0:T(8,128)(2,1)}, u32[]{:S(2)}, u32[]{:S(2)}) %collective-permute-start.33) | collective-permute-done | bytes 1048608 | tf_op jit(solution)/shard_map/ppermute | solution.py:77
  1136.3 16.0 multiply_convert_fusion
  1153.0 11.7 fusion.45
  1171.1 11.3 convert_bitcast_fusion
  1182.5 14.5 fusion.40
  1197.0 10.6 pad_maximum_fusion
  1310.2 12.3 copy.369
  1356.9 10.8 convolution_convert_fusion.6
  1380.2 12.4 dynamic-slice_bitcast_fusion.7
  1451.8 36.6 %collective-permute-done.40 = bf16[2,2,256,2048]{3,2,1,0:T(8,128)(2,1)} collective-permute-done((bf16[2,2,256,2048]{3,2,1,0:T(8,128)(2,1)}, bf16[2,2,256,2048]{3,2,1,0:T(8,128)(2,1)}, u32[]{:S(2)}, u32[]{:S(2)}) %collective-permute-start.40) | collective-permute-done | bytes 4194336 | tf_op jit(solution)/shard_map/ppermute | solution.py:126
  1507.2 16.1 collective-permute-done.44
  1555.6 65.6 %collective-permute-done.42 = bf16[256,2048]{1,0:T(8,128)(2,1)} collective-permute-done((bf16[256,2048]{1,0:T(8,128)(2,1)}, bf16[256,2048]{1,0:T(8,128)(2,1)}, u32[]{:S(2)}, u32[]{:S(2)}) %collective-permute-start.42) | collective-permute-done | bytes 1048608 | tf_op jit(solution)/shard_map/ppermute | solution.py:77
  1671.1 32.6 %reduce-scatter.30.cloned.1.call-done = bf16[1,512,1408]{2,1,0:T(8,128)(2,1)} async-done(((bf16[2,512,1408]{2,1,0:T(8,128)(2,1)}), bf16[1,512,1408]{2,1,0:T(8,128)(2,1)}) %reduce-scatter.30.cloned.1.call-update) | async-done | bytes 1441808 | tf_op jit(solution)/shard_map/reduce_scatter | solution.py:94
  1703.7 73.8 %reduce-scatter.32.cloned.1.call-done = bf16[1,512,1408]{2,1,0:T(8,128)(2,1)} async-done(((bf16[2,512,1408]{2,1,0:T(8,128)(2,1)}), bf16[1,512,1408]{2,1,0:T(8,128)(2,1)}) %reduce-scatter.32.cloned.1.call-update) | async-done | bytes 1441808 | tf_op jit(solution)/shard_map/reduce_scatter | solution.py:94
  1777.5 36.6 %reduce-scatter.38.cloned.1.call-done = bf16[512,384]{1,0:T(8,128)(2,1)} async-done(((bf16[2048,384]{1,0:T(8,128)(2,1)}), bf16[512,384]{1,0:T(8,128)(2,1)}) %reduce-scatter.38.cloned.1.call-update) | async-done | bytes 393232 | tf_op jit(solution)/shard_map/reduce_scatter | solution.py:202
  1873.2 21.8 %all-to-all-done.7 = bf16[4,640,256]{2,1,0:T(8,128)(2,1)} async-done(((bf16[4,640,256]{2,1,0:T(8,128)(2,1)}), bf16[4,640,256]{2,1,0:T(8,128)(2,1)}, u32[]{:S(2)}, u32[]{:S(2)}) %all-to-all-start.7) | async-done | bytes 1310752 | tf_op jit(solution)/shard_map/all_to_all | solution.py:223
  (982 shorter events, 824.4 us)
Async XLA Ops:
  7.2 67.9 %collective-permute-start = (s32[2048,6]{0,1:T(8,128)}, s32[2048,6]{0,1:T(8,128)S(1)}, u32[]{:S(2)}, u32[]{:S(2)}) collective-permute-start(s32[2048,6]{0,1:T(8,128)} %param.47), channel_id=1, source_target_pairs={{0,16},{8,24},{16,0},{24,8},{1,17},{9,25},{17,1},{25,9},{2,18},{10... | collective-permute-start | bytes 147464 | tf_op jit(solution)/shard_map/ppermute | solution.py:77
  11.3 63.8 %collective-permute-start.1 = (f32[2048,6]{0,1:T(8,128)}, f32[2048,6]{0,1:T(8,128)S(1)}, u32[]{:S(2)}, u32[]{:S(2)}) collective-permute-start(f32[2048,6]{0,1:T(8,128)} %param.48), channel_id=1, source_target_pairs={{0,16},{8,24},{16,0},{24,8},{1,17},{9,25},{17,1},{25,9},{2,18},{10... | collective-permute-start | bytes 147464 | tf_op jit(solution)/shard_map/ppermute | solution.py:77
  24.2 36.0 %all-to-all-start.2 = ((bf16[4,640,256]{2,1,0:T(8,128)(2,1)}), bf16[4,640,256]{2,1,0:T(8,128)(2,1)S(1)}, u32[]{:S(2)}, u32[]{:S(2)}) async-start(bf16[4,640,256]{2,1,0:T(8,128)(2,1)} %bitcast.6), calls=%async_computation.2 | async-start | bytes 2621440 | tf_op jit(solution)/shard_map/all_to_all | solution.py:223
  29.4 135.9 %all-gather.15.cloned.1.call-start = ((), (), s32[]{:S(2)}) async-start(), calls=%async_computation.40 | async-start | bytes 4362240 | tf_op jit(solution)/shard_map/all_gather | solution.py:193
  97.8 245.0 %reduce-scatter.18.cloned.1.call-start = ((), (), s32[]{:S(2)}) async-start(), calls=%async_computation.24 | async-start | bytes 4325376 | tf_op jit(solution)/shard_map/reduce_scatter | solution.py:94
  171.0 33.2 %collective-permute-start.8 = (bf16[1,256,576]{2,1,0:T(8,128)(2,1)S(1)}, bf16[1,256,576]{2,1,0:T(8,128)(2,1)}, u32[]{:S(2)}, u32[]{:S(2)}) collective-permute-start(bf16[1,256,576]{2,1,0:T(8,128)(2,1)S(1)} %broadcast_in_dim.274), channel_id=1, source_target_pairs={{0,2},{1,5},{2,0},{3,7},{4,6},{5,1},{6,4},{7,3},{8,10},{9,13},{10,... | collective-permute-start | bytes 884744 | tf_op jit(solution)/shard_map/ppermute | solution.py:126
  172.6 35.6 %collective-permute-start.7 = (bf16[1,256,576]{2,1,0:T(8,128)(2,1)S(1)}, bf16[1,256,576]{2,1,0:T(8,128)(2,1)}, u32[]{:S(2)}, u32[]{:S(2)}) collective-permute-start(bf16[1,256,576]{2,1,0:T(8,128)(2,1)S(1)} %broadcast_in_dim.274), channel_id=1, source_target_pairs={{0,1},{1,0},{2,3},{3,2},{4,5},{5,4},{6,7},{7,6},{8,9},{9,8},{10,11... | collective-permute-start | bytes 884744 | tf_op jit(solution)/shard_map/ppermute | solution.py:116
  204.1 224.4 %reduce-scatter.20.cloned.1.call-start = ((), (), s32[]{:S(2)}) async-start(), calls=%async_computation.25 | async-start | bytes 4325376 | tf_op jit(solution)/shard_map/reduce_scatter | solution.py:94
  282.2 177.1 %reduce-scatter.16.cloned.1.call-start = ((), (), s32[]{:S(2)}) async-start(), calls=%async_computation.23 | async-start | bytes 4325376 | tf_op jit(solution)/shard_map/reduce_scatter | solution.py:94
  295.9 279.4 %all-gather.19.cloned.1.call-start = ((), (), s32[]{:S(2)}) async-start(), calls=%async_computation.42 | async-start | bytes 8650752 | tf_op jit(solution)/shard_map/all_gather | solution.py:108
  341.0 87.5 %collective-permute-start.15 = (bf16[256,2048]{1,0:T(8,128)(2,1)}, bf16[256,2048]{1,0:T(8,128)(2,1)}, u32[]{:S(2)}, u32[]{:S(2)}) collective-permute-start(bf16[256,2048]{1,0:T(8,128)(2,1)} %multiply_convert_fusion.13), channel_id=1, source_target_pairs={{0,16},{8,24},{16,0},{24,8},{1,17},{9,25},{17,1},{25,9},{2,18},{10... | collective-permute-start | bytes 3145736 | tf_op jit(solution)/shard_map/ppermute | solution.py:77
  432.3 227.9 %all-gather.17.cloned.1.call-start = ((), (), s32[]{:S(2)}) async-start(), calls=%async_computation.41 | async-start | bytes 8650752 | tf_op jit(solution)/shard_map/all_gather | solution.py:108
  463.3 335.8 %all-gather.21.cloned.1.call-start = ((), (), s32[]{:S(2)}) async-start(), calls=%async_computation.43 | async-start | bytes 8650752 | tf_op jit(solution)/shard_map/all_gather | solution.py:108
  506.2 48.8 %collective-permute-start.19 = (bf16[2,2,256,2048]{3,2,1,0:T(8,128)(2,1)}, bf16[2,2,256,2048]{3,2,1,0:T(8,128)(2,1)}, u32[]{:S(2)}, u32[]{:S(2)}) collective-permute-start(bf16[2,2,256,2048]{3,2,1,0:T(8,128)(2,1)} %pad_maximum_fusion.3), channel_id=1, source_target_pairs={{0,4},{1,3},{2,6},{3,1},{4,0},{5,7},{6,2},{7,5},{8,12},{9,11},{10,... | collective-permute-start | bytes 12582920 | tf_op jit(solution)/shard_map/ppermute | solution.py:126
  515.9 43.8 %all-to-all-start.3 = ((bf16[4,640,256]{2,1,0:T(8,128)(2,1)}), bf16[4,640,256]{2,1,0:T(8,128)(2,1)}, u32[]{:S(2)}, u32[]{:S(2)}) async-start(bf16[4,640,256]{2,1,0:T(8,128)(2,1)} %bitcast.74), calls=%async_computation.5 | async-start | bytes 2621440 | tf_op jit(solution)/shard_map/all_to_all | solution.py:223
  520.3 468.5 %all-gather.11.cloned.1.call-start = ((), (), s32[]{:S(2)}) async-start(), calls=%async_computation.26 | async-start | bytes 1802240 | tf_op jit(solution)/shard_map/all_gather | solution.py:193
  522.3 44.3 %collective-permute-start.16 = (bf16[1,2,256,2048]{3,2,1,0:T(8,128)(2,1)}, bf16[1,2,256,2048]{3,2,1,0:T(8,128)(2,1)}, u32[]{:S(2)}, u32[]{:S(2)}) collective-permute-start(bf16[1,2,256,2048]{3,2,1,0:T(8,128)(2,1)} %get-tuple-element.764), channel_id=1, source_target_pairs={{0,1},{1,0},{2,3},{3,2},{4,5},{5,4},{6,7},{7,6},{8,9},{9,8},{10,11... | collective-permute-start | bytes 6291464 | tf_op jit(solution)/shard_map/ppermute | solution.py:116
  522.4 472.8 %all-gather.13.cloned.1.call-start = ((), (), s32[]{:S(2)}) async-start(), calls=%async_computation.27 | async-start | bytes 3604480 | tf_op jit(solution)/shard_map/all_gather | solution.py:193
  555.0 31.7 %collective-permute-start.20 = (bf16[2,2,256,2048]{3,2,1,0:T(8,128)(2,1)}, bf16[2,2,256,2048]{3,2,1,0:T(8,128)(2,1)}, u32[]{:S(2)}, u32[]{:S(2)}) collective-permute-start(bf16[2,2,256,2048]{3,2,1,0:T(8,128)(2,1)} %collective-permute-done.19), channel_id=1, source_target_pairs={{0,1},{1,0},{2,3},{3,2},{4,5},{5,4},{6,7},{7,6},{8,9},{9,8},{10,11... | collective-permute-start | bytes 12582920 | tf_op jit(solution)/shard_map/ppermute | solution.py:116
  566.6 46.7 %collective-permute-start.21 = (bf16[2048,256]{1,0:T(8,128)(2,1)}, bf16[2048,256]{1,0:T(8,128)(2,1)}, u32[]{:S(2)}, u32[]{:S(2)}) collective-permute-start(bf16[2048,256]{1,0:T(8,128)(2,1)} %fusion.106), channel_id=1, source_target_pairs={{0,16},{8,24},{16,0},{24,8},{1,17},{9,25},{17,1},{25,9},{2,18},{10... | collective-permute-start | bytes 3145736 | tf_op jit(solution)/shard_map/ppermute | solution.py:77
  566.6 469.2 %reduce-scatter.22.cloned.1.call-start = ((), (), s32[]{:S(2)}) async-start(), calls=%async_computation.28 | async-start | bytes 8650752 | tf_op jit(solution)/shard_map/reduce_scatter | solution.py:112
  624.8 104.3 %collective-permute-start.22 = (bf16[1,2,2048,256]{3,2,1,0:T(8,128)(2,1)}, bf16[1,2,2048,256]{3,2,1,0:T(8,128)(2,1)}, u32[]{:S(2)}, u32[]{:S(2)}) collective-permute-start(bf16[1,2,2048,256]{3,2,1,0:T(8,128)(2,1)} %get-tuple-element.762), channel_id=1, source_target_pairs={{0,1},{1,0},{2,3},{3,2},{4,5},{5,4},{6,7},{7,6},{8,9},{9,8},{10,11... | collective-permute-start | bytes 6291464 | tf_op jit(solution)/shard_map/ppermute | solution.py:116
  654.3 48.8 %collective-permute-start.25 = (bf16[2,2,2048,256]{3,2,1,0:T(8,128)(2,1)}, bf16[2,2,2048,256]{3,2,1,0:T(8,128)(2,1)}, u32[]{:S(2)}, u32[]{:S(2)}) collective-permute-start(bf16[2,2,2048,256]{3,2,1,0:T(8,128)(2,1)} %pad_maximum_fusion.4), channel_id=1, source_target_pairs={{0,4},{1,3},{2,6},{3,1},{4,0},{5,7},{6,2},{7,5},{8,12},{9,11},{10,... | collective-permute-start | bytes 12582920 | tf_op jit(solution)/shard_map/ppermute | solution.py:126
  703.1 36.8 %collective-permute-start.26 = (bf16[2,2,2048,256]{3,2,1,0:T(8,128)(2,1)}, bf16[2,2,2048,256]{3,2,1,0:T(8,128)(2,1)}, u32[]{:S(2)}, u32[]{:S(2)}) collective-permute-start(bf16[2,2,2048,256]{3,2,1,0:T(8,128)(2,1)} %collective-permute-done.25), channel_id=1, source_target_pairs={{0,1},{1,0},{2,3},{3,2},{4,5},{5,4},{6,7},{7,6},{8,9},{9,8},{10,11... | collective-permute-start | bytes 12582920 | tf_op jit(solution)/shard_map/ppermute | solution.py:116
  868.5 356.4 %reduce-scatter.24.cloned.1.call-start = ((), (), s32[]{:S(2)}) async-start(), calls=%async_computation.29 | async-start | bytes 8650752 | tf_op jit(solution)/shard_map/reduce_scatter | solution.py:112
  933.3 47.3 %collective-permute-start.27 = (bf16[4,256,2048]{2,1,0:T(8,128)(2,1)}, bf16[4,256,2048]{2,1,0:T(8,128)(2,1)}, u32[]{:S(2)}, u32[]{:S(2)}) collective-permute-start(bf16[4,256,2048]{2,1,0:T(8,128)(2,1)} %pad_maximum_fusion.5), channel_id=1, source_target_pairs={{0,1},{1,0},{2,3},{3,2},{4,5},{5,4},{6,7},{7,6},{8,9},{9,8},{10,11... | collective-permute-start | bytes 12582920 | tf_op jit(solution)/shard_map/ppermute | solution.py:116
  957.3 422.8 %reduce-scatter.28.cloned.1.call-start = ((), (), s32[]{:S(2)}) async-start(), calls=%async_computation.31 | async-start | bytes 8650752 | tf_op jit(solution)/shard_map/reduce_scatter | solution.py:112
  1080.0 48.6 %collective-permute-start.33 = (bf16[256,2048]{1,0:T(8,128)(2,1)}, bf16[256,2048]{1,0:T(8,128)(2,1)}, u32[]{:S(2)}, u32[]{:S(2)}) collective-permute-start(bf16[256,2048]{1,0:T(8,128)(2,1)} %add_bitcast_fusion.2), channel_id=1, source_target_pairs={{0,16},{8,24},{16,0},{24,8},{1,17},{9,25},{17,1},{25,9},{2,18},{10... | collective-permute-start | bytes 3145736 | tf_op jit(solution)/shard_map/ppermute | solution.py:77
  1085.2 458.8 %reduce-scatter.44.cloned.1.call-start = ((), (), s32[]{:S(2)}) async-start(), calls=%async_computation.39 | async-start | bytes 409600 | tf_op jit(solution)/shard_map/reduce_scatter | solution.py:202
  1170.5 37.6 %collective-permute-start.37 = (bf16[2,256,2048]{2,1,0:T(8,128)(2,1)}, bf16[2,256,2048]{2,1,0:T(8,128)(2,1)}, u32[]{:S(2)}, u32[]{:S(2)}) collective-permute-start(bf16[2,256,2048]{2,1,0:T(8,128)(2,1)} %pad_maximum_fusion.19), channel_id=1, source_target_pairs={{0,4},{1,3},{2,6},{3,1},{4,0},{5,7},{6,2},{7,5},{8,12},{9,11},{10,... | collective-permute-start | bytes 6291464 | tf_op jit(solution)/shard_map/ppermute | solution.py:126
  1348.5 322.5 %reduce-scatter.36.cloned.1.call-start = ((), (), s32[]{:S(2)}) async-start(), calls=%async_computation.35 | async-start | bytes 1802240 | tf_op jit(solution)/shard_map/reduce_scatter | solution.py:202
  1356.8 314.2 %reduce-scatter.34.cloned.1.call-start = ((), (), s32[]{:S(2)}) async-start(), calls=%async_computation.34 | async-start | bytes 3604480 | tf_op jit(solution)/shard_map/reduce_scatter | solution.py:202
  1367.7 303.3 %reduce-scatter.40.cloned.1.call-start = ((), (), s32[]{:S(2)}) async-start(), calls=%async_computation.37 | async-start | bytes 655360 | tf_op jit(solution)/shard_map/reduce_scatter | solution.py:202
  1372.8 298.2 %reduce-scatter.42.cloned.1.call-start = ((), (), s32[]{:S(2)}) async-start(), calls=%async_computation.38 | async-start | bytes 1310720 | tf_op jit(solution)/shard_map/reduce_scatter | solution.py:202
  1380.1 291.0 %reduce-scatter.26.cloned.1.call-start = ((), (), s32[]{:S(2)}) async-start(), calls=%async_computation.30 | async-start | bytes 4325376 | tf_op jit(solution)/shard_map/reduce_scatter | solution.py:94
  1397.6 306.1 %reduce-scatter.30.cloned.1.call-start = ((), (), s32[]{:S(2)}) async-start(), calls=%async_computation.32 | async-start | bytes 4325376 | tf_op jit(solution)/shard_map/reduce_scatter | solution.py:94
  1406.4 371.1 %reduce-scatter.32.cloned.1.call-start = ((), (), s32[]{:S(2)}) async-start(), calls=%async_computation.33 | async-start | bytes 4325376 | tf_op jit(solution)/shard_map/reduce_scatter | solution.py:94
  1439.6 48.8 %collective-permute-start.40 = (bf16[2,2,256,2048]{3,2,1,0:T(8,128)(2,1)}, bf16[2,2,256,2048]{3,2,1,0:T(8,128)(2,1)}, u32[]{:S(2)}, u32[]{:S(2)}) collective-permute-start(bf16[2,2,256,2048]{3,2,1,0:T(8,128)(2,1)} %slice.856), channel_id=1, source_target_pairs={{0,4},{1,3},{2,6},{3,1},{4,0},{5,7},{6,2},{7,5},{8,12},{9,11},{10,... | collective-permute-start | bytes 12582920 | tf_op jit(solution)/shard_map/ppermute | solution.py:126
  1440.5 373.6 %reduce-scatter.38.cloned.1.call-start = ((), (), s32[]{:S(2)}) async-start(), calls=%async_computation.36 | async-start | bytes 1966080 | tf_op jit(solution)/shard_map/reduce_scatter | solution.py:202
  1450.8 72.5 %collective-permute-start.44 = (bf16[2,256,2048]{2,1,0:T(8,128)(2,1)S(1)}, bf16[2,256,2048]{2,1,0:T(8,128)(2,1)}, u32[]{:S(2)}, u32[]{:S(2)}) collective-permute-start(bf16[2,256,2048]{2,1,0:T(8,128)(2,1)S(1)} %slice.867), channel_id=1, source_target_pairs={{0,4},{1,3},{2,6},{3,1},{4,0},{5,7},{6,2},{7,5},{8,12},{9,11},{10,... | collective-permute-start | bytes 6291464 | tf_op jit(solution)/shard_map/ppermute | solution.py:126
  1496.0 36.7 %collective-permute-start.41 = (bf16[1,2,256,2048]{3,2,1,0:T(8,128)(2,1)}, bf16[1,2,256,2048]{3,2,1,0:T(8,128)(2,1)}, u32[]{:S(2)}, u32[]{:S(2)}) collective-permute-start(bf16[1,2,256,2048]{3,2,1,0:T(8,128)(2,1)} %slice.858), channel_id=1, source_target_pairs={{0,2},{1,5},{2,0},{3,7},{4,6},{5,1},{6,4},{7,3},{8,10},{9,13},{10,... | collective-permute-start | bytes 6291464 | tf_op jit(solution)/shard_map/ppermute | solution.py:126
  1536.2 85.0 %collective-permute-start.42 = (bf16[256,2048]{1,0:T(8,128)(2,1)}, bf16[256,2048]{1,0:T(8,128)(2,1)}, u32[]{:S(2)}, u32[]{:S(2)}) collective-permute-start(bf16[256,2048]{1,0:T(8,128)(2,1)} %fusion.185), channel_id=1, source_target_pairs={{0,16},{8,24},{16,0},{24,8},{1,17},{9,25},{17,1},{25,9},{2,18},{10... | collective-permute-start | bytes 3145736 | tf_op jit(solution)/shard_map/ppermute | solution.py:77
  1545.0 91.1 %collective-permute-start.61 = (bf16[1,64,576]{2,1,0:T(8,128)(2,1)}, bf16[1,64,576]{2,1,0:T(8,128)(2,1)S(1)}, u32[]{:S(2)}, u32[]{:S(2)}) collective-permute-start(bf16[1,64,576]{2,1,0:T(8,128)(2,1)} %bitcast.704), channel_id=1, source_target_pairs={{0,2},{1,5},{2,0},{3,7},{4,6},{5,1},{6,4},{7,3},{8,10},{9,13},{10,... | collective-permute-start | bytes 221192 | tf_op jit(solution)/shard_map/ppermute | solution.py:126
  1545.9 92.8 %collective-permute-start.60 = (bf16[1,64,576]{2,1,0:T(8,128)(2,1)}, bf16[1,64,576]{2,1,0:T(8,128)(2,1)S(1)}, u32[]{:S(2)}, u32[]{:S(2)}) collective-permute-start(bf16[1,64,576]{2,1,0:T(8,128)(2,1)} %bitcast.705), channel_id=1, source_target_pairs={{0,1},{1,0},{2,3},{3,2},{4,5},{5,4},{6,7},{7,6},{8,9},{9,8},{10,11... | collective-permute-start | bytes 221192 | tf_op jit(solution)/shard_map/ppermute | solution.py:116
  1551.3 69.9 %collective-permute-start.50 = (f32[4608]{0:T(1024)S(1)}, f32[4608]{0:T(1024)S(1)}, u32[]{:S(2)}, u32[]{:S(2)}) collective-permute-start(f32[4608]{0:T(1024)S(1)} %fusion.251), channel_id=1, source_target_pairs={{0,2},{1,3},{2,0},{3,1},{4,6},{5,7},{6,4},{7,5},{8,10},{9,11},{10,... | collective-permute-start | bytes 55304 | tf_op jit(solution)/shard_map/ppermute | solution.py:116
  1646.7 170.6 %all-to-all-start.4 = ((bf16[256,8,256]{2,0,1:T(8,128)(2,1)}), bf16[256,8,256]{2,0,1:T(8,128)(2,1)}, u32[]{:S(2)}, u32[]{:S(2)}) async-start(bf16[256,8,256]{2,0,1:T(8,128)(2,1)} %bitcast.654), calls=%async_computation.9 | async-start | bytes 2097152 | tf_op jit(solution)/shard_map/all_to_all | solution.py:603
  1823.6 36.1 %all-to-all-start.5 = ((bf16[4,640,256]{2,1,0:T(8,128)(2,1)}), bf16[4,640,256]{2,1,0:T(8,128)(2,1)}, u32[]{:S(2)}, u32[]{:S(2)}) async-start(bf16[4,640,256]{2,1,0:T(8,128)(2,1)} %bitcast.695), calls=%async_computation.10 | async-start | bytes 2621440 | tf_op jit(solution)/shard_map/all_to_all | solution.py:223
  1859.7 35.3 %all-to-all-start.7 = ((bf16[4,640,256]{2,1,0:T(8,128)(2,1)}), bf16[4,640,256]{2,1,0:T(8,128)(2,1)}, u32[]{:S(2)}, u32[]{:S(2)}) async-start(bf16[4,640,256]{2,1,0:T(8,128)(2,1)} %bitcast.694), calls=%async_computation.12 | async-start | bytes 2621440 | tf_op jit(solution)/shard_map/all_to_all | solution.py:223
  (243 other events, 4357.1 us)
Sparse Core Ops, SparseCore 0:
  98.0 67.3 all-gather.14
  204.2 70.1 reduce-scatter.17
  282.3 100.9 reduce-scatter.19
  386.0 73.3 reduce-scatter.15
  461.4 94.5 all-gather.18
  558.0 96.9 all-gather.16
  656.6 73.6 all-gather.20
  731.9 34.9 all-gather.10
  769.1 58.0 all-gather.12
  868.6 71.5 reduce-scatter.21
  957.4 71.5 reduce-scatter.23
  1085.3 92.2 reduce-scatter.27
  1348.6 20.0 reduce-scatter.43
  1370.9 31.4 reduce-scatter.35
  1405.1 55.0 reduce-scatter.33
  1462.9 21.3 reduce-scatter.39
  1486.4 25.5 reduce-scatter.41
  1514.2 115.8 reduce-scatter.25
  1632.4 71.2 reduce-scatter.29
  1705.9 71.5 reduce-scatter.31
  1779.8 34.2 reduce-scatter.37

commit v9 on v5

--- a/solution.py
+++ b/solution.py
@@ -84,35 +84,39 @@
     return [1 << b for b in range((lax.axis_size("row") // 2).bit_length() - 1)]
 
 
-def expert_gather(kept, given, axis, hold):
+def half_pieces(first, item):
+    items = {first: item}
+    for bit in half_bits():
+        items.update({key ^ bit: row_swap(items[key], bit) for key in list(items)})
+    return items
+
+
+def placed(pieces, start, width):
+    index = lax.axis_index("row")
+    rows = pieces[0].shape[0]
+    out = jnp.zeros((rows * lax.axis_size("row"), width), pieces[0].dtype)
+    for key, piece in pieces.items():
+        out = lax.dynamic_update_slice_in_dim(
+            out, piece[:, start : start + width], jnp.bitwise_xor(index, key) * rows, 0
+        )
+    return out
+
+
+def expert_scatter(values, holds):
     count = lax.axis_size("row")
     index = lax.axis_index("row")
-    width = kept.shape[axis]
-    shape = list(kept.shape)
-    shape[axis] = width * count
-    out = jnp.zeros(shape, kept.dtype)
-    (arrived,) = after((mate(given),), hold)
-    for first, item in ((count // 2, arrived), (0, kept)):
-        items = {first: item}
-        for bit in half_bits():
-            new = after([row_swap(items[key], bit) for key in items], hold)
-            items.update({key ^ bit: piece for key, piece in zip(list(items), new)})
-        for key, piece in items.items():
-            out = lax.dynamic_update_slice_in_dim(
-                out, piece, jnp.bitwise_xor(index, key) * width, axis
-            )
-    return out
-
-
-def expert_scatter(value, axis, holds):
-    count = lax.axis_size("row")
-    index = lax.axis_index("row")
-    width = value.shape[axis] // count
+    rows = values[0].shape[0] // count
     sums = []
     for first, hold in zip((count // 2, 0), holds):
         items = {
-            key: lax.dynamic_slice_in_dim(
-                value, jnp.bitwise_xor(index, key ^ first) * width, width, axis
+            key: jnp.concatenate(
+                [
+                    lax.dynamic_slice_in_dim(
+                        value, jnp.bitwise_xor(index, key ^ first) * rows, rows, 0
+                    )
+                    for value in values
+                ],
+                axis=1,
             )
             for key in range(count // 2)
         }
@@ -175,16 +179,16 @@
     return out
 
 
-def cube_scatter(value):
+def cube_scatter(value, axis=0):
     count = lax.axis_size("col")
     index = lax.axis_index("col")
-    rows = value.shape[0] // count
+    rows = value.shape[axis] // count
     value = row_major(value)
 
     def blocks(device):
         return jnp.stack(
             [
-                lax.dynamic_slice_in_dim(value, block_at(device, place) * rows, rows, 0)
+                lax.dynamic_slice_in_dim(value, block_at(device, place) * rows, rows, axis)
                 for place in range(count // 2)
             ]
         )
@@ -226,12 +230,12 @@
     return (index[:, None] == jnp.arange(width, dtype=jnp.int32)[None, :]).astype(BF16)
 
 
-def exchange(value, sent_of, slot_of, hold=()):
+def exchange(value, sent_of, slot_of):
     count = lax.axis_size("row")
     sent = row_major(dot(onehot(sent_of, value.shape[0]), value).astype(BF16))
     sent = sent.reshape(count, -1, value.shape[1])
     got = lax.all_to_all(sent, "row", split_axis=0, concat_axis=0, tiled=True)
-    (got,) = after((got.reshape(-1, value.shape[1]),), hold)
+    got = got.reshape(-1, value.shape[1])
     return row_major(dot(onehot(slot_of, got.shape[0]), got).astype(BF16))
 
 
@@ -326,55 +330,59 @@
         (jnp.int32(1), jnp.zeros((group_rows, 2 * slice_width), BF16)),
     )[1]
     dealt_x = exchange(tokens, out_list, in_slots) + more[:, :slice_width]
+    dealt_x, mate_routes, mate_gates = after((dealt_x, mate(routes), mate(gate_weights)), ())
     routes_late, gates_late = after((routes, gate_weights), (dealt_x,))
     pick, weight = chosen(routes_late, gates_late)
-    mate_pick, mate_weight = chosen(mate(routes_late), mate(gates_late))
+    mate_pick, mate_weight = chosen(mate_routes, mate_gates)
     full_x = cube_gather(dealt_x, 1)
 
     query_width = w_query.shape[1]
     lat_rows = rows_in // col_count
     w_latent_s = lax.dynamic_slice_in_dim(w_latent, col_index * lat_rows, lat_rows, 0)
-    lat_wide = w_latent.shape[1]
-    first_s = jnp.concatenate(
-        [
-            w_query,
-            w_latent_s.reshape(-1, query_width),
-            jnp.concatenate([attn_gain, ffn_gain, latent_gain]).reshape(-1, query_width),
-        ],
-        axis=0,
-    )
+    parts = [
+        w_query,
+        w_latent_s.reshape(-1, query_width),
+        jnp.concatenate([w_output, w_expand], axis=0).reshape(-1, query_width),
+        jnp.concatenate([attn_gain, ffn_gain, latent_gain]).reshape(-1, query_width),
+    ]
+    first_s = jnp.concatenate(parts, axis=0)
     first_s = jnp.pad(first_s, ((0, -first_s.shape[0] % 16), (0, 0)))
     (first_s,) = after((first_s,), (dealt_x,))
     first_w = row_gather(first_s[None], 0)
-    query_w = first_w[:, :rows_in].reshape(dim, query_width)
-    lat_end = rows_in + lat_rows * lat_wide // query_width
-    latent_w = cube_gather(first_w[:, rows_in:lat_end].reshape(row_count * lat_rows, lat_wide), 0)
-    latent_w = latent_w.reshape(col_count, row_count, lat_rows, lat_wide).transpose(1, 0, 2, 3)
-    latent_w = latent_w.reshape(dim, lat_wide)
-    gains = first_w[:, lat_end:].reshape(row_count, -1)
+    pieces, start = [], 0
+    for part in parts:
+        pieces.append(first_w[:, start : start + part.shape[0]])
+        start += part.shape[0]
+    query_w = pieces[0].reshape(dim, query_width)
+    latent_w = cube_gather(pieces[1].reshape(row_count * lat_rows, w_latent.shape[1]), 0)
+    latent_w = latent_w.reshape(col_count, row_count, lat_rows, -1).transpose(1, 0, 2, 3)
+    latent_w = latent_w.reshape(dim, w_latent.shape[1])
+    out_rows, out_width = w_output.shape
+    rest_w = pieces[2].reshape(row_count, -1, out_width)
+    output_w = rest_w[:, :out_rows].transpose(1, 0, 2).reshape(out_rows, dim)
+    expand_w = rest_w[:, out_rows:].reshape(-1, out_width)
+    gains = pieces[3].reshape(row_count, -1)
     gain_one = gains[:, :wide].reshape(-1).astype(F32)
     gain_two = gains[:, wide : 2 * wide].reshape(-1).astype(F32)
-    latent_g = gains[:, 2 * wide : 2 * wide + latent_gain.shape[0]].reshape(-1).astype(F32)
-
-    out_rows = w_output.shape[0]
-    rest_s = jnp.concatenate([w_output.reshape(-1, w_expand.shape[1]), w_expand])
-    (rest_s,) = after((rest_s,), (dealt_x,))
-    rest_w = row_gather(rest_s[None], 0)
-    out_count = w_output.size // w_expand.shape[1]
-    output_w = rest_w[:, :out_count].reshape(row_count, out_rows, -1)
-    output_w = output_w.transpose(1, 0, 2).reshape(out_rows, dim)
-    expand_w = rest_w[:, out_count:].reshape(-1, w_expand.shape[1])
-
-    def of_expert(value, number):
-        return lax.dynamic_index_in_dim(value, number, 0, False)
-
-    def both_parts(number):
-        return jnp.concatenate([of_expert(expert_gate, number), of_expert(expert_up, number)], 1)
-
-    gate_up_parts = after((both_parts(host), both_parts(1 - host)), (first_w,))
-    down_parts = after(
-        (of_expert(expert_down, host), of_expert(expert_down, 1 - host)), (first_w, rest_w)
-    )
+    latent_g = gains[:, 2 * wide :].reshape(-1).astype(F32)
+
+    (cotangent_s,) = after((cotangent,), (dealt_x,))
+    dealt_dy = exchange(cotangent_s, out_list, in_slots) + more[:, slice_width:]
+
+    def expert_part(number):
+        parts = [lax.dynamic_index_in_dim(v, number, 0, False) for v in (expert_gate, expert_up)]
+        down = lax.dynamic_index_in_dim(expert_down, number, 0, False)
+        return jnp.concatenate(parts + [down.T], axis=1)
+
+    kept, given = after((expert_part(host), expert_part(1 - host)), (first_w,))
+    width_ff = expert_gate.shape[2]
+    kept_pieces = half_pieces(0, kept)
+    mate_gu, mate_down = mate(given[:, : 2 * width_ff]), mate(given[:, 2 * width_ff :])
+    shared_gu_s, shared_d_s = after(
+        (jnp.concatenate([shared_gate, shared_up], axis=1), shared_down), (first_w,)
+    )
+    shared_gu_w = row_gather(shared_gu_s, 0)
+    shared_d_w = row_gather(shared_d_s, 1)
 
     head_count = query_w.shape[1] // (NOPE + ROPE)
     softmax_scale = (NOPE + ROPE) ** (-0.5)
@@ -383,12 +391,14 @@
     residual = full_x.astype(F32)
     scale_one = lax.rsqrt(jnp.mean(residual * residual, axis=-1, keepdims=True) + EPSILON)
     normed_one = (residual * scale_one * gain_one).astype(BF16)
-    (cotangent_s,) = after((cotangent,), (normed_one,))
     query_raw = dot(normed_one, query_w)
     query_raw = query_raw.reshape(group_rows, head_count, NOPE + ROPE)
     query_heads = jnp.concatenate(
         [query_raw[..., :NOPE], rotate(query_raw[..., NOPE:], position, 1.0)], axis=-1
     ).astype(BF16)
+    keys = sorted(kept_pieces)
+    query_heads, *pieces = after([query_heads] + [kept_pieces[key] for key in keys], ())
+    kept_pieces = dict(zip(keys, pieces))
     latent = dot(normed_one, latent_w)
     latent_front = latent[:, :LAT]
     scale_lat = lax.rsqrt(jnp.mean(latent_front * latent_front, axis=-1, keepdims=True) + EPSILON)
@@ -405,8 +415,6 @@
         axis=-1,
     )
     value_heads = expanded[..., NOPE:]
-    dealt_dy = exchange(cotangent_s, out_list, in_slots, (expanded,)) + more[:, slice_width:]
-    full_dy = cube_gather(dealt_dy, 1)
 
     def block_scores(first_row, last_row):
         raw_scores = (
@@ -444,7 +452,17 @@
     mixed = (
         jnp.concatenate(mixed_blocks, axis=0).reshape(group_rows, head_count * VDIM).astype(BF16)
     )
-    attn_part = cube_scatter(dot(mixed, output_w).astype(BF16))
+    attn_terms, mate_down = after((dot(mixed, output_w).astype(BF16), mate_down), ())
+    attn_part = cube_scatter(attn_terms)
+    dy_pair = after((dealt_dy, mate(dealt_dy)), (attn_part,))
+    both_dy = cube_gather(jnp.concatenate(dy_pair, axis=0), 1)
+    full_dy, mate_dy = both_dy[:group_rows], both_dy[group_rows:]
+    mate_down, mate_gu = after((mate_down, mate_gu), (attn_part,))
+    down_pieces = half_pieces(row_count // 2, mate_down)
+    gu_pieces = half_pieces(row_count // 2, mate_gu)
+    kept_down = {key: piece[:, 2 * width_ff :] for key, piece in kept_pieces.items()}
+    gate_up_w = placed({**kept_pieces, **gu_pieces}, 0, 2 * width_ff)
+    down_t = placed({**kept_down, **down_pieces}, 0, width_ff)
     x_part = my_part(full_x).astype(F32)
     hidden_part = x_part + attn_part
     scale_two = lax.rsqrt(jnp.mean(hidden_part * hidden_part, axis=-1, keepdims=True) + EPSILON)
@@ -454,15 +472,6 @@
     normed_two = cube_gather(normed_part, 0)
     (mate_part,) = after((mate_part,), (normed_two,))
     mate_two = cube_gather(mate_part, 0)
-    (dealt_mate_dy,) = after((mate(dealt_dy),), (normed_part,))
-    mate_dy = cube_gather(dealt_mate_dy, 1)
-    gate_up_w = expert_gather(*gate_up_parts, 0, (normed_part,))
-    down_w = expert_gather(*down_parts, 1, (normed_part,))
-    shared_gu_s, shared_d_s = after(
-        (jnp.concatenate([shared_gate, shared_up], axis=1), shared_down), (normed_part,)
-    )
-    shared_gu_w = row_gather(shared_gu_s, 0)
-    shared_d_w = row_gather(shared_d_s, 1)
 
     place_late, rank_late, here_late, source_late, my_rank_late = after(
         (place_in, rank_here, from_here, my_source, my_rank), (normed_part,)
@@ -498,8 +507,15 @@
             [(grad_hidden * up_slope).astype(BF16), (grad_hidden * act).astype(BF16)], axis=1
         )
 
-    def queued_sum(value, axis):
+    def row_sum(value, axis):
         return row_scatter(value.astype(BF16), axis)
+
+    shared_hidden, shared_act, shared_us = forward(normed_two, shared_gu_w)
+    grad_shared_gu = backward(dot_nt(full_dy, shared_d_w), shared_act, shared_us)
+    grad_two = dot_nt(grad_shared_gu, shared_gu_w)
+    moe_terms = dot(shared_hidden, shared_d_w)
+    grad_sgu = row_sum(dot_tn(normed_two, grad_shared_gu), 0)
+    grad_sd = row_sum(dot_tn(shared_hidden, full_dy), 1)
 
     rows = jnp.concatenate(
         [dot(pick, normed_two).astype(BF16), dot(mate_pick, mate_two).astype(BF16)], axis=0
@@ -512,43 +528,31 @@
         axis=0,
     )
     hidden, act, up_slope = forward(rows, gate_up_w)
-    grad_gate_up = backward(dot_nt(grad_result, down_w), act, up_slope)
+    grad_gate_up = backward(dot(grad_result, down_t), act, up_slope)
     mate_rows = dot_nt(grad_gate_up[capacity:], gate_up_w).astype(BF16)
     mate_grad = dot_tn(mate_pick, mate_rows).astype(BF16)
-    mate_grad_part = mate(cube_scatter(mate_grad).astype(BF16))
-    own_gate_up, normed_s, dy_s = after(
-        (grad_gate_up[:capacity], normed_two, full_dy), (mate_grad,)
-    )
+    (own_gate_up,) = after((grad_gate_up[:capacity],), (mate_grad,))
     own_rows = dot_nt(own_gate_up, gate_up_w).astype(BF16)
-    shared_hidden, shared_act, shared_us = forward(normed_s, shared_gu_w)
-    grad_shared_gu = backward(dot_nt(dy_s, shared_d_w), shared_act, shared_us)
-    grad_two = dot_nt(grad_shared_gu, shared_gu_w)
     grad_two = (grad_two + dot_tn(pick, own_rows)).astype(BF16)
-    grad_two_part = cube_scatter(grad_two)
-    late = after((rows, grad_gate_up, hidden, grad_result), (grad_two,))
-    grad_gu = dot_tn(late[0], late[1]).astype(BF16)
-    grad_down = dot_tn(late[2], late[3]).astype(BF16)
-    late = after((normed_two, grad_shared_gu, shared_hidden, full_dy), (grad_two,))
-    grad_sgu = queued_sum(dot_tn(late[0], late[1]), 0)
-    grad_sd = queued_sum(dot_tn(late[2], late[3]), 1)
-
-    (mate_grad_part,) = after((mate_grad_part,), (grad_two_part,))
-    grad_two_part = grad_two_part + mate_grad_part.astype(F32)
+    mate_grad = mate(cube_scatter(mate_grad).astype(BF16))
+    grad_gu = dot_tn(rows, grad_gate_up).astype(BF16)
+    grad_down = dot_tn(grad_result, hidden).astype(BF16)
+
+    grad_two_part = cube_scatter(grad_two) + mate_grad.astype(F32)
     dy_part = my_part(full_dy).astype(F32)
     hidden_back, gain_two_grad = norm_back(grad_two_part, unit_two, scale_two, gain_two)
     grad_hidden_part = dy_part + hidden_back
     grad_attn = cube_gather(grad_hidden_part.astype(BF16), 0)
 
-    hidden_late, shared_late = after((hidden, shared_hidden), (grad_hidden_part,))
+    (hidden_late,) = after((hidden,), (grad_hidden_part,))
     weights = jnp.concatenate([weight, mate_weight])
-    result_rows = (weights[:, None] * dot(hidden_late, down_w)).astype(BF16)
+    result_rows = (weights[:, None] * dot_nt(hidden_late, down_t)).astype(BF16)
     mate_terms = dot_tn(mate_pick, result_rows[capacity:]).astype(BF16)
-    moe_terms = dot(shared_late, shared_d_w) + dot_tn(pick, result_rows[:capacity])
-    mate_terms, moe_terms = after((mate_terms, moe_terms.astype(BF16)), (grad_attn,))
-    mate_terms = mate(cube_scatter(mate_terms).astype(BF16))
-    moe_part = cube_scatter(moe_terms)
-
-    grad_output_w = queued_sum(dot_tn(mixed, grad_attn), 1)
+    moe_terms = (moe_terms + dot_tn(pick, result_rows[:capacity])).astype(BF16)
+    (both_terms,) = after((jnp.stack([moe_terms, mate_terms]),), (grad_attn,))
+    both_terms = cube_scatter(both_terms, 1)
+    moe_part, mate_terms = both_terms[0], mate(both_terms[1].astype(BF16))
+
     grad_mixed = dot_nt(grad_attn, output_w).astype(BF16)
     grad_mixed = grad_mixed.reshape(group_rows, head_count, VDIM)
     grad_query_blocks = []
@@ -591,15 +595,19 @@
         .astype(BF16)
         .reshape(group_rows, head_count * (NOPE + ROPE))
     )
+    own_sum, mate_sum = expert_scatter([grad_gu, grad_down], ((grad_attn,), (grad_attn,)))
+    grad_query_raw, mate_sum, grad_sgu, grad_sd = after(
+        (grad_query_raw, mate_sum, grad_sgu, grad_sd), ()
+    )
+    other_gu, other_down = mate(mate_sum[:, : 2 * width_ff]), mate(mate_sum[:, 2 * width_ff :])
     grad_one = dot_nt(grad_query_raw, query_w).astype(BF16)
+    grad_one_part, other_down = after((cube_scatter(grad_one), other_down), ())
 
     mate_terms, moe_part = after((mate_terms, moe_part), (grad_one,))
     result_part = (hidden_part + (moe_part + mate_terms.astype(F32))).astype(BF16)
     result_slice = lax.all_to_all(result_part, "col", split_axis=1, concat_axis=0, tiled=True)
-
-    grad_one = cube_scatter(grad_one)
-    own_gu, mate_gu = expert_scatter(grad_gu, 0, ((grad_attn,), (grad_one,)))
-    own_down, mate_down = expert_scatter(grad_down, 1, ((grad_attn,), (grad_one,)))
+    result = exchange(result_slice, back_list, back_slots)
+
     grad_expanded = jnp.concatenate([grad_keys[..., :NOPE], grad_values], axis=-1).astype(BF16)
     grad_expanded = grad_expanded.reshape(group_rows, head_count * (NOPE + VDIM))
     grad_compressed = dot_nt(grad_expanded, expand_w)
@@ -612,14 +620,13 @@
     )
     grad_latent_part = jnp.concatenate([grad_front, grad_latent_part[:, LAT:]], axis=1).astype(BF16)
     latent_term = dot_nt(grad_latent_part, latent_w)
-    grad_one = grad_one + latent_term
+    grad_one = grad_one_part + latent_term
     scale_one_part = my_part(scale_one)
     input_back, gain_one_grad = norm_back(
         grad_one, x_part * scale_one_part, scale_one_part, gain_one
     )
     grad_input = (grad_hidden_part + input_back).astype(BF16)
     grad_slice = lax.all_to_all(grad_input, "col", split_axis=1, concat_axis=0, tiled=True)
-    result = exchange(result_slice, back_list, back_slots, (grad_input,))
     tokens_grad = exchange(grad_slice, back_list, back_slots)
 
     def more_back(carry):
@@ -635,20 +642,27 @@
     )[1]
     result, tokens_grad = more[:, :slice_width], more[:, slice_width:]
 
-    grad_expand_w = queued_sum(dot_tn(compressed, grad_expanded), 0)
-    grad_query_w = queued_sum(dot_tn(normed_one, grad_query_raw), 0)
+    late = after((normed_one, compressed, mixed), (grad_one,))
+    grad_expand_w = row_sum(dot_tn(late[1], grad_expanded), 0)
+    grad_query_w = row_sum(dot_tn(late[0], grad_query_raw), 0)
+    grad_output_w = row_sum(dot_tn(late[2], grad_attn), 1)
     grad_latent = cube_gather(grad_latent_part, 0)
     my_columns = lax.dynamic_index_in_dim(
-        normed_one.reshape(group_rows, row_count, col_count, lat_rows), col_index, 2, False
+        late[0].reshape(group_rows, row_count, col_count, lat_rows), col_index, 2, False
     ).reshape(group_rows, row_count * lat_rows)
-    grad_latent_w = cube_gather(queued_sum(dot_tn(my_columns, grad_latent), 0), 0)
+    (grad_latent_w,) = after((row_sum(dot_tn(my_columns, grad_latent), 0),), (grad_one_part,))
+    grad_latent_w = cube_gather(grad_latent_w, 0)
+    sums = after(
+        (own_sum, other_gu, other_down, grad_sgu, grad_sd, grad_query_w, grad_expand_w, grad_output_w),
+        (grad_slice,),
+    )
+    own_sum, other_gu, other_down, grad_sgu, grad_sd, grad_query_w, grad_expand_w, grad_output_w = sums
     gain_grads = small_sum(jnp.concatenate([gain_one_grad, gain_two_grad, latent_gain_grad]))
-    width_ff = expert_gate.shape[2]
-    other_gu, other_down = after((mate(mate_gu), mate(mate_down)), (grad_input,))
-
     def in_order(own, other):
         return jnp.stack([jnp.where(host == 0, own, other), jnp.where(host == 0, other, own)])
 
+    expert_gu = in_order(own_sum[:, : 2 * width_ff], other_gu).astype(F32)
+    expert_d = in_order(own_sum[:, 2 * width_ff :].T, other_down.T).astype(F32)
     width_two = gain_one_grad.shape[0]
     width_lat = latent_gain_grad.shape[0]
 
@@ -669,9 +683,9 @@
         grad_sgu[:, : shared_gate.shape[1]].astype(F32),
         grad_sgu[:, shared_gate.shape[1] :].astype(F32),
         grad_sd.astype(F32),
-        in_order(own_gu[:, :width_ff], other_gu[:, :width_ff]).astype(F32),
-        in_order(own_gu[:, width_ff:], other_gu[:, width_ff:]).astype(F32),
-        in_order(own_down, other_down).astype(F32),
+        expert_gu[:, :, :width_ff],
+        expert_gu[:, :, width_ff:],
+        expert_d,
     )
 
 

time: 1950 us -> 1910 us (0.979)
  waiting for transfers between devices: 827 us -> 726 us
  local copies, waits for them, and re-layouts: 278 us -> 340 us
  matrix products: 437 us -> 458 us
    ppermute x3, waiting for transfers between devices: 130 us -> 70.5 us  [small_sum(): lax.ppermute(value, 'row', [(j, (j + k) % count) for j in range(count)])]
    ppermute x18 -> x15, waiting for transfers between devices: 459 us -> 402 us  [row_swap(): lax.ppermute(value, 'row', [(j, j ^ bit) for j in range(lax.axis_size('ro...]
    slice x3 -> x9, local copies, waits for them, and re-layouts: 4.43 us -> 34.5 us  [the longest x1 9.59 us: body(): expert_gu[:, :, width_ff:]]
    ppermute x37 -> x33, waiting for transfers between devices: 10 us -> 40 us  [swap(): lax.ppermute(value, 'col', [(j, j ^ bit) for j in range(lax.axis_size('co...]
    all_gather x4 -> x3, waiting for transfers between devices: 46 us -> 19.8 us  [row_gather(): return lax.all_gather(shard, 'row', axis=axis, tiled=True)]
    dot_general x20, matrix products: 176 us -> 200 us  [dot(): return jnp.dot(left, right, preferred_element_type=F32)]
    unnamed x432 -> x410, local copies, waits for them, and re-layouts: 46.3 us -> 61.6 us
    ppermute x32 -> x28, starting transfers between devices: 39.5 us -> 32.9 us  [chip_swap(): lax.ppermute(value, 'col', [(j, j ^ (other if j % 2 else bits)[step]) for...]
  transfers between devices with their start and end apart: 106 -> 94, of which waited for: 36 -> 31; matrix products, arithmetic and copies ran while one was open for 43% -> 53% of each run, Pallas kernels for 0% -> 0%
where the time goes in v9:
time: 1910 us; the launch traced here: 1900 us
  waiting for transfers between devices  726 us (38%)
  matrix products  458 us (24%)
  local copies, waits for them, and re-layouts  340 us (18%)
  other arithmetic  267 us (14%)
  starting transfers between devices  89.5 us (5%)
    ppermute x15, waiting for transfers between devices, row_swap(): lax.ppermute(value, 'row', [(j, j ^ bit) for j in range(lax.axis_size('ro...  402 us
    dot_general x20, matrix products, dot(): return jnp.dot(left, right, preferred_element_type=F32)  200 us
    dot_general x12, matrix products, dot_tn(): lax.dot_general(left, right, (((0,), (0,)), ((), ())), preferred_element_...  133 us
    ppermute x28, waiting for transfers between devices, chip_swap(): lax.ppermute(value, 'col', [(j, j ^ (other if j % 2 else bits)[step]) for...  121 us
    dot_general x9, matrix products, dot_nt(): lax.dot_general(left, right, (((1,), (1,)), ((), ())), preferred_element_...  90.4 us
    dynamic_update_slice x61, local copies, waits for them, and re-layouts, cube_gather(): lax.dynamic_update_slice_in_dim(out, item, block_at(owner, place) * width...  75.7 us
    ppermute x3, waiting for transfers between devices, small_sum(): lax.ppermute(value, 'row', [(j, (j + k) % count) for j in range(count)])  70.5 us
    unnamed x410, local copies, waits for them, and re-layouts  61.6 us
  transfers between devices with their start and end apart: 94, of which 31 were waited for; matrix products, arithmetic and copies ran while one was open for 53% of the time, Pallas kernels for 0%

profile of v9, /device:TPU:0, one launch (start us, length us, event | category | flops | bytes accessed | tf_op | source)
XLA Modules:
  0.0 1898.7 jit_solution(6259969064187744692)
XLA Ops:
  62.3 18.0 all-to-all-done.2
  121.6 9.5 collective-permute-done.5
  134.6 19.8 %all-gather.9.cloned.1.call-done = bf16[4544,384]{1,0:T(8,128)(2,1)} async-done(((bf16[1136,384]{1,0:T(8,128)(2,1)}), bf16[4544,384]{1,0:T(8,128)(2,1)}) %all-gather.9.cloned.1.call-update) | async-done | bytes 3489808 | tf_op jit(solution)/shard_map/all_gather | solution.py:207
  220.7 10.0 fusion.284
  251.9 85.1 %collective-permute-done.7 = bf16[512,4224]{1,0:T(8,128)(2,1)} collective-permute-done((bf16[512,4224]{1,0:T(8,128)(2,1)}, bf16[512,4224]{1,0:T(8,128)(2,1)}, u32[]{:S(2)}, u32[]{:S(2)}) %collective-permute-start.7) | collective-permute-done | bytes 4325408 | tf_op jit(solution)/shard_map/ppermute | solution.py:76
  374.5 27.8 %all-to-all-done.3 = bf16[4,640,256]{2,1,0:T(8,128)(2,1)} async-done(((bf16[4,640,256]{2,1,0:T(8,128)(2,1)}), bf16[4,640,256]{2,1,0:T(8,128)(2,1)}, u32[]{:S(2)}, u32[]{:S(2)}) %all-to-all-start.3) | async-done | bytes 1310752 | tf_op jit(solution)/shard_map/all_to_all | solution.py:237
  438.6 10.8 collective-permute-done.16
  457.5 9.2 collective-permute-done.17
  475.9 64.7 %collective-permute-done.30 = bf16[2048,256]{1,0:T(8,128)(2,1)} collective-permute-done((bf16[2048,256]{1,0:T(8,128)(2,1)}, bf16[2048,256]{1,0:T(8,128)(2,1)}, u32[]{:S(2)}, u32[]{:S(2)}) %collective-permute-start.30) | collective-permute-done | bytes 1048608 | tf_op jit(solution)/shard_map/ppermute | solution.py:76
  544.7 57.6 %collective-permute-done.14 = bf16[512,2816]{1,0:T(8,128)(2,1)} collective-permute-done((bf16[512,2816]{1,0:T(8,128)(2,1)}, bf16[512,2816]{1,0:T(8,128)(2,1)}, u32[]{:S(2)}, u32[]{:S(2)}) %collective-permute-start.14) | collective-permute-done | bytes 2883616 | tf_op jit(solution)/shard_map/ppermute | solution.py:76
  610.9 23.4 %select_reduce_fusion.2 = (s32[2048]{0:T(1024)S(1)}, s32[2048]{0:T(1024)S(1)}) fusion(s32[4,2048]{1,0:T(4,128)S(1)} %copy-done.98, pred[4,2048]{1,0:T(4,128)(4,1)S(1)} %copy-done.156, s32[4,2048]{1,0:T(4,128)S(1)} %copy-done.87), kind=kLoop, calls=%fused_computation.32 | loop fusion | flops 100659200 | bytes 90112 | tf_op jit(solution)/shard_map/reduce_sum | solution.py:482
  669.6 10.7 collective-permute-done.22
  681.3 53.4 %collective-permute-done.18 = bf16[512,2816]{1,0:T(8,128)(2,1)S(1)} collective-permute-done((bf16[512,2816]{1,0:T(8,128)(2,1)}, bf16[512,2816]{1,0:T(8,128)(2,1)S(1)}, u32[]{:S(2)}, u32[]{:S(2)}) %collective-permute-start.18) | collective-permute-done | bytes 2883616 | tf_op jit(solution)/shard_map/ppermute | solution.py:76
  743.9 11.0 fusion.285
  755.4 12.9 fusion.87
  777.3 21.1 %collective-permute-done.28 = bf16[2,256,2048]{2,1,0:T(8,128)(2,1)} collective-permute-done((bf16[2,256,2048]{2,1,0:T(8,128)(2,1)S(1)}, bf16[2,256,2048]{2,1,0:T(8,128)(2,1)}, u32[]{:S(2)}, u32[]{:S(2)}) %collective-permute-start.28) | collective-permute-done | bytes 2097184 | tf_op jit(solution)/shard_map/ppermute | solution.py:145
  807.6 11.1 multiply_convert_fusion.11
  827.7 12.9 multiply_convert_fusion.6
  840.6 11.7 convolution_convert_fusion.3
  860.7 12.8 multiply_convert_fusion.5
  877.9 11.3 fusion.88
  891.2 35.2 %fusion.62 = f32[2048,2816]{1,0:T(8,128)} fusion(bf16[2048,2816]{1,0:T(8,128)(2,1)} %constant_dynamic-update-slice_fusion.5, bf16[1024,2048]{1,0:T(8,128)(2,1)S(1)} %fusion.88, bf16[1024,2048]{1,0:T(8,128)(2,1)S(1)} %copy-done.179), kind=kOutput, calls=%fused_computation.134 | convolution fusion | flops 23639097344 | bytes 42991616 | tf_op jit(solution)/shard_map/dot_general | solution.py:60
  926.4 26.0 %multiply_convert_fusion.1 = (bf16[2048,1408]{1,0:T(8,128)(2,1)}, bf16[2048,1408]{1,0:T(8,128)(2,1)}, bf16[2048,1408]{1,0:T(8,128)(2,1)}) fusion(f32[2048,2816]{1,0:T(8,128)} %fusion.62, bf16[2048,1408]{1,0:T(8,128)(2,1)} %constant_dynamic-update-slice_fusion, bf16[1024,2048]{1,0:T(8,128)(2,1)} %multiply_convert_fusion.5, bf16[1024,2048]{1,0:T(8,128)(2,1)S(1)} %copy-done.177), kind=kOutput, calls=%fused_computation.67 | convolution fusion | flops 11871191040 | bytes 54525952 | tf_op jit(solution)/shard_map/dot_general | solution.py:60
  952.4 18.3 fusion.58
  976.5 10.1 fusion.53
  986.6 16.7 fusion.365
  1003.2 12.0 fusion.50
  1015.2 13.3 add_convert_fusion.2
  1040.3 30.6 %fusion.32 = bf16[2048,2816]{1,0:T(8,128)(2,1)} fusion(bf16[2048,1408]{1,0:T(8,128)(2,1)S(1)} %bitcast.582, bf16[2048,1408]{1,0:T(8,128)(2,1)} %get-tuple-element.677, bf16[1024,2048]{1,0:T(8,128)(2,1)} %copy-done.180, bf16[1024,2048]{1,0:T(8,128)(2,1)} %fusion.87), kind=kOutput, calls=%fused_computation.72 | convolution fusion | flops 23667933184 | bytes 31457280 | tf_op jit(solution)/shard_map/dot_general | solution.py:68
  1084.2 17.9 convolution_convert_fusion.2
  1102.1 23.8 %collective-permute-done.41 = bf16[2,256,2048]{2,1,0:T(8,128)(2,1)S(1)} collective-permute-done((bf16[2,256,2048]{2,1,0:T(8,128)(2,1)S(1)}, bf16[2,256,2048]{2,1,0:T(8,128)(2,1)S(1)}, u32[]{:S(2)}, u32[]{:S(2)}) %collective-permute-start.41) | collective-permute-done | bytes 2097184 | tf_op jit(solution)/shard_map/ppermute | solution.py:145
  1156.2 36.9 %collective-permute-done.43 = bf16[256,2048]{1,0:T(8,128)(2,1)S(1)} collective-permute-done((bf16[256,2048]{1,0:T(8,128)(2,1)S(1)}, bf16[256,2048]{1,0:T(8,128)(2,1)S(1)}, u32[]{:S(2)}, u32[]{:S(2)}) %collective-permute-start.43) | collective-permute-done | bytes 1048608 | tf_op jit(solution)/shard_map/ppermute | solution.py:76
  1198.2 17.1 multiply_convert_fusion
  1216.4 11.4 convert_bitcast_fusion
  1227.8 11.9 fusion.49
  1334.9 11.4 fusion.41
  1346.4 10.6 pad_maximum_fusion
  1361.5 11.5 dynamic-slice_bitcast_fusion.7
  1410.8 16.3 collective-permute-done.72
  1451.8 70.6 %collective-permute-done.57 = bf16[512,1408]{1,0:T(8,128)(2,1)} collective-permute-done((bf16[512,1408]{1,0:T(8,128)(2,1)}, bf16[512,1408]{1,0:T(8,128)(2,1)}, u32[]{:S(2)}, u32[]{:S(2)}) %collective-permute-start.57) | collective-permute-done | bytes 1441824 | tf_op jit(solution)/shard_map/ppermute | solution.py:76
  1526.3 12.5 copy.371
  1581.5 9.1 convolution_convert_fusion.6
  1590.6 37.0 %collective-permute-done.63 = f32[4608]{0:T(1024)S(1)} collective-permute-done((f32[4608]{0:T(1024)S(1)}, f32[4608]{0:T(1024)S(1)}, u32[]{:S(2)}, u32[]{:S(2)}) %collective-permute-start.63) | collective-permute-done | bytes 18464 | tf_op jit(solution)/shard_map/ppermute | solution.py:135
  1650.2 70.4 %collective-permute-done.65 = f32[4608]{0:T(1024)S(1)} collective-permute-done((f32[4608]{0:T(1024)S(1)}, f32[4608]{0:T(1024)S(1)}, u32[]{:S(2)}, u32[]{:S(2)}) %collective-permute-start.65) | collective-permute-done | bytes 18464 | tf_op jit(solution)/shard_map/ppermute | solution.py:225
  1788.0 33.6 %collective-permute-done.52 = bf16[256,2048]{1,0:T(8,128)(2,1)S(1)} collective-permute-done((bf16[256,2048]{1,0:T(8,128)(2,1)S(1)}, bf16[256,2048]{1,0:T(8,128)(2,1)S(1)}, u32[]{:S(2)}, u32[]{:S(2)}) %collective-permute-start.52) | collective-permute-done | bytes 1048608 | tf_op jit(solution)/shard_map/ppermute | solution.py:76
  1832.1 10.8 all-to-all-done.4
  1860.1 9.6 fusion.267
  1872.5 9.6 all-to-all-done.5
  (984 shorter events, 781.5 us)
Async XLA Ops:
  7.2 78.8 %collective-permute-start = (s32[2048,6]{0,1:T(8,128)}, s32[2048,6]{0,1:T(8,128)}, u32[]{:S(2)}, u32[]{:S(2)}) collective-permute-start(s32[2048,6]{0,1:T(8,128)} %param.47), channel_id=1, source_target_pairs={{0,16},{8,24},{16,0},{24,8},{1,17},{9,25},{17,1},{25,9},{2,18},{10... | collective-permute-start | bytes 147464 | tf_op jit(solution)/shard_map/ppermute | solution.py:76
  11.3 74.7 %collective-permute-start.1 = (f32[2048,6]{0,1:T(8,128)}, f32[2048,6]{0,1:T(8,128)}, u32[]{:S(2)}, u32[]{:S(2)}) collective-permute-start(f32[2048,6]{0,1:T(8,128)} %param.48), channel_id=1, source_target_pairs={{0,16},{8,24},{16,0},{24,8},{1,17},{9,25},{17,1},{25,9},{2,18},{10... | collective-permute-start | bytes 147464 | tf_op jit(solution)/shard_map/ppermute | solution.py:76
  49.5 105.0 %all-gather.9.cloned.1.call-start = ((), (), s32[]{:S(2)}) async-start(), calls=%async_computation.22 | async-start | bytes 4362240 | tf_op jit(solution)/shard_map/all_gather | solution.py:207
  86.0 657.9 %all-gather.5.cloned.1.call-start = ((), (), s32[]{:S(2)}) async-start(), calls=%async_computation.14 | async-start | bytes 3604480 | tf_op jit(solution)/shard_map/all_gather | solution.py:207
  131.2 45.4 %collective-permute-start.6 = (bf16[2,2048,256]{2,1,0:T(8,128)(2,1)}, bf16[2,2048,256]{2,1,0:T(8,128)(2,1)}, u32[]{:S(2)}, u32[]{:S(2)}) collective-permute-start(bf16[2,2048,256]{2,1,0:T(8,128)(2,1)} %collective-permute-done.5), channel_id=1, source_target_pairs={{0,1},{1,0},{2,3},{3,2},{4,5},{5,4},{6,7},{7,6},{8,9},{9,8},{10,11... | collective-permute-start | bytes 6291464 | tf_op jit(solution)/shard_map/ppermute | solution.py:135
  158.4 51.0 %collective-permute-start.8 = (bf16[1,256,576]{2,1,0:T(8,128)(2,1)S(1)}, bf16[1,256,576]{2,1,0:T(8,128)(2,1)}, u32[]{:S(2)}, u32[]{:S(2)}) collective-permute-start(bf16[1,256,576]{2,1,0:T(8,128)(2,1)S(1)} %broadcast_in_dim.240), channel_id=1, source_target_pairs={{0,1},{1,0},{2,3},{3,2},{4,5},{5,4},{6,7},{7,6},{8,9},{9,8},{10,11... | collective-permute-start | bytes 884744 | tf_op jit(solution)/shard_map/ppermute | solution.py:135
  161.8 197.6 %collective-permute-start.13 = (bf16[512,1408]{1,0:T(8,128)(2,1)}, bf16[512,1408]{1,0:T(8,128)(2,1)}, u32[]{:S(2)}, u32[]{:S(2)}) collective-permute-start(bf16[512,1408]{1,0:T(8,128)(2,1)} %slice.741), channel_id=1, source_target_pairs={{0,16},{8,24},{16,0},{24,8},{1,17},{9,25},{17,1},{25,9},{2,18},{10... | collective-permute-start | bytes 4325384 | tf_op jit(solution)/shard_map/ppermute | solution.py:76
  174.8 162.2 %collective-permute-start.7 = (bf16[512,4224]{1,0:T(8,128)(2,1)}, bf16[512,4224]{1,0:T(8,128)(2,1)}, u32[]{:S(2)}, u32[]{:S(2)}) collective-permute-start(bf16[512,4224]{1,0:T(8,128)(2,1)} %pad_maximum_fusion.12), channel_id=1, source_target_pairs={{0,8},{8,0},{16,24},{24,16},{1,9},{9,1},{17,25},{25,17},{2,10},{10... | collective-permute-start | bytes 12976136 | tf_op jit(solution)/shard_map/ppermute | solution.py:76
  364.6 52.1 %collective-permute-start.15 = (bf16[4,256,2048]{2,1,0:T(8,128)(2,1)}, bf16[4,256,2048]{2,1,0:T(8,128)(2,1)}, u32[]{:S(2)}, u32[]{:S(2)}) collective-permute-start(bf16[4,256,2048]{2,1,0:T(8,128)(2,1)} %pad_maximum_fusion.16), channel_id=1, source_target_pairs={{0,1},{1,0},{2,3},{3,2},{4,5},{5,4},{6,7},{7,6},{8,9},{9,8},{10,11... | collective-permute-start | bytes 12582920 | tf_op jit(solution)/shard_map/ppermute | solution.py:135
  369.9 437.8 %all-gather.7.cloned.1.call-start = ((), (), s32[]{:S(2)}) async-start(), calls=%async_computation.15 | async-start | bytes 1802240 | tf_op jit(solution)/shard_map/all_gather | solution.py:207
  408.2 132.4 %collective-permute-start.30 = (bf16[2048,256]{1,0:T(8,128)(2,1)}, bf16[2048,256]{1,0:T(8,128)(2,1)}, u32[]{:S(2)}, u32[]{:S(2)}) collective-permute-start(bf16[2048,256]{1,0:T(8,128)(2,1)} %fusion.121), channel_id=1, source_target_pairs={{0,16},{8,24},{16,0},{24,8},{1,17},{9,25},{17,1},{25,9},{2,18},{10... | collective-permute-start | bytes 3145736 | tf_op jit(solution)/shard_map/ppermute | solution.py:76
  410.0 192.3 %collective-permute-start.14 = (bf16[512,2816]{1,0:T(8,128)(2,1)}, bf16[512,2816]{1,0:T(8,128)(2,1)}, u32[]{:S(2)}, u32[]{:S(2)}) collective-permute-start(bf16[512,2816]{1,0:T(8,128)(2,1)} %slice.742), channel_id=1, source_target_pairs={{0,16},{8,24},{16,0},{24,8},{1,17},{9,25},{17,1},{25,9},{2,18},{10... | collective-permute-start | bytes 8650760 | tf_op jit(solution)/shard_map/ppermute | solution.py:76
  413.0 902.9 %reduce-scatter.9.cloned.1.call-start = ((), (), s32[]{:S(2)}) async-start(), calls=%async_computation.17 | async-start | bytes 1802240 | tf_op jit(solution)/shard_map/reduce_scatter | solution.py:216
  474.4 170.4 %collective-permute-start.20 = (bf16[1,256,2048]{2,1,0:T(8,128)(2,1)}, bf16[1,256,2048]{2,1,0:T(8,128)(2,1)}, u32[]{:S(2)}, u32[]{:S(2)}) collective-permute-start(bf16[1,256,2048]{2,1,0:T(8,128)(2,1)} %bitcast.65), channel_id=1, source_target_pairs={{0,2},{1,5},{2,0},{3,7},{4,6},{5,1},{6,4},{7,3},{8,10},{9,13},{10,... | collective-permute-start | bytes 3145736 | tf_op jit(solution)/shard_map/ppermute | solution.py:145
  475.9 173.6 %collective-permute-start.19 = (bf16[1,256,2048]{2,1,0:T(8,128)(2,1)}, bf16[1,256,2048]{2,1,0:T(8,128)(2,1)}, u32[]{:S(2)}, u32[]{:S(2)}) collective-permute-start(bf16[1,256,2048]{2,1,0:T(8,128)(2,1)} %bitcast.65), channel_id=1, source_target_pairs={{0,1},{1,0},{2,3},{3,2},{4,5},{5,4},{6,7},{7,6},{8,9},{9,8},{10,11... | collective-permute-start | bytes 3145736 | tf_op jit(solution)/shard_map/ppermute | solution.py:135
  543.2 115.1 %collective-permute-start.32 = (bf16[1,4096,256]{2,1,0:T(8,128)(2,1)S(1)}, bf16[1,4096,256]{2,1,0:T(8,128)(2,1)}, u32[]{:S(2)}, u32[]{:S(2)}) collective-permute-start(bf16[1,4096,256]{2,1,0:T(8,128)(2,1)S(1)} %bitcast.561), channel_id=1, source_target_pairs={{0,2},{1,5},{2,0},{3,7},{4,6},{5,1},{6,4},{7,3},{8,10},{9,13},{10,... | collective-permute-start | bytes 6291464 | tf_op jit(solution)/shard_map/ppermute | solution.py:145
  544.7 113.6 %collective-permute-start.31 = (bf16[1,4096,256]{2,1,0:T(8,128)(2,1)S(1)}, bf16[1,4096,256]{2,1,0:T(8,128)(2,1)}, u32[]{:S(2)}, u32[]{:S(2)}) collective-permute-start(bf16[1,4096,256]{2,1,0:T(8,128)(2,1)S(1)} %bitcast.562), channel_id=1, source_target_pairs={{0,1},{1,0},{2,3},{3,2},{4,5},{5,4},{6,7},{7,6},{8,9},{9,8},{10,11... | collective-permute-start | bytes 6291464 | tf_op jit(solution)/shard_map/ppermute | solution.py:135
  603.2 51.0 %collective-permute-start.36 = (bf16[512,1408]{1,0:T(8,128)(2,1)}, bf16[512,1408]{1,0:T(8,128)(2,1)}, u32[]{:S(2)}, u32[]{:S(2)}) collective-permute-start(bf16[512,1408]{1,0:T(8,128)(2,1)} %collective-permute-done.13), channel_id=1, source_target_pairs={{0,8},{8,0},{16,24},{24,16},{1,9},{9,1},{17,25},{25,17},{2,10},{10... | collective-permute-start | bytes 4325384 | tf_op jit(solution)/shard_map/ppermute | solution.py:76
  644.9 97.5 %collective-permute-start.24 = (bf16[256,2048]{1,0:T(8,128)(2,1)}, bf16[256,2048]{1,0:T(8,128)(2,1)}, u32[]{:S(2)}, u32[]{:S(2)}) collective-permute-start(bf16[256,2048]{1,0:T(8,128)(2,1)} %get-tuple-element.662), channel_id=1, source_target_pairs={{0,16},{8,24},{16,0},{24,8},{1,17},{9,25},{17,1},{25,9},{2,18},{10... | collective-permute-start | bytes 3145736 | tf_op jit(solution)/shard_map/ppermute | solution.py:76
  649.5 85.3 %collective-permute-start.18 = (bf16[512,2816]{1,0:T(8,128)(2,1)}, bf16[512,2816]{1,0:T(8,128)(2,1)S(1)}, u32[]{:S(2)}, u32[]{:S(2)}) collective-permute-start(bf16[512,2816]{1,0:T(8,128)(2,1)} %collective-permute-done.14), channel_id=1, source_target_pairs={{0,8},{8,0},{16,24},{24,16},{1,9},{9,1},{17,25},{25,17},{2,10},{10... | collective-permute-start | bytes 8650760 | tf_op jit(solution)/shard_map/ppermute | solution.py:76
  658.3 79.3 %collective-permute-start.33 = (bf16[1,4096,256]{2,1,0:T(8,128)(2,1)}, bf16[1,4096,256]{2,1,0:T(8,128)(2,1)S(1)}, u32[]{:S(2)}, u32[]{:S(2)}) collective-permute-start(bf16[1,4096,256]{2,1,0:T(8,128)(2,1)} %collective-permute-done.32), channel_id=1, source_target_pairs={{0,1},{1,0},{2,3},{3,2},{4,5},{5,4},{6,7},{7,6},{8,9},{9,8},{10,11... | collective-permute-start | bytes 6291464 | tf_op jit(solution)/shard_map/ppermute | solution.py:135
  669.1 85.9 %collective-permute-start.34 = (bf16[2,4096,256]{2,1,0:T(8,128)(2,1)}, bf16[2,4096,256]{2,1,0:T(8,128)(2,1)}, u32[]{:S(2)}, u32[]{:S(2)}) collective-permute-start(bf16[2,4096,256]{2,1,0:T(8,128)(2,1)} %pad_maximum_fusion.17), channel_id=1, source_target_pairs={{0,4},{1,3},{2,6},{3,1},{4,0},{5,7},{6,2},{7,5},{8,12},{9,11},{10,... | collective-permute-start | bytes 12582920 | tf_op jit(solution)/shard_map/ppermute | solution.py:145
  680.3 59.0 %collective-permute-start.23 = (bf16[2,256,2048]{2,1,0:T(8,128)(2,1)S(1)}, bf16[2,256,2048]{2,1,0:T(8,128)(2,1)S(1)}, u32[]{:S(2)}, u32[]{:S(2)}) collective-permute-start(bf16[2,256,2048]{2,1,0:T(8,128)(2,1)S(1)} %collective-permute-done.22), channel_id=1, source_target_pairs={{0,1},{1,0},{2,3},{3,2},{4,5},{5,4},{6,7},{7,6},{8,9},{9,8},{10,11... | collective-permute-start | bytes 6291464 | tf_op jit(solution)/shard_map/ppermute | solution.py:135
  754.9 44.8 %collective-permute-start.35 = (bf16[2,4096,256]{2,1,0:T(8,128)(2,1)}, bf16[2,4096,256]{2,1,0:T(8,128)(2,1)S(1)}, u32[]{:S(2)}, u32[]{:S(2)}) collective-permute-start(bf16[2,4096,256]{2,1,0:T(8,128)(2,1)} %collective-permute-done.34), channel_id=1, source_target_pairs={{0,1},{1,0},{2,3},{3,2},{4,5},{5,4},{6,7},{7,6},{8,9},{9,8},{10,11... | collective-permute-start | bytes 12582920 | tf_op jit(solution)/shard_map/ppermute | solution.py:135
  798.4 75.1 %collective-permute-start.29 = (bf16[2,256,2048]{2,1,0:T(8,128)(2,1)}, bf16[2,256,2048]{2,1,0:T(8,128)(2,1)S(1)}, u32[]{:S(2)}, u32[]{:S(2)}) collective-permute-start(bf16[2,256,2048]{2,1,0:T(8,128)(2,1)} %collective-permute-done.28), channel_id=1, source_target_pairs={{0,1},{1,0},{2,3},{3,2},{4,5},{5,4},{6,7},{7,6},{8,9},{9,8},{10,11... | collective-permute-start | bytes 6291464 | tf_op jit(solution)/shard_map/ppermute | solution.py:135
  827.6 488.2 %reduce-scatter.7.cloned.1.call-start = ((), (), s32[]{:S(2)}) async-start(), calls=%async_computation.16 | async-start | bytes 3604480 | tf_op jit(solution)/shard_map/reduce_scatter | solution.py:216
  860.6 788.8 %reduce-scatter.17.cloned.1.call-start = ((), (), s32[]{:S(2)}) async-start(), calls=%async_computation.21 | async-start | bytes 409600 | tf_op jit(solution)/shard_map/reduce_scatter | solution.py:216
  1077.2 61.5 %collective-permute-start.38 = (bf16[2,256,2048]{2,1,0:T(8,128)(2,1)}, bf16[2,256,2048]{2,1,0:T(8,128)(2,1)}, u32[]{:S(2)}, u32[]{:S(2)}) collective-permute-start(bf16[2,256,2048]{2,1,0:T(8,128)(2,1)} %slice.916), channel_id=1, source_target_pairs={{0,4},{1,3},{2,6},{3,1},{4,0},{5,7},{6,2},{7,5},{8,12},{9,11},{10,... | collective-permute-start | bytes 6291464 | tf_op jit(solution)/shard_map/ppermute | solution.py:145
  1082.3 43.6 %collective-permute-start.41 = (bf16[2,256,2048]{2,1,0:T(8,128)(2,1)S(1)}, bf16[2,256,2048]{2,1,0:T(8,128)(2,1)S(1)}, u32[]{:S(2)}, u32[]{:S(2)}) collective-permute-start(bf16[2,256,2048]{2,1,0:T(8,128)(2,1)S(1)} %slice.920), channel_id=1, source_target_pairs={{0,4},{1,3},{2,6},{3,1},{4,0},{5,7},{6,2},{7,5},{8,12},{9,11},{10,... | collective-permute-start | bytes 6291464 | tf_op jit(solution)/shard_map/ppermute | solution.py:145
  1145.9 47.1 %collective-permute-start.43 = (bf16[256,2048]{1,0:T(8,128)(2,1)S(1)}, bf16[256,2048]{1,0:T(8,128)(2,1)S(1)}, u32[]{:S(2)}, u32[]{:S(2)}) collective-permute-start(bf16[256,2048]{1,0:T(8,128)(2,1)S(1)} %fusion.180), channel_id=1, source_target_pairs={{0,16},{8,24},{16,0},{24,8},{1,17},{9,25},{17,1},{25,9},{2,18},{10... | collective-permute-start | bytes 3145736 | tf_op jit(solution)/shard_map/ppermute | solution.py:76
  1153.3 136.9 %collective-permute-start.53 = (bf16[512,4224]{1,0:T(8,128)(2,1)}, bf16[512,4224]{1,0:T(8,128)(2,1)}, u32[]{:S(2)}, u32[]{:S(2)}) collective-permute-start(bf16[512,4224]{1,0:T(8,128)(2,1)} %pad_maximum_fusion.14), channel_id=1, source_target_pairs={{0,8},{8,0},{16,24},{24,16},{1,9},{9,1},{17,25},{25,17},{2,10},{10... | collective-permute-start | bytes 12976136 | tf_op jit(solution)/shard_map/ppermute | solution.py:76
  1197.6 45.3 %collective-permute-start.44 = (bf16[1,256,2048]{2,1,0:T(8,128)(2,1)S(1)}, bf16[1,256,2048]{2,1,0:T(8,128)(2,1)S(1)}, u32[]{:S(2)}, u32[]{:S(2)}) collective-permute-start(bf16[1,256,2048]{2,1,0:T(8,128)(2,1)S(1)} %get-tuple-element.659), channel_id=1, source_target_pairs={{0,1},{1,0},{2,3},{3,2},{4,5},{5,4},{6,7},{7,6},{8,9},{9,8},{10,11... | collective-permute-start | bytes 3145736 | tf_op jit(solution)/shard_map/ppermute | solution.py:135
  1334.6 51.6 %collective-permute-start.54 = (bf16[4,256,2048]{2,1,0:T(8,128)(2,1)}, bf16[4,256,2048]{2,1,0:T(8,128)(2,1)}, u32[]{:S(2)}, u32[]{:S(2)}) collective-permute-start(bf16[4,256,2048]{2,1,0:T(8,128)(2,1)} %pad_maximum_fusion.20), channel_id=1, source_target_pairs={{0,1},{1,0},{2,3},{3,2},{4,5},{5,4},{6,7},{7,6},{8,9},{9,8},{10,11... | collective-permute-start | bytes 12582920 | tf_op jit(solution)/shard_map/ppermute | solution.py:135
  1384.7 175.2 %collective-permute-start.49 = (bf16[4,2,256,2048]{3,2,1,0:T(8,128)(2,1)}, bf16[4,2,256,2048]{3,2,1,0:T(8,128)(2,1)}, u32[]{:S(2)}, u32[]{:S(2)}) collective-permute-start(bf16[4,2,256,2048]{3,2,1,0:T(8,128)(2,1)} %pad_maximum_fusion.7), channel_id=1, source_target_pairs={{0,1},{1,0},{2,3},{3,2},{4,5},{5,4},{6,7},{7,6},{8,9},{9,8},{10,11... | collective-permute-start | bytes 25165832 | tf_op jit(solution)/shard_map/ppermute | solution.py:135
  1398.0 147.6 %collective-permute-start.67 = (bf16[512,4224]{1,0:T(8,128)(2,1)}, bf16[512,4224]{1,0:T(8,128)(2,1)}, u32[]{:S(2)}, u32[]{:S(2)}) collective-permute-start(bf16[512,4224]{1,0:T(8,128)(2,1)} %pad_maximum_fusion.15), channel_id=1, source_target_pairs={{0,8},{8,0},{16,24},{24,16},{1,9},{9,1},{17,25},{25,17},{2,10},{10... | collective-permute-start | bytes 12976136 | tf_op jit(solution)/shard_map/ppermute | solution.py:76
  1410.8 111.6 %collective-permute-start.57 = (bf16[512,1408]{1,0:T(8,128)(2,1)}, bf16[512,1408]{1,0:T(8,128)(2,1)}, u32[]{:S(2)}, u32[]{:S(2)}) collective-permute-start(bf16[512,1408]{1,0:T(8,128)(2,1)} %slice.810), channel_id=1, source_target_pairs={{0,16},{8,24},{16,0},{24,8},{1,17},{9,25},{17,1},{25,9},{2,18},{10... | collective-permute-start | bytes 4325384 | tf_op jit(solution)/shard_map/ppermute | solution.py:76
  1541.8 214.7 %reduce-scatter.13.cloned.1.call-start = ((), (), s32[]{:S(2)}) async-start(), calls=%async_computation.19 | async-start | bytes 655360 | tf_op jit(solution)/shard_map/reduce_scatter | solution.py:216
  1545.6 210.8 %collective-permute-start.68 = (bf16[512,2816]{1,0:T(8,128)(2,1)}, bf16[512,2816]{1,0:T(8,128)(2,1)}, u32[]{:S(2)}, u32[]{:S(2)}) collective-permute-start(bf16[512,2816]{1,0:T(8,128)(2,1)} %slice.828), channel_id=1, source_target_pairs={{0,16},{8,24},{16,0},{24,8},{1,17},{9,25},{17,1},{25,9},{2,18},{10... | collective-permute-start | bytes 8650760 | tf_op jit(solution)/shard_map/ppermute | solution.py:76
  1551.1 205.4 %reduce-scatter.15.cloned.1.call-start = ((), (), s32[]{:S(2)}) async-start(), calls=%async_computation.20 | async-start | bytes 1310720 | tf_op jit(solution)/shard_map/reduce_scatter | solution.py:216
  1572.8 160.8 %collective-permute-start.50 = (bf16[2,2,256,2048]{3,2,1,0:T(8,128)(2,1)}, bf16[2,2,256,2048]{3,2,1,0:T(8,128)(2,1)}, u32[]{:S(2)}, u32[]{:S(2)}) collective-permute-start(bf16[2,2,256,2048]{3,2,1,0:T(8,128)(2,1)} %slice.930), channel_id=1, source_target_pairs={{0,4},{1,3},{2,6},{3,1},{4,0},{5,7},{6,2},{7,5},{8,12},{9,11},{10,... | collective-permute-start | bytes 12582920 | tf_op jit(solution)/shard_map/ppermute | solution.py:145
  1576.6 51.0 %collective-permute-start.63 = (f32[4608]{0:T(1024)S(1)}, f32[4608]{0:T(1024)S(1)}, u32[]{:S(2)}, u32[]{:S(2)}) collective-permute-start(f32[4608]{0:T(1024)S(1)} %add.859), channel_id=1, source_target_pairs={{0,4},{1,5},{2,6},{3,7},{4,0},{5,1},{6,2},{7,3},{8,12},{9,13},{10,... | collective-permute-start | bytes 55304 | tf_op jit(solution)/shard_map/ppermute | solution.py:135
  1577.9 55.3 %all-to-all-start.6 = ((bf16[256,8,256]{2,0,1:T(8,128)(2,1)}), bf16[256,8,256]{2,0,1:T(8,128)(2,1)S(1)}, u32[]{:S(2)}, u32[]{:S(2)}) async-start(bf16[256,8,256]{2,0,1:T(8,128)(2,1)} %bitcast.524), calls=%async_computation.8 | async-start | bytes 2097152 | tf_op jit(solution)/shard_map/all_to_all | solution.py:629
  1581.4 178.5 %reduce-scatter.11.cloned.1.call-start = ((), (), s32[]{:S(2)}) async-start(), calls=%async_computation.18 | async-start | bytes 1966080 | tf_op jit(solution)/shard_map/reduce_scatter | solution.py:216
  1629.6 91.0 %collective-permute-start.65 = (f32[4608]{0:T(1024)S(1)}, f32[4608]{0:T(1024)S(1)}, u32[]{:S(2)}, u32[]{:S(2)}) collective-permute-start(f32[4608]{0:T(1024)S(1)} %add.860), channel_id=1, source_target_pairs={{0,16},{8,24},{16,0},{24,8},{1,17},{9,25},{17,1},{25,9},{2,18},{10... | collective-permute-start | bytes 55304 | tf_op jit(solution)/shard_map/ppermute | solution.py:225
  1629.6 91.0 %collective-permute-start.64 = (f32[4608]{0:T(1024)S(1)}, f32[4608]{0:T(1024)S(1)}, u32[]{:S(2)}, u32[]{:S(2)}) collective-permute-start(f32[4608]{0:T(1024)S(1)} %add.860), channel_id=1, source_target_pairs={{0,8},{8,16},{16,24},{24,0},{1,9},{9,17},{17,25},{25,1},{2,10},{10... | collective-permute-start | bytes 55304 | tf_op jit(solution)/shard_map/ppermute | solution.py:225
  1640.5 110.0 %all-to-all-start.7 = ((bf16[4,640,256]{2,1,0:T(8,128)(2,1)}), bf16[4,640,256]{2,1,0:T(8,128)(2,1)}, u32[]{:S(2)}, u32[]{:S(2)}) async-start(bf16[4,640,256]{2,1,0:T(8,128)(2,1)} %bitcast.610), calls=%async_computation.9 | async-start | bytes 2621440 | tf_op jit(solution)/shard_map/all_to_all | solution.py:237
  1649.4 71.3 %collective-permute-start.75 = (bf16[1,64,576]{2,1,0:T(8,128)(2,1)}, bf16[1,64,576]{2,1,0:T(8,128)(2,1)S(1)}, u32[]{:S(2)}, u32[]{:S(2)}) collective-permute-start(bf16[1,64,576]{2,1,0:T(8,128)(2,1)} %bitcast.624), channel_id=1, source_target_pairs={{0,2},{1,5},{2,0},{3,7},{4,6},{5,1},{6,4},{7,3},{8,10},{9,13},{10,... | collective-permute-start | bytes 221192 | tf_op jit(solution)/shard_map/ppermute | solution.py:145
  1773.0 48.6 %collective-permute-start.52 = (bf16[256,2048]{1,0:T(8,128)(2,1)S(1)}, bf16[256,2048]{1,0:T(8,128)(2,1)S(1)}, u32[]{:S(2)}, u32[]{:S(2)}) collective-permute-start(bf16[256,2048]{1,0:T(8,128)(2,1)S(1)} %fusion.181), channel_id=1, source_target_pairs={{0,16},{8,24},{16,0},{24,8},{1,17},{9,25},{17,1},{25,9},{2,18},{10... | collective-permute-start | bytes 3145736 | tf_op jit(solution)/shard_map/ppermute | solution.py:76
  (243 other events, 4092.4 us)
Sparse Core Ops, SparseCore 0:
  86.1 68.2 all-gather.8
  158.6 106.9 all-gather.4
  413.1 116.8 all-gather.6
  827.7 31.6 reduce-scatter.8
  861.6 55.0 reduce-scatter.6
  1541.9 80.8 reduce-scatter.16
  1625.7 48.4 reduce-scatter.12
  1676.5 37.2 reduce-scatter.14
  1716.7 43.1 reduce-scatter.10

commit v10 on v4

--- a/solution.py
+++ b/solution.py
@@ -286,34 +286,19 @@
     )
     rounds = (jnp.max(all_counts) + room - 1) // room
 
-    inverse_group = jnp.arange(row_count, dtype=jnp.int32)[:, None, None]
-    here_hit = (place_in[:, :, None] == token_ids[None, None, :]) & from_here[:, :, None]
-    rank_of = jnp.sum(jnp.where(here_hit, rank_here[:, :, None], 0), axis=(0, 1))
-    group_of = jnp.sum(jnp.where(here_hit, inverse_group, 0), axis=(0, 1))
-
-    def maps(step):
+    def maps_out(step):
         places = step * room + jnp.arange(room, dtype=jnp.int32)
-
-        def listed(row_of, rank):
-            hit = (rank[None, None, :] == places[None, :, None]) & (
-                row_of[None, None, :] == jnp.arange(row_count, dtype=jnp.int32)[:, None, None]
-            )
-            return jnp.sum(jnp.where(hit, token_ids[None, None, :] + 1, 0), axis=2).reshape(-1) - 1
-
-        def slots(row_of, rank):
-            inside = (rank >= places[0]) & (rank < places[0] + room)
-            return jnp.where(inside, row_of * room + rank - places[0], -1)
-
         hit = rank_here[:, None, :] == places[None, :, None]
-        out_tokens = jnp.sum(jnp.where(hit, place_in[:, None, :] + 1, 0), axis=2).reshape(-1) - 1
-        dealt = (my_source, my_rank)
-        return out_tokens, slots(*dealt), listed(*dealt), slots(group_of, rank_of)
-
-    out_list, in_slots, back_list, back_slots = maps(0)
+        listed = jnp.sum(jnp.where(hit, place_in[:, None, :] + 1, 0), axis=2).reshape(-1) - 1
+        slot = my_rank - step * room
+        inside = (slot >= 0) & (slot < room)
+        return listed, jnp.where(inside, my_source * room + slot, -1)
+
+    out_list, in_slots = maps_out(0)
 
     def more_dealt(carry):
         step, total = carry
-        out_more, in_more, _, _ = maps(step)
+        out_more, in_more = maps_out(step)
         given = jnp.concatenate([tokens, cotangent], axis=1)
         return step + 1, total + exchange(given, out_more, in_more)
 
@@ -329,8 +314,6 @@
         token_weight = jnp.sum(jnp.where(named, group_gates, 0.0), axis=1)
         return pick.astype(BF16), jnp.sum(jnp.where(pick, token_weight[None, :], 0.0), axis=1)
 
-    pick, weight = chosen(routes, gate_weights)
-    mate_pick, mate_weight = chosen(mate(routes), mate(gate_weights))
     document, position = documents(doc_lengths[0], group_rows)
 
     rows_in, dim = w_query.shape[0], w_query.shape[0] * row_count
@@ -342,6 +325,10 @@
         (jnp.int32(1), jnp.zeros((group_rows, 2 * slice_width), BF16)),
     )[1]
     dealt_x = exchange(tokens, out_list, in_slots) + more[:, :slice_width]
+    dealt_x, mate_routes, mate_gates = after((dealt_x, mate(routes), mate(gate_weights)), ())
+    routes_late, gates_late = after((routes, gate_weights), (dealt_x,))
+    pick, weight = chosen(routes_late, gates_late)
+    mate_pick, mate_weight = chosen(mate_routes, mate_gates)
     full_x = cube_gather(dealt_x, 1)
 
     query_width = w_query.shape[1]
@@ -475,6 +462,27 @@
     (mate_part,) = after((mate_part,), (normed_two,))
     mate_two = cube_gather(mate_part, 0)
 
+    place_late, rank_late, here_late, source_late, my_rank_late = after(
+        (place_in, rank_here, from_here, my_source, my_rank), (normed_part,)
+    )
+    hit = (place_late[:, :, None] == token_ids[None, None, :]) & here_late[:, :, None]
+    rank_of = jnp.sum(jnp.where(hit, rank_late[:, :, None], 0), axis=(0, 1))
+    groups = jnp.arange(row_count, dtype=jnp.int32)
+    group_of = jnp.sum(jnp.where(hit, groups[:, None, None], 0), axis=(0, 1))
+
+    def maps_back(step):
+        places = step * room + jnp.arange(room, dtype=jnp.int32)
+        hit = (my_rank_late[None, None, :] == places[None, :, None]) & (
+            source_late[None, None, :] == groups[:, None, None]
+        )
+        listed = jnp.sum(jnp.where(hit, token_ids[None, None, :] + 1, 0), axis=2).reshape(-1) - 1
+        slot = rank_of - step * room
+        inside = (slot >= 0) & (slot < room)
+        return listed, jnp.where(inside, group_of * room + slot, -1)
+
+    back_list, back_slots = maps_back(0)
+    gate_up_w, back_list, back_slots = after((gate_up_w, back_list, back_slots), ())
+
     def forward(rows, gate_up_w):
         width = gate_up_w.shape[1] // 2
         gate_up = dot(rows, gate_up_w)
@@ -491,8 +499,6 @@
     ordered = []
 
     def queued_sum(value, axis):
-        if len(ordered) > 1:
-            (value,) = after((value,), (ordered[-2],))
         ordered.append(row_scatter(value.astype(BF16), axis))
         return ordered[-1]
 
@@ -612,7 +618,7 @@
 
     def more_back(carry):
         step, total = carry
-        _, _, back_more, slots_more = maps(step)
+        back_more, slots_more = maps_back(step)
         dealt = jnp.concatenate([result_slice, grad_slice], axis=1)
         return step + 1, total + exchange(dealt, back_more, slots_more)
 

time: 1730 us -> 1720 us (level)
    ppermute x18, waiting for transfers between devices: 364 us -> 332 us  [row_swap(): lax.ppermute(value, 'row', [(j, j ^ bit) for j in range(lax.axis_size('ro...]
    ppermute x30, waiting for transfers between devices: 83 us -> 101 us  [chip_swap(): lax.ppermute(value, 'col', [(j, j ^ (other if j % 2 else bits)[step]) for...]
    dynamic_update_slice x59 -> x60, local copies, waits for them, and re-layouts: 83.6 us -> 90.2 us  [cube_gather(): lax.dynamic_update_slice_in_dim(out, item, block_at(owner, place) * width...]
    unnamed x408 -> x398, local copies, waits for them, and re-layouts: 39.6 us -> 37.7 us
  transfers between devices with their start and end apart: 101 -> 101, of which waited for: 34 -> 31; matrix products, arithmetic and copies ran while one was open for 52% -> 53% of each run, Pallas kernels for 0% -> 0%
where the time goes in v10:
time: 1720 us; the launch traced here: 1710 us
  waiting for transfers between devices  600 us (35%)
  matrix products  455 us (26%)
  local copies, waits for them, and re-layouts  304 us (18%)
  other arithmetic  240 us (14%)
  starting transfers between devices  94.1 us (5%)
  between operations  18.4 us (1%)
    ppermute x18, waiting for transfers between devices, row_swap(): lax.ppermute(value, 'row', [(j, j ^ bit) for j in range(lax.axis_size('ro...  332 us
    dot_general x20, matrix products, dot(): return jnp.dot(left, right, preferred_element_type=F32)  189 us
    dot_general x12, matrix products, dot_tn(): lax.dot_general(left, right, (((0,), (0,)), ((), ())), preferred_element_...  137 us
    ppermute x30, waiting for transfers between devices, chip_swap(): lax.ppermute(value, 'col', [(j, j ^ (other if j % 2 else bits)[step]) for...  101 us
    dot_general x9, matrix products, dot_nt(): lax.dot_general(left, right, (((1,), (1,)), ((), ())), preferred_element_...  94.5 us
    dynamic_update_slice x60, local copies, waits for them, and re-layouts, cube_gather(): lax.dynamic_update_slice_in_dim(out, item, block_at(owner, place) * width...  90.2 us
    reduce_scatter x6, waiting for transfers between devices, row_scatter(): return lax.psum_scatter(value, 'row', scatter_dimension=axis, tiled=True)  66.1 us
    all_gather x4, waiting for transfers between devices, row_gather(): return lax.all_gather(shard, 'row', axis=axis, tiled=True)  51.4 us
  transfers between devices with their start and end apart: 101, of which 31 were waited for; matrix products, arithmetic and copies ran while one was open for 53% of the time, Pallas kernels for 0%

profile of v10, /device:TPU:0, one launch (start us, length us, event | category | flops | bytes accessed | tf_op | source)
XLA Modules:
  0.0 1711.3 jit_solution(1836062634074562859)
XLA Ops:
  51.9 18.1 %all-to-all-done.2 = bf16[4,640,256]{2,1,0:T(8,128)(2,1)} async-done(((bf16[4,640,256]{2,1,0:T(8,128)(2,1)}), bf16[4,640,256]{2,1,0:T(8,128)(2,1)}, u32[]{:S(2)}, u32[]{:S(2)}) %all-to-all-start.2) | async-done | bytes 1310752 | tf_op jit(solution)/shard_map/all_to_all | solution.py:232
  101.7 29.3 %all-gather.11.cloned.1.call-done = bf16[2496,384]{1,0:T(8,128)(2,1)} async-done(((bf16[624,384]{1,0:T(8,128)(2,1)}), bf16[2496,384]{1,0:T(8,128)(2,1)}) %all-gather.11.cloned.1.call-update) | async-done | bytes 1916944 | tf_op jit(solution)/shard_map/all_gather | solution.py:202
  177.7 22.1 %all-gather.13.cloned.1.call-done = bf16[1536,512]{1,0:T(8,128)(2,1)} async-done(((bf16[384,512]{1,0:T(8,128)(2,1)}), bf16[1536,512]{1,0:T(8,128)(2,1)}) %all-gather.13.cloned.1.call-update) | async-done | bytes 1572880 | tf_op jit(solution)/shard_map/all_gather | solution.py:202
  211.8 10.3 collective-permute-done.29
  256.8 105.7 %collective-permute-done.36 = bf16[1408,512]{1,0:T(8,128)(2,1)} collective-permute-done((bf16[1408,512]{1,0:T(8,128)(2,1)}, bf16[1408,512]{1,0:T(8,128)(2,1)}, u32[]{:S(2)}, u32[]{:S(2)}) %collective-permute-start.36) | collective-permute-done | bytes 1441824 | tf_op jit(solution)/shard_map/ppermute | solution.py:76
  377.1 8.7 fusion.29
  385.9 9.1 fusion.285
  445.8 33.0 %collective-permute-done.3 = bf16[512,2816]{1,0:T(8,128)(2,1)} collective-permute-done((bf16[512,2816]{1,0:T(8,128)(2,1)}, bf16[512,2816]{1,0:T(8,128)(2,1)}, u32[]{:S(2)}, u32[]{:S(2)}) %collective-permute-start.3) | collective-permute-done | bytes 2883616 | tf_op jit(solution)/shard_map/ppermute | solution.py:76
  504.8 12.3 copy.346
  532.0 37.4 %collective-permute-done.16 = bf16[2,256,2048]{2,1,0:T(8,128)(2,1)S(1)} collective-permute-done((bf16[2,256,2048]{2,1,0:T(8,128)(2,1)S(1)}, bf16[2,256,2048]{2,1,0:T(8,128)(2,1)S(1)}, u32[]{:S(2)}, u32[]{:S(2)}) %collective-permute-start.16) | collective-permute-done | bytes 2097184 | tf_op jit(solution)/shard_map/ppermute | solution.py:140
  599.3 23.4 %select_reduce_fusion.2 = (s32[2048]{0:T(1024)S(1)}, s32[2048]{0:T(1024)S(1)}) fusion(s32[4,2048]{1,0:T(4,128)S(1)} %copy-done.105, pred[4,2048]{1,0:T(4,128)(4,1)S(1)} %copy-done.146, s32[4,2048]{1,0:T(4,128)S(1)} %copy-done.95), kind=kLoop, calls=%fused_computation.32 | loop fusion | flops 100659200 | bytes 90112 | tf_op jit(solution)/shard_map/reduce_sum | solution.py:471
  635.9 12.6 multiply_convert_fusion.6
  648.5 8.6 collective-permute-done.21
  657.1 13.0 multiply_convert_fusion.5
  670.1 8.3 slice.879
  692.7 11.0 fusion.286
  703.7 11.1 multiply_convert_fusion.12
  715.9 7.7 convolution_convert_fusion.7
  725.6 13.4 fusion.88
  739.1 8.4 convolution_convert_fusion.3
  774.0 11.6 fusion.87
  787.5 34.5 %fusion.62 = f32[2048,2816]{1,0:T(8,128)} fusion(bf16[2048,2816]{1,0:T(8,128)(2,1)} %constant_dynamic-update-slice_fusion.8, bf16[1024,2048]{1,0:T(8,128)(2,1)S(1)} %fusion.87, bf16[1024,2048]{1,0:T(8,128)(2,1)S(1)} %copy-done.170), kind=kOutput, calls=%fused_computation.130 | convolution fusion | flops 23639097344 | bytes 42991616 | tf_op jit(solution)/shard_map/dot_general | solution.py:60
  822.1 26.7 %multiply_convert_fusion.1 = (bf16[2048,1408]{1,0:T(8,128)(2,1)}, bf16[2048,1408]{1,0:T(8,128)(2,1)}, bf16[2048,1408]{1,0:T(8,128)(2,1)}) fusion(f32[2048,2816]{1,0:T(8,128)} %fusion.62, bf16[1408,2048]{1,0:T(8,128)(2,1)} %constant_dynamic-update-slice_fusion, bf16[1024,2048]{1,0:T(8,128)(2,1)} %multiply_convert_fusion.5, ...), kind=kOutput, calls=%fused_computation.65 | convolution fusion | flops 11871191040 | bytes 54525952 | tf_op jit(solution)/shard_map/dot_general | solution.py:64
  855.1 17.3 %fusion.58 = bf16[1024,2048]{1,0:T(8,128)(2,1)} fusion(bf16[2048,2816]{1,0:T(8,128)(2,1)} %constant_dynamic-update-slice_fusion.8, bf16[2048,1408]{1,0:T(8,128)(2,1)} %get-tuple-element.520, bf16[2048,1408]{1,0:T(8,128)(2,1)S(1)} %copy-done.34), kind=kOutput, calls=%fused_computation.125 | convolution fusion | flops 11822694400 | bytes 27262976 | tf_op jit(solution)/shard_map/dot_general | solution.py:64
  872.4 17.7 %convolution_convert_fusion.2 = bf16[1408,2048]{1,0:T(8,128)(2,1)} fusion(bf16[2048,1408]{1,0:T(8,128)(2,1)} %get-tuple-element.435, bf16[1024,2048]{1,0:T(8,128)(2,1)} %multiply_convert_fusion.5, bf16[1024,2048]{1,0:T(8,128)(2,1)S(1)} %copy-done.167), kind=kOutput, calls=%fused_computation.114 | convolution fusion | flops 11830820864 | bytes 19922944 | tf_op jit(solution)/shard_map/dot_general | solution.py:68
  890.1 10.9 fusion.52
  904.2 15.2 fusion.364
  919.4 11.9 fusion.46
  931.3 11.8 add_convert_fusion.1
  952.5 30.9 %fusion.32 = bf16[2048,2816]{1,0:T(8,128)(2,1)} fusion(bf16[2048,1408]{1,0:T(8,128)(2,1)S(1)} %bitcast.589, bf16[2048,1408]{1,0:T(8,128)(2,1)} %get-tuple-element.520, bf16[1024,2048]{1,0:T(8,128)(2,1)} %copy-done.171, bf16[1024,2048]{1,0:T(8,128)(2,1)} %fusion.88), kind=kOutput, calls=%fused_computation.70 | convolution fusion | flops 23667933184 | bytes 31457280 | tf_op jit(solution)/shard_map/dot_general | solution.py:68
  999.2 17.8 %multiply_convert_fusion = bf16[2048,2048]{1,0:T(8,128)(2,1)} fusion(bf16[2048,1408]{1,0:T(8,128)(2,1)S(1)} %bitcast.664, bf16[1408,2048]{1,0:T(8,128)(2,1)} %constant_dynamic-update-slice_fusion, f32[2048]{0:T(1024)S(1)} %copy-done.154), kind=kOutput, calls=%fused_computation.57 | convolution fusion | flops 11819548672 | bytes 19931136 | tf_op jit(solution)/shard_map/dot_general | solution.py:60
  1026.3 14.2 fusion.45
  1040.6 17.9 %collective-permute-done.39 = bf16[2,256,2048]{2,1,0:T(8,128)(2,1)S(1)} collective-permute-done((bf16[2,256,2048]{2,1,0:T(8,128)(2,1)S(1)}, bf16[2,256,2048]{2,1,0:T(8,128)(2,1)S(1)}, u32[]{:S(2)}, u32[]{:S(2)}) %collective-permute-start.39) | collective-permute-done | bytes 2097184 | tf_op jit(solution)/shard_map/ppermute | solution.py:140
  1063.5 13.3 fusion.53
  1077.0 57.3 %collective-permute-done.44 = bf16[256,2048]{1,0:T(8,128)(2,1)S(1)} collective-permute-done((bf16[256,2048]{1,0:T(8,128)(2,1)S(1)}, bf16[256,2048]{1,0:T(8,128)(2,1)S(1)}, u32[]{:S(2)}, u32[]{:S(2)}) %collective-permute-start.44) | collective-permute-done | bytes 1048608 | tf_op jit(solution)/shard_map/ppermute | solution.py:76
  1138.8 11.0 add_convert_fusion
  1160.8 67.7 %collective-permute-done.80 = bf16[512,2816]{1,0:T(8,128)(2,1)} collective-permute-done((bf16[512,2816]{1,0:T(8,128)(2,1)}, bf16[512,2816]{1,0:T(8,128)(2,1)}, u32[]{:S(2)}, u32[]{:S(2)}) %collective-permute-start.80) | collective-permute-done | bytes 2883616 | tf_op jit(solution)/shard_map/ppermute | solution.py:76
  1228.5 8.3 add_convert_fusion.8
  1286.7 7.9 fusion.176
  1328.3 10.5 dynamic-slice_bitcast_fusion.21
  1369.3 7.1 convolution_convert_fusion.8
  1423.4 44.7 %reduce-scatter.13.cloned.1.call-done = bf16[256,512]{1,0:T(8,128)(2,1)} async-done(((bf16[256,2048]{1,0:T(8,128)(2,1)}), bf16[256,512]{1,0:T(8,128)(2,1)}) %reduce-scatter.13.cloned.1.call-update) | async-done | bytes 262160 | tf_op jit(solution)/shard_map/reduce_scatter | solution.py:211
  1469.9 21.4 %reduce-scatter.9.cloned.1.call-done = bf16[64,576]{1,0:T(8,128)(2,1)} async-done(((bf16[256,576]{1,0:T(8,128)(2,1)}), bf16[64,576]{1,0:T(8,128)(2,1)}) %reduce-scatter.9.cloned.1.call-update) | async-done | bytes 73744 | tf_op jit(solution)/shard_map/reduce_scatter | solution.py:211
  1512.7 9.3 collective-permute-done.60
  1532.3 43.9 %collective-permute-done.81 = bf16[512,2816]{1,0:T(8,128)(2,1)} collective-permute-done((bf16[512,2816]{1,0:T(8,128)(2,1)}, bf16[512,2816]{1,0:T(8,128)(2,1)}, u32[]{:S(2)}, u32[]{:S(2)}) %collective-permute-start.81) | collective-permute-done | bytes 2883616 | tf_op jit(solution)/shard_map/ppermute | solution.py:76
  1583.9 14.4 collective-permute-done.56
  1612.2 9.1 all-to-all-done.4
  1681.5 14.2 all-to-all-done.5
  (980 shorter events, 710.9 us)
Async XLA Ops:
  7.2 68.7 %collective-permute-start = (s32[2048,6]{0,1:T(8,128)}, s32[2048,6]{0,1:T(8,128)}, u32[]{:S(2)}, u32[]{:S(2)}) collective-permute-start(s32[2048,6]{0,1:T(8,128)} %param.47), channel_id=1, source_target_pairs={{0,16},{8,24},{16,0},{24,8},{1,17},{9,25},{17,1},{25,9},{2,18},{10... | collective-permute-start | bytes 147464 | tf_op jit(solution)/shard_map/ppermute | solution.py:76
  11.3 64.6 %collective-permute-start.1 = (f32[2048,6]{0,1:T(8,128)}, f32[2048,6]{0,1:T(8,128)S(1)}, u32[]{:S(2)}, u32[]{:S(2)}) collective-permute-start(f32[2048,6]{0,1:T(8,128)} %param.48), channel_id=1, source_target_pairs={{0,16},{8,24},{16,0},{24,8},{1,17},{9,25},{17,1},{25,9},{2,18},{10... | collective-permute-start | bytes 147464 | tf_op jit(solution)/shard_map/ppermute | solution.py:76
  39.1 91.9 %all-gather.11.cloned.1.call-start = ((), (), s32[]{:S(2)}) async-start(), calls=%async_computation.22 | async-start | bytes 2396160 | tf_op jit(solution)/shard_map/all_gather | solution.py:202
  76.0 123.8 %all-gather.13.cloned.1.call-start = ((), (), s32[]{:S(2)}) async-start(), calls=%async_computation.23 | async-start | bytes 1966080 | tf_op jit(solution)/shard_map/all_gather | solution.py:202
  87.3 57.2 %collective-permute-start.5 = (bf16[1,2048,256]{2,1,0:T(8,128)(2,1)}, bf16[1,2048,256]{2,1,0:T(8,128)(2,1)}, u32[]{:S(2)}, u32[]{:S(2)}) collective-permute-start(bf16[1,2048,256]{2,1,0:T(8,128)(2,1)} %bitcast.14), channel_id=1, source_target_pairs={{0,1},{1,0},{2,3},{3,2},{4,5},{5,4},{6,7},{7,6},{8,9},{9,8},{10,11... | collective-permute-start | bytes 3145736 | tf_op jit(solution)/shard_map/ppermute | solution.py:130
  98.1 54.3 %all-to-all-start.3 = ((bf16[4,640,256]{2,1,0:T(8,128)(2,1)}), bf16[4,640,256]{2,1,0:T(8,128)(2,1)S(1)}, u32[]{:S(2)}, u32[]{:S(2)}) async-start(bf16[4,640,256]{2,1,0:T(8,128)(2,1)} %bitcast.12), calls=%async_computation.3 | async-start | bytes 2621440 | tf_op jit(solution)/shard_map/all_to_all | solution.py:232
  101.6 591.1 %all-gather.9.cloned.1.call-start = ((), (), s32[]{:S(2)}) async-start(), calls=%async_computation.15 | async-start | bytes 3604480 | tf_op jit(solution)/shard_map/all_gather | solution.py:202
  131.0 572.7 %all-gather.7.cloned.1.call-start = ((), (), s32[]{:S(2)}) async-start(), calls=%async_computation.14 | async-start | bytes 1802240 | tf_op jit(solution)/shard_map/all_gather | solution.py:202
  142.5 90.8 %collective-permute-start.8 = (bf16[2,2048,256]{2,1,0:T(8,128)(2,1)}, bf16[2,2048,256]{2,1,0:T(8,128)(2,1)}, u32[]{:S(2)}, u32[]{:S(2)}) collective-permute-start(bf16[2,2048,256]{2,1,0:T(8,128)(2,1)} %pad_maximum_fusion.24), channel_id=1, source_target_pairs={{0,4},{1,3},{2,6},{3,1},{4,0},{5,7},{6,2},{7,5},{8,12},{9,11},{10,... | collective-permute-start | bytes 6291464 | tf_op jit(solution)/shard_map/ppermute | solution.py:140
  157.9 64.2 %collective-permute-start.29 = (bf16[2048,256]{1,0:T(8,128)(2,1)}, bf16[2048,256]{1,0:T(8,128)(2,1)}, u32[]{:S(2)}, u32[]{:S(2)}) collective-permute-start(bf16[2048,256]{1,0:T(8,128)(2,1)} %fusion.121), channel_id=1, source_target_pairs={{0,16},{8,24},{16,0},{24,8},{1,17},{9,25},{17,1},{25,9},{2,18},{10... | collective-permute-start | bytes 3145736 | tf_op jit(solution)/shard_map/ppermute | solution.py:76
  157.9 328.6 %collective-permute-start.2 = (bf16[512,2816]{1,0:T(8,128)(2,1)}, bf16[512,2816]{1,0:T(8,128)(2,1)}, u32[]{:S(2)}, u32[]{:S(2)}) collective-permute-start(bf16[512,2816]{1,0:T(8,128)(2,1)} %pad_maximum_fusion.18), channel_id=1, source_target_pairs={{0,8},{8,0},{16,24},{24,16},{1,9},{9,1},{17,25},{25,17},{2,10},{10... | collective-permute-start | bytes 8650760 | tf_op jit(solution)/shard_map/ppermute | solution.py:76
  160.9 284.8 %collective-permute-start.35 = (bf16[1408,512]{1,0:T(8,128)(2,1)}, bf16[1408,512]{1,0:T(8,128)(2,1)}, u32[]{:S(2)}, u32[]{:S(2)}) collective-permute-start(bf16[1408,512]{1,0:T(8,128)(2,1)} %get-tuple-element.432), channel_id=1, source_target_pairs={{0,8},{8,0},{16,24},{24,16},{1,9},{9,1},{17,25},{25,17},{2,10},{10... | collective-permute-start | bytes 4325384 | tf_op jit(solution)/shard_map/ppermute | solution.py:76
  204.3 558.4 %reduce-scatter.17.cloned.1.call-start = ((), (), s32[]{:S(2)}) async-start(), calls=%async_computation.21 | async-start | bytes 1802240 | tf_op jit(solution)/shard_map/reduce_scatter | solution.py:211
  233.3 130.1 %collective-permute-start.9 = (bf16[2,2048,256]{2,1,0:T(8,128)(2,1)}, bf16[2,2048,256]{2,1,0:T(8,128)(2,1)}, u32[]{:S(2)}, u32[]{:S(2)}) collective-permute-start(bf16[2,2048,256]{2,1,0:T(8,128)(2,1)} %collective-permute-done.8), channel_id=1, source_target_pairs={{0,1},{1,0},{2,3},{3,2},{4,5},{5,4},{6,7},{7,6},{8,9},{9,8},{10,11... | collective-permute-start | bytes 6291464 | tf_op jit(solution)/shard_map/ppermute | solution.py:130
  242.0 120.4 %collective-permute-start.36 = (bf16[1408,512]{1,0:T(8,128)(2,1)}, bf16[1408,512]{1,0:T(8,128)(2,1)}, u32[]{:S(2)}, u32[]{:S(2)}) collective-permute-start(bf16[1408,512]{1,0:T(8,128)(2,1)} %get-tuple-element.433), channel_id=1, source_target_pairs={{0,16},{8,24},{16,0},{24,8},{1,17},{9,25},{17,1},{25,9},{2,18},{10... | collective-permute-start | bytes 4325384 | tf_op jit(solution)/shard_map/ppermute | solution.py:76
  249.9 228.9 %collective-permute-start.3 = (bf16[512,2816]{1,0:T(8,128)(2,1)}, bf16[512,2816]{1,0:T(8,128)(2,1)}, u32[]{:S(2)}, u32[]{:S(2)}) collective-permute-start(bf16[512,2816]{1,0:T(8,128)(2,1)} %pad_maximum_fusion.19), channel_id=1, source_target_pairs={{0,16},{8,24},{16,0},{24,8},{1,17},{9,25},{17,1},{25,9},{2,18},{10... | collective-permute-start | bytes 8650760 | tf_op jit(solution)/shard_map/ppermute | solution.py:76
  362.5 131.2 %collective-permute-start.31 = (bf16[1,4096,256]{2,1,0:T(8,128)(2,1)}, bf16[1,4096,256]{2,1,0:T(8,128)(2,1)}, u32[]{:S(2)}, u32[]{:S(2)}) collective-permute-start(bf16[1,4096,256]{2,1,0:T(8,128)(2,1)} %get-tuple-element.607), channel_id=1, source_target_pairs={{0,2},{1,5},{2,0},{3,7},{4,6},{5,1},{6,4},{7,3},{8,10},{9,13},{10,... | collective-permute-start | bytes 6291464 | tf_op jit(solution)/shard_map/ppermute | solution.py:140
  363.4 120.5 %collective-permute-start.37 = (bf16[1408,512]{1,0:T(8,128)(2,1)}, bf16[1408,512]{1,0:T(8,128)(2,1)}, u32[]{:S(2)}, u32[]{:S(2)}) collective-permute-start(bf16[1408,512]{1,0:T(8,128)(2,1)} %collective-permute-done.36), channel_id=1, source_target_pairs={{0,8},{8,0},{16,24},{24,16},{1,9},{9,1},{17,25},{25,17},{2,10},{10... | collective-permute-start | bytes 4325384 | tf_op jit(solution)/shard_map/ppermute | solution.py:76
  484.0 87.6 %collective-permute-start.4 = (bf16[512,2816]{1,0:T(8,128)(2,1)}, bf16[512,2816]{1,0:T(8,128)(2,1)}, u32[]{:S(2)}, u32[]{:S(2)}) collective-permute-start(bf16[512,2816]{1,0:T(8,128)(2,1)} %collective-permute-done.3), channel_id=1, source_target_pairs={{0,8},{8,0},{16,24},{24,16},{1,9},{9,1},{17,25},{25,17},{2,10},{10... | collective-permute-start | bytes 8650760 | tf_op jit(solution)/shard_map/ppermute | solution.py:76
  498.3 76.9 %collective-permute-start.33 = (bf16[2,4096,256]{2,1,0:T(8,128)(2,1)}, bf16[2,4096,256]{2,1,0:T(8,128)(2,1)}, u32[]{:S(2)}, u32[]{:S(2)}) collective-permute-start(bf16[2,4096,256]{2,1,0:T(8,128)(2,1)} %pad_maximum_fusion.11), channel_id=1, source_target_pairs={{0,4},{1,3},{2,6},{3,1},{4,0},{5,7},{6,2},{7,5},{8,12},{9,11},{10,... | collective-permute-start | bytes 12582920 | tf_op jit(solution)/shard_map/ppermute | solution.py:140
  593.0 85.3 %collective-permute-start.18 = (bf16[1,256,2048]{2,1,0:T(8,128)(2,1)S(1)}, bf16[1,256,2048]{2,1,0:T(8,128)(2,1)}, u32[]{:S(2)}, u32[]{:S(2)}) collective-permute-start(bf16[1,256,2048]{2,1,0:T(8,128)(2,1)S(1)} %bitcast.593), channel_id=1, source_target_pairs={{0,1},{1,0},{2,3},{3,2},{4,5},{5,4},{6,7},{7,6},{8,9},{9,8},{10,11... | collective-permute-start | bytes 3145736 | tf_op jit(solution)/shard_map/ppermute | solution.py:130
  593.1 97.8 %collective-permute-start.23 = (bf16[256,2048]{1,0:T(8,128)(2,1)S(1)}, bf16[256,2048]{1,0:T(8,128)(2,1)S(1)}, u32[]{:S(2)}, u32[]{:S(2)}) collective-permute-start(bf16[256,2048]{1,0:T(8,128)(2,1)S(1)} %get-tuple-element.507), channel_id=1, source_target_pairs={{0,16},{8,24},{16,0},{24,8},{1,17},{9,25},{17,1},{25,9},{2,18},{10... | collective-permute-start | bytes 3145736 | tf_op jit(solution)/shard_map/ppermute | solution.py:76
  691.2 65.8 %collective-permute-start.24 = (bf16[1,256,2048]{2,1,0:T(8,128)(2,1)S(1)}, bf16[1,256,2048]{2,1,0:T(8,128)(2,1)}, u32[]{:S(2)}, u32[]{:S(2)}) collective-permute-start(bf16[1,256,2048]{2,1,0:T(8,128)(2,1)S(1)} %bitcast.597), channel_id=1, source_target_pairs={{0,1},{1,0},{2,3},{3,2},{4,5},{5,4},{6,7},{7,6},{8,9},{9,8},{10,11... | collective-permute-start | bytes 3145736 | tf_op jit(solution)/shard_map/ppermute | solution.py:130
  723.6 434.8 %reduce-scatter.15.cloned.1.call-start = ((), (), s32[]{:S(2)}) async-start(), calls=%async_computation.20 | async-start | bytes 3604480 | tf_op jit(solution)/shard_map/reduce_scatter | solution.py:211
  757.0 664.7 %reduce-scatter.11.cloned.1.call-start = ((), (), s32[]{:S(2)}) async-start(), calls=%async_computation.18 | async-start | bytes 655360 | tf_op jit(solution)/shard_map/reduce_scatter | solution.py:211
  948.3 68.7 %collective-permute-start.38 = (bf16[4,256,2048]{2,1,0:T(8,128)(2,1)}, bf16[4,256,2048]{2,1,0:T(8,128)(2,1)}, u32[]{:S(2)}, u32[]{:S(2)}) collective-permute-start(bf16[4,256,2048]{2,1,0:T(8,128)(2,1)} %pad_maximum_fusion.12), channel_id=1, source_target_pairs={{0,1},{1,0},{2,3},{3,2},{4,5},{5,4},{6,7},{7,6},{8,9},{9,8},{10,11... | collective-permute-start | bytes 12582920 | tf_op jit(solution)/shard_map/ppermute | solution.py:130
  986.6 163.3 %collective-permute-start.83 = (bf16[1408,512]{1,0:T(8,128)(2,1)S(1)}, bf16[1408,512]{1,0:T(8,128)(2,1)S(1)}, u32[]{:S(2)}, u32[]{:S(2)}) collective-permute-start(bf16[1408,512]{1,0:T(8,128)(2,1)S(1)} %get-tuple-element.579), channel_id=1, source_target_pairs={{0,8},{8,0},{16,24},{24,16},{1,9},{9,1},{17,25},{25,17},{2,10},{10... | collective-permute-start | bytes 4325384 | tf_op jit(solution)/shard_map/ppermute | solution.py:76
  987.2 249.6 %collective-permute-start.82 = (bf16[1408,512]{1,0:T(8,128)(2,1)}, bf16[1408,512]{1,0:T(8,128)(2,1)}, u32[]{:S(2)}, u32[]{:S(2)}) collective-permute-start(bf16[1408,512]{1,0:T(8,128)(2,1)} %get-tuple-element.578), channel_id=1, source_target_pairs={{0,8},{8,0},{16,24},{24,16},{1,9},{9,1},{17,25},{25,17},{2,10},{10... | collective-permute-start | bytes 4325384 | tf_op jit(solution)/shard_map/ppermute | solution.py:76
  994.3 166.5 %collective-permute-start.57 = (bf16[512,2816]{1,0:T(8,128)(2,1)}, bf16[512,2816]{1,0:T(8,128)(2,1)}, u32[]{:S(2)}, u32[]{:S(2)}) collective-permute-start(bf16[512,2816]{1,0:T(8,128)(2,1)} %get-tuple-element.525), channel_id=1, source_target_pairs={{0,8},{8,0},{16,24},{24,16},{1,9},{9,1},{17,25},{25,17},{2,10},{10... | collective-permute-start | bytes 8650760 | tf_op jit(solution)/shard_map/ppermute | solution.py:76
  1060.6 73.7 %collective-permute-start.44 = (bf16[256,2048]{1,0:T(8,128)(2,1)S(1)}, bf16[256,2048]{1,0:T(8,128)(2,1)S(1)}, u32[]{:S(2)}, u32[]{:S(2)}) collective-permute-start(bf16[256,2048]{1,0:T(8,128)(2,1)S(1)} %fusion.180), channel_id=1, source_target_pairs={{0,16},{8,24},{16,0},{24,8},{1,17},{9,25},{17,1},{25,9},{2,18},{10... | collective-permute-start | bytes 3145736 | tf_op jit(solution)/shard_map/ppermute | solution.py:76
  1076.8 151.7 %collective-permute-start.80 = (bf16[512,2816]{1,0:T(8,128)(2,1)}, bf16[512,2816]{1,0:T(8,128)(2,1)}, u32[]{:S(2)}, u32[]{:S(2)}) collective-permute-start(bf16[512,2816]{1,0:T(8,128)(2,1)} %get-tuple-element.524), channel_id=1, source_target_pairs={{0,8},{8,0},{16,24},{24,16},{1,9},{9,1},{17,25},{25,17},{2,10},{10... | collective-permute-start | bytes 8650760 | tf_op jit(solution)/shard_map/ppermute | solution.py:76
  1152.8 84.0 %collective-permute-start.84 = (bf16[1408,512]{1,0:T(8,128)(2,1)}, bf16[1408,512]{1,0:T(8,128)(2,1)}, u32[]{:S(2)}, u32[]{:S(2)}) collective-permute-start(bf16[1408,512]{1,0:T(8,128)(2,1)} %add_convert_fusion.16), channel_id=1, source_target_pairs={{0,16},{8,24},{16,0},{24,8},{1,17},{9,25},{17,1},{25,9},{2,18},{10... | collective-permute-start | bytes 4325384 | tf_op jit(solution)/shard_map/ppermute | solution.py:76
  1157.8 85.3 %collective-permute-start.48 = (bf16[2,256,2048]{2,1,0:T(8,128)(2,1)}, bf16[2,256,2048]{2,1,0:T(8,128)(2,1)}, u32[]{:S(2)}, u32[]{:S(2)}) collective-permute-start(bf16[2,256,2048]{2,1,0:T(8,128)(2,1)} %pad_maximum_fusion.28), channel_id=1, source_target_pairs={{0,4},{1,3},{2,6},{3,1},{4,0},{5,7},{6,2},{7,5},{8,12},{9,11},{10,... | collective-permute-start | bytes 6291464 | tf_op jit(solution)/shard_map/ppermute | solution.py:140
  1324.2 74.0 %collective-permute-start.58 = (bf16[4,256,2048]{2,1,0:T(8,128)(2,1)}, bf16[4,256,2048]{2,1,0:T(8,128)(2,1)}, u32[]{:S(2)}, u32[]{:S(2)}) collective-permute-start(bf16[4,256,2048]{2,1,0:T(8,128)(2,1)} %pad_maximum_fusion.16), channel_id=1, source_target_pairs={{0,1},{1,0},{2,3},{3,2},{4,5},{5,4},{6,7},{7,6},{8,9},{9,8},{10,11... | collective-permute-start | bytes 12582920 | tf_op jit(solution)/shard_map/ppermute | solution.py:130
  1353.3 114.8 %reduce-scatter.13.cloned.1.call-start = ((), (), s32[]{:S(2)}) async-start(), calls=%async_computation.19 | async-start | bytes 1310720 | tf_op jit(solution)/shard_map/reduce_scatter | solution.py:211
  1376.4 114.9 %reduce-scatter.9.cloned.1.call-start = ((), (), s32[]{:S(2)}) async-start(), calls=%async_computation.17 | async-start | bytes 409600 | tf_op jit(solution)/shard_map/reduce_scatter | solution.py:211
  1378.2 198.0 %collective-permute-start.81 = (bf16[512,2816]{1,0:T(8,128)(2,1)}, bf16[512,2816]{1,0:T(8,128)(2,1)}, u32[]{:S(2)}, u32[]{:S(2)}) collective-permute-start(bf16[512,2816]{1,0:T(8,128)(2,1)} %get-tuple-element.440), channel_id=1, source_target_pairs={{0,16},{8,24},{16,0},{24,8},{1,17},{9,25},{17,1},{25,9},{2,18},{10... | collective-permute-start | bytes 8650760 | tf_op jit(solution)/shard_map/ppermute | solution.py:76
  1391.6 241.1 %reduce-scatter.7.cloned.1.call-start = ((), (), s32[]{:S(2)}) async-start(), calls=%async_computation.16 | async-start | bytes 1966080 | tf_op jit(solution)/shard_map/reduce_scatter | solution.py:211
  1397.3 95.5 %collective-permute-start.54 = (bf16[2,256,2048]{2,1,0:T(8,128)(2,1)}, bf16[2,256,2048]{2,1,0:T(8,128)(2,1)}, u32[]{:S(2)}, u32[]{:S(2)}) collective-permute-start(bf16[2,256,2048]{2,1,0:T(8,128)(2,1)} %slice.906), channel_id=1, source_target_pairs={{0,4},{1,3},{2,6},{3,1},{4,0},{5,7},{6,2},{7,5},{8,12},{9,11},{10,... | collective-permute-start | bytes 6291464 | tf_op jit(solution)/shard_map/ppermute | solution.py:140
  1407.1 89.7 %collective-permute-start.59 = (bf16[2,256,2048]{2,1,0:T(8,128)(2,1)}, bf16[2,256,2048]{2,1,0:T(8,128)(2,1)}, u32[]{:S(2)}, u32[]{:S(2)}) collective-permute-start(bf16[2,256,2048]{2,1,0:T(8,128)(2,1)} %slice.915), channel_id=1, source_target_pairs={{0,4},{1,3},{2,6},{3,1},{4,0},{5,7},{6,2},{7,5},{8,12},{9,11},{10,... | collective-permute-start | bytes 6291464 | tf_op jit(solution)/shard_map/ppermute | solution.py:140
  1415.0 85.6 %collective-permute-start.51 = (bf16[2,256,2048]{2,1,0:T(8,128)(2,1)}, bf16[2,256,2048]{2,1,0:T(8,128)(2,1)S(1)}, u32[]{:S(2)}, u32[]{:S(2)}) collective-permute-start(bf16[2,256,2048]{2,1,0:T(8,128)(2,1)} %slice.902), channel_id=1, source_target_pairs={{0,4},{1,3},{2,6},{3,1},{4,0},{5,7},{6,2},{7,5},{8,12},{9,11},{10,... | collective-permute-start | bytes 6291464 | tf_op jit(solution)/shard_map/ppermute | solution.py:140
  1491.3 89.6 %collective-permute-start.76 = (bf16[1,64,576]{2,1,0:T(8,128)(2,1)}, bf16[1,64,576]{2,1,0:T(8,128)(2,1)}, u32[]{:S(2)}, u32[]{:S(2)}) collective-permute-start(bf16[1,64,576]{2,1,0:T(8,128)(2,1)} %bitcast.638), channel_id=1, source_target_pairs={{0,2},{1,5},{2,0},{3,7},{4,6},{5,1},{6,4},{7,3},{8,10},{9,13},{10,... | collective-permute-start | bytes 221192 | tf_op jit(solution)/shard_map/ppermute | solution.py:140
  1502.6 80.8 %collective-permute-start.52 = (bf16[1,256,2048]{2,1,0:T(8,128)(2,1)}, bf16[1,256,2048]{2,1,0:T(8,128)(2,1)}, u32[]{:S(2)}, u32[]{:S(2)}) collective-permute-start(bf16[1,256,2048]{2,1,0:T(8,128)(2,1)} %slice.904), channel_id=1, source_target_pairs={{0,2},{1,5},{2,0},{3,7},{4,6},{5,1},{6,4},{7,3},{8,10},{9,13},{10,... | collective-permute-start | bytes 3145736 | tf_op jit(solution)/shard_map/ppermute | solution.py:140
  1512.1 86.2 %collective-permute-start.56 = (bf16[256,2048]{1,0:T(8,128)(2,1)}, bf16[256,2048]{1,0:T(8,128)(2,1)}, u32[]{:S(2)}, u32[]{:S(2)}) collective-permute-start(bf16[256,2048]{1,0:T(8,128)(2,1)} %fusion.181), channel_id=1, source_target_pairs={{0,16},{8,24},{16,0},{24,8},{1,17},{9,25},{17,1},{25,9},{2,18},{10... | collective-permute-start | bytes 3145736 | tf_op jit(solution)/shard_map/ppermute | solution.py:76
  1527.6 73.9 %all-to-all-start.6 = ((bf16[256,8,256]{2,0,1:T(8,128)(2,1)}), bf16[256,8,256]{2,0,1:T(8,128)(2,1)}, u32[]{:S(2)}, u32[]{:S(2)}) async-start(bf16[256,8,256]{2,0,1:T(8,128)(2,1)} %bitcast.595), calls=%async_computation.6 | async-start | bytes 2097152 | tf_op jit(solution)/shard_map/all_to_all | solution.py:616
  1580.9 55.2 %collective-permute-start.75 = (bf16[1,64,576]{2,1,0:T(8,128)(2,1)S(1)}, bf16[1,64,576]{2,1,0:T(8,128)(2,1)}, u32[]{:S(2)}, u32[]{:S(2)}) collective-permute-start(bf16[1,64,576]{2,1,0:T(8,128)(2,1)S(1)} %bitcast.639), channel_id=1, source_target_pairs={{0,1},{1,0},{2,3},{3,2},{4,5},{5,4},{6,7},{7,6},{8,9},{9,8},{10,11... | collective-permute-start | bytes 221192 | tf_op jit(solution)/shard_map/ppermute | solution.py:130
  1582.5 63.4 %collective-permute-start.78 = (bf16[2,64,576]{2,1,0:T(8,128)(2,1)}, bf16[2,64,576]{2,1,0:T(8,128)(2,1)}, u32[]{:S(2)}, u32[]{:S(2)}) collective-permute-start(bf16[2,64,576]{2,1,0:T(8,128)(2,1)} %pad_maximum_fusion.48), channel_id=1, source_target_pairs={{0,4},{1,3},{2,6},{3,1},{4,0},{5,7},{6,2},{7,5},{8,12},{9,11},{10,... | collective-permute-start | bytes 442376 | tf_op jit(solution)/shard_map/ppermute | solution.py:140
  1583.2 58.3 %collective-permute-start.77 = (bf16[1,64,576]{2,1,0:T(8,128)(2,1)}, bf16[1,64,576]{2,1,0:T(8,128)(2,1)}, u32[]{:S(2)}, u32[]{:S(2)}) collective-permute-start(bf16[1,64,576]{2,1,0:T(8,128)(2,1)} %collective-permute-done.76), channel_id=1, source_target_pairs={{0,1},{1,0},{2,3},{3,2},{4,5},{5,4},{6,7},{7,6},{8,9},{9,8},{10,11... | collective-permute-start | bytes 221192 | tf_op jit(solution)/shard_map/ppermute | solution.py:130
  (246 other events, 4583.6 us)
Sparse Core Ops, SparseCore 0:
  76.1 54.8 all-gather.10
  133.1 66.6 all-gather.12
  202.0 144.9 all-gather.8
  348.3 110.5 all-gather.6
  723.7 32.6 reduce-scatter.16
  758.6 55.0 reduce-scatter.14
  1353.4 21.0 reduce-scatter.10
  1376.8 91.2 reduce-scatter.12
  1471.0 20.2 reduce-scatter.8
  1493.5 64.7 reduce-scatter.6

commit v11 on v10

--- a/solution.py
+++ b/solution.py
@@ -174,16 +174,16 @@
     return out
 
 
-def cube_scatter(value):
+def cube_scatter(value, axis=0):
     count = lax.axis_size("col")
     index = lax.axis_index("col")
-    rows = value.shape[0] // count
+    rows = value.shape[axis] // count
     value = row_major(value)
 
     def blocks(device):
         return jnp.stack(
             [
-                lax.dynamic_slice_in_dim(value, block_at(device, place) * rows, rows, 0)
+                lax.dynamic_slice_in_dim(value, block_at(device, place) * rows, rows, axis)
                 for place in range(count // 2)
             ]
         )
@@ -542,8 +542,8 @@
     mate_terms = dot_tn(mate_pick, result_rows[capacity:]).astype(BF16)
     moe_terms = (moe_terms + dot_tn(pick, result_rows[:capacity])).astype(BF16)
     mate_terms, moe_terms = after((mate_terms, moe_terms), (grad_attn,))
-    mate_terms = mate(cube_scatter(mate_terms).astype(BF16))
-    moe_part = cube_scatter(moe_terms) + mate_terms.astype(F32)
+    both_terms = cube_scatter(jnp.stack([moe_terms, mate_terms]), 1)
+    moe_part = both_terms[0] + mate(both_terms[1].astype(BF16)).astype(F32)
     result_part = (hidden_part + moe_part).astype(BF16)
     result_slice = lax.all_to_all(result_part, "col", split_axis=1, concat_axis=0, tiled=True)
     result = exchange(result_slice, back_list, back_slots)
@@ -593,7 +593,6 @@
     )
     own_gu, mate_gu = expert_scatter(grad_gu, 0)
     own_down, mate_down = expert_scatter(grad_down, 1)
-    grad_query_raw, mate_gu = after((grad_query_raw, mate_gu), ())
     grad_one = cube_scatter(dot_nt(grad_query_raw, query_w).astype(BF16))
     grad_expanded = jnp.concatenate([grad_keys[..., :NOPE], grad_values], axis=-1).astype(BF16)
     grad_expanded = grad_expanded.reshape(group_rows, head_count * (NOPE + VDIM))

time: 1720 us -> 1710 us (level)
  other arithmetic: 240 us -> 268 us
  waiting for transfers between devices: 600 us -> 575 us
    reduce_scatter x6, waiting for transfers between devices: 66.1 us -> 1.73 us  [row_scatter(): return lax.psum_scatter(value, 'row', scatter_dimension=axis, tiled=True)]
    ppermute x18, waiting for transfers between devices: 332 us -> 372 us  [row_swap(): lax.ppermute(value, 'row', [(j, j ^ bit) for j in range(lax.axis_size('ro...]
    all_to_all x4, waiting for transfers between devices: 36.6 us -> 75.6 us  [exchange(): got = lax.all_to_all(sent, 'row', split_axis=0, concat_axis=0, tiled=True)]
    all_gather x4, waiting for transfers between devices: 51.4 us -> 20.7 us  [row_gather(): return lax.all_gather(shard, 'row', axis=axis, tiled=True)]
    ppermute x30 -> x28, waiting for transfers between devices: 101 us -> 93.3 us  [chip_swap(): lax.ppermute(value, 'col', [(j, j ^ (other if j % 2 else bits)[step]) for...]
    unnamed x398 -> x362, local copies, waits for them, and re-layouts: 37.7 us -> 40.3 us
    convert_element_type x14 -> x12, other arithmetic: 33 us -> 35.3 us  [cube_scatter(): held = held.astype(BF16)]
  transfers between devices with their start and end apart: 101 -> 98, of which waited for: 31 -> 27; matrix products, arithmetic and copies ran while one was open for 53% -> 57% of each run, Pallas kernels for 0% -> 0%
where the time goes in v11:
time: 1710 us; the launch traced here: 1700 us
  waiting for transfers between devices  575 us (34%)
  matrix products  446 us (26%)
  local copies, waits for them, and re-layouts  298 us (17%)
  other arithmetic  268 us (16%)
  starting transfers between devices  90.5 us (5%)
  between operations  18.5 us (1%)
    ppermute x18, waiting for transfers between devices, row_swap(): lax.ppermute(value, 'row', [(j, j ^ bit) for j in range(lax.axis_size('ro...  372 us
    dot_general x20, matrix products, dot(): return jnp.dot(left, right, preferred_element_type=F32)  187 us
    dot_general x12, matrix products, dot_tn(): lax.dot_general(left, right, (((0,), (0,)), ((), ())), preferred_element_...  126 us
    dot_general x9, matrix products, dot_nt(): lax.dot_general(left, right, (((1,), (1,)), ((), ())), preferred_element_...  97 us
    ppermute x28, waiting for transfers between devices, chip_swap(): lax.ppermute(value, 'col', [(j, j ^ (other if j % 2 else bits)[step]) for...  93.3 us
    dynamic_update_slice x60, local copies, waits for them, and re-layouts, cube_gather(): lax.dynamic_update_slice_in_dim(out, item, block_at(owner, place) * width...  91.1 us
    all_to_all x4, waiting for transfers between devices, exchange(): got = lax.all_to_all(sent, 'row', split_axis=0, concat_axis=0, tiled=True)  75.6 us
    unnamed x362, local copies, waits for them, and re-layouts  40.3 us
  transfers between devices with their start and end apart: 98, of which 27 were waited for; matrix products, arithmetic and copies ran while one was open for 57% of the time, Pallas kernels for 0%

profile of v11, /device:TPU:0, one launch (start us, length us, event | category | flops | bytes accessed | tf_op | source)
XLA Modules:
  0.0 1695.9 jit_solution(16878550631525997065)
XLA Ops:
  52.7 18.6 %all-to-all-done.2 = bf16[4,640,256]{2,1,0:T(8,128)(2,1)} async-done(((bf16[4,640,256]{2,1,0:T(8,128)(2,1)}), bf16[4,640,256]{2,1,0:T(8,128)(2,1)}, u32[]{:S(2)}, u32[]{:S(2)}) %all-to-all-start.2) | async-done | bytes 1310752 | tf_op jit(solution)/shard_map/all_to_all | solution.py:232
  97.8 20.7 %all-gather.11.cloned.1.call-done = bf16[2496,384]{1,0:T(8,128)(2,1)} async-done(((bf16[624,384]{1,0:T(8,128)(2,1)}), bf16[2496,384]{1,0:T(8,128)(2,1)}) %all-gather.11.cloned.1.call-update) | async-done | bytes 1916944 | tf_op jit(solution)/shard_map/all_gather | solution.py:202
  138.0 41.9 %all-to-all-done.3 = bf16[4,640,256]{2,1,0:T(8,128)(2,1)} async-done(((bf16[4,640,256]{2,1,0:T(8,128)(2,1)}), bf16[4,640,256]{2,1,0:T(8,128)(2,1)}, u32[]{:S(2)}, u32[]{:S(2)}) %all-to-all-start.3) | async-done | bytes 1310752 | tf_op jit(solution)/shard_map/all_to_all | solution.py:232
  216.5 53.4 %collective-permute-done.29 = bf16[2048,256]{1,0:T(8,128)(2,1)} collective-permute-done((bf16[2048,256]{1,0:T(8,128)(2,1)}, bf16[2048,256]{1,0:T(8,128)(2,1)}, u32[]{:S(2)}, u32[]{:S(2)}) %collective-permute-start.29) | collective-permute-done | bytes 1048608 | tf_op jit(solution)/shard_map/ppermute | solution.py:76
  304.7 98.2 %collective-permute-done.36 = bf16[1408,512]{1,0:T(8,128)(2,1)} collective-permute-done((bf16[1408,512]{1,0:T(8,128)(2,1)}, bf16[1408,512]{1,0:T(8,128)(2,1)}, u32[]{:S(2)}, u32[]{:S(2)}) %collective-permute-start.36) | collective-permute-done | bytes 1441824 | tf_op jit(solution)/shard_map/ppermute | solution.py:76
  416.8 8.7 fusion.29
  425.5 9.1 fusion.302
  485.7 16.5 collective-permute-done.3
  528.2 12.3 copy.346
  554.9 38.2 %collective-permute-done.16 = bf16[2,256,2048]{2,1,0:T(8,128)(2,1)S(1)} collective-permute-done((bf16[2,256,2048]{2,1,0:T(8,128)(2,1)S(1)}, bf16[2,256,2048]{2,1,0:T(8,128)(2,1)S(1)}, u32[]{:S(2)}, u32[]{:S(2)}) %collective-permute-start.16) | collective-permute-done | bytes 2097184 | tf_op jit(solution)/shard_map/ppermute | solution.py:140
  601.9 7.0 collective-permute-done.17
  625.5 24.2 %select_reduce_fusion.2 = (s32[2048]{0:T(1024)S(1)}, s32[2048]{0:T(1024)S(1)}) fusion(s32[4,2048]{1,0:T(4,128)} %get-tuple-element.417, pred[4,2048]{1,0:T(4,128)(4,1)S(1)} %copy-done.131, s32[4,2048]{1,0:T(4,128)} %get-tuple-element.419), kind=kLoop, calls=%fused_computation.32 | loop fusion | flops 100659200 | bytes 90112 | tf_op jit(solution)/shard_map/reduce_sum | solution.py:471
  662.3 12.6 multiply_convert_fusion.6
  674.9 9.2 collective-permute-done.21
  684.1 12.9 multiply_convert_fusion.5
  697.0 8.3 slice.873
  719.1 11.0 fusion.303
  730.2 11.1 multiply_convert_fusion.12
  742.4 7.7 convolution_convert_fusion.7
  752.6 13.7 fusion.88
  766.4 8.4 convolution_convert_fusion.3
  800.7 11.5 fusion.87
  814.2 34.6 %fusion.62 = f32[2048,2816]{1,0:T(8,128)} fusion(bf16[2048,2816]{1,0:T(8,128)(2,1)} %constant_dynamic-update-slice_fusion.8, bf16[1024,2048]{1,0:T(8,128)(2,1)S(1)} %fusion.87, bf16[1024,2048]{1,0:T(8,128)(2,1)S(1)} %copy-done.155), kind=kOutput, calls=%fused_computation.147 | convolution fusion | flops 23639097344 | bytes 42991616 | tf_op jit(solution)/shard_map/dot_general | solution.py:60
  848.8 26.6 %multiply_convert_fusion.1 = (bf16[2048,1408]{1,0:T(8,128)(2,1)}, bf16[2048,1408]{1,0:T(8,128)(2,1)}, bf16[2048,1408]{1,0:T(8,128)(2,1)}) fusion(f32[2048,2816]{1,0:T(8,128)} %fusion.62, bf16[1408,2048]{1,0:T(8,128)(2,1)} %constant_dynamic-update-slice_fusion, bf16[1024,2048]{1,0:T(8,128)(2,1)} %multiply_convert_fusion.5, ...), kind=kOutput, calls=%fused_computation.82 | convolution fusion | flops 11871191040 | bytes 54525952 | tf_op jit(solution)/shard_map/dot_general | solution.py:64
  882.0 15.8 fusion.58
  897.8 10.1 fusion.52
  913.4 15.1 fusion.381
  928.6 12.0 fusion.46
  940.6 11.2 add_convert_fusion.2
  960.8 30.8 %fusion.32 = bf16[2048,2816]{1,0:T(8,128)(2,1)} fusion(bf16[2048,1408]{1,0:T(8,128)(2,1)S(1)} %bitcast.581, bf16[2048,1408]{1,0:T(8,128)(2,1)} %get-tuple-element.516, bf16[1024,2048]{1,0:T(8,128)(2,1)} %copy-done.156, bf16[1024,2048]{1,0:T(8,128)(2,1)} %fusion.88), kind=kOutput, calls=%fused_computation.87 | convolution fusion | flops 23667933184 | bytes 31457280 | tf_op jit(solution)/shard_map/dot_general | solution.py:68
  998.0 16.2 convolution_convert_fusion.2
  1024.5 17.0 %multiply_convert_fusion = bf16[2048,2048]{1,0:T(8,128)(2,1)S(1)} fusion(bf16[2048,1408]{1,0:T(8,128)(2,1)} %get-tuple-element.433, bf16[1408,2048]{1,0:T(8,128)(2,1)} %constant_dynamic-update-slice_fusion, f32[2048]{0:T(1024)S(1)} %copy-done.138), kind=kOutput, calls=%fused_computation.74 | convolution fusion | flops 11819548672 | bytes 19931136 | tf_op jit(solution)/shard_map/dot_general | solution.py:60
  1041.6 17.5 %collective-permute-done.39 = bf16[2,256,2048]{2,1,0:T(8,128)(2,1)S(1)} collective-permute-done((bf16[2,256,2048]{2,1,0:T(8,128)(2,1)S(1)}, bf16[2,256,2048]{2,1,0:T(8,128)(2,1)S(1)}, u32[]{:S(2)}, u32[]{:S(2)}) %collective-permute-start.39) | collective-permute-done | bytes 2097184 | tf_op jit(solution)/shard_map/ppermute | solution.py:140
  1061.5 11.6 fusion.45
  1074.8 34.3 %collective-permute-done.44 = bf16[256,2048]{1,0:T(8,128)(2,1)S(1)} collective-permute-done((bf16[256,2048]{1,0:T(8,128)(2,1)S(1)}, bf16[256,2048]{1,0:T(8,128)(2,1)S(1)}, u32[]{:S(2)}, u32[]{:S(2)}) %collective-permute-start.44) | collective-permute-done | bytes 1048608 | tf_op jit(solution)/shard_map/ppermute | solution.py:76
  1114.1 11.1 fusion.53
  1134.0 10.5 add_convert_fusion.1
  1193.4 7.3 fusion.153
  1215.7 7.2 fusion.193
  1231.9 7.4 pad_maximum_fusion.6
  1255.5 8.3 convolution_convert_fusion
  1288.3 7.3 add_convert_fusion.9
  1312.1 7.4 add_convert_fusion
  1340.1 90.5 %collective-permute-done.81 = bf16[1408,512]{1,0:T(8,128)(2,1)} collective-permute-done((bf16[1408,512]{1,0:T(8,128)(2,1)}, bf16[1408,512]{1,0:T(8,128)(2,1)}, u32[]{:S(2)}, u32[]{:S(2)}) %collective-permute-start.81) | collective-permute-done | bytes 1441824 | tf_op jit(solution)/shard_map/ppermute | solution.py:76
  1462.5 29.7 %collective-permute-done.78 = bf16[512,2816]{1,0:T(8,128)(2,1)} collective-permute-done((bf16[512,2816]{1,0:T(8,128)(2,1)}, bf16[512,2816]{1,0:T(8,128)(2,1)}, u32[]{:S(2)}, u32[]{:S(2)}) %collective-permute-start.78) | collective-permute-done | bytes 2883616 | tf_op jit(solution)/shard_map/ppermute | solution.py:76
  1525.2 49.5 %collective-permute-done.53 = bf16[256,2048]{1,0:T(8,128)(2,1)} collective-permute-done((bf16[256,2048]{1,0:T(8,128)(2,1)}, bf16[256,2048]{1,0:T(8,128)(2,1)}, u32[]{:S(2)}, u32[]{:S(2)}) %collective-permute-start.53) | collective-permute-done | bytes 1048608 | tf_op jit(solution)/shard_map/ppermute | solution.py:76
  1588.8 9.0 all-to-all-done.4
  1664.7 15.1 all-to-all-done.5
  (931 shorter events, 709.3 us)
Async XLA Ops:
  7.2 69.3 %collective-permute-start = (s32[2048,6]{0,1:T(8,128)}, s32[2048,6]{0,1:T(8,128)}, u32[]{:S(2)}, u32[]{:S(2)}) collective-permute-start(s32[2048,6]{0,1:T(8,128)} %param.47), channel_id=1, source_target_pairs={{0,16},{8,24},{16,0},{24,8},{1,17},{9,25},{17,1},{25,9},{2,18},{10... | collective-permute-start | bytes 147464 | tf_op jit(solution)/shard_map/ppermute | solution.py:76
  11.3 65.2 %collective-permute-start.1 = (f32[2048,6]{0,1:T(8,128)}, f32[2048,6]{0,1:T(8,128)}, u32[]{:S(2)}, u32[]{:S(2)}) collective-permute-start(f32[2048,6]{0,1:T(8,128)} %param.48), channel_id=1, source_target_pairs={{0,16},{8,24},{16,0},{24,8},{1,17},{9,25},{17,1},{25,9},{2,18},{10... | collective-permute-start | bytes 147464 | tf_op jit(solution)/shard_map/ppermute | solution.py:76
  40.4 78.1 %all-gather.11.cloned.1.call-start = ((), (), s32[]{:S(2)}) async-start(), calls=%async_computation.22 | async-start | bytes 2396160 | tf_op jit(solution)/shard_map/all_gather | solution.py:202
  76.5 128.1 %all-gather.13.cloned.1.call-start = ((), (), s32[]{:S(2)}) async-start(), calls=%async_computation.23 | async-start | bytes 1966080 | tf_op jit(solution)/shard_map/all_gather | solution.py:202
  89.0 630.1 %all-gather.9.cloned.1.call-start = ((), (), s32[]{:S(2)}) async-start(), calls=%async_computation.15 | async-start | bytes 3604480 | tf_op jit(solution)/shard_map/all_gather | solution.py:202
  118.6 61.3 %all-to-all-start.3 = ((bf16[4,640,256]{2,1,0:T(8,128)(2,1)}), bf16[4,640,256]{2,1,0:T(8,128)(2,1)}, u32[]{:S(2)}, u32[]{:S(2)}) async-start(bf16[4,640,256]{2,1,0:T(8,128)(2,1)} %bitcast.621), calls=%async_computation.3 | async-start | bytes 2621440 | tf_op jit(solution)/shard_map/all_to_all | solution.py:232
  122.9 607.3 %all-gather.7.cloned.1.call-start = ((), (), s32[]{:S(2)}) async-start(), calls=%async_computation.14 | async-start | bytes 1802240 | tf_op jit(solution)/shard_map/all_gather | solution.py:202
  133.0 148.3 %collective-permute-start.8 = (bf16[2,2048,256]{2,1,0:T(8,128)(2,1)}, bf16[2,2048,256]{2,1,0:T(8,128)(2,1)}, u32[]{:S(2)}, u32[]{:S(2)}) collective-permute-start(bf16[2,2048,256]{2,1,0:T(8,128)(2,1)} %pad_maximum_fusion.23), channel_id=1, source_target_pairs={{0,4},{1,3},{2,6},{3,1},{4,0},{5,7},{6,2},{7,5},{8,12},{9,11},{10,... | collective-permute-start | bytes 6291464 | tf_op jit(solution)/shard_map/ppermute | solution.py:140
  134.5 67.7 %collective-permute-start.7 = (bf16[1,2048,256]{2,1,0:T(8,128)(2,1)S(1)}, bf16[1,2048,256]{2,1,0:T(8,128)(2,1)}, u32[]{:S(2)}, u32[]{:S(2)}) collective-permute-start(bf16[1,2048,256]{2,1,0:T(8,128)(2,1)S(1)} %collective-permute-done.6), channel_id=1, source_target_pairs={{0,1},{1,0},{2,3},{3,2},{4,5},{5,4},{6,7},{7,6},{8,9},{9,8},{10,11... | collective-permute-start | bytes 3145736 | tf_op jit(solution)/shard_map/ppermute | solution.py:130
  185.8 84.0 %collective-permute-start.29 = (bf16[2048,256]{1,0:T(8,128)(2,1)}, bf16[2048,256]{1,0:T(8,128)(2,1)}, u32[]{:S(2)}, u32[]{:S(2)}) collective-permute-start(bf16[2048,256]{1,0:T(8,128)(2,1)} %fusion.121), channel_id=1, source_target_pairs={{0,16},{8,24},{16,0},{24,8},{1,17},{9,25},{17,1},{25,9},{2,18},{10... | collective-permute-start | bytes 3145736 | tf_op jit(solution)/shard_map/ppermute | solution.py:76
  185.8 324.3 %collective-permute-start.2 = (bf16[512,2816]{1,0:T(8,128)(2,1)}, bf16[512,2816]{1,0:T(8,128)(2,1)}, u32[]{:S(2)}, u32[]{:S(2)}) collective-permute-start(bf16[512,2816]{1,0:T(8,128)(2,1)} %pad_maximum_fusion.17), channel_id=1, source_target_pairs={{0,8},{8,0},{16,24},{24,16},{1,9},{9,1},{17,25},{25,17},{2,10},{10... | collective-permute-start | bytes 8650760 | tf_op jit(solution)/shard_map/ppermute | solution.py:76
  185.8 299.8 %collective-permute-start.35 = (bf16[1408,512]{1,0:T(8,128)(2,1)}, bf16[1408,512]{1,0:T(8,128)(2,1)}, u32[]{:S(2)}, u32[]{:S(2)}) collective-permute-start(bf16[1408,512]{1,0:T(8,128)(2,1)} %get-tuple-element.430), channel_id=1, source_target_pairs={{0,8},{8,0},{16,24},{24,16},{1,9},{9,1},{17,25},{25,17},{2,10},{10... | collective-permute-start | bytes 4325384 | tf_op jit(solution)/shard_map/ppermute | solution.py:76
  209.1 580.3 %reduce-scatter.17.cloned.1.call-start = ((), (), s32[]{:S(2)}) async-start(), calls=%async_computation.21 | async-start | bytes 1802240 | tf_op jit(solution)/shard_map/reduce_scatter | solution.py:211
  213.3 74.7 %collective-permute-start.10 = (bf16[1,256,576]{2,1,0:T(8,128)(2,1)S(1)}, bf16[1,256,576]{2,1,0:T(8,128)(2,1)}, u32[]{:S(2)}, u32[]{:S(2)}) collective-permute-start(bf16[1,256,576]{2,1,0:T(8,128)(2,1)S(1)} %broadcast_in_dim.239), channel_id=1, source_target_pairs={{0,1},{1,0},{2,3},{3,2},{4,5},{5,4},{6,7},{7,6},{8,9},{9,8},{10,11... | collective-permute-start | bytes 884744 | tf_op jit(solution)/shard_map/ppermute | solution.py:130
  281.3 123.1 %collective-permute-start.9 = (bf16[2,2048,256]{2,1,0:T(8,128)(2,1)}, bf16[2,2048,256]{2,1,0:T(8,128)(2,1)}, u32[]{:S(2)}, u32[]{:S(2)}) collective-permute-start(bf16[2,2048,256]{2,1,0:T(8,128)(2,1)} %collective-permute-done.8), channel_id=1, source_target_pairs={{0,1},{1,0},{2,3},{3,2},{4,5},{5,4},{6,7},{7,6},{8,9},{9,8},{10,11... | collective-permute-start | bytes 6291464 | tf_op jit(solution)/shard_map/ppermute | solution.py:130
  289.6 113.2 %collective-permute-start.36 = (bf16[1408,512]{1,0:T(8,128)(2,1)}, bf16[1408,512]{1,0:T(8,128)(2,1)}, u32[]{:S(2)}, u32[]{:S(2)}) collective-permute-start(bf16[1408,512]{1,0:T(8,128)(2,1)} %get-tuple-element.431), channel_id=1, source_target_pairs={{0,16},{8,24},{16,0},{24,8},{1,17},{9,25},{17,1},{25,9},{2,18},{10... | collective-permute-start | bytes 4325384 | tf_op jit(solution)/shard_map/ppermute | solution.py:76
  297.9 204.3 %collective-permute-start.3 = (bf16[512,2816]{1,0:T(8,128)(2,1)}, bf16[512,2816]{1,0:T(8,128)(2,1)}, u32[]{:S(2)}, u32[]{:S(2)}) collective-permute-start(bf16[512,2816]{1,0:T(8,128)(2,1)} %pad_maximum_fusion.18), channel_id=1, source_target_pairs={{0,16},{8,24},{16,0},{24,8},{1,17},{9,25},{17,1},{25,9},{2,18},{10... | collective-permute-start | bytes 8650760 | tf_op jit(solution)/shard_map/ppermute | solution.py:76
  402.9 114.4 %collective-permute-start.31 = (bf16[1,4096,256]{2,1,0:T(8,128)(2,1)}, bf16[1,4096,256]{2,1,0:T(8,128)(2,1)}, u32[]{:S(2)}, u32[]{:S(2)}) collective-permute-start(bf16[1,4096,256]{2,1,0:T(8,128)(2,1)} %get-tuple-element.595), channel_id=1, source_target_pairs={{0,2},{1,5},{2,0},{3,7},{4,6},{5,1},{6,4},{7,3},{8,10},{9,13},{10,... | collective-permute-start | bytes 6291464 | tf_op jit(solution)/shard_map/ppermute | solution.py:140
  404.4 102.9 %collective-permute-start.37 = (bf16[1408,512]{1,0:T(8,128)(2,1)}, bf16[1408,512]{1,0:T(8,128)(2,1)}, u32[]{:S(2)}, u32[]{:S(2)}) collective-permute-start(bf16[1408,512]{1,0:T(8,128)(2,1)} %collective-permute-done.36), channel_id=1, source_target_pairs={{0,8},{8,0},{16,24},{24,16},{1,9},{9,1},{17,25},{25,17},{2,10},{10... | collective-permute-start | bytes 4325384 | tf_op jit(solution)/shard_map/ppermute | solution.py:76
  507.3 87.9 %collective-permute-start.4 = (bf16[512,2816]{1,0:T(8,128)(2,1)}, bf16[512,2816]{1,0:T(8,128)(2,1)}, u32[]{:S(2)}, u32[]{:S(2)}) collective-permute-start(bf16[512,2816]{1,0:T(8,128)(2,1)} %collective-permute-done.3), channel_id=1, source_target_pairs={{0,8},{8,0},{16,24},{24,16},{1,9},{9,1},{17,25},{25,17},{2,10},{10... | collective-permute-start | bytes 8650760 | tf_op jit(solution)/shard_map/ppermute | solution.py:76
  521.9 77.0 %collective-permute-start.33 = (bf16[2,4096,256]{2,1,0:T(8,128)(2,1)}, bf16[2,4096,256]{2,1,0:T(8,128)(2,1)}, u32[]{:S(2)}, u32[]{:S(2)}) collective-permute-start(bf16[2,4096,256]{2,1,0:T(8,128)(2,1)} %pad_maximum_fusion.12), channel_id=1, source_target_pairs={{0,4},{1,3},{2,6},{3,1},{4,0},{5,7},{6,2},{7,5},{8,12},{9,11},{10,... | collective-permute-start | bytes 12582920 | tf_op jit(solution)/shard_map/ppermute | solution.py:140
  545.5 47.5 %collective-permute-start.16 = (bf16[2,256,2048]{2,1,0:T(8,128)(2,1)S(1)}, bf16[2,256,2048]{2,1,0:T(8,128)(2,1)S(1)}, u32[]{:S(2)}, u32[]{:S(2)}) collective-permute-start(bf16[2,256,2048]{2,1,0:T(8,128)(2,1)S(1)} %slice.851), channel_id=1, source_target_pairs={{0,4},{1,3},{2,6},{3,1},{4,0},{5,7},{6,2},{7,5},{8,12},{9,11},{10,... | collective-permute-start | bytes 6291464 | tf_op jit(solution)/shard_map/ppermute | solution.py:140
  598.8 51.5 %collective-permute-start.34 = (bf16[2,4096,256]{2,1,0:T(8,128)(2,1)}, bf16[2,4096,256]{2,1,0:T(8,128)(2,1)}, u32[]{:S(2)}, u32[]{:S(2)}) collective-permute-start(bf16[2,4096,256]{2,1,0:T(8,128)(2,1)} %collective-permute-done.33), channel_id=1, source_target_pairs={{0,1},{1,0},{2,3},{3,2},{4,5},{5,4},{6,7},{7,6},{8,9},{9,8},{10,11... | collective-permute-start | bytes 12582920 | tf_op jit(solution)/shard_map/ppermute | solution.py:130
  616.6 88.7 %collective-permute-start.18 = (bf16[1,256,2048]{2,1,0:T(8,128)(2,1)S(1)}, bf16[1,256,2048]{2,1,0:T(8,128)(2,1)}, u32[]{:S(2)}, u32[]{:S(2)}) collective-permute-start(bf16[1,256,2048]{2,1,0:T(8,128)(2,1)S(1)} %bitcast.583), channel_id=1, source_target_pairs={{0,1},{1,0},{2,3},{3,2},{4,5},{5,4},{6,7},{7,6},{8,9},{9,8},{10,11... | collective-permute-start | bytes 3145736 | tf_op jit(solution)/shard_map/ppermute | solution.py:130
  616.6 101.2 %collective-permute-start.23 = (bf16[256,2048]{1,0:T(8,128)(2,1)S(1)}, bf16[256,2048]{1,0:T(8,128)(2,1)S(1)}, u32[]{:S(2)}, u32[]{:S(2)}) collective-permute-start(bf16[256,2048]{1,0:T(8,128)(2,1)S(1)} %get-tuple-element.503), channel_id=1, source_target_pairs={{0,16},{8,24},{16,0},{24,8},{1,17},{9,25},{17,1},{25,9},{2,18},{10... | collective-permute-start | bytes 3145736 | tf_op jit(solution)/shard_map/ppermute | solution.py:76
  718.8 64.7 %collective-permute-start.24 = (bf16[1,256,2048]{2,1,0:T(8,128)(2,1)S(1)}, bf16[1,256,2048]{2,1,0:T(8,128)(2,1)}, u32[]{:S(2)}, u32[]{:S(2)}) collective-permute-start(bf16[1,256,2048]{2,1,0:T(8,128)(2,1)S(1)} %bitcast.586), channel_id=1, source_target_pairs={{0,1},{1,0},{2,3},{3,2},{4,5},{5,4},{6,7},{7,6},{8,9},{9,8},{10,11... | collective-permute-start | bytes 3145736 | tf_op jit(solution)/shard_map/ppermute | solution.py:130
  750.1 394.3 %reduce-scatter.15.cloned.1.call-start = ((), (), s32[]{:S(2)}) async-start(), calls=%async_computation.20 | async-start | bytes 3604480 | tf_op jit(solution)/shard_map/reduce_scatter | solution.py:211
  783.4 739.2 %reduce-scatter.9.cloned.1.call-start = ((), (), s32[]{:S(2)}) async-start(), calls=%async_computation.17 | async-start | bytes 409600 | tf_op jit(solution)/shard_map/reduce_scatter | solution.py:211
  956.5 61.5 %collective-permute-start.38 = (bf16[4,256,2048]{2,1,0:T(8,128)(2,1)}, bf16[4,256,2048]{2,1,0:T(8,128)(2,1)}, u32[]{:S(2)}, u32[]{:S(2)}) collective-permute-start(bf16[4,256,2048]{2,1,0:T(8,128)(2,1)} %pad_maximum_fusion.13), channel_id=1, source_target_pairs={{0,1},{1,0},{2,3},{3,2},{4,5},{5,4},{6,7},{7,6},{8,9},{9,8},{10,11... | collective-permute-start | bytes 12582920 | tf_op jit(solution)/shard_map/ppermute | solution.py:130
  1016.0 130.9 %collective-permute-start.80 = (bf16[1408,512]{1,0:T(8,128)(2,1)}, bf16[1408,512]{1,0:T(8,128)(2,1)}, u32[]{:S(2)}, u32[]{:S(2)}) collective-permute-start(bf16[1408,512]{1,0:T(8,128)(2,1)} %get-tuple-element.567), channel_id=1, source_target_pairs={{0,8},{8,0},{16,24},{24,16},{1,9},{9,1},{17,25},{25,17},{2,10},{10... | collective-permute-start | bytes 4325384 | tf_op jit(solution)/shard_map/ppermute | solution.py:76
  1016.1 324.1 %collective-permute-start.79 = (bf16[1408,512]{1,0:T(8,128)(2,1)}, bf16[1408,512]{1,0:T(8,128)(2,1)}, u32[]{:S(2)}, u32[]{:S(2)}) collective-permute-start(bf16[1408,512]{1,0:T(8,128)(2,1)} %get-tuple-element.566), channel_id=1, source_target_pairs={{0,8},{8,0},{16,24},{24,16},{1,9},{9,1},{17,25},{25,17},{2,10},{10... | collective-permute-start | bytes 4325384 | tf_op jit(solution)/shard_map/ppermute | solution.py:76
  1061.3 47.8 %collective-permute-start.44 = (bf16[256,2048]{1,0:T(8,128)(2,1)S(1)}, bf16[256,2048]{1,0:T(8,128)(2,1)S(1)}, u32[]{:S(2)}, u32[]{:S(2)}) collective-permute-start(bf16[256,2048]{1,0:T(8,128)(2,1)S(1)} %fusion.197), channel_id=1, source_target_pairs={{0,16},{8,24},{16,0},{24,8},{1,17},{9,25},{17,1},{25,9},{2,18},{10... | collective-permute-start | bytes 3145736 | tf_op jit(solution)/shard_map/ppermute | solution.py:76
  1134.0 152.9 %collective-permute-start.76 = (bf16[512,2816]{1,0:T(8,128)(2,1)}, bf16[512,2816]{1,0:T(8,128)(2,1)}, u32[]{:S(2)}, u32[]{:S(2)}) collective-permute-start(bf16[512,2816]{1,0:T(8,128)(2,1)} %get-tuple-element.528), channel_id=1, source_target_pairs={{0,8},{8,0},{16,24},{24,16},{1,9},{9,1},{17,25},{25,17},{2,10},{10... | collective-permute-start | bytes 8650760 | tf_op jit(solution)/shard_map/ppermute | solution.py:76
  1157.2 129.7 %collective-permute-start.77 = (bf16[512,2816]{1,0:T(8,128)(2,1)}, bf16[512,2816]{1,0:T(8,128)(2,1)}, u32[]{:S(2)}, u32[]{:S(2)}) collective-permute-start(bf16[512,2816]{1,0:T(8,128)(2,1)} %get-tuple-element.529), channel_id=1, source_target_pairs={{0,8},{8,0},{16,24},{24,16},{1,9},{9,1},{17,25},{25,17},{2,10},{10... | collective-permute-start | bytes 8650760 | tf_op jit(solution)/shard_map/ppermute | solution.py:76
  1239.3 72.8 %collective-permute-start.50 = (bf16[4,2,256,2048]{3,2,1,0:T(8,128)(2,1)}, bf16[4,2,256,2048]{3,2,1,0:T(8,128)(2,1)}, u32[]{:S(2)}, u32[]{:S(2)}) collective-permute-start(bf16[4,2,256,2048]{3,2,1,0:T(8,128)(2,1)} %pad_maximum_fusion.6), channel_id=1, source_target_pairs={{0,1},{1,0},{2,3},{3,2},{4,5},{5,4},{6,7},{7,6},{8,9},{9,8},{10,11... | collective-permute-start | bytes 25165832 | tf_op jit(solution)/shard_map/ppermute | solution.py:130
  1297.2 133.4 %collective-permute-start.81 = (bf16[1408,512]{1,0:T(8,128)(2,1)}, bf16[1408,512]{1,0:T(8,128)(2,1)}, u32[]{:S(2)}, u32[]{:S(2)}) collective-permute-start(bf16[1408,512]{1,0:T(8,128)(2,1)} %add_convert_fusion.14), channel_id=1, source_target_pairs={{0,16},{8,24},{16,0},{24,8},{1,17},{9,25},{17,1},{25,9},{2,18},{10... | collective-permute-start | bytes 4325384 | tf_op jit(solution)/shard_map/ppermute | solution.py:76
  1304.0 188.1 %collective-permute-start.78 = (bf16[512,2816]{1,0:T(8,128)(2,1)}, bf16[512,2816]{1,0:T(8,128)(2,1)}, u32[]{:S(2)}, u32[]{:S(2)}) collective-permute-start(bf16[512,2816]{1,0:T(8,128)(2,1)} %get-tuple-element.527), channel_id=1, source_target_pairs={{0,16},{8,24},{16,0},{24,8},{1,17},{9,25},{17,1},{25,9},{2,18},{10... | collective-permute-start | bytes 8650760 | tf_op jit(solution)/shard_map/ppermute | solution.py:76
  1323.9 130.6 %collective-permute-start.51 = (bf16[2,2,256,2048]{3,2,1,0:T(8,128)(2,1)}, bf16[2,2,256,2048]{3,2,1,0:T(8,128)(2,1)}, u32[]{:S(2)}, u32[]{:S(2)}) collective-permute-start(bf16[2,2,256,2048]{3,2,1,0:T(8,128)(2,1)} %slice.896), channel_id=1, source_target_pairs={{0,4},{1,3},{2,6},{3,1},{4,0},{5,7},{6,2},{7,5},{8,12},{9,11},{10,... | collective-permute-start | bytes 12582920 | tf_op jit(solution)/shard_map/ppermute | solution.py:140
  1331.5 277.0 %reduce-scatter.11.cloned.1.call-start = ((), (), s32[]{:S(2)}) async-start(), calls=%async_computation.18 | async-start | bytes 655360 | tf_op jit(solution)/shard_map/reduce_scatter | solution.py:211
  1339.2 110.1 %collective-permute-start.55 = (bf16[2,256,2048]{2,1,0:T(8,128)(2,1)}, bf16[2,256,2048]{2,1,0:T(8,128)(2,1)}, u32[]{:S(2)}, u32[]{:S(2)}) collective-permute-start(bf16[2,256,2048]{2,1,0:T(8,128)(2,1)} %slice.907), channel_id=1, source_target_pairs={{0,4},{1,3},{2,6},{3,1},{4,0},{5,7},{6,2},{7,5},{8,12},{9,11},{10,... | collective-permute-start | bytes 6291464 | tf_op jit(solution)/shard_map/ppermute | solution.py:140
  1437.3 172.8 %reduce-scatter.13.cloned.1.call-start = ((), (), s32[]{:S(2)}) async-start(), calls=%async_computation.19 | async-start | bytes 1310720 | tf_op jit(solution)/shard_map/reduce_scatter | solution.py:211
  1448.8 164.8 %reduce-scatter.7.cloned.1.call-start = ((), (), s32[]{:S(2)}) async-start(), calls=%async_computation.16 | async-start | bytes 1966080 | tf_op jit(solution)/shard_map/reduce_scatter | solution.py:211
  1453.5 49.1 %collective-permute-start.56 = (bf16[1,256,2048]{2,1,0:T(8,128)(2,1)}, bf16[1,256,2048]{2,1,0:T(8,128)(2,1)}, u32[]{:S(2)}, u32[]{:S(2)}) collective-permute-start(bf16[1,256,2048]{2,1,0:T(8,128)(2,1)} %slice.909), channel_id=1, source_target_pairs={{0,2},{1,5},{2,0},{3,7},{4,6},{5,1},{6,4},{7,3},{8,10},{9,13},{10,... | collective-permute-start | bytes 3145736 | tf_op jit(solution)/shard_map/ppermute | solution.py:140
  1510.2 64.5 %collective-permute-start.53 = (bf16[256,2048]{1,0:T(8,128)(2,1)}, bf16[256,2048]{1,0:T(8,128)(2,1)}, u32[]{:S(2)}, u32[]{:S(2)}) collective-permute-start(bf16[256,2048]{1,0:T(8,128)(2,1)} %fusion.198), channel_id=1, source_target_pairs={{0,16},{8,24},{16,0},{24,8},{1,17},{9,25},{17,1},{25,9},{2,18},{10... | collective-permute-start | bytes 3145736 | tf_op jit(solution)/shard_map/ppermute | solution.py:76
  1513.6 64.5 %all-to-all-start.6 = ((bf16[256,8,256]{2,0,1:T(8,128)(2,1)}), bf16[256,8,256]{2,0,1:T(8,128)(2,1)}, u32[]{:S(2)}, u32[]{:S(2)}) async-start(bf16[256,8,256]{2,0,1:T(8,128)(2,1)} %bitcast.524), calls=%async_computation.6 | async-start | bytes 2097152 | tf_op jit(solution)/shard_map/all_to_all | solution.py:615
  1522.7 79.5 %collective-permute-start.72 = (bf16[1,64,576]{2,1,0:T(8,128)(2,1)}, bf16[1,64,576]{2,1,0:T(8,128)(2,1)}, u32[]{:S(2)}, u32[]{:S(2)}) collective-permute-start(bf16[1,64,576]{2,1,0:T(8,128)(2,1)} %bitcast.630), channel_id=1, source_target_pairs={{0,2},{1,5},{2,0},{3,7},{4,6},{5,1},{6,4},{7,3},{8,10},{9,13},{10,... | collective-permute-start | bytes 221192 | tf_op jit(solution)/shard_map/ppermute | solution.py:140
  1524.6 92.5 %collective-permute-start.71 = (bf16[1,64,576]{2,1,0:T(8,128)(2,1)}, bf16[1,64,576]{2,1,0:T(8,128)(2,1)}, u32[]{:S(2)}, u32[]{:S(2)}) collective-permute-start(bf16[1,64,576]{2,1,0:T(8,128)(2,1)} %bitcast.631), channel_id=1, source_target_pairs={{0,1},{1,0},{2,3},{3,2},{4,5},{5,4},{6,7},{7,6},{8,9},{9,8},{10,11... | collective-permute-start | bytes 221192 | tf_op jit(solution)/shard_map/ppermute | solution.py:130
  1524.6 79.7 %collective-permute-start.60 = (f32[4608]{0:T(1024)S(1)}, f32[4608]{0:T(1024)S(1)}, u32[]{:S(2)}, u32[]{:S(2)}) collective-permute-start(f32[4608]{0:T(1024)S(1)} %pad_maximum_fusion.50), channel_id=1, source_target_pairs={{0,1},{1,0},{2,3},{3,2},{4,5},{5,4},{6,7},{7,6},{8,9},{9,8},{10,11... | collective-permute-start | bytes 55304 | tf_op jit(solution)/shard_map/ppermute | solution.py:130
  (224 other events, 4313.1 us)
Sparse Core Ops, SparseCore 0:
  76.6 41.8 all-gather.10
  120.7 58.6 all-gather.12
  181.6 102.7 all-gather.8
  285.8 96.9 all-gather.6
  750.3 30.6 reduce-scatter.16
  783.6 54.6 reduce-scatter.14
  1331.6 161.3 reduce-scatter.8
  1495.8 20.1 reduce-scatter.10
  1518.9 53.7 reduce-scatter.12
  1574.9 38.6 reduce-scatter.6

commit v12 on v11

--- a/solution.py
+++ b/solution.py
@@ -546,7 +546,6 @@
     moe_part = both_terms[0] + mate(both_terms[1].astype(BF16)).astype(F32)
     result_part = (hidden_part + moe_part).astype(BF16)
     result_slice = lax.all_to_all(result_part, "col", split_axis=1, concat_axis=0, tiled=True)
-    result = exchange(result_slice, back_list, back_slots)
 
     grad_output_w = queued_sum(dot_tn(mixed, grad_attn), 1)
     grad_mixed = dot_nt(grad_attn, output_w).astype(BF16)
@@ -613,18 +612,18 @@
     )
     grad_input = (grad_hidden_part + input_back).astype(BF16)
     grad_slice = lax.all_to_all(grad_input, "col", split_axis=1, concat_axis=0, tiled=True)
-    tokens_grad = exchange(grad_slice, back_list, back_slots)
+    dealt_back = jnp.concatenate([result_slice, grad_slice], axis=1)
+    given_back = exchange(dealt_back, back_list, back_slots)
 
     def more_back(carry):
         step, total = carry
         back_more, slots_more = maps_back(step)
-        dealt = jnp.concatenate([result_slice, grad_slice], axis=1)
-        return step + 1, total + exchange(dealt, back_more, slots_more)
+        return step + 1, total + exchange(dealt_back, back_more, slots_more)
 
     more = lax.while_loop(
         lambda carry: carry[0] < rounds,
         more_back,
-        (jnp.int32(1), jnp.concatenate([result, tokens_grad], axis=1)),
+        (jnp.int32(1), given_back),
     )[1]
     result, tokens_grad = more[:, :slice_width], more[:, slice_width:]
 

time: 1710 us -> 1820 us (1.064)
  waiting for transfers between devices: 575 us -> 682 us
    ppermute x18, waiting for transfers between devices: 372 us -> 457 us  [row_swap(): lax.ppermute(value, 'row', [(j, j ^ bit) for j in range(lax.axis_size('ro...]
    ppermute x28, waiting for transfers between devices: 93.3 us -> 137 us  [chip_swap(): lax.ppermute(value, 'col', [(j, j ^ (other if j % 2 else bits)[step]) for...]
    all_to_all x4 -> x3, waiting for transfers between devices: 75.6 us -> 61 us  [exchange(): got = lax.all_to_all(sent, 'row', split_axis=0, concat_axis=0, tiled=True)]
    dot_general x20 -> x18, matrix products: 187 us -> 184 us  [dot(): return jnp.dot(left, right, preferred_element_type=F32)]
    unnamed x362 -> x332, local copies, waits for them, and re-layouts: 40.3 us -> 39.2 us
  transfers between devices with their start and end apart: 98 -> 97, of which waited for: 27 -> 26; matrix products, arithmetic and copies ran while one was open for 57% -> 54% of each run, Pallas kernels for 0% -> 0%
where the time goes in v12:
time: 1820 us; the launch traced here: 1810 us
  waiting for transfers between devices  682 us (37%)
  matrix products  459 us (25%)
  local copies, waits for them, and re-layouts  304 us (17%)
  other arithmetic  266 us (15%)
  starting transfers between devices  82.1 us (5%)
    ppermute x18, waiting for transfers between devices, row_swap(): lax.ppermute(value, 'row', [(j, j ^ bit) for j in range(lax.axis_size('ro...  457 us
    dot_general x18, matrix products, dot(): return jnp.dot(left, right, preferred_element_type=F32)  184 us
    dot_general x12, matrix products, dot_tn(): lax.dot_general(left, right, (((0,), (0,)), ((), ())), preferred_element_...  137 us
    ppermute x28, waiting for transfers between devices, chip_swap(): lax.ppermute(value, 'col', [(j, j ^ (other if j % 2 else bits)[step]) for...  137 us
    dot_general x9, matrix products, dot_nt(): lax.dot_general(left, right, (((1,), (1,)), ((), ())), preferred_element_...  99 us
    dynamic_update_slice x60, local copies, waits for them, and re-layouts, cube_gather(): lax.dynamic_update_slice_in_dim(out, item, block_at(owner, place) * width...  98.3 us
    all_to_all x3, waiting for transfers between devices, exchange(): got = lax.all_to_all(sent, 'row', split_axis=0, concat_axis=0, tiled=True)  61 us
    unnamed x332, local copies, waits for them, and re-layouts  39.2 us
  transfers between devices with their start and end apart: 97, of which 26 were waited for; matrix products, arithmetic and copies ran while one was open for 54% of the time, Pallas kernels for 0%

profile of v12, /device:TPU:0, one launch (start us, length us, event | category | flops | bytes accessed | tf_op | source)
XLA Modules:
  0.0 1812.3 jit_solution(4830359576788053618)
XLA Ops:
  53.0 18.7 %all-to-all-done.2 = bf16[4,640,256]{2,1,0:T(8,128)(2,1)} async-done(((bf16[4,640,256]{2,1,0:T(8,128)(2,1)}), bf16[4,640,256]{2,1,0:T(8,128)(2,1)}, u32[]{:S(2)}, u32[]{:S(2)}) %all-to-all-start.2) | async-done | bytes 1310752 | tf_op jit(solution)/shard_map/all_to_all | solution.py:232
  98.2 20.7 %all-gather.11.cloned.1.call-done = bf16[2496,384]{1,0:T(8,128)(2,1)} async-done(((bf16[624,384]{1,0:T(8,128)(2,1)}), bf16[2496,384]{1,0:T(8,128)(2,1)}) %all-gather.11.cloned.1.call-update) | async-done | bytes 1916944 | tf_op jit(solution)/shard_map/all_gather | solution.py:202
  138.0 42.3 %all-to-all-done.3 = bf16[4,640,256]{2,1,0:T(8,128)(2,1)} async-done(((bf16[4,640,256]{2,1,0:T(8,128)(2,1)}), bf16[4,640,256]{2,1,0:T(8,128)(2,1)}, u32[]{:S(2)}, u32[]{:S(2)}) %all-to-all-start.3) | async-done | bytes 1310752 | tf_op jit(solution)/shard_map/all_to_all | solution.py:232
  217.1 53.4 %collective-permute-done.29 = bf16[2048,256]{1,0:T(8,128)(2,1)} collective-permute-done((bf16[2048,256]{1,0:T(8,128)(2,1)}, bf16[2048,256]{1,0:T(8,128)(2,1)}, u32[]{:S(2)}, u32[]{:S(2)}) %collective-permute-start.29) | collective-permute-done | bytes 1048608 | tf_op jit(solution)/shard_map/ppermute | solution.py:76
  304.9 98.3 %collective-permute-done.36 = bf16[1408,512]{1,0:T(8,128)(2,1)} collective-permute-done((bf16[1408,512]{1,0:T(8,128)(2,1)}, bf16[1408,512]{1,0:T(8,128)(2,1)}, u32[]{:S(2)}, u32[]{:S(2)}) %collective-permute-start.36) | collective-permute-done | bytes 1441824 | tf_op jit(solution)/shard_map/ppermute | solution.py:76
  417.1 8.7 fusion.27
  425.9 9.1 fusion.296
  485.9 16.7 collective-permute-done.3
  528.2 12.3 copy.346
  555.6 38.1 %collective-permute-done.16 = bf16[2,256,2048]{2,1,0:T(8,128)(2,1)S(1)} collective-permute-done((bf16[2,256,2048]{2,1,0:T(8,128)(2,1)S(1)}, bf16[2,256,2048]{2,1,0:T(8,128)(2,1)S(1)}, u32[]{:S(2)}, u32[]{:S(2)}) %collective-permute-start.16) | collective-permute-done | bytes 2097184 | tf_op jit(solution)/shard_map/ppermute | solution.py:140
  602.0 7.6 collective-permute-done.17
  625.5 24.2 %select_reduce_fusion.2 = (s32[2048]{0:T(1024)S(1)}, s32[2048]{0:T(1024)S(1)}) fusion(s32[4,2048]{1,0:T(4,128)} %get-tuple-element.406, pred[4,2048]{1,0:T(4,128)(4,1)S(1)} %copy-done.120, s32[4,2048]{1,0:T(4,128)} %get-tuple-element.408), kind=kLoop, calls=%fused_computation.32 | loop fusion | flops 100659200 | bytes 90112 | tf_op jit(solution)/shard_map/reduce_sum | solution.py:471
  662.7 12.6 multiply_convert_fusion.6
  675.3 8.7 collective-permute-done.21
  684.0 12.8 multiply_convert_fusion.5
  696.8 8.4 slice.873
  719.4 11.0 fusion.297
  730.4 11.1 multiply_convert_fusion.12
  742.7 7.7 convolution_convert_fusion.7
  752.5 14.0 fusion.83
  766.4 8.4 convolution_convert_fusion.3
  800.9 11.5 fusion.82
  814.4 34.6 %fusion.58 = f32[2048,2816]{1,0:T(8,128)} fusion(bf16[2048,2816]{1,0:T(8,128)(2,1)} %constant_dynamic-update-slice_fusion.8, bf16[1024,2048]{1,0:T(8,128)(2,1)S(1)} %fusion.82, bf16[1024,2048]{1,0:T(8,128)(2,1)S(1)} %copy-done.143), kind=kOutput, calls=%fused_computation.143 | convolution fusion | flops 23639097344 | bytes 42991616 | tf_op jit(solution)/shard_map/dot_general | solution.py:60
  849.0 26.4 %multiply_convert_fusion.1 = (bf16[2048,1408]{1,0:T(8,128)(2,1)}, bf16[2048,1408]{1,0:T(8,128)(2,1)}, bf16[2048,1408]{1,0:T(8,128)(2,1)}) fusion(f32[2048,2816]{1,0:T(8,128)} %fusion.58, bf16[1408,2048]{1,0:T(8,128)(2,1)} %constant_dynamic-update-slice_fusion, bf16[1024,2048]{1,0:T(8,128)(2,1)} %multiply_convert_fusion.5, ...), kind=kOutput, calls=%fused_computation.80 | convolution fusion | flops 11871191040 | bytes 54525952 | tf_op jit(solution)/shard_map/dot_general | solution.py:64
  881.9 15.8 fusion.54
  897.7 10.1 fusion.48
  911.6 17.0 fusion.372
  932.3 12.0 fusion.42
  944.3 11.7 add_convert_fusion.2
  966.6 31.8 %fusion.30 = bf16[2048,2816]{1,0:T(8,128)(2,1)} fusion(bf16[2048,1408]{1,0:T(8,128)(2,1)} %get-tuple-element.504, bf16[2048,1408]{1,0:T(8,128)(2,1)} %get-tuple-element.505, bf16[1024,2048]{1,0:T(8,128)(2,1)} %copy-done.144, bf16[1024,2048]{1,0:T(8,128)(2,1)} %fusion.83), kind=kOutput, calls=%fused_computation.85 | convolution fusion | flops 23667933184 | bytes 31457280 | tf_op jit(solution)/shard_map/dot_general | solution.py:68
  1007.1 17.5 multiply_convert_fusion
  1024.6 14.6 collective-permute-done.39
  1042.3 18.9 %convolution_convert_fusion.2 = bf16[1408,2048]{1,0:T(8,128)(2,1)} fusion(bf16[2048,1408]{1,0:T(8,128)(2,1)} %get-tuple-element.422, bf16[1024,2048]{1,0:T(8,128)(2,1)} %multiply_convert_fusion.5, bf16[1024,2048]{1,0:T(8,128)(2,1)} %multiply_convert_fusion.6), kind=kOutput, calls=%fused_computation.127 | convolution fusion | flops 11830820864 | bytes 19922944 | tf_op jit(solution)/shard_map/dot_general | solution.py:68
  1061.2 27.5 %collective-permute-done.44 = bf16[256,2048]{1,0:T(8,128)(2,1)S(1)} collective-permute-done((bf16[256,2048]{1,0:T(8,128)(2,1)S(1)}, bf16[256,2048]{1,0:T(8,128)(2,1)S(1)}, u32[]{:S(2)}, u32[]{:S(2)}) %collective-permute-start.44) | collective-permute-done | bytes 1048608 | tf_op jit(solution)/shard_map/ppermute | solution.py:76
  1094.2 11.8 fusion.41
  1112.4 11.5 fusion.49
  1124.0 11.2 add_convert_fusion.1
  1208.6 7.3 pad_maximum_fusion.6
  1340.3 9.3 collective-permute-done.51
  1356.5 15.4 collective-permute-done.55
  1388.9 22.0 %collective-permute-done.56 = bf16[1,256,2048]{2,1,0:T(8,128)(2,1)} collective-permute-done((bf16[1,256,2048]{2,1,0:T(8,128)(2,1)}, bf16[1,256,2048]{2,1,0:T(8,128)(2,1)}, u32[]{:S(2)}, u32[]{:S(2)}) %collective-permute-start.56) | collective-permute-done | bytes 1048608 | tf_op jit(solution)/shard_map/ppermute | solution.py:140
  1428.4 64.5 %collective-permute-done.76 = bf16[512,2816]{1,0:T(8,128)(2,1)} collective-permute-done((bf16[512,2816]{1,0:T(8,128)(2,1)}, bf16[512,2816]{1,0:T(8,128)(2,1)}, u32[]{:S(2)}, u32[]{:S(2)}) %collective-permute-start.76) | collective-permute-done | bytes 2883616 | tf_op jit(solution)/shard_map/ppermute | solution.py:76
  1492.9 60.2 %collective-permute-done.77 = bf16[512,2816]{1,0:T(8,128)(2,1)} collective-permute-done((bf16[512,2816]{1,0:T(8,128)(2,1)}, bf16[512,2816]{1,0:T(8,128)(2,1)}, u32[]{:S(2)}, u32[]{:S(2)}) %collective-permute-start.77) | collective-permute-done | bytes 2883616 | tf_op jit(solution)/shard_map/ppermute | solution.py:76
  1553.1 7.4 add_convert_fusion.9
  1567.8 9.6 convolution_convert_fusion.6
  1583.0 9.0 fusion.60
  1602.8 135.9 %collective-permute-done.78 = bf16[512,2816]{1,0:T(8,128)(2,1)} collective-permute-done((bf16[512,2816]{1,0:T(8,128)(2,1)}, bf16[512,2816]{1,0:T(8,128)(2,1)}, u32[]{:S(2)}, u32[]{:S(2)}) %collective-permute-start.78) | collective-permute-done | bytes 2883616 | tf_op jit(solution)/shard_map/ppermute | solution.py:76
  1793.3 8.6 fusion.93
  (895 shorter events, 716.9 us)
Async XLA Ops:
  7.2 69.6 %collective-permute-start = (s32[2048,6]{0,1:T(8,128)}, s32[2048,6]{0,1:T(8,128)}, u32[]{:S(2)}, u32[]{:S(2)}) collective-permute-start(s32[2048,6]{0,1:T(8,128)} %param.47), channel_id=1, source_target_pairs={{0,16},{8,24},{16,0},{24,8},{1,17},{9,25},{17,1},{25,9},{2,18},{10... | collective-permute-start | bytes 147464 | tf_op jit(solution)/shard_map/ppermute | solution.py:76
  11.3 65.5 %collective-permute-start.1 = (f32[2048,6]{0,1:T(8,128)}, f32[2048,6]{0,1:T(8,128)}, u32[]{:S(2)}, u32[]{:S(2)}) collective-permute-start(f32[2048,6]{0,1:T(8,128)} %param.48), channel_id=1, source_target_pairs={{0,16},{8,24},{16,0},{24,8},{1,17},{9,25},{17,1},{25,9},{2,18},{10... | collective-permute-start | bytes 147464 | tf_op jit(solution)/shard_map/ppermute | solution.py:76
  40.8 78.2 %all-gather.11.cloned.1.call-start = ((), (), s32[]{:S(2)}) async-start(), calls=%async_computation.21 | async-start | bytes 2396160 | tf_op jit(solution)/shard_map/all_gather | solution.py:202
  76.9 128.1 %all-gather.13.cloned.1.call-start = ((), (), s32[]{:S(2)}) async-start(), calls=%async_computation.22 | async-start | bytes 1966080 | tf_op jit(solution)/shard_map/all_gather | solution.py:202
  87.4 47.0 %collective-permute-start.5 = (bf16[1,2048,256]{2,1,0:T(8,128)(2,1)S(1)}, bf16[1,2048,256]{2,1,0:T(8,128)(2,1)}, u32[]{:S(2)}, u32[]{:S(2)}) collective-permute-start(bf16[1,2048,256]{2,1,0:T(8,128)(2,1)S(1)} %bitcast.578), channel_id=1, source_target_pairs={{0,1},{1,0},{2,3},{3,2},{4,5},{5,4},{6,7},{7,6},{8,9},{9,8},{10,11... | collective-permute-start | bytes 3145736 | tf_op jit(solution)/shard_map/ppermute | solution.py:130
  87.4 44.1 %collective-permute-start.6 = (bf16[1,2048,256]{2,1,0:T(8,128)(2,1)S(1)}, bf16[1,2048,256]{2,1,0:T(8,128)(2,1)S(1)}, u32[]{:S(2)}, u32[]{:S(2)}) collective-permute-start(bf16[1,2048,256]{2,1,0:T(8,128)(2,1)S(1)} %bitcast.579), channel_id=1, source_target_pairs={{0,2},{1,5},{2,0},{3,7},{4,6},{5,1},{6,4},{7,3},{8,10},{9,13},{10,... | collective-permute-start | bytes 3145736 | tf_op jit(solution)/shard_map/ppermute | solution.py:140
  89.4 630.0 %all-gather.9.cloned.1.call-start = ((), (), s32[]{:S(2)}) async-start(), calls=%async_computation.14 | async-start | bytes 3604480 | tf_op jit(solution)/shard_map/all_gather | solution.py:202
  119.0 61.3 %all-to-all-start.3 = ((bf16[4,640,256]{2,1,0:T(8,128)(2,1)}), bf16[4,640,256]{2,1,0:T(8,128)(2,1)}, u32[]{:S(2)}, u32[]{:S(2)}) async-start(bf16[4,640,256]{2,1,0:T(8,128)(2,1)} %bitcast.610), calls=%async_computation.3 | async-start | bytes 2621440 | tf_op jit(solution)/shard_map/all_to_all | solution.py:232
  123.3 607.2 %all-gather.7.cloned.1.call-start = ((), (), s32[]{:S(2)}) async-start(), calls=%async_computation.13 | async-start | bytes 1802240 | tf_op jit(solution)/shard_map/all_gather | solution.py:202
  133.0 148.5 %collective-permute-start.8 = (bf16[2,2048,256]{2,1,0:T(8,128)(2,1)}, bf16[2,2048,256]{2,1,0:T(8,128)(2,1)}, u32[]{:S(2)}, u32[]{:S(2)}) collective-permute-start(bf16[2,2048,256]{2,1,0:T(8,128)(2,1)} %pad_maximum_fusion.23), channel_id=1, source_target_pairs={{0,4},{1,3},{2,6},{3,1},{4,0},{5,7},{6,2},{7,5},{8,12},{9,11},{10,... | collective-permute-start | bytes 6291464 | tf_op jit(solution)/shard_map/ppermute | solution.py:140
  134.5 68.1 %collective-permute-start.7 = (bf16[1,2048,256]{2,1,0:T(8,128)(2,1)S(1)}, bf16[1,2048,256]{2,1,0:T(8,128)(2,1)}, u32[]{:S(2)}, u32[]{:S(2)}) collective-permute-start(bf16[1,2048,256]{2,1,0:T(8,128)(2,1)S(1)} %collective-permute-done.6), channel_id=1, source_target_pairs={{0,1},{1,0},{2,3},{3,2},{4,5},{5,4},{6,7},{7,6},{8,9},{9,8},{10,11... | collective-permute-start | bytes 3145736 | tf_op jit(solution)/shard_map/ppermute | solution.py:130
  186.2 84.2 %collective-permute-start.29 = (bf16[2048,256]{1,0:T(8,128)(2,1)}, bf16[2048,256]{1,0:T(8,128)(2,1)}, u32[]{:S(2)}, u32[]{:S(2)}) collective-permute-start(bf16[2048,256]{1,0:T(8,128)(2,1)} %fusion.115), channel_id=1, source_target_pairs={{0,16},{8,24},{16,0},{24,8},{1,17},{9,25},{17,1},{25,9},{2,18},{10... | collective-permute-start | bytes 3145736 | tf_op jit(solution)/shard_map/ppermute | solution.py:76
  186.2 324.5 %collective-permute-start.2 = (bf16[512,2816]{1,0:T(8,128)(2,1)}, bf16[512,2816]{1,0:T(8,128)(2,1)}, u32[]{:S(2)}, u32[]{:S(2)}) collective-permute-start(bf16[512,2816]{1,0:T(8,128)(2,1)} %pad_maximum_fusion.17), channel_id=1, source_target_pairs={{0,8},{8,0},{16,24},{24,16},{1,9},{9,1},{17,25},{25,17},{2,10},{10... | collective-permute-start | bytes 8650760 | tf_op jit(solution)/shard_map/ppermute | solution.py:76
  186.3 299.5 %collective-permute-start.35 = (bf16[1408,512]{1,0:T(8,128)(2,1)}, bf16[1408,512]{1,0:T(8,128)(2,1)}, u32[]{:S(2)}, u32[]{:S(2)}) collective-permute-start(bf16[1408,512]{1,0:T(8,128)(2,1)} %get-tuple-element.419), channel_id=1, source_target_pairs={{0,8},{8,0},{16,24},{24,16},{1,9},{9,1},{17,25},{25,17},{2,10},{10... | collective-permute-start | bytes 4325384 | tf_op jit(solution)/shard_map/ppermute | solution.py:76
  209.5 580.2 %reduce-scatter.17.cloned.1.call-start = ((), (), s32[]{:S(2)}) async-start(), calls=%async_computation.20 | async-start | bytes 1802240 | tf_op jit(solution)/shard_map/reduce_scatter | solution.py:211
  213.7 74.8 %collective-permute-start.10 = (bf16[1,256,576]{2,1,0:T(8,128)(2,1)S(1)}, bf16[1,256,576]{2,1,0:T(8,128)(2,1)}, u32[]{:S(2)}, u32[]{:S(2)}) collective-permute-start(bf16[1,256,576]{2,1,0:T(8,128)(2,1)S(1)} %broadcast_in_dim.239), channel_id=1, source_target_pairs={{0,1},{1,0},{2,3},{3,2},{4,5},{5,4},{6,7},{7,6},{8,9},{9,8},{10,11... | collective-permute-start | bytes 884744 | tf_op jit(solution)/shard_map/ppermute | solution.py:130
  281.5 123.1 %collective-permute-start.9 = (bf16[2,2048,256]{2,1,0:T(8,128)(2,1)}, bf16[2,2048,256]{2,1,0:T(8,128)(2,1)}, u32[]{:S(2)}, u32[]{:S(2)}) collective-permute-start(bf16[2,2048,256]{2,1,0:T(8,128)(2,1)} %collective-permute-done.8), channel_id=1, source_target_pairs={{0,1},{1,0},{2,3},{3,2},{4,5},{5,4},{6,7},{7,6},{8,9},{9,8},{10,11... | collective-permute-start | bytes 6291464 | tf_op jit(solution)/shard_map/ppermute | solution.py:130
  290.1 113.2 %collective-permute-start.36 = (bf16[1408,512]{1,0:T(8,128)(2,1)}, bf16[1408,512]{1,0:T(8,128)(2,1)}, u32[]{:S(2)}, u32[]{:S(2)}) collective-permute-start(bf16[1408,512]{1,0:T(8,128)(2,1)} %get-tuple-element.420), channel_id=1, source_target_pairs={{0,16},{8,24},{16,0},{24,8},{1,17},{9,25},{17,1},{25,9},{2,18},{10... | collective-permute-start | bytes 4325384 | tf_op jit(solution)/shard_map/ppermute | solution.py:76
  298.1 204.5 %collective-permute-start.3 = (bf16[512,2816]{1,0:T(8,128)(2,1)}, bf16[512,2816]{1,0:T(8,128)(2,1)}, u32[]{:S(2)}, u32[]{:S(2)}) collective-permute-start(bf16[512,2816]{1,0:T(8,128)(2,1)} %pad_maximum_fusion.18), channel_id=1, source_target_pairs={{0,16},{8,24},{16,0},{24,8},{1,17},{9,25},{17,1},{25,9},{2,18},{10... | collective-permute-start | bytes 8650760 | tf_op jit(solution)/shard_map/ppermute | solution.py:76
  403.3 114.6 %collective-permute-start.31 = (bf16[1,4096,256]{2,1,0:T(8,128)(2,1)}, bf16[1,4096,256]{2,1,0:T(8,128)(2,1)}, u32[]{:S(2)}, u32[]{:S(2)}) collective-permute-start(bf16[1,4096,256]{2,1,0:T(8,128)(2,1)} %get-tuple-element.584), channel_id=1, source_target_pairs={{0,2},{1,5},{2,0},{3,7},{4,6},{5,1},{6,4},{7,3},{8,10},{9,13},{10,... | collective-permute-start | bytes 6291464 | tf_op jit(solution)/shard_map/ppermute | solution.py:140
  404.7 103.1 %collective-permute-start.37 = (bf16[1408,512]{1,0:T(8,128)(2,1)}, bf16[1408,512]{1,0:T(8,128)(2,1)}, u32[]{:S(2)}, u32[]{:S(2)}) collective-permute-start(bf16[1408,512]{1,0:T(8,128)(2,1)} %collective-permute-done.36), channel_id=1, source_target_pairs={{0,8},{8,0},{16,24},{24,16},{1,9},{9,1},{17,25},{25,17},{2,10},{10... | collective-permute-start | bytes 4325384 | tf_op jit(solution)/shard_map/ppermute | solution.py:76
  507.8 87.5 %collective-permute-start.4 = (bf16[512,2816]{1,0:T(8,128)(2,1)}, bf16[512,2816]{1,0:T(8,128)(2,1)}, u32[]{:S(2)}, u32[]{:S(2)}) collective-permute-start(bf16[512,2816]{1,0:T(8,128)(2,1)} %collective-permute-done.3), channel_id=1, source_target_pairs={{0,8},{8,0},{16,24},{24,16},{1,9},{9,1},{17,25},{25,17},{2,10},{10... | collective-permute-start | bytes 8650760 | tf_op jit(solution)/shard_map/ppermute | solution.py:76
  522.5 76.4 %collective-permute-start.33 = (bf16[2,4096,256]{2,1,0:T(8,128)(2,1)}, bf16[2,4096,256]{2,1,0:T(8,128)(2,1)}, u32[]{:S(2)}, u32[]{:S(2)}) collective-permute-start(bf16[2,4096,256]{2,1,0:T(8,128)(2,1)} %pad_maximum_fusion.12), channel_id=1, source_target_pairs={{0,4},{1,3},{2,6},{3,1},{4,0},{5,7},{6,2},{7,5},{8,12},{9,11},{10,... | collective-permute-start | bytes 12582920 | tf_op jit(solution)/shard_map/ppermute | solution.py:140
  545.6 48.1 %collective-permute-start.16 = (bf16[2,256,2048]{2,1,0:T(8,128)(2,1)S(1)}, bf16[2,256,2048]{2,1,0:T(8,128)(2,1)S(1)}, u32[]{:S(2)}, u32[]{:S(2)}) collective-permute-start(bf16[2,256,2048]{2,1,0:T(8,128)(2,1)S(1)} %slice.851), channel_id=1, source_target_pairs={{0,4},{1,3},{2,6},{3,1},{4,0},{5,7},{6,2},{7,5},{8,12},{9,11},{10,... | collective-permute-start | bytes 6291464 | tf_op jit(solution)/shard_map/ppermute | solution.py:140
  598.9 51.4 %collective-permute-start.34 = (bf16[2,4096,256]{2,1,0:T(8,128)(2,1)}, bf16[2,4096,256]{2,1,0:T(8,128)(2,1)}, u32[]{:S(2)}, u32[]{:S(2)}) collective-permute-start(bf16[2,4096,256]{2,1,0:T(8,128)(2,1)} %collective-permute-done.33), channel_id=1, source_target_pairs={{0,1},{1,0},{2,3},{3,2},{4,5},{5,4},{6,7},{7,6},{8,9},{9,8},{10,11... | collective-permute-start | bytes 12582920 | tf_op jit(solution)/shard_map/ppermute | solution.py:130
  616.6 88.6 %collective-permute-start.18 = (bf16[1,256,2048]{2,1,0:T(8,128)(2,1)S(1)}, bf16[1,256,2048]{2,1,0:T(8,128)(2,1)}, u32[]{:S(2)}, u32[]{:S(2)}) collective-permute-start(bf16[1,256,2048]{2,1,0:T(8,128)(2,1)S(1)} %bitcast.572), channel_id=1, source_target_pairs={{0,1},{1,0},{2,3},{3,2},{4,5},{5,4},{6,7},{7,6},{8,9},{9,8},{10,11... | collective-permute-start | bytes 3145736 | tf_op jit(solution)/shard_map/ppermute | solution.py:130
  616.6 101.0 %collective-permute-start.23 = (bf16[256,2048]{1,0:T(8,128)(2,1)S(1)}, bf16[256,2048]{1,0:T(8,128)(2,1)S(1)}, u32[]{:S(2)}, u32[]{:S(2)}) collective-permute-start(bf16[256,2048]{1,0:T(8,128)(2,1)S(1)} %get-tuple-element.492), channel_id=1, source_target_pairs={{0,16},{8,24},{16,0},{24,8},{1,17},{9,25},{17,1},{25,9},{2,18},{10... | collective-permute-start | bytes 3145736 | tf_op jit(solution)/shard_map/ppermute | solution.py:76
  719.2 64.6 %collective-permute-start.24 = (bf16[1,256,2048]{2,1,0:T(8,128)(2,1)S(1)}, bf16[1,256,2048]{2,1,0:T(8,128)(2,1)}, u32[]{:S(2)}, u32[]{:S(2)}) collective-permute-start(bf16[1,256,2048]{2,1,0:T(8,128)(2,1)S(1)} %bitcast.576), channel_id=1, source_target_pairs={{0,1},{1,0},{2,3},{3,2},{4,5},{5,4},{6,7},{7,6},{8,9},{9,8},{10,11... | collective-permute-start | bytes 3145736 | tf_op jit(solution)/shard_map/ppermute | solution.py:130
  750.4 582.1 %reduce-scatter.15.cloned.1.call-start = ((), (), s32[]{:S(2)}) async-start(), calls=%async_computation.19 | async-start | bytes 3604480 | tf_op jit(solution)/shard_map/reduce_scatter | solution.py:211
  783.7 961.8 %reduce-scatter.9.cloned.1.call-start = ((), (), s32[]{:S(2)}) async-start(), calls=%async_computation.16 | async-start | bytes 409600 | tf_op jit(solution)/shard_map/reduce_scatter | solution.py:211
  1042.1 46.6 %collective-permute-start.44 = (bf16[256,2048]{1,0:T(8,128)(2,1)S(1)}, bf16[256,2048]{1,0:T(8,128)(2,1)S(1)}, u32[]{:S(2)}, u32[]{:S(2)}) collective-permute-start(bf16[256,2048]{1,0:T(8,128)(2,1)S(1)} %fusion.191), channel_id=1, source_target_pairs={{0,16},{8,24},{16,0},{24,8},{1,17},{9,25},{17,1},{25,9},{2,18},{10... | collective-permute-start | bytes 3145736 | tf_op jit(solution)/shard_map/ppermute | solution.py:76
  1215.9 73.4 %collective-permute-start.50 = (bf16[4,2,256,2048]{3,2,1,0:T(8,128)(2,1)}, bf16[4,2,256,2048]{3,2,1,0:T(8,128)(2,1)}, u32[]{:S(2)}, u32[]{:S(2)}) collective-permute-start(bf16[4,2,256,2048]{3,2,1,0:T(8,128)(2,1)} %pad_maximum_fusion.6), channel_id=1, source_target_pairs={{0,1},{1,0},{2,3},{3,2},{4,5},{5,4},{6,7},{7,6},{8,9},{9,8},{10,11... | collective-permute-start | bytes 25165832 | tf_op jit(solution)/shard_map/ppermute | solution.py:130
  1272.3 46.3 %collective-permute-start.54 = (bf16[4,256,2048]{2,1,0:T(8,128)(2,1)}, bf16[4,256,2048]{2,1,0:T(8,128)(2,1)}, u32[]{:S(2)}, u32[]{:S(2)}) collective-permute-start(bf16[4,256,2048]{2,1,0:T(8,128)(2,1)} %pad_maximum_fusion.15), channel_id=1, source_target_pairs={{0,1},{1,0},{2,3},{3,2},{4,5},{5,4},{6,7},{7,6},{8,9},{9,8},{10,11... | collective-permute-start | bytes 12582920 | tf_op jit(solution)/shard_map/ppermute | solution.py:130
  1282.2 95.1 %collective-permute-start.80 = (bf16[1408,512]{1,0:T(8,128)(2,1)}, bf16[1408,512]{1,0:T(8,128)(2,1)}, u32[]{:S(2)}, u32[]{:S(2)}) collective-permute-start(bf16[1408,512]{1,0:T(8,128)(2,1)} %get-tuple-element.556), channel_id=1, source_target_pairs={{0,8},{8,0},{16,24},{24,16},{1,9},{9,1},{17,25},{25,17},{2,10},{10... | collective-permute-start | bytes 4325384 | tf_op jit(solution)/shard_map/ppermute | solution.py:76
  1300.8 48.8 %collective-permute-start.51 = (bf16[2,2,256,2048]{3,2,1,0:T(8,128)(2,1)}, bf16[2,2,256,2048]{3,2,1,0:T(8,128)(2,1)}, u32[]{:S(2)}, u32[]{:S(2)}) collective-permute-start(bf16[2,2,256,2048]{3,2,1,0:T(8,128)(2,1)} %slice.896), channel_id=1, source_target_pairs={{0,4},{1,3},{2,6},{3,1},{4,0},{5,7},{6,2},{7,5},{8,12},{9,11},{10,... | collective-permute-start | bytes 12582920 | tf_op jit(solution)/shard_map/ppermute | solution.py:140
  1309.7 287.3 %collective-permute-start.79 = (bf16[1408,512]{1,0:T(8,128)(2,1)}, bf16[1408,512]{1,0:T(8,128)(2,1)}, u32[]{:S(2)}, u32[]{:S(2)}) collective-permute-start(bf16[1408,512]{1,0:T(8,128)(2,1)} %get-tuple-element.555), channel_id=1, source_target_pairs={{0,8},{8,0},{16,24},{24,16},{1,9},{9,1},{17,25},{25,17},{2,10},{10... | collective-permute-start | bytes 4325384 | tf_op jit(solution)/shard_map/ppermute | solution.py:76
  1313.2 179.7 %collective-permute-start.76 = (bf16[512,2816]{1,0:T(8,128)(2,1)}, bf16[512,2816]{1,0:T(8,128)(2,1)}, u32[]{:S(2)}, u32[]{:S(2)}) collective-permute-start(bf16[512,2816]{1,0:T(8,128)(2,1)} %get-tuple-element.517), channel_id=1, source_target_pairs={{0,8},{8,0},{16,24},{24,16},{1,9},{9,1},{17,25},{25,17},{2,10},{10... | collective-permute-start | bytes 8650760 | tf_op jit(solution)/shard_map/ppermute | solution.py:76
  1325.7 46.3 %collective-permute-start.55 = (bf16[2,256,2048]{2,1,0:T(8,128)(2,1)}, bf16[2,256,2048]{2,1,0:T(8,128)(2,1)S(1)}, u32[]{:S(2)}, u32[]{:S(2)}) collective-permute-start(bf16[2,256,2048]{2,1,0:T(8,128)(2,1)} %slice.907), channel_id=1, source_target_pairs={{0,4},{1,3},{2,6},{3,1},{4,0},{5,7},{6,2},{7,5},{8,12},{9,11},{10,... | collective-permute-start | bytes 6291464 | tf_op jit(solution)/shard_map/ppermute | solution.py:140
  1332.5 424.9 %reduce-scatter.11.cloned.1.call-start = ((), (), s32[]{:S(2)}) async-start(), calls=%async_computation.17 | async-start | bytes 655360 | tf_op jit(solution)/shard_map/reduce_scatter | solution.py:211
  1340.0 419.0 %reduce-scatter.13.cloned.1.call-start = ((), (), s32[]{:S(2)}) async-start(), calls=%async_computation.18 | async-start | bytes 1310720 | tf_op jit(solution)/shard_map/reduce_scatter | solution.py:211
  1349.6 203.5 %collective-permute-start.77 = (bf16[512,2816]{1,0:T(8,128)(2,1)}, bf16[512,2816]{1,0:T(8,128)(2,1)}, u32[]{:S(2)}, u32[]{:S(2)}) collective-permute-start(bf16[512,2816]{1,0:T(8,128)(2,1)} %get-tuple-element.518), channel_id=1, source_target_pairs={{0,8},{8,0},{16,24},{24,16},{1,9},{9,1},{17,25},{25,17},{2,10},{10... | collective-permute-start | bytes 8650760 | tf_op jit(solution)/shard_map/ppermute | solution.py:76
  1373.3 41.2 %collective-permute-start.52 = (bf16[1,2,256,2048]{3,2,1,0:T(8,128)(2,1)}, bf16[1,2,256,2048]{3,2,1,0:T(8,128)(2,1)}, u32[]{:S(2)}, u32[]{:S(2)}) collective-permute-start(bf16[1,2,256,2048]{3,2,1,0:T(8,128)(2,1)} %slice.898), channel_id=1, source_target_pairs={{0,2},{1,5},{2,0},{3,7},{4,6},{5,1},{6,4},{7,3},{8,10},{9,13},{10,... | collective-permute-start | bytes 6291464 | tf_op jit(solution)/shard_map/ppermute | solution.py:140
  1410.9 186.1 %collective-permute-start.81 = (bf16[1408,512]{1,0:T(8,128)(2,1)}, bf16[1408,512]{1,0:T(8,128)(2,1)}, u32[]{:S(2)}, u32[]{:S(2)}) collective-permute-start(bf16[1408,512]{1,0:T(8,128)(2,1)} %add_convert_fusion.14), channel_id=1, source_target_pairs={{0,16},{8,24},{16,0},{24,8},{1,17},{9,25},{17,1},{25,9},{2,18},{10... | collective-permute-start | bytes 4325384 | tf_op jit(solution)/shard_map/ppermute | solution.py:76
  1418.3 142.1 %collective-permute-start.53 = (bf16[256,2048]{1,0:T(8,128)(2,1)}, bf16[256,2048]{1,0:T(8,128)(2,1)}, u32[]{:S(2)}, u32[]{:S(2)}) collective-permute-start(bf16[256,2048]{1,0:T(8,128)(2,1)} %fusion.192), channel_id=1, source_target_pairs={{0,16},{8,24},{16,0},{24,8},{1,17},{9,25},{17,1},{25,9},{2,18},{10... | collective-permute-start | bytes 3145736 | tf_op jit(solution)/shard_map/ppermute | solution.py:76
  1424.2 139.1 %all-to-all-start.5 = ((bf16[256,8,256]{2,0,1:T(8,128)(2,1)}), bf16[256,8,256]{2,0,1:T(8,128)(2,1)}, u32[]{:S(2)}, u32[]{:S(2)}) async-start(bf16[256,8,256]{2,0,1:T(8,128)(2,1)} %bitcast.519), calls=%async_computation.5 | async-start | bytes 2097152 | tf_op jit(solution)/shard_map/all_to_all | solution.py:614
  1560.5 178.3 %collective-permute-start.78 = (bf16[512,2816]{1,0:T(8,128)(2,1)}, bf16[512,2816]{1,0:T(8,128)(2,1)}, u32[]{:S(2)}, u32[]{:S(2)}) collective-permute-start(bf16[512,2816]{1,0:T(8,128)(2,1)} %get-tuple-element.516), channel_id=1, source_target_pairs={{0,16},{8,24},{16,0},{24,8},{1,17},{9,25},{17,1},{25,9},{2,18},{10... | collective-permute-start | bytes 8650760 | tf_op jit(solution)/shard_map/ppermute | solution.py:76
  1567.5 193.2 %reduce-scatter.7.cloned.1.call-start = ((), (), s32[]{:S(2)}) async-start(), calls=%async_computation.15 | async-start | bytes 1966080 | tf_op jit(solution)/shard_map/reduce_scatter | solution.py:211
  1591.9 201.3 %all-to-all-start.6 = ((bf16[4,640,512]{2,1,0:T(8,128)(2,1)}), bf16[4,640,512]{2,1,0:T(8,128)(2,1)}, u32[]{:S(2)}, u32[]{:S(2)}) async-start(bf16[4,640,512]{2,1,0:T(8,128)(2,1)} %bitcast.585), calls=%async_computation.6 | async-start | bytes 5242880 | tf_op jit(solution)/shard_map/all_to_all | solution.py:232
  (208 other events, 3905.9 us)
Sparse Core Ops, SparseCore 0:
  77.0 41.8 all-gather.10
  121.1 58.7 all-gather.12
  182.0 102.6 all-gather.8
  286.2 97.2 all-gather.6
  750.6 30.6 reduce-scatter.16
  783.8 54.6 reduce-scatter.14
  1332.6 20.4 reduce-scatter.8
  1356.0 25.7 reduce-scatter.10
  1389.0 85.6 reduce-scatter.12
  1577.5 94.2 reduce-scatter.6
